TPU v7x, 32 devices: a whole 2x2x4 slice. The times are simulated.
32 devices in a mesh: dp: 8 (over y, x, core), tensor: 4 (over z).
Axes of the slice: x: 2, y: 2, z: 4, core: 2. Of those that a mesh axis runs over, the one named last changes fastest.
Arguments:
- tokens: bfloat16 [13312, 1152], P(('dp', 'tensor')), may hold values from -6 to 6
- cotangent: bfloat16 [13312, 1152], P(('dp', 'tensor')), may hold values from -6 to 6
- item_bucket: int32 [13], replicated, may hold values from 0 to 2
- text_len: int32 [13], replicated, may hold values from 75 to 300
- t_mod: float32 [13, 6, 1152], replicated, may hold values from -1.75 to 1.75
- text_tokens: bfloat16 [300, 1152], P('tensor'), may hold values from -6 to 6
- shift_table: float32 [6, 1152], replicated, may hold values from 0.5 to 1.5
- w_qkv: bfloat16 [1152, 3, 1152], P(None, None, 'tensor'), may hold values from -0.1875 to 0.1875
- w_out: bfloat16 [1152, 1152], P('tensor'), may hold values from -0.1875 to 0.1875
- out_bias: float32 [1152], replicated, may hold values from -1.75 to 1.75
- w_xq: bfloat16 [1152, 1152], P(None, 'tensor'), may hold values from -0.1875 to 0.1875
- xq_bias: float32 [1152], P('tensor'), may hold values from -1.75 to 1.75
- w_xkv: bfloat16 [1152, 2, 1152], P(None, None, 'tensor'), may hold values from -0.1875 to 0.1875
- xv_bias: float32 [1152], P('tensor'), may hold values from -0.625 to 0.625
- w_xo: bfloat16 [1152, 1152], P('tensor'), may hold values from -1.5 to 1.5
- xo_bias: float32 [1152], replicated, may hold values from -1.75 to 1.75
- w_in: bfloat16 [1152, 2, 2880], P(None, None, 'tensor'), may hold values from -0.1875 to 0.1875
- in_bias: float32 [2, 2880], P(None, 'tensor'), may hold values from -1.75 to 1.75
- dw_weight: float32 [9, 2, 2880], P(None, None, 'tensor'), may hold values from -2 to 2
- dw_bias: float32 [2, 2880], P(None, 'tensor'), may hold values from -1.75 to 1.75
- w_pt: bfloat16 [2880, 1152], P('tensor'), may hold values from -0.109375 to 0.109375
Outputs:
- out_tokens: bfloat16 [13312, 1152], P(('dp', 'tensor'))
- d_tokens: float32 [13312, 1152], P(('dp', 'tensor'))
- d_t_mod: float32 [13, 6, 1152], replicated
- d_text: float32 [300, 1152], P('tensor')
- d_shift_table: float32 [6, 1152], replicated
- d_w_qkv: float32 [1152, 3, 1152], P(None, None, 'tensor')
- d_w_out: float32 [1152, 1152], P('tensor')
- d_out_bias: float32 [1152], replicated
- d_w_xq: float32 [1152, 1152], P(None, 'tensor')
- d_xq_bias: float32 [1152], P('tensor')
- d_w_xkv: float32 [1152, 2, 1152], P(None, None, 'tensor')
- d_xv_bias: float32 [1152], P('tensor')
- d_w_xo: float32 [1152, 1152], P('tensor')
- d_xo_bias: float32 [1152], replicated
- d_w_in: float32 [1152, 2, 2880], P(None, None, 'tensor')
- d_in_bias: float32 [2, 2880], P(None, 'tensor')
- d_dw_weight: float32 [9, 2, 2880], P(None, None, 'tensor')
- d_dw_bias: float32 [2, 2880], P(None, 'tensor')
- d_w_pt: float32 [2880, 1152], P('tensor')
All inputs are finite; a program needn't handle non-finite values.
Results may differ from a plain program's by a relative error of at most 0.035.
Values may be sent and summed in bfloat16 or wider, within the bound.
No kernel may reach another device: no remote copies, remote signals or barrier semaphores. Data moves between devices by JAX's collectives and lax.ppermute only.
A program may use at most 320 MiB of HBM per device.

v0:
```python
import jax
import jax.numpy as jnp
from jax import lax
from jax.sharding import PartitionSpec as P

HEAD = 32
XHEAD = 72
TXT = 300
SIDE = 32
ITEM_SLOTS = 1024
HALO = 41


norm_eps = 1e-06
highest = lax.Precision.HIGHEST


def padded(block, sides, width):
    for axis, dim in sides:
        count = lax.axis_size(axis)
        forward = [(i, i + 1) for i in range(count - 1)]
        backward = [(target, source) for source, target in forward]
        low = lax.ppermute(
            lax.slice_in_dim(block, block.shape[dim] - width, None, axis=dim), axis, forward
        )
        high = lax.ppermute(lax.slice_in_dim(block, 0, width, axis=dim), axis, backward)
        block = jnp.concatenate([low, block, high], axis=dim)
    return block


def grid_table(bucket):
    grid_height = jnp.where(
        bucket == 0, SIDE, jnp.where(bucket == 1, 3 * SIDE // 4, 3 * SIDE // 2)
    ).astype(jnp.int32)
    grid_width = jnp.where(
        bucket == 0, SIDE, jnp.where(bucket == 1, 5 * SIDE // 4, 5 * SIDE // 8)
    ).astype(jnp.int32)
    return (grid_height, grid_width)


def inside_tap(inner_pos, grid_height, grid_width, row_step, col_step):
    grid_row = inner_pos // grid_width
    grid_col = inner_pos % grid_width
    return (
        (inner_pos < grid_height * grid_width)
        & (grid_row + row_step >= 0)
        & (grid_row + row_step < grid_height)
        & (grid_col + col_step >= 0)
        & (grid_col + col_step < grid_width)
    )


def norm_parts(values):
    centred = values - jnp.mean(values, axis=-1, keepdims=True)
    inv_std = lax.rsqrt(jnp.mean(centred * centred, axis=-1, keepdims=True) + norm_eps)
    return (centred * inv_std, inv_std)


def norm_back(grad_in, normal, inv_std, scale):
    scaled = grad_in * (1.0 + scale)
    return (
        scaled
        - jnp.mean(scaled, axis=-1, keepdims=True)
        - normal * jnp.mean(scaled * normal, axis=-1, keepdims=True)
    ) * inv_std


def silu_slope(values):
    sig_val = jax.nn.sigmoid(values)
    return sig_val * (1.0 + values * (1.0 - sig_val))


def spread_rows(tables, first_item, item_of, window):
    padding = jnp.zeros((window,) + tables.shape[1:], tables.dtype)
    picked = lax.dynamic_slice_in_dim(
        jnp.concatenate([padding, tables, padding], axis=0), first_item + window, window, 0
    )
    result = jnp.zeros((item_of.shape[0],) + tables.shape[1:], tables.dtype)
    for column in range(window):
        row_hit = (item_of == first_item + column).reshape((-1,) + (1,) * (tables.ndim - 1))
        result = jnp.where(row_hit, picked[column][None], result)
    return result


def place_items(pieces, first_item, window, item_count):
    placed = []
    for piece_rows in pieces:
        zero_rows = jnp.zeros((item_count + 2 * window,) + piece_rows.shape[1:], jnp.float32)
        placed.append(
            lax.dynamic_update_slice_in_dim(zero_rows, piece_rows, first_item + window, 0)[
                window : window + item_count
            ]
        )
    return tuple(placed)


def gather_rows(values):
    return lax.all_gather(values, "tensor", axis=0, tiled=True)


def grid_halo(values):
    return padded(values, (("dp", 0),), HALO)


def sum_rows(project, source):
    return lax.psum_scatter(project(source), "tensor", scatter_dimension=0, tiled=True)


def item_sums(part_one, part_two, first_item, window, span_start, span_rows):
    flat_rows = jnp.concatenate(
        [part_one.reshape(window, -1), part_two.reshape(window, -1)], axis=1
    )
    near_rows = padded(flat_rows.astype(jnp.bfloat16), (("dp", 0),), window).astype(flat_rows.dtype)
    padding = jnp.zeros_like(flat_rows)
    below_first = (span_start - span_rows) // ITEM_SLOTS
    above_first = (span_start + span_rows) // ITEM_SLOTS
    from_below = lax.dynamic_slice_in_dim(
        jnp.concatenate([near_rows[:window], padding], axis=0), first_item - below_first, window, 0
    )
    from_above = lax.dynamic_slice_in_dim(
        jnp.concatenate([padding, near_rows[2 * window :]], axis=0),
        window - (above_first - first_item),
        window,
        0,
    )
    summed = flat_rows + from_below + from_above
    split_at = part_one[0].size
    return (
        summed[:, :split_at].reshape(part_one.shape),
        summed[:, split_at:].reshape(part_two.shape),
    )


def tap_rows(extended, span_rows, bucket, row_step, col_step):
    if row_step == 0:
        return lax.slice_in_dim(extended, HALO + col_step, HALO + col_step + span_rows, axis=0)
    shifted = []
    for grid_width in (SIDE, 5 * SIDE // 4, 5 * SIDE // 8):
        begin = HALO + row_step * grid_width + col_step
        shifted.append(lax.slice_in_dim(extended, begin, begin + span_rows, axis=0))
    return jnp.where(
        (bucket == 0)[:, None],
        shifted[0],
        jnp.where((bucket == 1)[:, None], shifted[1], shifted[2]),
    )


def local(
    tokens,
    cotangent,
    item_bucket,
    text_len,
    t_mod,
    text_tokens,
    shift_table,
    w_qkv,
    w_out,
    out_bias,
    w_xq,
    xq_bias,
    w_xkv,
    xv_bias,
    w_xo,
    xo_bias,
    w_in,
    in_bias,
    dw_weight,
    dw_bias,
    w_pt,
):
    bfloat = jnp.bfloat16
    single = jnp.float32
    group_size = lax.axis_size("tensor")
    own_rows = tokens.shape[0]
    span_rows = own_rows * group_size
    item_count = t_mod.shape[0]
    heads_here = w_qkv.shape[2] // HEAD
    xheads_here = w_xq.shape[1] // XHEAD
    channels = w_in.shape[2]
    scale_x = XHEAD ** (-0.5)
    group_index = lax.axis_index("tensor")
    span_start = lax.axis_index("dp") * span_rows
    own_start = span_start + group_index * own_rows
    window_s = span_rows // ITEM_SLOTS + 2
    window_r = own_rows // ITEM_SLOTS + 2
    first_s = span_start // ITEM_SLOTS
    first_r = own_start // ITEM_SLOTS
    places_s = span_start + jnp.arange(span_rows, dtype=jnp.int32)
    item_s = places_s // ITEM_SLOTS
    inner_s = places_s % ITEM_SLOTS
    item_r = (own_start + jnp.arange(own_rows, dtype=jnp.int32)) // ITEM_SLOTS
    bucket_s = spread_rows(item_bucket, first_s, item_s, window_s)
    height_s, width_s = grid_table(bucket_s)
    valid_s = inner_s < height_s * width_s
    valid_r = lax.dynamic_slice_in_dim(valid_s, group_index * own_rows, own_rows, 0)
    live_r = valid_r.astype(single)[:, None]
    row_mod = spread_rows(shift_table[None] + t_mod, first_r, item_r, window_r)
    shift_a, scale_a, gate_a, shift_f, scale_f, gate_f = [row_mod[:, number] for number in range(6)]
    tokens_f = tokens.astype(single)
    normal_a, inv_std_a = norm_parts(tokens_f)
    normed = (normal_a * (1.0 + scale_a) + shift_a).astype(bfloat)
    normed_all = gather_rows(normed)
    qkv = jnp.einsum("nd,dke->nke", normed_all, w_qkv, preferred_element_type=single)
    query_h = jax.nn.softplus(qkv[:, 0]).astype(bfloat).reshape(span_rows, heads_here, HEAD)
    keys_h = jax.nn.softplus(qkv[:, 1]).astype(bfloat).reshape(span_rows, heads_here, HEAD)
    values_h = qkv[:, 2].astype(bfloat).reshape(span_rows, heads_here, HEAD)
    item_ids = first_s + jnp.arange(window_s, dtype=jnp.int32)
    picked = item_s[:, None] == item_ids[None, :]
    picked_live = picked & valid_s[:, None]
    keys_pick = jnp.where(picked_live[:, :, None, None], keys_h[:, None], jnp.zeros((), bfloat))
    state_part = jnp.einsum("njhd,nhe->jhde", keys_pick, values_h, preferred_element_type=single)
    total_part = jnp.einsum(
        "nj,nhd->jhd", picked_live.astype(bfloat), keys_h, preferred_element_type=single
    )
    kv_state, key_total = item_sums(
        state_part, total_part, first_s, window_s, span_start, span_rows
    )
    pick_f = picked.astype(single)
    query_f = query_h.astype(single)
    numerator = jnp.einsum(
        "nj,njhe->nhe",
        pick_f,
        jnp.einsum("nhd,jhde->njhe", query_f, kv_state, precision=highest),
        precision=highest,
    )
    denominator = jnp.einsum(
        "nj,njh->nh",
        pick_f,
        jnp.einsum("nhd,jhd->njh", query_f, key_total, precision=highest),
        precision=highest,
    )
    attn_ratio = numerator / denominator[:, :, None]
    attn = attn_ratio.astype(bfloat).reshape(span_rows, heads_here * HEAD)
    attn_out = (
        sum_rows(lambda piece_rows: jnp.dot(piece_rows, w_out, preferred_element_type=single), attn)
        + out_bias
    )
    after_attn = tokens_f + live_r * gate_a * attn_out
    cross_in = after_attn.astype(bfloat)
    cross_all = gather_rows(cross_in)
    text_all = gather_rows(text_tokens)
    text_kv = jnp.einsum("td,dke->tke", text_all, w_xkv, preferred_element_type=single)
    xkeys = text_kv[:, 0].astype(bfloat).reshape(TXT, xheads_here, XHEAD)
    xvals = (text_kv[:, 1] + xv_bias).astype(bfloat).reshape(TXT, xheads_here, XHEAD)
    xquery = (
        (jnp.dot(cross_all, w_xq, preferred_element_type=single) + xq_bias)
        .astype(bfloat)
        .reshape(span_rows, xheads_here, XHEAD)
    )
    length_s = spread_rows(text_len, first_s, item_s, window_s)
    key_live = jnp.arange(TXT, dtype=jnp.int32)[None, :] < length_s[:, None]
    raw_scores = jnp.where(
        key_live[:, None, :],
        jnp.einsum("nhd,thd->nht", xquery, xkeys, preferred_element_type=single) * scale_x,
        -1e30,
    )
    row_max = jnp.max(raw_scores, axis=-1, keepdims=True)
    shifted = jnp.exp(raw_scores - row_max)
    row_total = jnp.sum(shifted, axis=-1, keepdims=True)
    log_total = row_max + jnp.log(row_total)
    probs_low = (shifted / row_total).astype(bfloat)
    cross_mix = (
        jnp.einsum("nht,thd->nhd", probs_low, xvals, preferred_element_type=single)
        .astype(bfloat)
        .reshape(span_rows, xheads_here * XHEAD)
    )
    cross_out = (
        sum_rows(
            lambda piece_rows: jnp.dot(piece_rows, w_xo, preferred_element_type=single), cross_mix
        )
        + xo_bias
    )
    after_cross = after_attn + live_r * cross_out
    normal_f, inv_std_f = norm_parts(after_cross)
    normed_ffn = (normal_f * (1.0 + scale_f) + shift_f).astype(bfloat)
    ffn_all = gather_rows(normed_ffn)
    expand = jnp.einsum("nd,dkf->nkf", ffn_all, w_in, preferred_element_type=single) + in_bias
    active = jax.nn.silu(expand).astype(bfloat).reshape(span_rows, 2 * channels)
    active_ext = grid_halo(active)
    weight_taps = dw_weight.reshape(9, 2 * channels)
    conv_sum = jnp.zeros((span_rows, 2 * channels), single)
    for row_step in (-1, 0, 1):
        for col_step in (-1, 0, 1):
            inside = inside_tap(inner_s, height_s, width_s, row_step, col_step)
            moved = jnp.where(
                inside[:, None],
                tap_rows(active_ext, span_rows, bucket_s, row_step, col_step),
                jnp.zeros((), bfloat),
            )
            conv_sum = conv_sum + moved * weight_taps[3 * row_step + col_step + 4]
    conv_out = (conv_sum + dw_bias.reshape(2 * channels)).reshape(span_rows, 2, channels)
    glu_out = (conv_out[:, 0] * jax.nn.silu(conv_out[:, 1])).astype(bfloat)
    ffn_out = sum_rows(
        lambda piece_rows: jnp.dot(piece_rows, w_pt, preferred_element_type=single), glu_out
    )
    out_tokens = (after_cross + live_r * gate_f * ffn_out).astype(bfloat)
    grad_out = cotangent.astype(single)
    d_gate_f = grad_out * live_r * ffn_out
    d_ffn_all = gather_rows((grad_out * live_r * gate_f).astype(bfloat))
    d_w_pt = jnp.einsum("nf,nd->fd", glu_out, d_ffn_all, preferred_element_type=single)
    d_glu = jnp.einsum("nd,fd->nf", d_ffn_all, w_pt, preferred_element_type=single)
    value_c = conv_out[:, 0]
    gate_c = conv_out[:, 1]
    d_conv = jnp.stack([d_glu * jax.nn.silu(gate_c), d_glu * value_c * silu_slope(gate_c)], axis=1)
    d_conv = d_conv.reshape(span_rows, 2 * channels).astype(bfloat)
    d_dw_bias = jnp.sum(d_conv, axis=0, dtype=single).reshape(2, channels)
    d_conv_ext = grid_halo(d_conv)
    d_active = jnp.zeros((span_rows, 2 * channels), single)
    d_taps = []
    for row_step in (-1, 0, 1):
        for col_step in (-1, 0, 1):
            inside = inside_tap(inner_s, height_s, width_s, row_step, col_step)
            moved = jnp.where(
                inside[:, None],
                tap_rows(active_ext, span_rows, bucket_s, row_step, col_step),
                jnp.zeros((), bfloat),
            )
            d_taps.append(jnp.einsum("nc,nc->c", moved, d_conv, preferred_element_type=single))
            reached = inside_tap(inner_s, height_s, width_s, -row_step, -col_step)
            arriving = jnp.where(
                reached[:, None],
                tap_rows(d_conv_ext, span_rows, bucket_s, -row_step, -col_step),
                jnp.zeros((), bfloat),
            )
            d_active = d_active + arriving * weight_taps[3 * row_step + col_step + 4]
    d_dw_weight = jnp.stack(d_taps, axis=0).reshape(9, 2, channels)
    d_expand = d_active.reshape(span_rows, 2, channels) * silu_slope(expand)
    d_in_bias = jnp.sum(d_expand, axis=0)
    d_expand_low = d_expand.astype(bfloat)
    ffn_rows_b = gather_rows(normed_ffn)
    d_w_in = jnp.einsum("nd,nkf->dkf", ffn_rows_b, d_expand_low, preferred_element_type=single)
    d_normed_ffn = sum_rows(
        lambda piece_rows: jnp.einsum(
            "nkf,dkf->nd", piece_rows, w_in, preferred_element_type=single
        ),
        d_expand_low,
    )
    grad_cross = grad_out + norm_back(d_normed_ffn, normal_f, inv_std_f, scale_f)
    d_cross = grad_cross * live_r
    d_xo_bias = jnp.sum(d_cross, axis=0)
    d_cross_all = gather_rows(d_cross.astype(bfloat))
    d_w_xo = jnp.einsum("nf,nd->fd", cross_mix, d_cross_all, preferred_element_type=single)
    d_mix = (
        jnp.einsum("nd,fd->nf", d_cross_all, w_xo, preferred_element_type=single)
        .astype(bfloat)
        .reshape(span_rows, xheads_here, XHEAD)
    )
    again_scores = jnp.where(
        key_live[:, None, :],
        jnp.einsum("nhd,thd->nht", xquery, xkeys, preferred_element_type=single) * scale_x,
        -1e30,
    )
    probs_f = jnp.exp(again_scores - log_total)
    probs_again = probs_f.astype(bfloat)
    d_probs = jnp.einsum("nhd,thd->nht", d_mix, xvals, preferred_element_type=single)
    d_vals = jnp.einsum("nht,nhd->thd", probs_again, d_mix, preferred_element_type=single)
    row_dot = jnp.sum(probs_f * d_probs, axis=-1, keepdims=True)
    d_scores = (probs_f * (d_probs - row_dot) * scale_x).astype(bfloat)
    d_query = jnp.einsum("nht,thd->nhd", d_scores, xkeys, preferred_element_type=single).reshape(
        span_rows, xheads_here * XHEAD
    )
    d_keys = jnp.einsum("nht,nhd->thd", d_scores, xquery, preferred_element_type=single)
    d_xq_bias = jnp.sum(d_query, axis=0)
    d_query_low = d_query.astype(bfloat)
    cross_rows_b = gather_rows(cross_in)
    d_w_xq = jnp.einsum("nd,nf->df", cross_rows_b, d_query_low, preferred_element_type=single)
    d_cross_in = sum_rows(
        lambda piece_rows: jnp.einsum("nf,df->nd", piece_rows, w_xq, preferred_element_type=single),
        d_query_low,
    )
    grad_attn = grad_cross + d_cross_in
    d_attn_out = grad_attn * live_r * gate_a
    d_gate_a = grad_attn * live_r * attn_out
    d_out_bias = jnp.sum(d_attn_out, axis=0)
    d_attn_all = gather_rows(d_attn_out.astype(bfloat))
    d_w_out = jnp.einsum("nf,nd->fd", attn, d_attn_all, preferred_element_type=single)
    d_ratio = jnp.einsum("nd,fd->nf", d_attn_all, w_out, preferred_element_type=single).reshape(
        span_rows, heads_here, HEAD
    )
    d_numer = d_ratio / denominator[:, :, None]
    d_denom = -jnp.sum(d_ratio * attn_ratio, axis=-1) / denominator
    per_query = (
        jnp.einsum("nhe,jhde->njhd", d_numer, kv_state, precision=highest)
        + key_total[None] * d_denom[:, None, :, None]
    )
    d_query_h = jnp.einsum("nj,njhd->nhd", pick_f, per_query, precision=highest)
    query_pick = jnp.where(picked[:, :, None, None], query_f[:, None], 0.0)
    d_state_part = jnp.einsum("njhd,nhe->jhde", query_pick, d_numer, precision=highest)
    d_total_part = jnp.einsum("njhd,nh->jhd", query_pick, d_denom, precision=highest)
    d_state, d_total = item_sums(
        d_state_part, d_total_part, first_s, window_s, span_start, span_rows
    )
    live_f = picked_live.astype(single)
    values_f = values_h.astype(single)
    keys_f = keys_h.astype(single)
    d_keys_h = jnp.einsum(
        "nj,njhd->nhd",
        live_f,
        jnp.einsum("nhe,jhde->njhd", values_f, d_state, precision=highest) + d_total[None],
        precision=highest,
    )
    d_values_h = jnp.einsum(
        "nj,njhe->nhe",
        live_f,
        jnp.einsum("nhd,jhde->njhe", keys_f, d_state, precision=highest),
        precision=highest,
    )
    slope_q = jax.nn.sigmoid(qkv[:, 0]).reshape(span_rows, heads_here, HEAD)
    slope_k = jax.nn.sigmoid(qkv[:, 1]).reshape(span_rows, heads_here, HEAD)
    d_qkv = jnp.stack([d_query_h * slope_q, d_keys_h * slope_k, d_values_h], axis=1)
    d_qkv = d_qkv.reshape(span_rows, 3, heads_here * HEAD).astype(bfloat)
    normed_rows_b = gather_rows(normed)
    d_w_qkv = jnp.einsum("nd,nke->dke", normed_rows_b, d_qkv, preferred_element_type=single)
    d_normed = sum_rows(
        lambda piece_rows: jnp.einsum(
            "nke,dke->nd", piece_rows, w_qkv, preferred_element_type=single
        ),
        d_qkv,
    )
    d_tokens = grad_attn + norm_back(d_normed, normal_a, inv_std_a, scale_a)
    mod_rows = jnp.stack(
        [d_normed, d_normed * normal_a, d_gate_a, d_normed_ffn, d_normed_ffn * normal_f, d_gate_f],
        axis=1,
    )
    pick_r = (item_r[:, None] == first_r + jnp.arange(window_r, dtype=jnp.int32)[None, :]).astype(
        single
    )
    mod_part = jnp.einsum("nj,nkd->jkd", pick_r, mod_rows, precision=highest)
    (mod_table,) = place_items((mod_part,), first_r, window_r, item_count)
    d_t_mod, d_out_bias, d_xo_bias = lax.psum((mod_table, d_out_bias, d_xo_bias), ("dp", "tensor"))
    d_shift_table = jnp.sum(d_t_mod, axis=0)
    (
        d_w_qkv,
        d_w_out,
        d_w_xq,
        d_xq_bias,
        d_keys,
        d_vals,
        d_w_xo,
        d_w_in,
        d_in_bias,
        d_dw_weight,
        d_dw_bias,
        d_w_pt,
    ) = (
        lax.psum(d_w_qkv.astype(jnp.bfloat16), "dp").astype(jnp.float32),
        lax.psum(d_w_out.astype(jnp.bfloat16), "dp").astype(jnp.float32),
        lax.psum(d_w_xq.astype(jnp.bfloat16), "dp").astype(jnp.float32),
        lax.psum(d_xq_bias.astype(jnp.bfloat16), "dp").astype(jnp.float32),
        lax.psum(d_keys.astype(jnp.bfloat16), "dp").astype(jnp.float32),
        lax.psum(d_vals.astype(jnp.bfloat16), "dp").astype(jnp.float32),
        lax.psum(d_w_xo.astype(jnp.bfloat16), "dp").astype(jnp.float32),
        lax.psum(d_w_in.astype(jnp.bfloat16), "dp").astype(jnp.float32),
        lax.psum(d_in_bias.astype(jnp.bfloat16), "dp").astype(jnp.float32),
        lax.psum(d_dw_weight.astype(jnp.bfloat16), "dp").astype(jnp.float32),
        lax.psum(d_dw_bias.astype(jnp.bfloat16), "dp").astype(jnp.float32),
        lax.psum(d_w_pt.astype(jnp.bfloat16), "dp").astype(jnp.float32),
    )
    d_xv_bias = jnp.sum(d_vals, axis=0).reshape(xheads_here * XHEAD)
    d_text_kv = (
        jnp.stack([d_keys, d_vals], axis=1).reshape(TXT, 2, xheads_here * XHEAD).astype(bfloat)
    )
    d_w_xkv = jnp.einsum("td,tke->dke", text_all, d_text_kv, preferred_element_type=single)
    d_text = sum_rows(
        lambda piece_rows: jnp.einsum(
            "tke,dke->td", piece_rows, w_xkv, preferred_element_type=single
        ),
        d_text_kv,
    )
    return (
        out_tokens,
        d_tokens,
        d_t_mod,
        d_text,
        d_shift_table,
        d_w_qkv,
        d_w_out,
        d_out_bias,
        d_w_xq,
        d_xq_bias,
        d_w_xkv,
        d_xv_bias,
        d_w_xo,
        d_xo_bias,
        d_w_in,
        d_in_bias,
        d_dw_weight,
        d_dw_bias,
        d_w_pt,
    )


def solution(mesh):
    placed = (
        P(("dp", "tensor"), None),
        P(("dp", "tensor"), None),
        P(),
        P(),
        P(),
        P("tensor", None),
        P(),
        P(None, None, "tensor"),
        P("tensor", None),
        P(),
        P(None, "tensor"),
        P("tensor"),
        P(None, None, "tensor"),
        P("tensor"),
        P("tensor", None),
        P(),
        P(None, None, "tensor"),
        P(None, "tensor"),
        P(None, None, "tensor"),
        P(None, "tensor"),
        P("tensor", None),
    )
    return jax.shard_map(
        local,
        mesh=mesh,
        in_specs=placed,
        out_specs=(
            P(("dp", "tensor"), None),
            P(("dp", "tensor"), None),
            P(),
            P("tensor", None),
            P(),
            P(None, None, "tensor"),
            P("tensor", None),
            P(),
            P(None, "tensor"),
            P("tensor"),
            P(None, None, "tensor"),
            P("tensor"),
            P("tensor", None),
            P(),
            P(None, None, "tensor"),
            P(None, "tensor"),
            P(None, None, "tensor"),
            P(None, "tensor"),
            P("tensor", None),
        ),
        check_vma=False,
    )
```

profile of v0, /device:TPU:0, one launch (start us, length us, event | category | flops | bytes accessed | tf_op | source)
XLA Modules:
  0.0 1949.7 jit_solution(2070240652052646924)
XLA Ops:
  25.4 71.2 %all-gather.8.cloned.1.call-done = bf16[1664,1152]{1,0:T(8,128)(2,1)} async-done(((bf16[416,1152]{1,0:T(8,128)(2,1)}), bf16[1664,1152]{1,0:T(8,128)(2,1)}) %all-gather.8.cloned.1.call-update) | async-done | bytes 3833872 | tf_op jit(solution)/shard_map/all_gather | solution.py:98
  96.6 6.9 fusion.113
  132.9 5.3 fusion.271
  138.5 132.5 %reduce-scatter.9.cloned.1.call-done = f32[416,1152]{1,0:T(8,128)} async-done(((f32[1664,1152]{1,0:T(8,128)}), f32[416,1152]{1,0:T(8,128)}) %reduce-scatter.9.cloned.1.call-update) | async-done | bytes 1916944 | tf_op jit(solution)/shard_map/reduce_scatter | solution.py:106
  274.7 24.0 %all-gather = bf16[4,75,1152]{2,1,0:T(8,128)(2,1)} all-gather(bf16[1,75,1152]{2,1,0:T(8,128)(2,1)S(1)} %bitcast.386), channel_id=1, replica_groups=mesh['dp'=8,'tensor'=4] {'tensor'}, dimensions={0}, use_global_device_ids=true | all-gather | bytes 864000 | tf_op jit(solution)/shard_map/all_gather | solution.py:98
  309.9 44.7 %all-gather.10.cloned.1.call-done = bf16[1664,1152]{1,0:T(8,128)(2,1)} async-done(((bf16[416,1152]{1,0:T(8,128)(2,1)}), bf16[1664,1152]{1,0:T(8,128)(2,1)}) %all-gather.10.cloned.1.call-update) | async-done | bytes 3833872 | tf_op jit(solution)/shard_map/all_gather | solution.py:98
  364.5 5.3 fusion.273
  370.0 132.6 %reduce-scatter.11.cloned.1.call-done = f32[416,1152]{1,0:T(8,128)} async-done(((f32[1664,1152]{1,0:T(8,128)}), f32[416,1152]{1,0:T(8,128)}) %reduce-scatter.11.cloned.1.call-update) | async-done | bytes 1916944 | tf_op jit(solution)/shard_map/reduce_scatter | solution.py:106
  502.5 5.6 fusion.261
  527.5 61.4 %all-gather.12.cloned.1.call-done = bf16[1664,1152]{1,0:T(8,128)(2,1)} async-done(((bf16[416,1152]{1,0:T(8,128)(2,1)}), bf16[1664,1152]{1,0:T(8,128)(2,1)}) %all-gather.12.cloned.1.call-update) | async-done | bytes 3833872 | tf_op jit(solution)/shard_map/all_gather | solution.py:98
  589.0 12.3 multiply_convert_fusion
  611.4 92.5 %add_add_fusion = (f32[1664,1440]{0,1:T(8,128)}, bf16[1664,1440]{0,1:T(8,128)(2,1)}, bf16[1664,1440]{0,1:T(8,128)(2,1)}, bf16[1664,1440]{0,1:T(8,128)(2,1)}, bf1...) fusion(f32[1440]{0:T(1024)} %add.788, f32[1440]{0:T(1024)} %mul.467, ...), kind=kLoop, calls=%fused_computation.59 | loop fusion | flops 306708480 | bytes 43442944 | tf_op jit(solution)/shard_map/add | solution.py:291
  704.0 10.0 multiply_bitcast_fusion.1
  717.9 8.8 collective-permute-start.5
  731.1 86.3 %multiply_add_fusion = f32[1664,1440]{0,1:T(8,128)} fusion(bf16[41,1440]{0,1:T(8,128)(2,1)} %copy-done.47, bf16[41,1440]{0,1:T(8,128)(2,1)} %copy-done.48, bf16[1664,1440]{0,1:T(8,128)(2,1)} %bitcast.346, f32[1440]{0:T(1024)} %mul.467, f32[1440]{0:T(1024)} %mul.464, f32[1440]{0:T(1024)} %mul.461, f32[1440]{0:T(1024)} %mul.458, f32[1440]{0:T(1024)} %mul.455, ...), kind=kLoop, calls=%fused_computation.58 | loop fusion | flops 304312320 | bytes 14683264 | tf_op jit(solution)/shard_map/add | solution.py:325
  817.3 9.0 fusion.243
  828.5 10.0 convolution_bitcast_fusion.1
  838.6 4.6 multiply_convert_fusion.1
  844.6 6.0 fusion.274
  850.7 124.5 %reduce-scatter.15.cloned.1.call-done = f32[416,1152]{1,0:T(8,128)} async-done(((f32[1664,1152]{1,0:T(8,128)}), f32[416,1152]{1,0:T(8,128)}) %reduce-scatter.15.cloned.1.call-update) | async-done | bytes 1916944 | tf_op jit(solution)/shard_map/reduce_scatter | solution.py:106
  977.9 133.2 %reduce-scatter.13.cloned.1.call-done = f32[416,1152]{1,0:T(8,128)} async-done(((f32[1664,1152]{1,0:T(8,128)}), f32[416,1152]{1,0:T(8,128)}) %reduce-scatter.13.cloned.1.call-update) | async-done | bytes 1916944 | tf_op jit(solution)/shard_map/reduce_scatter | solution.py:106
  1111.1 5.2 multiply_reduce_fusion.3
  1120.4 73.9 %all-gather.16.cloned.1.call-done = bf16[1664,1152]{1,0:T(8,128)(2,1)} async-done(((bf16[416,1152]{1,0:T(8,128)(2,1)}), bf16[1664,1152]{1,0:T(8,128)(2,1)}) %all-gather.16.cloned.1.call-update) | async-done | bytes 3833872 | tf_op jit(solution)/shard_map/all_gather | solution.py:98
  1198.0 5.1 fusion.198
  1203.2 15.5 fusion.265
  1218.7 6.8 fusion.275
  1225.6 131.8 %reduce-scatter.17.cloned.1.call-done = f32[416,1152]{1,0:T(8,128)} async-done(((f32[1664,1152]{1,0:T(8,128)}), f32[416,1152]{1,0:T(8,128)}) %reduce-scatter.17.cloned.1.call-update) | async-done | bytes 1916944 | tf_op jit(solution)/shard_map/reduce_scatter | solution.py:106
  1357.3 4.6 fusion.192
  1362.0 7.7 convolution_convert_fusion.1
  1369.7 10.6 convolution_convert_fusion
  1380.3 14.8 fusion.176
  1395.1 4.9 convolution_convert_fusion.4
  1402.4 5.5 fusion.180
  1408.0 29.4 %all-gather.18.cloned.1.call-done = bf16[1664,1152]{1,0:T(8,128)(2,1)} async-done(((bf16[416,1152]{1,0:T(8,128)(2,1)}), bf16[1664,1152]{1,0:T(8,128)(2,1)}) %all-gather.18.cloned.1.call-update) | async-done | bytes 3833872 | tf_op jit(solution)/shard_map/all_gather | solution.py:98
  1441.8 11.2 fusion.171
  1453.0 7.0 fusion.24
  1460.0 9.7 fusion.11
  1492.2 5.3 fusion.117
  1497.8 9.7 convolution_bitcast_fusion
  1510.5 27.6 %fusion.10 = (bf16[1440]{0:T(1024)(128)(2,1)S(1)}, bf16[1440]{0:T(1024)(128)(2,1)S(1)}, bf16[1440]{0:T(1024)(128)(2,1)S(1)}, bf16[1440]{0:T(1024)(128)(2,1)S(1)}...) fusion(bf16[1440,1664]{1,0:T(8,128)(2,1)} %bitcast.347, ...), kind=kLoop, calls=%fused_computation.55 | loop fusion | flops 93437280 | bytes 38605632 | tf_op jit(solution)/shard_map/nc,nc->c/dot_general | solution.py:318
  1539.1 24.6 %all-reduce.5 = (bf16[288]{0:T(512)(128)(2,1)S(1)}, bf16[2,720]{1,0:T(2,128)(2,1)S(1)}, bf16[9,2,720]{2,1,0:T(2,128)(2,1)S(1)}, bf16[2,720]{1,0:T(2,128)(2,1)S(1)}) all-reduce(bf16[288]{0:T(512)(128)(2,1)S(1)} %convert_element_type.328, bf16[2,720]{1,0:T(2,128)(2,1)S(1)} %get-tuple-element.52, ...), channel_id=1, replica_groups=mesh['dp'=8,'tensor'=4] {'dp'}, use_global_device_ids=true, to_apply=%region_29.30 | all-reduce | flops 16128 | bytes 64512 | tf_op jit(solution)/shard_map/psum | solution.py:449
  1566.2 71.9 %all-reduce.12.cloned.1.call-done = (bf16[300,4,72]{0,2,1:T(8,128)(2,1)}, bf16[300,1,288]{0,2,1:T(8,128)(2,1)}, bf16[1152,3,288]{0,2,1:T(8,128)(2,1)}, bf16[288,...) async-done(((bf16[300,4,72]{0,2,1:T(8,128)(2,1)}, ...) | async-done | bytes 9303568 | tf_op jit(solution)/shard_map/psum | solution.py:451
  1641.6 57.8 %fusion = f32[80,1152]{1,0:T(8,128)S(1)} fusion(f32[300,1152]{1,0:T(8,128)} %convolution_bitcast_fusion.3), kind=kCustom, calls=%all-reduce-scatter | all-reduce-scatter fusion | flops 368641 | bytes 1751552
  1700.0 7.2 collective-permute-start.8
  1728.9 68.3 %reduce-scatter.19.cloned.1.call-done = f32[416,1152]{1,0:T(8,128)} async-done(((f32[1664,1152]{1,0:T(8,128)}), f32[416,1152]{1,0:T(8,128)}) %reduce-scatter.19.cloned.1.call-update) | async-done | bytes 1916944 | tf_op jit(solution)/shard_map/reduce_scatter | solution.py:106
  1811.5 5.1 fusion.148
  1816.6 40.7 %all-reduce.4 = (f32[1152]{0:T(1024)}, f32[1152]{0:T(1024)}) all-reduce(f32[1152]{0:T(1024)S(1)} %get-tuple-element.23, f32[1152]{0:T(1024)S(1)} %copy-done.68), channel_id=1, replica_groups=mesh['dp'=8,'tensor'=4] {'dp','tensor'}, use_global_device_ids=true, to_apply=%region_26.27 | all-reduce | flops 2304 | bytes 18432 | tf_op jit(solution)/shard_map/psum | solution.py:430
  1857.3 82.1 %all-reduce.10.cloned.1.call-done = f32[13,6,1152]{2,0,1:T(8,128)} async-done(((f32[13,6,1152]{2,0,1:T(8,128)}), f32[13,6,1152]{2,0,1:T(8,128)}) %all-reduce.10.cloned.1.call-update) | async-done | bytes 359440 | tf_op jit(solution)/shard_map/psum | solution.py:430
  (408 shorter events, 202.7 us)
Async XLA Ops:
  7.2 581.8 %copy-start = (bf16[1152,2,720]{0,2,1:T(8,128)(2,1)S(1)}, bf16[1152,2,720]{0,2,1:T(8,128)(2,1)}, u32[]{:S(2)}) copy-start(bf16[1152,2,720]{0,2,1:T(8,128)(2,1)} %param.37) | copy-start | bytes 9953284
  7.2 89.4 %all-gather.8.cloned.1.call-start = ((), (), s32[]{:S(2)}) async-start(), calls=%async_computation.6 | async-start | bytes 4792320 | tf_op jit(solution)/shard_map/all_gather | solution.py:98
  19.0 252.0 %reduce-scatter.9.cloned.1.call-start = ((), (), s32[]{:S(2)}) async-start(), calls=%async_computation.7 | async-start | bytes 9584640 | tf_op jit(solution)/shard_map/reduce_scatter | solution.py:106
  25.3 78.2 %copy-start.72 = (pred[1664,3]{0,1:T(4,128)(4,1)}, pred[1664,3]{0,1:T(4,128)(4,1)S(1)}, u32[]{:S(2)}) copy-start(pred[1664,3]{0,1:T(4,128)(4,1)S(1)} %get-tuple-element.62) | copy-start | bytes 14980
  25.3 101.1 %copy-start.50 = (f32[1664,3]{0,1:T(4,128)}, f32[1664,3]{0,1:T(4,128)S(1)}, u32[]{:S(2)}) copy-start(f32[1664,3]{0,1:T(4,128)S(1)} %convert.73) | copy-start | bytes 59908
  25.4 97.9 %copy-start.85 = (pred[3]{0:T(512)(128)(4,1)}, pred[3]{0:T(512)(128)(4,1)S(1)}, u32[]{:S(2)}) copy-start(pred[3]{0:T(512)(128)(4,1)S(1)} %dynamic-slice.2) | copy-start | bytes 13
  114.3 8.7 collective-permute-start.1
  115.6 7.4 collective-permute-start
  138.3 132.6 %copy-start.56 = (f32[1152]{0:T(1024)S(1)}, f32[1152]{0:T(1024)}, u32[]{:S(2)}) copy-start(f32[1152]{0:T(1024)} %param.30) | copy-start | bytes 13828
  138.3 136.4 %copy-start.53 = (bf16[75,1152]{1,0:T(8,128)(2,1)S(1)}, bf16[75,1152]{1,0:T(8,128)(2,1)}, u32[]{:S(2)}) copy-start(bf16[75,1152]{1,0:T(8,128)(2,1)} %param.26) | copy-start | bytes 518404
  138.3 216.3 %all-gather.10.cloned.1.call-start = ((), (), s32[]{:S(2)}) async-start(), calls=%async_computation.8 | async-start | bytes 4792320 | tf_op jit(solution)/shard_map/all_gather | solution.py:98
  274.6 29.5 %copy-start.92 = (s32[19]{0:T(128)S(1)}, s32[19]{0:T(128)}, u32[]{:S(2)}) copy-start(s32[19]{0:T(128)} %get-tuple-element.126) | copy-start | bytes 232
  274.6 227.9 %reduce-scatter.11.cloned.1.call-start = ((), (), s32[]{:S(2)}) async-start(), calls=%async_computation.9 | async-start | bytes 9584640 | tf_op jit(solution)/shard_map/reduce_scatter | solution.py:106
  305.5 55.9 %copy-start.77 = (f32[4,72]{1,0:T(4,128)}, f32[4,72]{1,0:T(4,128)S(1)}, u32[]{:S(2)}) copy-start(f32[4,72]{1,0:T(4,128)S(1)} %add.760) | copy-start | bytes 3460
  369.9 219.1 %all-gather.12.cloned.1.call-start = ((), (), s32[]{:S(2)}) async-start(), calls=%async_computation.10 | async-start | bytes 4792320 | tf_op jit(solution)/shard_map/all_gather | solution.py:98
  513.5 190.6 %all-gather.14.cloned.1.call-start = ((), (), s32[]{:S(2)}) async-start(), calls=%async_computation.12 | async-start | bytes 4792320 | tf_op jit(solution)/shard_map/all_gather | solution.py:98
  589.0 19.3 copy-start.81
  604.5 4.5 collective-permute-start.2
  607.0 4.5 collective-permute-start.3
  609.0 366.2 %reduce-scatter.15.cloned.1.call-start = ((), (), s32[]{:S(2)}) async-start(), calls=%async_computation.13 | async-start | bytes 9584640 | tf_op jit(solution)/shard_map/reduce_scatter | solution.py:106
  717.9 10.3 collective-permute-start.5
  726.8 3.6 collective-permute-start.4
  838.5 272.6 %reduce-scatter.13.cloned.1.call-start = ((), (), s32[]{:S(2)}) async-start(), calls=%async_computation.11 | async-start | bytes 9584640 | tf_op jit(solution)/shard_map/reduce_scatter | solution.py:106
  850.6 124.5 %copy-start.5 = (f32[416,1152]{1,0:T(8,128)S(1)}, f32[416,1152]{1,0:T(8,128)}, u32[]{:S(2)}) copy-start(f32[416,1152]{1,0:T(8,128)} %copy-done.4) | copy-start | bytes 5750788
  850.6 124.5 %copy-start.63 = (f32[416]{0:T(512)S(1)}, f32[416]{0:T(512)}, u32[]{:S(2)}) copy-start(f32[416]{0:T(512)} %copy-done.62) | copy-start | bytes 4996
  850.6 260.5 %copy-start.19 = (bf16[416,1152]{1,0:T(8,128)(2,1)S(1)}, bf16[416,1152]{1,0:T(8,128)(2,1)}, u32[]{:S(2)}) copy-start(bf16[416,1152]{1,0:T(8,128)(2,1)} %param.22) | copy-start | bytes 2875396
  850.6 343.6 %all-gather.16.cloned.1.call-start = ((), (), s32[]{:S(2)}) async-start(), calls=%async_computation.14 | async-start | bytes 4792320 | tf_op jit(solution)/shard_map/all_gather | solution.py:98
  1118.7 79.3 %copy-start.36 = (f32[300,1,288]{0,2,1:T(8,128)S(1)}, f32[300,1,288]{0,2,1:T(8,128)}, u32[]{:S(2)}) copy-start(f32[300,1,288]{0,2,1:T(8,128)} %slice.445) | copy-start | bytes 1036804
  1118.8 238.6 %reduce-scatter.17.cloned.1.call-start = ((), (), s32[]{:S(2)}) async-start(), calls=%async_computation.15 | async-start | bytes 9584640 | tf_op jit(solution)/shard_map/reduce_scatter | solution.py:106
  1225.5 211.9 %all-gather.18.cloned.1.call-start = ((), (), s32[]{:S(2)}) async-start(), calls=%async_computation.16 | async-start | bytes 4792320 | tf_op jit(solution)/shard_map/all_gather | solution.py:98
  1361.9 276.2 %all-reduce.12.cloned.1.call-start = ((), (), s32[]{:S(2)}) async-start(), calls=%async_computation.19 | async-start | bytes 18800640 | tf_op jit(solution)/shard_map/psum | solution.py:451
  1408.0 33.4 %copy-start.38 = (f32[1664,9]{0,1:T(8,128)S(1)}, f32[1664,9]{0,1:T(8,128)}, u32[]{:S(2)}) copy-start(f32[1664,9]{0,1:T(8,128)} %copy-done.37) | copy-start | bytes 179716
  1408.0 33.8 %copy-start.73 = (pred[1664,3]{0,1:T(4,128)(4,1)S(1)}, pred[1664,3]{0,1:T(4,128)(4,1)}, u32[]{:S(2)}) copy-start(pred[1664,3]{0,1:T(4,128)(4,1)} %copy-done.72) | copy-start | bytes 14980
  1460.0 19.9 %copy-start.23 = (bf16[1664,9,32]{0,2,1:T(8,128)(2,1)S(1)}, bf16[1664,9,32]{0,2,1:T(8,128)(2,1)}, u32[]{:S(2)}) copy-start(bf16[1664,9,32]{0,2,1:T(8,128)(2,1)} %copy-done.22) | copy-start | bytes 2875396
  1471.3 10.9 collective-permute-start.7
  1472.9 9.4 collective-permute-start.6
  1497.6 299.6 %reduce-scatter.19.cloned.1.call-start = ((), (), s32[]{:S(2)}) async-start(), calls=%async_computation.17 | async-start | bytes 9584640 | tf_op jit(solution)/shard_map/reduce_scatter | solution.py:106
  1507.5 431.9 %all-reduce.10.cloned.1.call-start = ((), (), s32[]{:S(2)}) async-start(), calls=%async_computation.18 | async-start | bytes 884736 | tf_op jit(solution)/shard_map/psum | solution.py:430
  1510.5 28.5 %copy-start.87 = (bf16[4,72]{1,0:T(4,128)(2,1)S(1)}, bf16[4,72]{1,0:T(4,128)(2,1)}, u32[]{:S(2)}) copy-start(bf16[4,72]{1,0:T(4,128)(2,1)} %get-tuple-element.98) | copy-start | bytes 1732
  1510.5 28.6 %copy-start.75 = (bf16[2,720]{1,0:T(2,128)(2,1)S(1)}, bf16[2,720]{1,0:T(2,128)(2,1)}, u32[]{:S(2)}) copy-start(bf16[2,720]{1,0:T(2,128)(2,1)} %get-tuple-element.50) | copy-start | bytes 8644
  1538.1 169.1 %copy-start.27 = (bf16[300,1152,1]{1,0,2:T(8,128)(2,1)S(1)}, bf16[300,1152,1]{1,0,2:T(8,128)(2,1)}, u32[]{:S(2)}) copy-start(bf16[300,1152,1]{1,0,2:T(8,128)(2,1)} %reshape.587) | copy-start | bytes 2073604
  1638.1 69.1 %copy-start.44 = (bf16[300,4,72]{0,2,1:T(8,128)(2,1)S(1)}, bf16[300,4,72]{0,2,1:T(8,128)(2,1)}, u32[]{:S(2)}) copy-start(bf16[300,4,72]{0,2,1:T(8,128)(2,1)} %get-tuple-element.42) | copy-start | bytes 518404
  1638.1 69.2 %copy-start.52 = (bf16[300,1,288]{0,2,1:T(8,128)(2,1)S(1)}, bf16[300,1,288]{0,2,1:T(8,128)(2,1)}, u32[]{:S(2)}) copy-start(bf16[300,1,288]{0,2,1:T(8,128)(2,1)} %get-tuple-element.43) | copy-start | bytes 518404
  1700.0 24.9 %collective-permute-start.8 = (f32[15,1152]{1,0:T(8,128)}, f32[15,1152]{1,0:T(8,128)S(1)}, u32[]{:S(2)}, u32[]{:S(2)}) collective-permute-start(f32[15,1152]{1,0:T(8,128)} %slice.532), channel_id=1, source_target_pairs={{0,1},{1,2},{2,3},{4,5},{5,6},{6,7},{8,9},{9,10},{10,11},{12,13},{... | collective-permute-start | bytes 207368
  1721.7 75.5 %copy-start.7 = (bf16[416,1152]{1,0:T(8,128)(2,1)S(1)}, bf16[416,1152]{1,0:T(8,128)(2,1)}, u32[]{:S(2)}) copy-start(bf16[416,1152]{1,0:T(8,128)(2,1)} %param.21) | copy-start | bytes 2875396
  1721.7 75.5 %copy-start.61 = (f32[416]{0:T(512)S(1)}, f32[416]{0:T(512)}, u32[]{:S(2)}) copy-start(f32[416]{0:T(512)} %copy-done.60) | copy-start | bytes 4996
  1721.7 75.5 %copy-start.65 = (f32[416]{0:T(512)S(1)}, f32[416]{0:T(512)}, u32[]{:S(2)}) copy-start(f32[416]{0:T(512)} %copy-done.64) | copy-start | bytes 4996
  1811.5 131.4 %copy-start.1 = (bf16[1152,2,720]{0,2,1:T(8,128)(2,1)S(1)}, bf16[1152,2,720]{0,2,1:T(8,128)(2,1)}, u32[]{:S(2)}) copy-start(bf16[1152,2,720]{0,2,1:T(8,128)(2,1)} %param.37) | copy-start | bytes 9953284
  (75 other events, 378.6 us)
Sparse Core Ops, SparseCore 0:
  19.1 77.5 all-gather.7
  138.4 132.4 reduce-scatter.8
  274.8 79.7 all-gather.9
  370.0 132.4 reduce-scatter.10
  513.6 75.3 all-gather.11
  609.1 75.1 all-gather.13
  838.6 136.4 reduce-scatter.14
  977.6 133.5 reduce-scatter.12
  1118.9 75.3 all-gather.15
  1225.6 131.6 reduce-scatter.16
  1362.1 75.3 all-gather.17
  1497.7 140.3 all-reduce.11
  1640.4 156.7 reduce-scatter.18
  1811.7 127.7 all-reduce.9
where the time goes:
time: 1960 us; the launch traced here: 1950 us
  waiting for transfers between devices  1160 us (59%)
  other arithmetic  308 us (16%)
  matrix products  219 us (11%)
  blocking collectives  147 us (8%)
  local copies, waits for them, and re-layouts  65.1 us (3%)
  starting transfers between devices  31.9 us (2%)
    reduce_scatter x6, waiting for transfers between devices, sum_rows(): lax.psum_scatter(project(source), 'tensor', scatter_dimension=0, tiled=True)  723 us
    all_gather x6, waiting for transfers between devices, gather_rows(): return lax.all_gather(values, 'tensor', axis=0, tiled=True)  281 us
    add x1, other arithmetic, local(): conv_sum + dw_bias.reshape(2 * channels)  92.5 us
    add x1, other arithmetic, local(): d_active = d_active + arriving * weight_taps[3 * row_step + col_step + 4]  86.3 us
    psum x1, waiting for transfers between devices, local(): lax.psum((mod_table, d_out_bias, d_xo_bias), ('dp', 'tensor'))  82.1 us
    psum x1, waiting for transfers between devices, local(): lax.psum(d_vals.astype(jnp.bfloat16), 'dp').astype(jnp.float32)  71.9 us
    unnamed x1, blocking collectives  57.8 us
    psum x1, blocking collectives, local(): lax.psum((mod_table, d_out_bias, d_xo_bias), ('dp', 'tensor'))  40.7 us
  transfers between devices with their start and end apart: 23, of which 15 were waited for; matrix products, arithmetic and copies ran while one was open for 17% of the time, Pallas kernels for 0%

commit v1 on v0

v1 whole, which is shorter than its diff:
```python
import functools

import jax
import jax.numpy as jnp
from jax import lax
from jax.experimental import pallas as pl
from jax.experimental.pallas import tpu as pltpu
from jax.sharding import PartitionSpec as P

HEAD = 32
XHEAD = 72
XLANE = 128
TXT = 300
TXT_PAD = 384
SIDE = 32
ITEM_SLOTS = 1024
REACH = 48
BLOCK = 128

norm_eps = 1e-06
bfloat = jnp.bfloat16
single = jnp.float32
VMEM_BYTES = 60 * 1024 * 1024


def dot_nn(a, b):
    return lax.dot_general(a, b, (((1,), (0,)), ((), ())), preferred_element_type=single)


def dot_nt(a, b):
    return lax.dot_general(a, b, (((1,), (1,)), ((), ())), preferred_element_type=single)


def dot_tn(a, b):
    return lax.dot_general(a, b, (((0,), (0,)), ((), ())), preferred_element_type=single)


def swap(values, axis, bit):
    count = lax.axis_size(axis)
    return lax.ppermute(values, axis, [(i, i ^ bit) for i in range(count)])


def shift_devices(values, step):
    count = lax.axis_size("dp") * lax.axis_size("tensor")
    pairs = [(i, i + step) for i in range(count) if 0 <= i + step < count]
    return lax.ppermute(values, ("dp", "tensor"), pairs)


def bit_set(axis, bit):
    return (lax.axis_index(axis) // bit) % 2


def upper_bits():
    count = lax.axis_size("dp")
    bits = []
    bit = 2
    while bit < count:
        bits.append(bit)
        bit *= 2
    return bits


def turns(core):
    bits = upper_bits()
    cut = len(bits) // 2
    return bits[cut:] + bits[:cut] if core else bits


def turn_bit(number, sibling=False):
    core = lax.axis_index("dp") % 2
    first, second = turns(0)[number], turns(1)[number]
    return jnp.where(core == (1 if sibling else 0), first, second)


def swap_path(values, number):
    count = lax.axis_size("dp")
    return lax.ppermute(
        values, "dp", [(i, i ^ turns(i % 2)[number]) for i in range(count)]
    )


def turn_axes(values, place):
    count = len(upper_bits())
    axes = list(range(values.ndim))
    axes[place : place + count] = [place + turns(1).index(bit) for bit in turns(0)]
    return values.transpose(axes)


def own_turns(values, place, sibling=False):
    core = lax.axis_index("dp") % 2
    return jnp.where(core == (1 if sibling else 0), values, turn_axes(values, place))


def rank_of(step, parts):
    core = step % 2
    rank = jnp.bitwise_xor(lax.axis_index("dp"), core)
    for number in range(len(upper_bits())):
        if parts[number]:
            rank = jnp.bitwise_xor(rank, turn_bit(number, core == 1))
    return rank


def tie(*arrays):
    return lax.optimization_barrier(arrays)


def grow(values, axis, bit, place, absolute):
    other = swap(values, axis, bit)
    if absolute:
        high = bit_set(axis, bit) == 1
        return jnp.stack(
            [jnp.where(high, other, values), jnp.where(high, values, other)], axis=place
        )
    return jnp.stack([values, other], axis=place)


def grow_bits(values, axis, bits, absolute):
    have = []
    for bit in bits:
        values = grow(values, axis, bit, sum(h > bit for h in have), absolute)
        have.append(bit)
    return values


def total(terms):
    summed = terms[0].astype(single)
    for term in terms[1:]:
        summed = summed + term.astype(single)
    return summed.astype(bfloat)


def pick_at(terms, place, number):
    return [lax.index_in_dim(term, number, place, keepdims=False) for term in terms]


def gather_z(piece, absolute):
    return grow_bits(piece, "tensor", [2, 1], absolute)


def grow_path(values):
    for number in range(len(upper_bits())):
        values = jnp.stack([values, swap_path(values, number)])
    return values


def reduce_z(values):
    for bit, place in ((1, 1), (2, 0)):
        own = bit_set("tensor", bit)
        keep = lax.dynamic_index_in_dim(values, own, place, keepdims=False)
        send = lax.dynamic_index_in_dim(values, 1 - own, place, keepdims=False)
        values = total([keep, swap(send, "tensor", bit)])
    return values


def halve_path(terms, number, place):
    other = swap_path(total(pick_at(terms, place, 1)), number)
    return pick_at(terms, place, 0) + [other]


def halve_z(terms, place):
    for bit, spot in ((1, place + 1), (2, place)):
        other = swap(total(pick_at(terms, spot, 1)), "tensor", bit)
        terms = pick_at(terms, spot, 0) + [other]
    return total(terms)


def attention_rows(cols):
    rows = -(-3 * cols // lax.axis_size("dp"))
    return -(-rows // 16) * 16


def bits_of(number, count):
    return [(number >> place) % 2 for place in range(count)]


def row_cuts(rows, cols):
    return sorted({0, rows} | {end % rows for end in (cols, 2 * cols, 3 * cols)})


def assemble_kernel(ranks, group, rows, cols, own, first, second, *refs):
    *outs, out, sems, out_sems = refs
    me_z = lax.axis_index("tensor")
    cuts = row_cuts(rows, cols)
    count = len(upper_bits())
    copies = []

    def put(source, rank, peer, low, high):
        place = rank * rows + low
        kind = place // cols
        target = out.at[kind, peer, pl.ds(pl.multiple_of(place - kind * cols, 16), high - low)]
        copy = pltpu.make_async_copy(source, target, sems.at[len(copies)])
        copies.append((place < 3 * cols, copy))

    for low, high in zip(cuts[:-1], cuts[1:]):
        for rank in range(ranks):
            put(own.at[rank, low:high], rank, me_z, low, high)
        for step in range(ranks):
            source = (first, second)[step % 2]
            rank = rank_of(step, bits_of(step // 2, count))
            for peer in range(1, group):
                put(
                    source.at[step // 2, peer - 1, low:high],
                    rank,
                    jnp.bitwise_xor(me_z, peer),
                    low,
                    high,
                )
    for move in ("start", "wait"):
        for live, copy in copies:

            @pl.when(live)
            def _():
                getattr(copy, move)()

    stores = [
        pltpu.make_async_copy(out.at[kind], outs[kind], out_sems.at[kind]) for kind in range(3)
    ]
    for copy in stores:
        copy.start()
    for copy in stores:
        copy.wait()


def assemble(own, first, second, cols):
    ranks, rows, features = own.shape
    group = first.shape[1] + 1
    count = (len(row_cuts(rows, cols)) - 1) * ranks * group
    anywhere = pl.BlockSpec(memory_space=pl.ANY)
    return pl.pallas_call(
        functools.partial(assemble_kernel, ranks, group, rows, cols),
        in_specs=[anywhere] * 3,
        out_specs=[anywhere] * 3,
        out_shape=[jax.ShapeDtypeStruct((group, cols, features), own.dtype)] * 3,
        scratch_shapes=[
            pltpu.VMEM((3, group, cols, features), own.dtype),
            pltpu.SemaphoreType.DMA((count,)),
            pltpu.SemaphoreType.DMA((3,)),
        ],
        compiler_params=pltpu.CompilerParams(vmem_limit_bytes=VMEM_BYTES),
        cost_estimate=pl.CostEstimate(
            flops=0, bytes_accessed=4 * ranks * rows * group * features, transcendentals=0
        ),
    )(own, first, second)


def grads_kernel(ranks, group, rows, cols, pairs, *refs):
    inputs, (extra, keep, send, whole, sems) = refs[:-5], refs[-5:]
    me_z = lax.axis_index("tensor")
    count = len(upper_bits())
    for kind, (left, right) in enumerate(pairs):
        grad = dot_tn(inputs[left][...], inputs[right][...]).astype(bfloat)
        for peer in range(group):
            whole[peer, kind * cols : (kind + 1) * cols, :] = grad[peer * cols : (peer + 1) * cols]
    begin = len(pairs) * cols
    used = begin + extra.shape[1]
    for peer in range(group):
        whole[peer, begin:used, :] = extra[peer]
        if used < rows * ranks:
            whole[peer, used:, :] = jnp.zeros((rows * ranks - used, extra.shape[2]), bfloat)
    copies = []
    for step in range(ranks):
        parts = bits_of(step // 2, count)[::-1]
        place = pl.multiple_of(rank_of(step, parts) * rows, 16)
        for peer in range(group):
            source = whole.at[jnp.bitwise_xor(me_z, peer), pl.ds(place, rows)]
            target = (keep, send)[step % 2].at[step // 2, peer]
            copies.append(pltpu.make_async_copy(source, target, sems.at[len(copies)]))
    for copy in copies:
        copy.start()
    for copy in copies:
        copy.wait()


def grads_call(arrays, pairs, extra, rows, cols):
    ranks, group = lax.axis_size("dp"), lax.axis_size("tensor")
    features = extra.shape[-1]
    height = arrays[0].shape[0]
    inside = pl.BlockSpec(memory_space=pltpu.VMEM)
    anywhere = pl.BlockSpec(memory_space=pl.ANY)
    out = jax.ShapeDtypeStruct((ranks // 2, group, rows, features), bfloat)
    return pl.pallas_call(
        functools.partial(grads_kernel, ranks, group, rows, cols, pairs),
        in_specs=[inside] * (len(arrays) + 1),
        out_specs=[anywhere] * 2,
        out_shape=[out, out],
        scratch_shapes=[
            pltpu.VMEM((group, rows * ranks, features), bfloat),
            pltpu.SemaphoreType.DMA((ranks * group,)),
        ],
        compiler_params=pltpu.CompilerParams(vmem_limit_bytes=VMEM_BYTES),
        cost_estimate=pl.CostEstimate(
            flops=6 * height * features * features,
            bytes_accessed=2 * group * rows * ranks * features,
            transcendentals=0,
        ),
    )(*arrays, extra)


def core_terms(keep, send):
    shape = (2,) * (len(upper_bits()) + 2) + keep.shape[2:]
    return [keep.reshape(shape), swap(send, "dp", 1).reshape(shape)]


def flip_z(values, place):
    for number, bit in enumerate((2, 1)):
        values = jnp.where(
            bit_set("tensor", bit) == 1, jnp.flip(values, place + number), values
        )
    return values


def share_dp(piece):
    me_d = lax.axis_index("dp")
    shape = piece.shape
    count = len(upper_bits())
    for number in range(count):
        other = swap_path(piece, number)
        high = jnp.bitwise_and(me_d, turn_bit(number)) != 0
        piece = jnp.stack([jnp.where(high, other, piece), jnp.where(high, piece, other)])
    other = turn_axes(swap(piece, "dp", 1), 0)
    high = me_d % 2 == 1
    piece = jnp.stack([jnp.where(high, other, piece), jnp.where(high, piece, other)], axis=count)
    return own_turns(piece, 0).reshape((lax.axis_size("dp"),) + shape)


def flip_dp(values, place):
    ranks = lax.axis_size("dp")
    shape = values.shape
    bits = upper_bits() + [1]
    bits.sort(reverse=True)
    values = values.reshape(shape[:place] + (2,) * len(bits) + shape[place + 1 :])
    for number, bit in enumerate(bits):
        values = jnp.where(
            bit_set("dp", bit) == 1, jnp.flip(values, place + number), values
        )
    return values.reshape(shape[:place] + (ranks,) + shape[place + 1 :])


def grid_table(bucket):
    grid_height = jnp.where(
        bucket == 0, SIDE, jnp.where(bucket == 1, 3 * SIDE // 4, 3 * SIDE // 2)
    ).astype(jnp.int32)
    grid_width = jnp.where(
        bucket == 0, SIDE, jnp.where(bucket == 1, 5 * SIDE // 4, 5 * SIDE // 8)
    ).astype(jnp.int32)
    return (grid_height, grid_width)


def inside_tap(inner_pos, grid_height, grid_width, row_step, col_step):
    grid_row = inner_pos // grid_width
    grid_col = inner_pos % grid_width
    return (
        (inner_pos < grid_height * grid_width)
        & (grid_row + row_step >= 0)
        & (grid_row + row_step < grid_height)
        & (grid_col + col_step >= 0)
        & (grid_col + col_step < grid_width)
    )


def look_up(table, item):
    known = item[:, None] == jnp.arange(table.shape[0], dtype=jnp.int32)[None, :]
    return jnp.sum(jnp.where(known, table[None, :], 0), axis=1)


def shift_blocks(slots, total, item_bucket, sign, limit):
    item = slots // ITEM_SLOTS
    inner = slots % ITEM_SLOTS
    height, width = grid_table(look_up(item_bucket, item))
    index = jnp.arange(slots.shape[0], dtype=jnp.int32)
    known = (slots >= 0) & (slots < total) & (index < limit)
    columns = jnp.arange(BLOCK + 2 * REACH, dtype=jnp.int32)
    taps = []
    for row_step in (-1, 0, 1):
        for col_step in (-1, 0, 1):
            down, right = sign * row_step, sign * col_step
            inside = known & inside_tap(inner, height, width, down, right)
            target = index % BLOCK + REACH + down * width + right
            taps.append(
                (columns[None, :] == target[:, None]) & inside[:, None]
            )
    return jnp.stack(taps, axis=0).astype(bfloat)


def fetch_weights(core, sources, held, sems):
    own, others = sources
    rows = held.shape[-2]
    chunks = []
    for chunk in range(4):
        first, second = chunk // 2, chunk % 2
        slot = chunk % 2
        rank = rank_of(core, (first, second))
        place = pl.multiple_of(rank * rows, 16)
        copies = []
        for kind in range(3):
            target = held.at[slot, kind]
            copies.append((own.at[kind, pl.ds(place, rows)], target.at[0]))
            copies.append(
                (others.at[first + 2 * second, :, kind * rows : (kind + 1) * rows], target.at[1:4])
            )
        chunks.append(
            [
                pltpu.make_async_copy(source, target, sems.at[slot, number])
                for number, (source, target) in enumerate(copies)
            ]
        )
    for chunk in range(4):

        @pl.when(pl.program_id(0) == chunk)
        def _():
            if chunk == 0:
                for copy in chunks[0]:
                    copy.start()
            if chunk < 3:
                for copy in chunks[chunk + 1]:
                    copy.start()
            for copy in chunks[chunk]:
                copy.wait()


def ffn_kernel(
    core,
    own_rows,
    own_pad,
    normed_ref,
    grad_ref,
    reach_ref,
    back_ref,
    last_ref,
    small_ref,
    *refs,
):
    count = 2 if core is not None else 1
    sources = refs[:count]
    ffn_ref, dnormed_ref, dweight_ref, dsmall_ref = refs[count : count + 4]
    active, slope, dconv, glu, dexpand, *buffers = refs[count + 4 :]
    if core is None:
        weight = lambda kind: sources[0][0, kind]
    else:
        held, sems = buffers
        fetch_weights(core, sources, held, sems)
        slot = lax.rem(pl.program_id(0), 2)
        weight = lambda kind: held[slot, kind].reshape(-1, held.shape[-1])
    @pl.when(pl.program_id(0) == 0)
    def _():
        ffn_ref[...] = jnp.zeros_like(ffn_ref)
        dnormed_ref[...] = jnp.zeros_like(dnormed_ref)

    normed = normed_ref[...]
    channels = small_ref.shape[2]
    for half in range(2):
        expand = dot_nt(normed, weight(half)) + small_ref[half, 10:11, :]
        sig = jax.nn.sigmoid(expand)
        active[half] = (expand * sig).astype(bfloat)
        mid, sig_mid = expand[2 * REACH : 2 * REACH + own_pad], sig[2 * REACH : 2 * REACH + own_pad]
        slope[half] = sig_mid * (1.0 + mid * (1.0 - sig_mid))
    dglu = dot_nt(grad_ref[...], weight(2))
    blocks = grad_ref.shape[0] // BLOCK
    for block in range(blocks):
        begin = block * BLOCK
        convs = []
        for half in range(2):
            moved = dot_nn(
                reach_ref[block], active[half, begin : begin + BLOCK + 2 * REACH, :]
            )
            total = small_ref[half, 9:10, :]
            for tap in range(9):
                total = total + moved[tap * BLOCK : (tap + 1) * BLOCK] * small_ref[half, tap : tap + 1, :]
            convs.append(total)
        value, gate = convs
        sig = jax.nn.sigmoid(gate)
        act = gate * sig
        grad = dglu[begin : begin + BLOCK]
        glu[begin : begin + BLOCK, :] = (value * act).astype(bfloat)
        dconv[0, begin : begin + BLOCK, :] = (grad * act).astype(bfloat)
        dconv[1, begin : begin + BLOCK, :] = (
            grad * value * (sig * (1.0 + gate * (1.0 - sig)))
        ).astype(bfloat)

    glu_own = glu[REACH : REACH + own_pad, :]
    if own_rows != own_pad:
        here = lax.broadcasted_iota(jnp.int32, (own_pad, channels), 0) < own_rows
        glu_own = jnp.where(here, glu_own.astype(single), 0.0).astype(bfloat)
    grad_own = grad_ref[REACH : REACH + own_pad, :]
    ffn_ref[...] += dot_nn(glu_own, weight(2))
    dweight_ref[0, 2] = dot_tn(glu_own, grad_own).astype(bfloat)
    normed_own = normed_ref[2 * REACH : 2 * REACH + own_pad, :]
    for half in range(2):
        dconv_own = dconv[half, REACH : REACH + own_pad, :].astype(single)
        if own_rows != own_pad:
            dconv_own = jnp.where(here, dconv_own, 0.0)
        dsmall_ref[half, 9:10, :] = jnp.sum(dconv_own, axis=0, keepdims=True)
        sums = [jnp.zeros((8, channels), single) for _ in range(9)]
        dbias = jnp.zeros((8, channels), single)
        for block in range(pl.cdiv(own_pad, BLOCK)):
            begin = block * BLOCK
            height = min(BLOCK, own_pad - begin)
            picks = back_ref[block] if height == BLOCK else last_ref[...]
            moved = dot_nn(picks, dconv[half, begin : begin + height + 2 * REACH, :])
            here_active = active[half, 2 * REACH + begin : 2 * REACH + begin + height, :].astype(single)
            total = jnp.zeros((height, channels), single)
            for tap in range(9):
                part = moved[tap * height : (tap + 1) * height]
                total = total + part * small_ref[half, tap : tap + 1, :]
                sums[tap] = sums[tap] + jnp.sum(
                    (part * here_active).reshape(height // 8, 8, channels), axis=0
                )
            grad = total * slope[half, begin : begin + height, :]
            dbias = dbias + jnp.sum(grad.reshape(height // 8, 8, channels), axis=0)
            dexpand[half, begin : begin + height, :] = grad.astype(bfloat)
        for tap in range(9):
            dsmall_ref[half, tap : tap + 1, :] = jnp.sum(sums[tap], axis=0, keepdims=True)
        dsmall_ref[half, 10:11, :] = jnp.sum(dbias, axis=0, keepdims=True)
        dsmall_ref[half, 11:16, :] = jnp.zeros((5, channels), single)
    for half in range(2):
        grad = dexpand[half]
        dnormed_ref[...] += dot_nn(grad, weight(half))
        dweight_ref[0, half] = dot_tn(grad, normed_own).astype(bfloat)


def ffn_call(core, own_rows, own_pad, normed, grad, reach, back, last, weights, small):
    wide, features = normed.shape
    tall = grad.shape[0]
    count = small.shape[2]
    steps = 4
    channels = count // steps
    direct = len(weights) > 1
    whole = lambda array: pl.BlockSpec(array.shape, lambda i: (0,) * array.ndim)
    rows = pl.BlockSpec((1, 3, channels, features), lambda i: (i, 0, 0, 0))
    tiny = pl.BlockSpec((2, 16, channels), lambda i: (0, 0, i))
    held = pl.BlockSpec((own_pad, features), lambda i: (0, 0))
    flops = 2 * count * features * (2 * wide + tall + 6 * own_pad) + 2 * count * 9 * 256 * 2 * (
        tall + own_pad
    )
    scratch = [
        pltpu.VMEM((2, wide, channels), bfloat),
        pltpu.VMEM((2, own_pad, channels), single),
        pltpu.VMEM((2, tall, channels), bfloat),
        pltpu.VMEM((tall, channels), bfloat),
        pltpu.VMEM((2, own_pad, channels), bfloat),
    ]
    if direct:
        group = weights[1].shape[1] + 1
        piece = weights[1].shape[2] // 3
        scratch += [
            pltpu.VMEM((2, 3, group, piece, features), bfloat),
            pltpu.SemaphoreType.DMA((2, 6)),
        ]
    return pl.pallas_call(
        functools.partial(ffn_kernel, core if direct else None, own_rows, own_pad),
        grid=(steps,),
        in_specs=[whole(normed), whole(grad), whole(reach), whole(back), whole(last), tiny]
        + ([pl.BlockSpec(memory_space=pl.ANY)] * 2 if direct else [rows]),
        out_specs=[held, held, rows, tiny],
        out_shape=[
            jax.ShapeDtypeStruct((own_pad, features), single),
            jax.ShapeDtypeStruct((own_pad, features), single),
            jax.ShapeDtypeStruct((steps, 3, channels, features), bfloat),
            jax.ShapeDtypeStruct((2, 16, count), single),
        ],
        scratch_shapes=scratch,
        compiler_params=pltpu.CompilerParams(vmem_limit_bytes=VMEM_BYTES),
        cost_estimate=pl.CostEstimate(
            flops=flops, bytes_accessed=12 * count * features, transcendentals=2 * count * tall
        ),
    )(normed, grad, reach, back, last, small, *weights)


def head_probs(query, keys, lengths):
    scores = dot_nt(query, keys) * (XHEAD ** (-0.5))
    place = lax.broadcasted_iota(jnp.int32, scores.shape, 1)
    live = place < lengths
    scores = jnp.where(live, scores, -1e30)
    top = jnp.max(scores, axis=-1, keepdims=True)
    powers = jnp.exp(scores - top)
    return powers / jnp.sum(powers, axis=-1, keepdims=True)


def cross_kernel(query_ref, keys_ref, vals_ref, length_ref, mix_ref):
    probs = head_probs(query_ref[...], keys_ref[0], length_ref[...])
    mix_ref[...] = dot_nn(probs.astype(bfloat), vals_ref[0]).astype(bfloat)


def cross_back_kernel(
    query_ref, keys_ref, vals_ref, length_ref, dmix_ref, dquery_ref, dkeys_ref, dvals_ref, dbias_ref
):
    query, keys, dmix = query_ref[...], keys_ref[0], dmix_ref[...]
    probs = head_probs(query, keys, length_ref[...])
    dprobs = dot_nt(dmix, vals_ref[0])
    dvals_ref[0] = dot_tn(dmix, probs.astype(bfloat))[:XHEAD].astype(bfloat)
    row_dot = jnp.sum(probs * dprobs, axis=-1, keepdims=True)
    dscores = (probs * (dprobs - row_dot) * (XHEAD ** (-0.5))).astype(bfloat)
    dquery = dot_nn(dscores, keys)
    dbias_ref[...] = jnp.sum(dquery, axis=0, keepdims=True)
    dquery_ref[...] = dquery.astype(bfloat)
    dkeys_ref[0] = dot_tn(query, dscores)[:XHEAD].astype(bfloat)


def cross_specs(rows):
    lane = pl.BlockSpec((rows, XLANE), lambda h: (0, h))
    text = pl.BlockSpec((1, TXT_PAD, XLANE), lambda h: (h, 0, 0))
    length = pl.BlockSpec((rows, 1), lambda h: (0, 0))
    return lane, text, length


def cross_call(query, keys, vals, lengths):
    rows, heads = query.shape[0], keys.shape[0]
    lane, text, length = cross_specs(rows)
    return pl.pallas_call(
        cross_kernel,
        grid=(heads,),
        in_specs=[lane, text, text, length],
        out_specs=lane,
        out_shape=jax.ShapeDtypeStruct((rows, heads * XLANE), bfloat),
        compiler_params=pltpu.CompilerParams(vmem_limit_bytes=VMEM_BYTES),
        cost_estimate=pl.CostEstimate(
            flops=4 * heads * rows * TXT_PAD * XLANE,
            bytes_accessed=8 * rows * heads * XLANE,
            transcendentals=heads * rows * TXT_PAD,
        ),
    )(query, keys, vals, lengths)


def cross_back_call(query, keys, vals, lengths, dmix):
    rows, heads = query.shape[0], keys.shape[0]
    lane, text, length = cross_specs(rows)
    return pl.pallas_call(
        cross_back_kernel,
        grid=(heads,),
        in_specs=[lane, text, text, length, lane],
        out_specs=[
            lane,
            pl.BlockSpec((1, XHEAD, TXT_PAD), lambda h: (h, 0, 0)),
            pl.BlockSpec((1, XHEAD, TXT_PAD), lambda h: (h, 0, 0)),
            pl.BlockSpec((1, XLANE), lambda h: (0, h)),
        ],
        out_shape=[
            jax.ShapeDtypeStruct((rows, heads * XLANE), bfloat),
            jax.ShapeDtypeStruct((heads, XHEAD, TXT_PAD), bfloat),
            jax.ShapeDtypeStruct((heads, XHEAD, TXT_PAD), bfloat),
            jax.ShapeDtypeStruct((1, heads * XLANE), single),
        ],
        compiler_params=pltpu.CompilerParams(vmem_limit_bytes=VMEM_BYTES),
        cost_estimate=pl.CostEstimate(
            flops=12 * heads * rows * TXT_PAD * XLANE,
            bytes_accessed=12 * rows * heads * XLANE,
            transcendentals=heads * rows * TXT_PAD,
        ),
    )(query, keys, vals, lengths, dmix)


def norm_parts(values):
    centred = values - jnp.mean(values, axis=-1, keepdims=True)
    inv_std = lax.rsqrt(jnp.mean(centred * centred, axis=-1, keepdims=True) + norm_eps)
    return (centred * inv_std, inv_std)


def norm_back(grad_in, normal, inv_std, scale):
    scaled = grad_in * (1.0 + scale)
    return (
        scaled
        - jnp.mean(scaled, axis=-1, keepdims=True)
        - normal * jnp.mean(scaled * normal, axis=-1, keepdims=True)
    ) * inv_std


def pad_rows(values, rows):
    return jnp.pad(values, ((0, rows - values.shape[0]),) + ((0, 0),) * (values.ndim - 1))


def pad_heads(rows, heads):
    features = rows.shape[1]
    shaped = rows.reshape(heads, XHEAD, features)
    return jnp.pad(shaped, ((0, 0), (0, XLANE - XHEAD), (0, 0))).reshape(heads * XLANE, features)


def drop_lanes(values, heads):
    return values.reshape(-1, heads, XLANE)[:, :, :XHEAD].reshape(-1, heads * XHEAD)


def local(
    tokens,
    cotangent,
    item_bucket,
    text_len,
    t_mod,
    text_tokens,
    shift_table,
    w_qkv,
    w_out,
    out_bias,
    w_xq,
    xq_bias,
    w_xkv,
    xv_bias,
    w_xo,
    xo_bias,
    w_in,
    in_bias,
    dw_weight,
    dw_bias,
    w_pt,
):
    group = lax.axis_size("tensor")
    ranks = lax.axis_size("dp")
    me_z = lax.axis_index("tensor")
    me_d = lax.axis_index("dp")
    own_rows, width = tokens.shape
    own_pad = -(-own_rows // 32) * 32
    tall = -(-(own_rows + 2 * REACH) // BLOCK) * BLOCK
    wide = tall + 2 * REACH
    total_rows = own_rows * group * ranks
    item_count = t_mod.shape[0]
    heads = width // HEAD
    xheads = width // XHEAD
    cols = w_xq.shape[1]
    channels = w_in.shape[2]
    padded_channels = -(-channels // 384) * 384
    own_start = (me_d * group + me_z) * own_rows
    first_item = own_start // ITEM_SLOTS
    last_item = (own_start + own_rows - 1) // ITEM_SLOTS
    two_items = last_item != first_item

    bits = upper_bits()
    att_piece = attention_rows(cols)
    att_pad = att_piece * ranks
    att_rows = 3 * cols
    rows_qkv = pad_rows(w_qkv.transpose(1, 2, 0).reshape(att_rows, width), att_pad)
    rows_mix = pad_rows(jnp.concatenate([w_out, w_xq.T, w_xo], axis=0), att_pad)
    ffn_piece = padded_channels // ranks
    half_count = padded_channels * group // 2
    rows_ffn = jnp.stack(
        [pad_rows(rows, padded_channels) for rows in (w_in[:, 0].T, w_in[:, 1].T, w_pt)]
    )
    own_qkv = rows_qkv.reshape(ranks, att_piece, width)
    own_mix = rows_mix.reshape(ranks, att_piece, width)
    piece_1 = lax.dynamic_index_in_dim(own_qkv, me_d, 0, keepdims=False)
    piece_2 = lax.dynamic_index_in_dim(own_mix, me_d, 0, keepdims=False)
    piece_3 = lax.dynamic_slice_in_dim(rows_ffn, me_d * ffn_piece, ffn_piece, 1)
    piece_3 = piece_3.reshape(3 * ffn_piece, width)

    def near_z(piece, far):
        near = swap(jnp.stack([piece, far]), "tensor", 1)
        return jnp.stack([near[0], far, near[1]])

    def turn(values, number):
        return jnp.stack([values, swap_path(values, number)])

    def rest_turns(values):
        for number in range(1, len(bits)):
            values = turn(values, number)
        return values.reshape((-1,) + values.shape[-3:])

    wave_1 = near_z(piece_1, swap(piece_1, "tensor", 2))
    piece_2, wave_1 = tie(piece_2, wave_1)
    far_2 = swap(piece_2, "tensor", 2)
    wave_1 = turn(wave_1, 0)
    far_2, wave_1 = tie(far_2, wave_1)
    wave_1 = rest_turns(wave_1)
    wave_2 = near_z(piece_2, far_2)
    wave_1, wave_2, piece_3, text_tokens = tie(wave_1, wave_2, piece_3, text_tokens)
    other_1 = swap(wave_1, "dp", 1)
    wave_2 = turn(wave_2, 0)
    far_3 = swap(piece_3, "tensor", 2)
    text_all = gather_z(text_tokens, True).reshape(TXT, width)
    wave_2, other_1 = tie(wave_2, other_1)
    wave_2 = rest_turns(wave_2)
    far_3, wave_2 = tie(far_3, wave_2)
    wave_3 = near_z(piece_3, far_3)
    other_2 = swap(wave_2, "dp", 1)
    wave_3, other_2 = tie(wave_3, other_2)
    wave_3 = turn(wave_3, 0)
    wave_3 = rest_turns(wave_3)
    other_3 = swap(wave_3, "dp", 1)

    wq, wk, wv = [
        part.reshape(width, width) for part in assemble(own_qkv, wave_1, other_1, cols)
    ]
    wo, wxq, wxo = [
        part.reshape(width, width) for part in assemble(own_mix, wave_2, other_2, cols)
    ]
    wxq_pad = pad_heads(wxq, xheads)
    wxo_pad = pad_heads(wxo, xheads)

    def ffn_half(core):
        count = len(bits)
        own = flip_dp(rows_ffn.reshape(3, ranks, ffn_piece, width), 1)
        own = own.reshape((3,) + (2,) * (count + 1) + (ffn_piece, width))
        own = jnp.moveaxis(lax.index_in_dim(own, core, count + 1, keepdims=False), 0, count)
        own = own_turns(own.transpose(tuple(range(count))[::-1] + (count, count + 1, count + 2)), 0, core == 1)
        others = (wave_3, other_3)[core]
        others = others.reshape((2,) * count + (group - 1, 3, ffn_piece, width))
        others = others.transpose(tuple(range(count))[::-1] + tuple(range(count, count + 4)))
        joined = jnp.concatenate([jnp.expand_dims(own, count), others], axis=count)
        joined = jnp.moveaxis(joined, count + 1, 2)
        return joined.reshape(4, 3, half_count // 4, width)

    direct = ffn_piece % 16 == 0 and len(bits) == 2
    weights_ffn = [
        [rows_ffn, (wave_3, other_3)[core]] if direct else [ffn_half(core)] for core in (0, 1)
    ]

    text_kv = jnp.einsum("td,dke->tke", text_all, w_xkv, preferred_element_type=single)
    xkv_own = jnp.stack([text_kv[:, 0], text_kv[:, 1] + xv_bias], axis=0).astype(bfloat)
    xkv_all = gather_z(xkv_own, True).reshape(group, 2, TXT, cols // XHEAD, XHEAD)
    xkv_all = xkv_all.transpose(1, 0, 3, 2, 4).reshape(2, xheads, TXT, XHEAD)
    xkv_all = jnp.pad(xkv_all, ((0, 0), (0, 0), (0, TXT_PAD - TXT), (0, XLANE - XHEAD)))
    xkeys, xvals = xkv_all[0], xkv_all[1]

    small = jnp.concatenate([dw_weight, dw_bias[None], in_bias[None]], axis=0)
    small = jnp.pad(small, ((0, 5), (0, 0), (0, padded_channels - channels)))
    small = flip_dp(small.reshape(16, 2, ranks, ffn_piece), 2)
    sizes = small.size
    small = jnp.concatenate([small.reshape(-1), xq_bias])
    small, other_1 = tie(small, other_1)
    small = gather_z(small, False).reshape(group, -1)
    xq_rel = small[:, sizes:]
    small = small[:, :sizes].reshape((group, 16, 2) + (2,) * (len(bits) + 1) + (ffn_piece,))
    small = jnp.moveaxis(small, 0, len(bits) + 3)
    down = tuple(range(2, 2 + len(bits)))
    small = small.transpose((len(bits) + 2, 1, 0) + down[::-1] + (len(bits) + 3, len(bits) + 4))
    small = [
        own_turns(small[core], 2, core == 1).reshape(2, 16, half_count) for core in (0, 1)
    ]
    xq_bias_all = jnp.stack(
        [lax.dynamic_index_in_dim(xq_rel, me_z ^ peer, 0, keepdims=False) for peer in range(group)]
    ).reshape(xheads, XHEAD)
    xq_bias_all = jnp.pad(xq_bias_all, ((0, 0), (0, XLANE - XHEAD))).reshape(xheads * XLANE)

    slots = own_start + jnp.arange(own_rows, dtype=jnp.int32)
    item = slots // ITEM_SLOTS
    inner = slots % ITEM_SLOTS
    bucket = look_up(item_bucket, item)
    grid_h, grid_w = grid_table(bucket)
    valid = inner < grid_h * grid_w
    live = valid.astype(single)[:, None]
    lengths = look_up(text_len, item)[:, None]
    in_first = (item == first_item)[:, None]
    in_second = jnp.logical_not(in_first)
    mod_first = shift_table + lax.dynamic_index_in_dim(t_mod, first_item, 0, keepdims=False)
    mod_second = shift_table + lax.dynamic_index_in_dim(t_mod, last_item, 0, keepdims=False)
    row_mod = lambda number: jnp.where(in_first, mod_first[number][None], mod_second[number][None])
    shift_a, scale_a, gate_a, shift_f, scale_f, gate_f = [row_mod(number) for number in range(6)]
    tokens_f = tokens.astype(single)
    grad_out = cotangent.astype(single)

    tall_slots = own_start - REACH + jnp.arange(tall, dtype=jnp.int32)
    reach = shift_blocks(tall_slots, total_rows, item_bucket, 1, tall)
    reach = reach.reshape(9, tall // BLOCK, BLOCK, -1).transpose(1, 0, 2, 3)
    reach = reach.reshape(tall // BLOCK, 9 * BLOCK, -1)
    pad_slots = own_start + jnp.arange(own_pad, dtype=jnp.int32)
    back = shift_blocks(pad_slots, total_rows, item_bucket, -1, own_rows)
    full_blocks = own_pad // BLOCK
    rest = own_pad - full_blocks * BLOCK
    back_full = back[:, : full_blocks * BLOCK].reshape(9, full_blocks, BLOCK, -1).transpose(1, 0, 2, 3)
    back_full = back_full.reshape(full_blocks, 9 * BLOCK, -1)
    rest = max(rest, 32)
    back_last = back[:, own_pad - rest :, : rest + 2 * REACH].reshape(9 * rest, -1)

    d_ffn = (grad_out * live * gate_f).astype(bfloat)
    above = shift_devices(d_ffn[own_rows - REACH :], 1)
    below = shift_devices(d_ffn[:REACH], -1)
    d_ffn_ext = pad_rows(jnp.concatenate([above, d_ffn, below], axis=0), tall)

    normal_a, inv_std_a = norm_parts(tokens_f)
    normed = (normal_a * (1.0 + scale_a) + shift_a).astype(bfloat)
    pre_q = dot_nt(normed, wq)
    pre_k = dot_nt(normed, wk)
    query = jax.nn.softplus(pre_q).astype(bfloat)
    keys = jax.nn.softplus(pre_k).astype(bfloat)
    values = dot_nt(normed, wv).astype(bfloat)
    lane = jnp.arange(width, dtype=jnp.int32) // HEAD
    same_head = lane[:, None] == lane[None, :]
    head_ones = same_head.astype(bfloat)
    zero = jnp.zeros((), bfloat)
    first_live = in_first & valid[:, None]
    second_live = in_second & valid[:, None]

    def packed(left, right, extra):
        full = jnp.where(same_head, dot_tn(left, right), 0.0)
        block = jnp.sum(full.reshape(heads, HEAD, width), axis=0)
        return jnp.concatenate([block, extra[None]], axis=0)

    def unpacked(block):
        return jnp.where(same_head, jnp.tile(block[:HEAD].astype(bfloat), (heads, 1)), zero)

    span_rows = own_rows * group
    span_start = me_d * span_rows
    span_first = span_start // ITEM_SLOTS
    span_last = (span_start + span_rows - 1) // ITEM_SLOTS
    span_items = (span_rows - 2) // ITEM_SLOTS + 2

    def over_items(first_part, second_part):
        parts = []
        for number in range(span_items):
            chosen = jnp.where(first_item - span_first == number, first_part, 0.0)
            also = two_items & (last_item - span_first == number)
            parts.append(chosen + jnp.where(also, second_part, 0.0))
        table = jnp.stack(parts)
        for bit in (1, 2):
            table = table + swap(table.astype(bfloat), "tensor", bit).astype(single)
        count = ranks - 1
        head_part = table[0].astype(bfloat)
        tail_part = lax.dynamic_index_in_dim(table, span_last - span_first, 0, keepdims=False)
        below = lax.ppermute(tail_part.astype(bfloat), "dp", [(i, i + 1) for i in range(count)])
        above = lax.ppermute(head_part, "dp", [(i + 1, i) for i in range(count)])
        below_same = (span_start - 1) // ITEM_SLOTS == span_first
        above_same = (span_start + span_rows) // ITEM_SLOTS == span_last
        sums = []
        for number in (first_item, last_item):
            part = lax.dynamic_index_in_dim(table, number - span_first, 0, keepdims=False)
            part = part + jnp.where(below_same & (number == span_first), below.astype(single), 0.0)
            part = part + jnp.where(above_same & (number == span_last), above.astype(single), 0.0)
            sums.append(part)
        return sums

    keys_1 = jnp.where(first_live, keys, zero)
    keys_2 = jnp.where(second_live, keys, zero)
    state_1, state_2 = over_items(
        packed(keys_1, values, jnp.sum(keys_1, axis=0, dtype=single)),
        packed(keys_2, values, jnp.sum(keys_2, axis=0, dtype=single)),
    )
    dense_1, dense_2 = unpacked(state_1), unpacked(state_2)
    total_row = jnp.where(in_first, state_1[HEAD][None], state_2[HEAD][None])
    query_1 = jnp.where(in_first, query, zero)
    query_2 = jnp.where(in_second, query, zero)
    numerator = dot_nn(query_1, dense_1) + dot_nn(query_2, dense_2)
    denominator = dot_nn((query.astype(single) * total_row).astype(bfloat), head_ones)
    attn_ratio = numerator / denominator
    attn = attn_ratio.astype(bfloat)
    attn_out = dot_nn(attn, wo) + out_bias
    after_attn = tokens_f + live * gate_a * attn_out

    cross_in = after_attn.astype(bfloat)
    xquery = (dot_nt(cross_in, wxq_pad) + xq_bias_all).astype(bfloat)
    cross_mix = cross_call(xquery, xkeys, xvals, lengths)
    cross_out = dot_nn(cross_mix, wxo_pad) + xo_bias
    after_cross = after_attn + live * cross_out

    normal_f, inv_std_f = norm_parts(after_cross)
    normed_ffn = (normal_f * (1.0 + scale_f) + shift_f).astype(bfloat)
    above = shift_devices(normed_ffn[own_rows - 2 * REACH :], 1)
    below = shift_devices(normed_ffn[: 2 * REACH], -1)
    normed_ext = pad_rows(jnp.concatenate([above, normed_ffn, below], axis=0), wide)
    tables = (reach, back_full, back_last)
    part_1 = ffn_call(
        1, own_rows, own_pad, normed_ext, d_ffn_ext, *tables, weights_ffn[1], small[1]
    )
    normed_ext, *part_1 = tie(normed_ext, *part_1)
    part_0 = ffn_call(
        0, own_rows, own_pad, normed_ext, d_ffn_ext, *tables, weights_ffn[0], small[0]
    )
    ffn_out = (part_0[0] + part_1[0])[:own_rows]
    d_normed_ffn = (part_0[1] + part_1[1])[:own_rows]
    ffn_other = swap(part_1[2], "dp", 1)
    d_normed_ffn, ffn_other = tie(d_normed_ffn, ffn_other)
    ffn_shape = (2, 2, 3) + (2,) * len(bits) + (ffn_piece, width)
    ffn_terms = [part_0[2].reshape(ffn_shape), ffn_other.reshape(ffn_shape)]
    ffn_terms = halve_path(ffn_terms, 0, 0)

    d_small = jnp.stack(
        [
            own_turns(
                part[3].astype(bfloat).reshape((2, 16) + (2,) * (len(bits) + 2) + (ffn_piece,)),
                2,
                core == 1,
            )
            for core, part in ((0, part_0), (1, part_1))
        ],
        axis=len(bits) + 2,
    )
    order = (len(bits) + 3, len(bits) + 4, 0, 1) + down[::-1] + (len(bits) + 2, len(bits) + 5)
    d_small = flip_z(d_small.transpose(order), 0)
    d_small = d_small.reshape(group, 2, 16, ranks, ffn_piece)[:, :, :11]
    d_small = flip_dp(d_small, 3).reshape(group, -1)
    small_rows = -(-d_small.shape[1] // (16 * width)) * 16
    d_small = jnp.pad(d_small, ((0, 0), (0, small_rows * width - d_small.shape[1])))
    d_small = d_small.reshape(group, small_rows, width)

    out_tokens = (after_cross + live * gate_f * ffn_out).astype(bfloat)
    d_gate_f = grad_out * live * ffn_out
    grad_cross = grad_out + norm_back(d_normed_ffn, normal_f, inv_std_f, scale_f)

    d_cross = grad_cross * live
    d_xo_bias = jnp.sum(d_cross, axis=0)
    d_cross_low = d_cross.astype(bfloat)
    d_mix = dot_nt(d_cross_low, wxo_pad).astype(bfloat)
    d_query_low, d_keys, d_vals, d_xq_part = cross_back_call(xquery, xkeys, xvals, lengths, d_mix)
    grad_attn = grad_cross + dot_nn(d_query_low, wxq_pad)
    grad_attn, ffn_terms[-1] = tie(grad_attn, ffn_terms[-1])
    for stage in range(1, len(bits)):
        ffn_terms = halve_path(ffn_terms, stage, 0 if stage == 1 else 1)

    d_attn_out = grad_attn * live * gate_a
    d_gate_a = grad_attn * live * attn_out
    d_out_bias = jnp.sum(d_attn_out, axis=0)
    d_attn_low = d_attn_out.astype(bfloat)
    d_ratio = dot_nt(d_attn_low, wo)

    text_rows = 2 * cols * TXT_PAD // width
    mix_rows = -(-(att_rows + text_rows + small_rows) // (16 * ranks)) * 16
    lanes = width // TXT_PAD
    d_kv = jnp.concatenate(
        [d_keys.reshape(group, cols, TXT_PAD), d_vals.reshape(group, cols, TXT_PAD)], axis=1
    )
    d_kv = jnp.concatenate(
        [d_kv[:, number * text_rows : (number + 1) * text_rows] for number in range(lanes)], axis=2
    )
    mix_grads = grads_call(
        [attn, d_attn_low, drop_lanes(d_query_low, xheads), cross_in, drop_lanes(cross_mix, xheads), d_cross_low],
        ((0, 1), (2, 3), (4, 5)),
        jnp.concatenate([d_kv, d_small], axis=1),
        mix_rows,
        cols,
    )
    mix_terms = core_terms(*mix_grads)
    d_numer = (d_ratio / denominator).astype(bfloat)
    d_denom = -dot_nn((d_ratio * attn_ratio).astype(bfloat), head_ones) / denominator
    d_numer_1 = jnp.where(in_first, d_numer, zero)
    d_numer_2 = jnp.where(in_second, d_numer, zero)
    query_f = query.astype(single)
    weighted = query_f * d_denom
    d_state_1, d_state_2 = over_items(
        packed(query, d_numer_1, jnp.sum(jnp.where(in_first, weighted, 0.0), axis=0)),
        packed(query, d_numer_2, jnp.sum(jnp.where(in_second, weighted, 0.0), axis=0)),
    )
    d_state_1, d_state_2, ffn_terms[-1], mix_terms[1] = tie(
        d_state_1, d_state_2, ffn_terms[-1], mix_terms[1]
    )
    for stage in range(len(bits)):
        mix_terms = halve_path(mix_terms, stage, 0)
    d_query = dot_nt(d_numer_1, dense_1) + dot_nt(d_numer_2, dense_2) + total_row * d_denom
    d_dense_1, d_dense_2 = unpacked(d_state_1), unpacked(d_state_2)
    values_1 = jnp.where(first_live, values, zero)
    values_2 = jnp.where(second_live, values, zero)
    d_total_row = jnp.where(in_first, d_state_1[HEAD][None], d_state_2[HEAD][None])
    d_keys_h = dot_nt(values_1, d_dense_1) + dot_nt(values_2, d_dense_2) + live * d_total_row
    d_values_low = (dot_nn(keys_1, d_dense_1) + dot_nn(keys_2, d_dense_2)).astype(bfloat)
    d_query_in = (d_query * jax.nn.sigmoid(pre_q)).astype(bfloat)
    d_keys_in = (d_keys_h * jax.nn.sigmoid(pre_k)).astype(bfloat)
    d_normed = dot_nn(d_query_in, wq) + dot_nn(d_keys_in, wk) + dot_nn(d_values_low, wv)
    d_tokens = grad_attn + norm_back(d_normed, normal_a, inv_std_a, scale_a)

    def mod_sum(rows):
        return jnp.stack(
            [
                jnp.sum(jnp.where(in_first, rows, 0.0), axis=0),
                jnp.sum(jnp.where(in_second, rows, 0.0), axis=0),
            ]
        )

    sums = jnp.stack(
        [
            mod_sum(rows)
            for rows in (
                d_normed,
                d_normed * normal_a,
                d_gate_a,
                d_normed_ffn,
                d_normed_ffn * normal_f,
                d_gate_f,
            )
        ],
        axis=1,
    )
    items = jnp.arange(item_count, dtype=jnp.int32)[:, None, None]
    mod_table = jnp.where(items == first_item, sums[0][None], 0.0) + jnp.where(
        (items == first_item + 1), sums[1][None], 0.0
    )
    xq_row = d_xq_part.reshape(xheads, XLANE)[:, :XHEAD].reshape(width)
    rows_all = jnp.concatenate(
        [mod_table.reshape(-1, width), jnp.stack([d_out_bias, d_xo_bias, xq_row], axis=0)], axis=0
    )
    spare = att_pad - att_rows
    rows_count = rows_all.shape[0]
    rows_all = pad_rows(rows_all.astype(bfloat), spare * group).reshape(group, spare, width)

    qkv_grads = grads_call(
        [d_query_in, d_keys_in, d_values_low, normed],
        ((0, 3), (1, 3), (2, 3)),
        rows_all,
        att_piece,
        cols,
    )
    qkv_terms = core_terms(*qkv_grads)
    qkv_terms[1], mix_terms[-1] = tie(qkv_terms[1], mix_terms[-1])
    for stage in range(len(bits)):
        qkv_terms = halve_path(qkv_terms, stage, 0)

    d_ffn_all = share_dp(halve_z(ffn_terms, 1)).transpose(1, 0, 2, 3)
    d_ffn_all = d_ffn_all.reshape(3, padded_channels, width)[:, :channels]
    d_w_in = jnp.stack([d_ffn_all[0].T, d_ffn_all[1].T], axis=1).astype(single)
    d_w_pt = d_ffn_all[2].astype(single)

    d_mix_all = share_dp(halve_z(mix_terms, 0)).reshape(-1, width)
    d_w_out = d_mix_all[:cols].astype(single)
    d_w_xq = d_mix_all[cols : 2 * cols].T.astype(single)
    d_w_xo = d_mix_all[2 * cols : 3 * cols].astype(single)
    d_kv = d_mix_all[att_rows : att_rows + text_rows]
    d_kv = jnp.concatenate(
        [d_kv[:, number * TXT_PAD : (number + 1) * TXT_PAD] for number in range(lanes)], axis=0
    )
    d_kv = d_kv.reshape(2, cols, TXT_PAD)[:, :, :TXT]
    d_xv_bias = jnp.sum(d_kv[1].astype(single), axis=1)
    d_w_xkv = jnp.einsum("td,ket->dke", text_all, d_kv, preferred_element_type=single)
    d_text = jnp.einsum("ket,dke->td", d_kv, w_xkv, preferred_element_type=single)
    d_text = reduce_z(d_text.astype(bfloat).reshape(2, 2, TXT // group, width)).astype(single)
    d_small = d_mix_all[att_rows + text_rows : att_rows + text_rows + small_rows].reshape(-1)
    d_small = d_small[: 22 * padded_channels].reshape(2, 11, padded_channels)[:, :, :channels]
    d_small = d_small.swapaxes(0, 1).astype(single)
    d_dw_weight, d_dw_bias, d_in_bias = d_small[:9], d_small[9], d_small[10]

    d_qkv_all = share_dp(halve_z(qkv_terms, 0)).reshape(-1, width)
    d_w_qkv = d_qkv_all[:att_rows].reshape(3, cols, width).transpose(2, 0, 1).astype(single)
    rows_all = gather_z(d_qkv_all[att_rows:], True).reshape(-1, width)[:rows_count].astype(single)
    d_t_mod = rows_all[:-3].reshape(mod_table.shape)
    d_out_bias, d_xo_bias = rows_all[-3], rows_all[-2]
    d_xq_bias = lax.dynamic_slice_in_dim(rows_all[-1], me_z * cols, cols, 0)
    d_shift_table = jnp.sum(d_t_mod, axis=0)
    return (
        out_tokens,
        d_tokens,
        d_t_mod,
        d_text,
        d_shift_table,
        d_w_qkv,
        d_w_out,
        d_out_bias,
        d_w_xq,
        d_xq_bias,
        d_w_xkv,
        d_xv_bias,
        d_w_xo,
        d_xo_bias,
        d_w_in,
        d_in_bias,
        d_dw_weight,
        d_dw_bias,
        d_w_pt,
    )


def solution(mesh):
    rows = P(("dp", "tensor"), None)
    placed = (
        rows,
        rows,
        P(),
        P(),
        P(),
        P("tensor", None),
        P(),
        P(None, None, "tensor"),
        P("tensor", None),
        P(),
        P(None, "tensor"),
        P("tensor"),
        P(None, None, "tensor"),
        P("tensor"),
        P("tensor", None),
        P(),
        P(None, None, "tensor"),
        P(None, "tensor"),
        P(None, None, "tensor"),
        P(None, "tensor"),
        P("tensor", None),
    )
    return jax.shard_map(
        local,
        mesh=mesh,
        in_specs=placed,
        out_specs=(
            rows,
            rows,
            P(),
            P("tensor", None),
            P(),
            P(None, None, "tensor"),
            P("tensor", None),
            P(),
            P(None, "tensor"),
            P("tensor"),
            P(None, None, "tensor"),
            P("tensor"),
            P("tensor", None),
            P(),
            P(None, None, "tensor"),
            P(None, "tensor"),
            P(None, None, "tensor"),
            P(None, "tensor"),
            P("tensor", None),
        ),
        check_vma=False,
    )
```

time: 1960 us -> 951 us (0.49)
  waiting for transfers between devices: 1160 us -> 320 us
  Pallas kernels: 0 us -> 170 us
  other arithmetic: 308 us -> 158 us
  blocking collectives: 147 us -> 0 us
  matrix products: 219 us -> 86.5 us
  local copies, waits for them, and re-layouts: 65.1 us -> 138 us
  starting transfers between devices: 31.9 us -> 66.9 us
    reduce_scatter x6 -> x0, waiting for transfers between devices: 723 us -> none  [sum_rows(): lax.psum_scatter(project(source), 'tensor', scatter_dimension=0, tiled=True)]
    ppermute x8 -> x61, waiting for transfers between devices: 4.47 us -> 320 us  [the longest x35 167 us: swap(): return lax.ppermute(values, axis, [(i, i ^ bit) for i in range(count)])]
    all_gather x6 -> x0, waiting for transfers between devices: 281 us -> none  [gather_rows(): return lax.all_gather(values, 'tensor', axis=0, tiled=True)]
    pallas_call x0 -> x8, Pallas kernels: none -> 170 us  [the longest x2 96.2 us: ffn_call(): pl.pallas_call(functools.partial(ffn_kernel, core if direct else None, ow...]
    add x8 -> x16, other arithmetic: 182 us -> 14.4 us  [the longest x4 9.64 us: total(): summed = summed + term.astype(single)]
    psum x2 -> x0, waiting for transfers between devices: 154 us -> none  [the longest x1 82.1 us: local(): lax.psum((mod_table, d_out_bias, d_xo_bias), ('dp', 'tensor'))]
    dot_general x36 -> x28, matrix products: 216 us -> 84.5 us  [the longest x12 32.7 us: dot_nn(): lax.dot_general(a, b, (((1,), (0,)), ((), ())), preferred_element_type=si...]
    psum x2 -> x0, blocking collectives: 65.3 us -> none  [the longest x1 40.7 us: local(): lax.psum((mod_table, d_out_bias, d_xo_bias), ('dp', 'tensor'))]
  transfers between devices with their start and end apart: 23 -> 61, of which waited for: 15 -> 39; matrix products, arithmetic and copies ran while one was open for 17% -> 32% of each run, Pallas kernels for 0% -> 12%
where the time goes in v1:
time: 951 us; the launch traced here: 942 us
  waiting for transfers between devices  320 us (34%)
  Pallas kernels  170 us (18%)
  other arithmetic  158 us (17%)
  local copies, waits for them, and re-layouts  138 us (15%)
  matrix products  86.5 us (9%)
  starting transfers between devices  66.9 us (7%)
    ppermute x35, waiting for transfers between devices, swap(): return lax.ppermute(values, axis, [(i, i ^ bit) for i in range(count)])  167 us
    ppermute x18, waiting for transfers between devices, swap_path(): lax.ppermute(values, 'dp', [(i, i ^ turns(i % 2)[number]) for i in range(...  136 us
    pallas_call x2, Pallas kernels, ffn_call(): pl.pallas_call(functools.partial(ffn_kernel, core if direct else None, ow...  96.2 us
    dot_general x12, matrix products, dot_nn(): lax.dot_general(a, b, (((1,), (0,)), ((), ())), preferred_element_type=si...  32.7 us
    ppermute x35, starting transfers between devices, swap(): return lax.ppermute(values, axis, [(i, i ^ bit) for i in range(count)])  29.9 us
    dot_general x10, matrix products, dot_nt(): lax.dot_general(a, b, (((1,), (1,)), ((), ())), preferred_element_type=si...  29.5 us
    another operation x6, other arithmetic, turn(): return jnp.stack([values, swap_path(values, number)])  24 us
    pallas_call x2, Pallas kernels, grads_call(): pl.pallas_call(functools.partial(grads_kernel, ranks, group, rows, cols,...  23.1 us
  transfers between devices with their start and end apart: 61, of which 39 were waited for; matrix products, arithmetic and copies ran while one was open for 32% of the time, Pallas kernels for 12%

profile of v1, /device:TPU:0, one launch (start us, length us, event | category | flops | bytes accessed | tf_op | source)
XLA Modules:
  0.0 942.4 jit_solution(11665053068681801822)
XLA Ops:
  41.7 12.5 %collective-permute-done.1 = bf16[2,112,1152]{2,1,0:T(8,128)(2,1)S(1)} collective-permute-done((bf16[2,112,1152]{2,1,0:T(8,128)(2,1)S(1)}, bf16[2,112,1152]{2,1,0:T(8,128)(2,1)S(1)}, u32[]{:S(2)}, u32[]{:S(2)}) %collective-permute-start.1) | collective-permute-done | bytes 516128 | tf_op jit(solution)/shard_map/ppermute | solution.py:40
  61.2 6.0 collective-permute-done.3
  68.5 6.4 collective-permute-done.2
  82.1 8.4 collective-permute-done.5
  105.1 8.1 collective-permute-done.18
  121.0 10.8 %collective-permute-done.19 = bf16[2,75,1152]{2,1,0:T(8,128)(2,1)} collective-permute-done((bf16[2,75,1152]{2,1,0:T(8,128)(2,1)}, bf16[2,75,1152]{2,1,0:T(8,128)(2,1)}, u32[]{:S(2)}, u32[]{:S(2)}) %collective-permute-start.19) | collective-permute-done | bytes 345632 | tf_op jit(solution)/shard_map/ppermute | solution.py:40
  136.5 4.5 collective-permute-done.13
  144.9 13.0 %collective-permute-done.12 = bf16[288,1152]{1,0:T(8,128)(2,1)} collective-permute-done((bf16[288,1152]{1,0:T(8,128)(2,1)}, bf16[288,1152]{1,0:T(8,128)(2,1)}, u32[]{:S(2)}, u32[]{:S(2)}) %collective-permute-start.12) | collective-permute-done | bytes 663584 | tf_op jit(solution)/shard_map/ppermute | solution.py:40
  157.9 8.5 collective-permute-done.20
  183.0 7.5 collective-permute-done.21
  193.7 4.6 copy.193
  202.5 8.0 shard_map.348
  211.5 5.2 convert_reduce_fusion.2
  233.6 5.7 compare_select_fusion.7
  242.2 5.5 fusion.65
  248.8 5.2 fusion.244
  269.0 31.5 %collective-permute-done.27 = bf16[2,3,288,1152]{3,2,1,0:T(8,128)(2,1)} collective-permute-done((bf16[2,3,288,1152]{3,2,1,0:T(8,128)(2,1)}, bf16[2,3,288,1152]{3,2,1,0:T(8,128)(2,1)}, u32[]{:S(2)}, u32[]{:S(2)}) %collective-permute-start.27) | collective-permute-done | bytes 3981344 | tf_op jit(solution)/shard_map/ppermute | solution.py:77
  300.6 7.3 pad_maximum_fusion
  316.2 4.4 collective-permute-done.11
  328.3 8.1 shard_map.349
  356.4 16.4 %shard_map.350 = bf16[416,2048]{1,0:T(8,128)(2,1)} custom-call(bf16[416,2048]{1,0:T(8,128)(2,1)} %add_convert_fusion.1.query_ref, bf16[16,384,128]{2,1,0:T(8,128)(2,1)} %get-tuple-element.291.keys_ref, bf16[16,384,128]{2,1,0:T(8,128)(2,1)} %get-tuple-element.290.vals_ref, s32[416,1]{1,0:T(8,128)} %copy.194.length_ref), custom_call_target="tpu_custom_call" | custom-call | flops 1308622848 | bytes 6815744 | tf_op jit(solution)/shard_map/pallas_call | solution.py:609
  372.9 6.2 fusion.269
  380.4 4.6 collective-permute-start.22
  390.5 8.9 collective-permute-done.23
  400.6 47.9 %shard_map.351 = (f32[416,1152]{1,0:T(8,128)}, f32[416,1152]{1,0:T(8,128)}, bf16[4,3,384,1152]{3,2,1,0:T(8,128)(2,1)}, f32[2,16,1536]{2,1,0:T(8,128)}) custom-call(bf16[608,1152]{1,0:T(8,128)(2,1)} %pad_maximum_fusion.13.normed_ref, bf16[512,1152]{1,0:T(8,128)(2,1)} %pad_maximum_fusion.17.grad_ref, bf16[4,1152,224]{2,1,0:T(8,128)(2,1)} %bitcast.648, ...), custom_call_target="tpu_custom_call" | custom-call | flops 28085059584 | bytes 21233664 | tf_op jit(solution)/shard_map/pallas_call | solution.py:549
  462.3 48.3 %shard_map.352 = (f32[416,1152]{1,0:T(8,128)}, f32[416,1152]{1,0:T(8,128)}, bf16[4,3,384,1152]{3,2,1,0:T(8,128)(2,1)}, f32[2,16,1536]{2,1,0:T(8,128)}) custom-call(bf16[608,1152]{1,0:T(8,128)(2,1)} %pad_maximum_fusion.13.normed_ref, bf16[512,1152]{1,0:T(8,128)(2,1)} %pad_maximum_fusion.17.grad_ref, bf16[4,1152,224]{2,1,0:T(8,128)(2,1)} %bitcast.649, ...), custom_call_target="tpu_custom_call" | custom-call | flops 28085059584 | bytes 21233664 | tf_op jit(solution)/shard_map/pallas_call | solution.py:549
  525.9 5.4 add_convert_fusion
  544.1 18.2 %shard_map.353 = (bf16[416,2048]{1,0:T(8,128)(2,1)}, bf16[16,72,384]{2,1,0:T(8,128)(2,1)}, bf16[16,72,384]{2,1,0:T(8,128)(2,1)}, f32[1,2048]{1,0:T(1,128)}) custom-call(bf16[416,2048]{1,0:T(8,128)(2,1)} %add_convert_fusion.1.query_ref, bf16[16,384,128]{2,1,0:T(8,128)(2,1)} %get-tuple-element.291.keys_ref, bf16[16,384,128]{2,1,0:T(8,128)(2,1)} %get-tuple-element.290.vals_ref, ...), custom_call_target="tpu_custom_call" | custom-call | flops 3925868544 | bytes 10223616 | tf_op jit(solution)/shard_map/pallas_call | solution.py:627
  580.5 4.9 convolution_add_fusion.5
  587.4 5.5 convert_add_fusion.2
  617.4 12.5 %shard_map.354 = (bf16[4,4,144,1152]{3,2,1,0:T(8,128)(2,1)}, bf16[4,4,144,1152]{3,2,1,0:T(8,128)(2,1)}) custom-call(bf16[416,1152]{1,0:T(8,128)(2,1)} %copy-done.153, bf16[416,1152]{1,0:T(8,128)(2,1)} %copy-done.63, bf16[416,1152]{1,0:T(8,128)(2,1)} %copy.210.refs_2_, bf16[416,1152]{1,0:T(8,128)(2,1)} %copy-done.154, bf16[416,1152]{1,0:T(8,128)(2,1)} %copy.211.refs_4_, ...), custom_call_target="tpu_custom_call" | custom-call | flops 3312451584 | bytes 10616832 | tf_op jit(solution)/shard_map/pallas_call | solution.py:281
  655.4 10.3 %collective-permute-done.32 = bf16[3,33,1152]{2,1,0:T(8,128)(2,1)S(1)} collective-permute-done((bf16[3,33,1152]{2,1,0:T(8,128)(2,1)S(1)}, bf16[3,33,1152]{2,1,0:T(8,128)(2,1)S(1)}, u32[]{:S(2)}, u32[]{:S(2)}) %collective-permute-start.32) | collective-permute-done | bytes 228128 | tf_op jit(solution)/shard_map/ppermute | solution.py:40
  672.2 9.0 collective-permute-done.35
  707.4 10.6 %shard_map.355 = (bf16[4,4,112,1152]{3,2,1,0:T(8,128)(2,1)}, bf16[4,4,112,1152]{3,2,1,0:T(8,128)(2,1)}) custom-call(bf16[416,1152]{1,0:T(8,128)(2,1)} %copy-done.152, bf16[416,1152]{1,0:T(8,128)(2,1)} %copy-done.144, bf16[416,1152]{1,0:T(8,128)(2,1)} %copy-done.147, bf16[416,1152]{1,0:T(8,128)(2,1)} %fusion.49.refs_3_, bf16[4,32,1152]{2,1,0:T(8,128)(2,1)} %bitcast.670), custom_call_target="tpu_custom_call" | custom-call | flops 3312451584 | bytes 8257536 | tf_op jit(solution)/shard_map/pallas_call | solution.py:281
  728.3 27.6 %collective-permute-done.57 = bf16[3,96,1152]{2,1,0:T(8,128)(2,1)S(1)} collective-permute-done((bf16[3,96,1152]{2,1,0:T(8,128)(2,1)S(1)}, bf16[3,96,1152]{2,1,0:T(8,128)(2,1)S(1)}, u32[]{:S(2)}, u32[]{:S(2)}) %collective-permute-start.57) | collective-permute-done | bytes 663584 | tf_op jit(solution)/shard_map/ppermute | solution.py:40
  761.2 12.9 %collective-permute-done.58 = bf16[3,96,1152]{2,1,0:T(8,128)(2,1)S(1)} collective-permute-done((bf16[3,96,1152]{2,1,0:T(8,128)(2,1)S(1)}, bf16[3,96,1152]{2,1,0:T(8,128)(2,1)S(1)}, u32[]{:S(2)}, u32[]{:S(2)}) %collective-permute-start.58) | collective-permute-done | bytes 663584 | tf_op jit(solution)/shard_map/ppermute | solution.py:77
  776.0 5.3 collective-permute-done.39
  784.8 10.8 %collective-permute-done.59 = bf16[2,3,96,1152]{3,2,1,0:T(8,128)(2,1)S(1)} collective-permute-done((bf16[2,3,96,1152]{3,2,1,0:T(8,128)(2,1)S(1)}, bf16[2,3,96,1152]{3,2,1,0:T(8,128)(2,1)S(1)}, u32[]{:S(2)}, u32[]{:S(2)}) %collective-permute-start.59) | collective-permute-done | bytes 1327136 | tf_op jit(solution)/shard_map/ppermute | solution.py:77
  800.4 16.5 %collective-permute-done.50 = bf16[144,1152]{1,0:T(8,128)(2,1)S(1)} collective-permute-done((bf16[144,1152]{1,0:T(8,128)(2,1)S(1)}, bf16[144,1152]{1,0:T(8,128)(2,1)S(1)}, u32[]{:S(2)}, u32[]{:S(2)}) %collective-permute-start.50) | collective-permute-done | bytes 331808 | tf_op jit(solution)/shard_map/ppermute | solution.py:40
  819.8 4.5 collective-permute-done.51
  825.9 16.5 %collective-permute-done.52 = bf16[2,144,1152]{2,1,0:T(8,128)(2,1)S(1)} collective-permute-done((bf16[2,144,1152]{2,1,0:T(8,128)(2,1)S(1)}, bf16[2,144,1152]{2,1,0:T(8,128)(2,1)S(1)}, u32[]{:S(2)}, u32[]{:S(2)}) %collective-permute-start.52) | collective-permute-done | bytes 663584 | tf_op jit(solution)/shard_map/ppermute | solution.py:77
  843.8 9.7 %collective-permute-done.40 = bf16[2,2,2,112,1152]{4,3,2,1,0:T(8,128)(2,1)S(1)} collective-permute-done((bf16[2,2,2,112,1152]{4,3,2,1,0:T(8,128)(2,1)S(1)}, bf16[2,2,2,112,1152]{4,3,2,1,0:T(8,128)(2,1)S(1)}, u32[]{:S(2)}, u32[]{:S(2)}) %collective-permute-start.40) | collective-permute-done | bytes 2064416 | tf_op jit(solution)/shard_map/ppermute | solution.py:77
  863.8 6.0 collective-permute-done.41
  879.0 5.2 collective-permute-done.42
  890.3 8.2 collective-permute-done.43
  901.7 4.7 collective-permute-done.44
  909.1 6.7 collective-permute-done.45
  922.4 9.4 collective-permute-done.55
  (774 shorter events, 414.8 us)
Async XLA Ops:
  3.3 35.3 %collective-permute-start = (bf16[112,1152]{1,0:T(8,128)(2,1)}, bf16[112,1152]{1,0:T(8,128)(2,1)}, u32[]{:S(2)}, u32[]{:S(2)}) collective-permute-start(bf16[112,1152]{1,0:T(8,128)(2,1)} %fusion.312), channel_id=1, source_target_pairs={{0,2},{1,3},{2,0},{3,1},{4,6},{5,7},{6,4},{7,5},{8,10},{9,11},{10,... | collective-permute-start | bytes 774152 | tf_op jit(solution)/shard_map/ppermute | solution.py:40
  40.0 14.2 %collective-permute-start.1 = (bf16[2,112,1152]{2,1,0:T(8,128)(2,1)S(1)}, bf16[2,112,1152]{2,1,0:T(8,128)(2,1)S(1)}, u32[]{:S(2)}, u32[]{:S(2)}) collective-permute-start(bf16[2,112,1152]{2,1,0:T(8,128)(2,1)S(1)} %pad_maximum_fusion.26), channel_id=1, source_target_pairs={{0,1},{1,0},{2,3},{3,2},{4,5},{5,4},{6,7},{7,6},{8,9},{9,8},{10,11... | collective-permute-start | bytes 1548296 | tf_op jit(solution)/shard_map/ppermute | solution.py:40
  55.3 11.9 %collective-permute-start.3 = (bf16[3,112,1152]{2,1,0:T(8,128)(2,1)S(1)}, bf16[3,112,1152]{2,1,0:T(8,128)(2,1)S(1)}, u32[]{:S(2)}, u32[]{:S(2)}) collective-permute-start(bf16[3,112,1152]{2,1,0:T(8,128)(2,1)S(1)} %pad_maximum_fusion.20), channel_id=1, source_target_pairs={{0,8},{4,20},{8,0},{12,28},{16,24},{20,4},{24,16},{28,12},{1,9},{5... | collective-permute-start | bytes 2322440 | tf_op jit(solution)/shard_map/ppermute | solution.py:77
  60.9 14.0 %collective-permute-start.2 = (bf16[112,1152]{1,0:T(8,128)(2,1)S(1)}, bf16[112,1152]{1,0:T(8,128)(2,1)S(1)}, u32[]{:S(2)}, u32[]{:S(2)}) collective-permute-start(bf16[112,1152]{1,0:T(8,128)(2,1)S(1)} %dynamic-slice_bitcast_fusion.1), channel_id=1, source_target_pairs={{0,2},{1,3},{2,0},{3,1},{4,6},{5,7},{6,4},{7,5},{8,10},{9,11},{10,... | collective-permute-start | bytes 774152 | tf_op jit(solution)/shard_map/ppermute | solution.py:40
  74.9 20.5 %collective-permute-start.4 = (bf16[2,3,112,1152]{3,2,1,0:T(8,128)(2,1)}, bf16[2,3,112,1152]{3,2,1,0:T(8,128)(2,1)}, u32[]{:S(2)}, u32[]{:S(2)}) collective-permute-start(bf16[2,3,112,1152]{3,2,1,0:T(8,128)(2,1)} %pad_maximum_fusion.11), channel_id=1, source_target_pairs={{0,16},{4,12},{8,24},{12,4},{16,0},{20,28},{24,8},{28,20},{1,17},{... | collective-permute-start | bytes 4644872 | tf_op jit(solution)/shard_map/ppermute | solution.py:77
  76.2 14.2 %collective-permute-start.5 = (bf16[2,112,1152]{2,1,0:T(8,128)(2,1)}, bf16[2,112,1152]{2,1,0:T(8,128)(2,1)}, u32[]{:S(2)}, u32[]{:S(2)}) collective-permute-start(bf16[2,112,1152]{2,1,0:T(8,128)(2,1)} %pad_maximum_fusion.27), channel_id=1, source_target_pairs={{0,1},{1,0},{2,3},{3,2},{4,5},{5,4},{6,7},{7,6},{8,9},{9,8},{10,11... | collective-permute-start | bytes 1548296 | tf_op jit(solution)/shard_map/ppermute | solution.py:40
  99.3 21.2 %collective-permute-start.7 = (bf16[4,3,112,1152]{3,2,1,0:T(8,128)(2,1)}, bf16[4,3,112,1152]{3,2,1,0:T(8,128)(2,1)}, u32[]{:S(2)}, u32[]{:S(2)}) collective-permute-start(bf16[4,3,112,1152]{3,2,1,0:T(8,128)(2,1)} %bitcast.14.first), channel_id=1, source_target_pairs={{0,4},{4,0},{8,12},{12,8},{16,20},{20,16},{24,28},{28,24},{1,5},{5... | collective-permute-start | bytes 9289736 | tf_op jit(solution)/shard_map/ppermute | solution.py:40
  103.7 14.4 %collective-permute-start.6 = (bf16[3,112,1152]{2,1,0:T(8,128)(2,1)S(1)}, bf16[3,112,1152]{2,1,0:T(8,128)(2,1)}, u32[]{:S(2)}, u32[]{:S(2)}) collective-permute-start(bf16[3,112,1152]{2,1,0:T(8,128)(2,1)S(1)} %pad_maximum_fusion.21), channel_id=1, source_target_pairs={{0,8},{4,20},{8,0},{12,28},{16,24},{20,4},{24,16},{28,12},{1,9},{5... | collective-permute-start | bytes 2322440 | tf_op jit(solution)/shard_map/ppermute | solution.py:77
  114.1 17.7 %collective-permute-start.19 = (bf16[2,75,1152]{2,1,0:T(8,128)(2,1)}, bf16[2,75,1152]{2,1,0:T(8,128)(2,1)}, u32[]{:S(2)}, u32[]{:S(2)}) collective-permute-start(bf16[2,75,1152]{2,1,0:T(8,128)(2,1)} %pad_maximum_fusion.32), channel_id=1, source_target_pairs={{0,1},{1,0},{2,3},{3,2},{4,5},{5,4},{6,7},{7,6},{8,9},{9,8},{10,11... | collective-permute-start | bytes 1036808 | tf_op jit(solution)/shard_map/ppermute | solution.py:40
  114.9 42.9 %collective-permute-start.12 = (bf16[288,1152]{1,0:T(8,128)(2,1)}, bf16[288,1152]{1,0:T(8,128)(2,1)}, u32[]{:S(2)}, u32[]{:S(2)}) collective-permute-start(bf16[288,1152]{1,0:T(8,128)(2,1)} %bitcast.640), channel_id=1, source_target_pairs={{0,2},{1,3},{2,0},{3,1},{4,6},{5,7},{6,4},{7,5},{8,10},{9,11},{10,... | collective-permute-start | bytes 1990664 | tf_op jit(solution)/shard_map/ppermute | solution.py:40
  120.5 20.5 %collective-permute-start.13 = (bf16[2,3,112,1152]{3,2,1,0:T(8,128)(2,1)}, bf16[2,3,112,1152]{3,2,1,0:T(8,128)(2,1)}, u32[]{:S(2)}, u32[]{:S(2)}) collective-permute-start(bf16[2,3,112,1152]{3,2,1,0:T(8,128)(2,1)} %pad_maximum_fusion.12), channel_id=1, source_target_pairs={{0,16},{4,12},{8,24},{12,4},{16,0},{20,28},{24,8},{28,20},{1,17},{... | collective-permute-start | bytes 4644872 | tf_op jit(solution)/shard_map/ppermute | solution.py:77
  136.4 30.0 %collective-permute-start.20 = (bf16[2,300,288]{1,2,0:T(8,128)(2,1)S(1)}, bf16[2,300,288]{1,2,0:T(8,128)(2,1)S(1)}, u32[]{:S(2)}, u32[]{:S(2)}) collective-permute-start(bf16[2,300,288]{1,2,0:T(8,128)(2,1)S(1)} %pad_maximum_fusion.29), channel_id=1, source_target_pairs={{0,2},{1,3},{2,0},{3,1},{4,6},{5,7},{6,4},{7,5},{8,10},{9,11},{10,... | collective-permute-start | bytes 1036808 | tf_op jit(solution)/shard_map/ppermute | solution.py:40
  157.9 65.7 %collective-permute-start.15 = (bf16[4,3,112,1152]{3,2,1,0:T(8,128)(2,1)}, bf16[4,3,112,1152]{3,2,1,0:T(8,128)(2,1)}, u32[]{:S(2)}, u32[]{:S(2)}) collective-permute-start(bf16[4,3,112,1152]{3,2,1,0:T(8,128)(2,1)} %bitcast.42.first), channel_id=1, source_target_pairs={{0,4},{4,0},{8,12},{12,8},{16,20},{20,16},{24,28},{28,24},{1,5},{5... | collective-permute-start | bytes 9289736 | tf_op jit(solution)/shard_map/ppermute | solution.py:40
  167.6 22.9 %collective-permute-start.21 = (bf16[2,2,300,288]{2,3,1,0:T(8,128)(2,1)}, bf16[2,2,300,288]{2,3,1,0:T(8,128)(2,1)}, u32[]{:S(2)}, u32[]{:S(2)}) collective-permute-start(bf16[2,2,300,288]{2,3,1,0:T(8,128)(2,1)} %pad_maximum_fusion.19), channel_id=1, source_target_pairs={{0,1},{1,0},{2,3},{3,2},{4,5},{5,4},{6,7},{7,6},{8,9},{9,8},{10,11... | collective-permute-start | bytes 2073608 | tf_op jit(solution)/shard_map/ppermute | solution.py:40
  170.8 48.6 %collective-permute-start.14 = (bf16[2,288,1152]{2,1,0:T(8,128)(2,1)}, bf16[2,288,1152]{2,1,0:T(8,128)(2,1)}, u32[]{:S(2)}, u32[]{:S(2)}) collective-permute-start(bf16[2,288,1152]{2,1,0:T(8,128)(2,1)} %pad_maximum_fusion.14), channel_id=1, source_target_pairs={{0,1},{1,0},{2,3},{3,2},{4,5},{5,4},{6,7},{7,6},{8,9},{9,8},{10,11... | collective-permute-start | bytes 3981320 | tf_op jit(solution)/shard_map/ppermute | solution.py:40
  210.5 37.4 %collective-permute-start.16 = (f32[24864]{0:T(1024)S(1)}, f32[24864]{0:T(1024)S(1)}, u32[]{:S(2)}, u32[]{:S(2)}) collective-permute-start(f32[24864]{0:T(1024)S(1)} %pad_maximum_fusion.40), channel_id=1, source_target_pairs={{0,2},{1,3},{2,0},{3,1},{4,6},{5,7},{6,4},{7,5},{8,10},{9,11},{10,... | collective-permute-start | bytes 298376 | tf_op jit(solution)/shard_map/ppermute | solution.py:40
  223.6 25.2 %collective-permute-start.26 = (bf16[3,288,1152]{2,1,0:T(8,128)(2,1)}, bf16[3,288,1152]{2,1,0:T(8,128)(2,1)}, u32[]{:S(2)}, u32[]{:S(2)}) collective-permute-start(bf16[3,288,1152]{2,1,0:T(8,128)(2,1)} %pad_maximum_fusion.9), channel_id=1, source_target_pairs={{0,8},{4,20},{8,0},{12,28},{16,24},{20,4},{24,16},{28,12},{1,9},{5... | collective-permute-start | bytes 5971976 | tf_op jit(solution)/shard_map/ppermute | solution.py:77
  254.0 46.6 %collective-permute-start.27 = (bf16[2,3,288,1152]{3,2,1,0:T(8,128)(2,1)}, bf16[2,3,288,1152]{3,2,1,0:T(8,128)(2,1)}, u32[]{:S(2)}, u32[]{:S(2)}) collective-permute-start(bf16[2,3,288,1152]{3,2,1,0:T(8,128)(2,1)} %get-tuple-element.272), channel_id=1, source_target_pairs={{0,16},{4,12},{8,24},{12,4},{16,0},{20,28},{24,8},{28,20},{1,17},{... | collective-permute-start | bytes 11943944 | tf_op jit(solution)/shard_map/ppermute | solution.py:77
  257.0 53.6 %collective-permute-start.9 = (bf16[3,33,1152]{2,1,0:T(8,128)(2,1)}, bf16[3,33,1152]{2,1,0:T(8,128)(2,1)}, u32[]{:S(2)}, u32[]{:S(2)}) collective-permute-start(bf16[3,33,1152]{2,1,0:T(8,128)(2,1)} %fusion.166), channel_id=1, source_target_pairs={{0,2},{1,3},{2,0},{3,1},{4,6},{5,7},{6,4},{7,5},{8,10},{9,11},{10,... | collective-permute-start | bytes 684296 | tf_op jit(solution)/shard_map/ppermute | solution.py:40
  307.8 92.8 %collective-permute-start.28 = (bf16[4,3,288,1152]{3,2,1,0:T(8,128)(2,1)}, bf16[4,3,288,1152]{3,2,1,0:T(8,128)(2,1)}, u32[]{:S(2)}, u32[]{:S(2)}) collective-permute-start(bf16[4,3,288,1152]{3,2,1,0:T(8,128)(2,1)} %bitcast.596), channel_id=1, source_target_pairs={{0,4},{4,0},{8,12},{12,8},{16,20},{20,16},{24,28},{28,24},{1,5},{5... | collective-permute-start | bytes 23887880 | tf_op jit(solution)/shard_map/ppermute | solution.py:40
  348.0 38.3 %collective-permute-start.24 = (bf16[48,1152]{1,0:T(8,128)(2,1)S(1)}, bf16[48,1152]{1,0:T(8,128)(2,1)S(1)}, u32[]{:S(2)}, u32[]{:S(2)}) collective-permute-start(bf16[48,1152]{1,0:T(8,128)(2,1)S(1)} %get-tuple-element.306), channel_id=1, source_target_pairs={{0,1},{1,2},{2,3},{3,4},{4,5},{5,6},{6,7},{7,8},{8,9},{9,10},{10,1... | collective-permute-start | bytes 331784 | tf_op jit(solution)/shard_map/ppermute | solution.py:46
  351.1 35.2 %collective-permute-start.25 = (bf16[48,1152]{1,0:T(8,128)(2,1)S(1)}, bf16[48,1152]{1,0:T(8,128)(2,1)S(1)}, u32[]{:S(2)}, u32[]{:S(2)}) collective-permute-start(bf16[48,1152]{1,0:T(8,128)(2,1)S(1)} %get-tuple-element.307), channel_id=1, source_target_pairs={{1,0},{2,1},{3,2},{4,3},{5,4},{6,5},{7,6},{8,7},{9,8},{10,9},{11,1... | collective-permute-start | bytes 331784 | tf_op jit(solution)/shard_map/ppermute | solution.py:46
  385.0 14.4 %collective-permute-start.23 = (bf16[96,1152]{1,0:T(8,128)(2,1)S(1)}, bf16[96,1152]{1,0:T(8,128)(2,1)S(1)}, u32[]{:S(2)}, u32[]{:S(2)}) collective-permute-start(bf16[96,1152]{1,0:T(8,128)(2,1)S(1)} %get-tuple-element.309), channel_id=1, source_target_pairs={{1,0},{2,1},{3,2},{4,3},{5,4},{6,5},{7,6},{8,7},{9,8},{10,9},{11,1... | collective-permute-start | bytes 663560 | tf_op jit(solution)/shard_map/ppermute | solution.py:46
  448.5 73.9 %collective-permute-start.29 = (bf16[4,3,384,1152]{3,2,1,0:T(8,128)(2,1)}, bf16[4,3,384,1152]{3,2,1,0:T(8,128)(2,1)}, u32[]{:S(2)}, u32[]{:S(2)}) collective-permute-start(bf16[4,3,384,1152]{3,2,1,0:T(8,128)(2,1)} %get-tuple-element.101), channel_id=1, source_target_pairs={{0,4},{4,0},{8,12},{12,8},{16,20},{20,16},{24,28},{28,24},{1,5},{5... | collective-permute-start | bytes 31850504 | tf_op jit(solution)/shard_map/ppermute | solution.py:40
  535.8 60.8 %collective-permute-start.30 = (bf16[2,3,2,2,96,1152]{5,4,1,2,3,0:T(8,128)(2,1)}, bf16[2,3,2,2,96,1152]{5,4,1,2,3,0:T(8,128)(2,1)}, u32[]{:S(2)}, u32[]{:S(2)}) collective-permute-start(bf16[2,3,2,2,96,1152]{5,4,1,2,3,0:T(8,128)(2,1)} %copy.201), channel_id=1, source_target_pairs={{0,8},{4,20},{8,0},{12,28},{16,24},{20,4},{24,16},{28,12},{1,9},{5... | collective-permute-start | bytes 15925256 | tf_op jit(solution)/shard_map/ppermute | solution.py:77
  639.1 11.5 %collective-permute-start.31 = (bf16[3,33,1152]{2,1,0:T(8,128)(2,1)S(1)}, bf16[3,33,1152]{2,1,0:T(8,128)(2,1)S(1)}, u32[]{:S(2)}, u32[]{:S(2)}) collective-permute-start(bf16[3,33,1152]{2,1,0:T(8,128)(2,1)S(1)} %fusion.159), channel_id=1, source_target_pairs={{0,1},{1,0},{2,3},{3,2},{4,5},{5,4},{6,7},{7,6},{8,9},{9,8},{10,11... | collective-permute-start | bytes 684296 | tf_op jit(solution)/shard_map/ppermute | solution.py:40
  639.7 41.6 %collective-permute-start.36 = (bf16[4,4,144,1152]{3,2,1,0:T(8,128)(2,1)}, bf16[4,4,144,1152]{3,2,1,0:T(8,128)(2,1)S(1)}, u32[]{:S(2)}, u32[]{:S(2)}) collective-permute-start(bf16[4,4,144,1152]{3,2,1,0:T(8,128)(2,1)} %get-tuple-element.112), channel_id=1, source_target_pairs={{0,4},{4,0},{8,12},{12,8},{16,20},{20,16},{24,28},{28,24},{1,5},{5... | collective-permute-start | bytes 15925256 | tf_op jit(solution)/shard_map/ppermute | solution.py:40
  649.3 32.0 %collective-permute-start.35 = (bf16[3,2,2,96,1152]{4,3,0,1,2:T(8,128)(2,1)S(1)}, bf16[3,2,2,96,1152]{4,3,0,1,2:T(8,128)(2,1)S(1)}, u32[]{:S(2)}, u32[]{:S(2)}) collective-permute-start(bf16[3,2,2,96,1152]{4,3,0,1,2:T(8,128)(2,1)S(1)} %fusion.5), channel_id=1, source_target_pairs={{0,16},{4,12},{8,24},{12,4},{16,0},{20,28},{24,8},{28,20},{1,17},{... | collective-permute-start | bytes 7962632 | tf_op jit(solution)/shard_map/ppermute | solution.py:77
  650.7 15.0 %collective-permute-start.32 = (bf16[3,33,1152]{2,1,0:T(8,128)(2,1)S(1)}, bf16[3,33,1152]{2,1,0:T(8,128)(2,1)S(1)}, u32[]{:S(2)}, u32[]{:S(2)}) collective-permute-start(bf16[3,33,1152]{2,1,0:T(8,128)(2,1)S(1)} %fusion.167), channel_id=1, source_target_pairs={{0,2},{1,3},{2,0},{3,1},{4,6},{5,7},{6,4},{7,5},{8,10},{9,11},{10,... | collective-permute-start | bytes 684296 | tf_op jit(solution)/shard_map/ppermute | solution.py:40
  688.6 32.3 %collective-permute-start.56 = (bf16[3,2,96,1152]{3,2,0,1:T(8,128)(2,1)}, bf16[3,2,96,1152]{3,2,0,1:T(8,128)(2,1)}, u32[]{:S(2)}, u32[]{:S(2)}) collective-permute-start(bf16[3,2,96,1152]{3,2,0,1:T(8,128)(2,1)} %fusion.74), channel_id=1, source_target_pairs={{0,1},{1,0},{2,3},{3,2},{4,5},{5,4},{6,7},{7,6},{8,9},{9,8},{10,11... | collective-permute-start | bytes 3981320 | tf_op jit(solution)/shard_map/ppermute | solution.py:40
  692.4 65.2 %collective-permute-start.38 = (bf16[2,2,2,144,1152]{4,3,1,2,0:T(8,128)(2,1)}, bf16[2,2,2,144,1152]{4,3,1,2,0:T(8,128)(2,1)}, u32[]{:S(2)}, u32[]{:S(2)}) collective-permute-start(bf16[2,2,2,144,1152]{4,3,1,2,0:T(8,128)(2,1)} %fusion.4), channel_id=1, source_target_pairs={{0,8},{4,20},{8,0},{12,28},{16,24},{20,4},{24,16},{28,12},{1,9},{5... | collective-permute-start | bytes 7962632 | tf_op jit(solution)/shard_map/ppermute | solution.py:77
  718.1 63.3 %collective-permute-start.37 = (bf16[4,4,112,1152]{3,2,1,0:T(8,128)(2,1)}, bf16[4,4,112,1152]{3,2,1,0:T(8,128)(2,1)S(1)}, u32[]{:S(2)}, u32[]{:S(2)}) collective-permute-start(bf16[4,4,112,1152]{3,2,1,0:T(8,128)(2,1)} %get-tuple-element.117), channel_id=1, source_target_pairs={{0,4},{4,0},{8,12},{12,8},{16,20},{20,16},{24,28},{28,24},{1,5},{5... | collective-permute-start | bytes 12386312 | tf_op jit(solution)/shard_map/ppermute | solution.py:40
  722.7 33.2 %collective-permute-start.57 = (bf16[3,96,1152]{2,1,0:T(8,128)(2,1)S(1)}, bf16[3,96,1152]{2,1,0:T(8,128)(2,1)S(1)}, u32[]{:S(2)}, u32[]{:S(2)}) collective-permute-start(bf16[3,96,1152]{2,1,0:T(8,128)(2,1)S(1)} %fusion.100), channel_id=1, source_target_pairs={{0,2},{1,3},{2,0},{3,1},{4,6},{5,7},{6,4},{7,5},{8,10},{9,11},{10,... | collective-permute-start | bytes 1990664 | tf_op jit(solution)/shard_map/ppermute | solution.py:40
  757.5 16.6 %collective-permute-start.58 = (bf16[3,96,1152]{2,1,0:T(8,128)(2,1)S(1)}, bf16[3,96,1152]{2,1,0:T(8,128)(2,1)S(1)}, u32[]{:S(2)}, u32[]{:S(2)}) collective-permute-start(bf16[3,96,1152]{2,1,0:T(8,128)(2,1)S(1)} %fusion.75), channel_id=1, source_target_pairs={{0,8},{4,20},{8,0},{12,28},{16,24},{20,4},{24,16},{28,12},{1,9},{5... | collective-permute-start | bytes 1990664 | tf_op jit(solution)/shard_map/ppermute | solution.py:77
  759.8 21.6 %collective-permute-start.39 = (bf16[2,2,144,1152]{3,2,0,1:T(8,128)(2,1)S(1)}, bf16[2,2,144,1152]{3,2,0,1:T(8,128)(2,1)S(1)}, u32[]{:S(2)}, u32[]{:S(2)}) collective-permute-start(bf16[2,2,144,1152]{3,2,0,1:T(8,128)(2,1)S(1)} %fusion.31), channel_id=1, source_target_pairs={{0,16},{4,12},{8,24},{12,4},{16,0},{20,28},{24,8},{28,20},{1,17},{... | collective-permute-start | bytes 3981320 | tf_op jit(solution)/shard_map/ppermute | solution.py:77
  774.4 21.2 %collective-permute-start.59 = (bf16[2,3,96,1152]{3,2,1,0:T(8,128)(2,1)S(1)}, bf16[2,3,96,1152]{3,2,1,0:T(8,128)(2,1)S(1)}, u32[]{:S(2)}, u32[]{:S(2)}) collective-permute-start(bf16[2,3,96,1152]{3,2,1,0:T(8,128)(2,1)S(1)} %pad_maximum_fusion.16), channel_id=1, source_target_pairs={{0,16},{4,12},{8,24},{12,4},{16,0},{20,28},{24,8},{28,20},{1,17},{... | collective-permute-start | bytes 3981320 | tf_op jit(solution)/shard_map/ppermute | solution.py:77
  781.7 17.6 %collective-permute-start.49 = (bf16[2,144,1152]{2,1,0:T(8,128)(2,1)S(1)}, bf16[2,144,1152]{2,1,0:T(8,128)(2,1)S(1)}, u32[]{:S(2)}, u32[]{:S(2)}) collective-permute-start(bf16[2,144,1152]{2,1,0:T(8,128)(2,1)S(1)} %fusion.99), channel_id=1, source_target_pairs={{0,1},{1,0},{2,3},{3,2},{4,5},{5,4},{6,7},{7,6},{8,9},{9,8},{10,11... | collective-permute-start | bytes 1990664 | tf_op jit(solution)/shard_map/ppermute | solution.py:40
  799.5 17.3 %collective-permute-start.50 = (bf16[144,1152]{1,0:T(8,128)(2,1)S(1)}, bf16[144,1152]{1,0:T(8,128)(2,1)S(1)}, u32[]{:S(2)}, u32[]{:S(2)}) collective-permute-start(bf16[144,1152]{1,0:T(8,128)(2,1)S(1)} %fusion.101), channel_id=1, source_target_pairs={{0,2},{1,3},{2,0},{3,1},{4,6},{5,7},{6,4},{7,5},{8,10},{9,11},{10,... | collective-permute-start | bytes 995336 | tf_op jit(solution)/shard_map/ppermute | solution.py:40
  799.9 56.3 %collective-permute-start.60 = (bf16[2,2,3,96,1152]{4,3,2,0,1:T(8,128)(2,1)S(1)}, bf16[2,2,3,96,1152]{4,3,2,0,1:T(8,128)(2,1)S(1)}, u32[]{:S(2)}, u32[]{:S(2)}) collective-permute-start(bf16[2,2,3,96,1152]{4,3,2,0,1:T(8,128)(2,1)S(1)} %pad_maximum_fusion.7), channel_id=1, source_target_pairs={{0,4},{4,0},{8,12},{12,8},{16,20},{20,16},{24,28},{28,24},{1,5},{5... | collective-permute-start | bytes 7962632 | tf_op jit(solution)/shard_map/ppermute | solution.py:40
  817.7 35.8 %collective-permute-start.40 = (bf16[2,2,2,112,1152]{4,3,2,1,0:T(8,128)(2,1)S(1)}, bf16[2,2,2,112,1152]{4,3,2,1,0:T(8,128)(2,1)S(1)}, u32[]{:S(2)}, u32[]{:S(2)}) collective-permute-start(bf16[2,2,2,112,1152]{4,3,2,1,0:T(8,128)(2,1)S(1)} %fusion.9), channel_id=1, source_target_pairs={{0,8},{4,20},{8,0},{12,28},{16,24},{20,4},{24,16},{28,12},{1,9},{5... | collective-permute-start | bytes 6193160 | tf_op jit(solution)/shard_map/ppermute | solution.py:77
  824.5 17.9 %collective-permute-start.52 = (bf16[2,144,1152]{2,1,0:T(8,128)(2,1)S(1)}, bf16[2,144,1152]{2,1,0:T(8,128)(2,1)S(1)}, u32[]{:S(2)}, u32[]{:S(2)}) collective-permute-start(bf16[2,144,1152]{2,1,0:T(8,128)(2,1)S(1)} %pad_maximum_fusion.23), channel_id=1, source_target_pairs={{0,16},{4,12},{8,24},{12,4},{16,0},{20,28},{24,8},{28,20},{1,17},{... | collective-permute-start | bytes 1990664 | tf_op jit(solution)/shard_map/ppermute | solution.py:77
  843.8 28.1 %collective-permute-start.53 = (bf16[2,2,144,1152]{3,2,0,1:T(8,128)(2,1)}, bf16[2,2,144,1152]{3,2,0,1:T(8,128)(2,1)}, u32[]{:S(2)}, u32[]{:S(2)}) collective-permute-start(bf16[2,2,144,1152]{3,2,0,1:T(8,128)(2,1)} %copy.227), channel_id=1, source_target_pairs={{0,4},{4,0},{8,12},{12,8},{16,20},{20,16},{24,28},{28,24},{1,5},{5... | collective-permute-start | bytes 3981320 | tf_op jit(solution)/shard_map/ppermute | solution.py:40
  854.9 14.9 %collective-permute-start.41 = (bf16[2,2,112,1152]{3,2,1,0:T(8,128)(2,1)}, bf16[2,2,112,1152]{3,2,1,0:T(8,128)(2,1)}, u32[]{:S(2)}, u32[]{:S(2)}) collective-permute-start(bf16[2,2,112,1152]{3,2,1,0:T(8,128)(2,1)} %fusion.47), channel_id=1, source_target_pairs={{0,16},{4,12},{8,24},{12,4},{16,0},{20,28},{24,8},{28,20},{1,17},{... | collective-permute-start | bytes 3096584 | tf_op jit(solution)/shard_map/ppermute | solution.py:77
  871.9 12.3 %collective-permute-start.42 = (bf16[2,112,1152]{2,1,0:T(8,128)(2,1)}, bf16[2,112,1152]{2,1,0:T(8,128)(2,1)}, u32[]{:S(2)}, u32[]{:S(2)}) collective-permute-start(bf16[2,112,1152]{2,1,0:T(8,128)(2,1)} %fusion.127), channel_id=1, source_target_pairs={{0,1},{1,0},{2,3},{3,2},{4,5},{5,4},{6,7},{7,6},{8,9},{9,8},{10,11... | collective-permute-start | bytes 1548296 | tf_op jit(solution)/shard_map/ppermute | solution.py:40
  886.4 12.2 %collective-permute-start.43 = (bf16[112,1152]{1,0:T(8,128)(2,1)}, bf16[112,1152]{1,0:T(8,128)(2,1)S(1)}, u32[]{:S(2)}, u32[]{:S(2)}) collective-permute-start(bf16[112,1152]{1,0:T(8,128)(2,1)} %fusion.128), channel_id=1, source_target_pairs={{0,2},{1,3},{2,0},{3,1},{4,6},{5,7},{6,4},{7,5},{8,10},{9,11},{10,... | collective-permute-start | bytes 774152 | tf_op jit(solution)/shard_map/ppermute | solution.py:40
  900.7 17.7 %collective-permute-start.54 = (bf16[2,75,1152]{2,1,0:T(8,128)(2,1)S(1)}, bf16[2,75,1152]{2,1,0:T(8,128)(2,1)S(1)}, u32[]{:S(2)}, u32[]{:S(2)}) collective-permute-start(bf16[2,75,1152]{2,1,0:T(8,128)(2,1)S(1)} %dynamic-slice_bitcast_fusion), channel_id=1, source_target_pairs={{0,1},{1,0},{2,3},{3,2},{4,5},{5,4},{6,7},{7,6},{8,9},{9,8},{10,11... | collective-permute-start | bytes 1036808 | tf_op jit(solution)/shard_map/ppermute | solution.py:40
  918.6 13.1 %collective-permute-start.55 = (bf16[75,1152]{1,0:T(8,128)(2,1)S(1)}, bf16[75,1152]{1,0:T(8,128)(2,1)S(1)}, u32[]{:S(2)}, u32[]{:S(2)}) collective-permute-start(bf16[75,1152]{1,0:T(8,128)(2,1)S(1)} %dynamic-slice_bitcast_fusion.2), channel_id=1, source_target_pairs={{0,2},{1,3},{2,0},{3,1},{4,6},{5,7},{6,4},{7,5},{8,10},{9,11},{10,... | collective-permute-start | bytes 518408 | tf_op jit(solution)/shard_map/ppermute | solution.py:40
  919.4 13.9 %collective-permute-start.47 = (bf16[32,1152]{1,0:T(8,128)(2,1)S(1)}, bf16[32,1152]{1,0:T(8,128)(2,1)S(1)}, u32[]{:S(2)}, u32[]{:S(2)}) collective-permute-start(bf16[32,1152]{1,0:T(8,128)(2,1)S(1)} %slice.748), channel_id=1, source_target_pairs={{0,2},{1,3},{2,0},{3,1},{4,6},{5,7},{6,4},{7,5},{8,10},{9,11},{10,... | collective-permute-start | bytes 221192 | tf_op jit(solution)/shard_map/ppermute | solution.py:40
  (179 other events, 1307.2 us)

commit v2 on v1

--- a/solution.py
+++ b/solution.py
@@ -16,6 +16,8 @@
 ITEM_SLOTS = 1024
 REACH = 48
 BLOCK = 128
+LANES = 384
+TABLE = 40
 
 norm_eps = 1e-06
 bfloat = jnp.bfloat16
@@ -157,11 +159,10 @@
     return pick_at(terms, place, 0) + [other]
 
 
-def halve_z(terms, place):
-    for bit, spot in ((1, place + 1), (2, place)):
-        other = swap(total(pick_at(terms, spot, 1)), "tensor", bit)
-        terms = pick_at(terms, spot, 0) + [other]
-    return total(terms)
+def halve_z_once(terms, bit, place):
+    place = place + 1 if bit == 1 else place
+    other = swap(total(pick_at(terms, place, 1)), "tensor", bit)
+    return pick_at(terms, place, 0) + [other]
 
 
 def attention_rows(cols):
@@ -177,7 +178,8 @@
     return sorted({0, rows} | {end % rows for end in (cols, 2 * cols, 3 * cols)})
 
 
-def assemble_kernel(ranks, group, rows, cols, own, first, second, *refs):
+def assemble_kernel(ranks, group, rows, cols, own, *refs):
+    sources, refs = refs[:4], refs[4:]
     *outs, out, sems, out_sems = refs
     me_z = lax.axis_index("tensor")
     cuts = row_cuts(rows, cols)
@@ -186,6 +188,8 @@
 
     def put(source, rank, peer, low, high):
         place = rank * rows + low
+        if isinstance(place, int) and place >= 3 * cols:
+            return
         kind = place // cols
         target = out.at[kind, peer, pl.ds(pl.multiple_of(place - kind * cols, 16), high - low)]
         copy = pltpu.make_async_copy(source, target, sems.at[len(copies)])
@@ -195,11 +199,12 @@
         for rank in range(ranks):
             put(own.at[rank, low:high], rank, me_z, low, high)
         for step in range(ranks):
-            source = (first, second)[step % 2]
+            place, upper = step // 2 // (ranks // 4), step // 2 % (ranks // 4)
+            source = sources[2 * (step % 2) + place]
             rank = rank_of(step, bits_of(step // 2, count))
             for peer in range(1, group):
                 put(
-                    source.at[step // 2, peer - 1, low:high],
+                    source.at[upper, peer - 1, low:high],
                     rank,
                     jnp.bitwise_xor(me_z, peer),
                     low,
@@ -221,14 +226,14 @@
         copy.wait()
 
 
-def assemble(own, first, second, cols):
+def assemble(own, parts, cols):
     ranks, rows, features = own.shape
-    group = first.shape[1] + 1
+    group = parts[0].shape[1] + 1
     count = (len(row_cuts(rows, cols)) - 1) * ranks * group
     anywhere = pl.BlockSpec(memory_space=pl.ANY)
     return pl.pallas_call(
         functools.partial(assemble_kernel, ranks, group, rows, cols),
-        in_specs=[anywhere] * 3,
+        in_specs=[anywhere] * 5,
         out_specs=[anywhere] * 3,
         out_shape=[jax.ShapeDtypeStruct((group, cols, features), own.dtype)] * 3,
         scratch_shapes=[
@@ -238,19 +243,27 @@
         ],
         compiler_params=pltpu.CompilerParams(vmem_limit_bytes=VMEM_BYTES),
         cost_estimate=pl.CostEstimate(
-            flops=0, bytes_accessed=4 * ranks * rows * group * features, transcendentals=0
+            flops=0, bytes_accessed=ranks * rows * group * features, transcendentals=0
         ),
-    )(own, first, second)
+    )(own, *parts)
 
 
 def grads_kernel(ranks, group, rows, cols, pairs, *refs):
-    inputs, (extra, keep, send, whole, sems) = refs[:-5], refs[-5:]
+    inputs, (extra, keep, send, whole, block, sems) = refs[:-6], refs[-6:]
     me_z = lax.axis_index("tensor")
     count = len(upper_bits())
     for kind, (left, right) in enumerate(pairs):
-        grad = dot_tn(inputs[left][...], inputs[right][...]).astype(bfloat)
+        grad = dot_tn(inputs[left][...], inputs[right][...])
+        each = cols // XHEAD
         for peer in range(group):
-            whole[peer, kind * cols : (kind + 1) * cols, :] = grad[peer * cols : (peer + 1) * cols]
+            if grad.shape[0] == group * cols:
+                rows_here = grad[peer * cols : (peer + 1) * cols]
+            else:
+                for head in range(each):
+                    place = (peer * each + head) * XLANE
+                    block[head * XHEAD : (head + 1) * XHEAD, :] = grad[place : place + XHEAD]
+                rows_here = block[...]
+            whole[peer, kind * cols : (kind + 1) * cols, :] = rows_here.astype(bfloat)
     begin = len(pairs) * cols
     used = begin + extra.shape[1]
     for peer in range(group):
@@ -278,22 +291,23 @@
     inside = pl.BlockSpec(memory_space=pltpu.VMEM)
     anywhere = pl.BlockSpec(memory_space=pl.ANY)
     out = jax.ShapeDtypeStruct((ranks // 2, group, rows, features), bfloat)
-    return pl.pallas_call(
+    return list(pl.pallas_call(
         functools.partial(grads_kernel, ranks, group, rows, cols, pairs),
         in_specs=[inside] * (len(arrays) + 1),
         out_specs=[anywhere] * 2,
         out_shape=[out, out],
         scratch_shapes=[
             pltpu.VMEM((group, rows * ranks, features), bfloat),
+            pltpu.VMEM((cols, features), single),
             pltpu.SemaphoreType.DMA((ranks * group,)),
         ],
         compiler_params=pltpu.CompilerParams(vmem_limit_bytes=VMEM_BYTES),
         cost_estimate=pl.CostEstimate(
-            flops=6 * height * features * features,
-            bytes_accessed=2 * group * rows * ranks * features,
+            flops=height * features * features,
+            bytes_accessed=group * rows * ranks * features // 2,
             transcendentals=0,
         ),
-    )(*arrays, extra)
+    )(*arrays, extra))
 
 
 def core_terms(keep, send):
@@ -309,18 +323,18 @@
     return values
 
 
-def share_dp(piece):
-    me_d = lax.axis_index("dp")
-    shape = piece.shape
+def share_turn(piece, number):
+    other = swap_path(piece, number)
+    high = jnp.bitwise_and(lax.axis_index("dp"), turn_bit(number)) != 0
+    return jnp.stack([jnp.where(high, other, piece), jnp.where(high, piece, other)])
+
+
+def share_core(piece):
     count = len(upper_bits())
-    for number in range(count):
-        other = swap_path(piece, number)
-        high = jnp.bitwise_and(me_d, turn_bit(number)) != 0
-        piece = jnp.stack([jnp.where(high, other, piece), jnp.where(high, piece, other)])
     other = turn_axes(swap(piece, "dp", 1), 0)
-    high = me_d % 2 == 1
+    high = lax.axis_index("dp") % 2 == 1
     piece = jnp.stack([jnp.where(high, other, piece), jnp.where(high, piece, other)], axis=count)
-    return own_turns(piece, 0).reshape((lax.axis_size("dp"),) + shape)
+    return own_turns(piece, 0).reshape((lax.axis_size("dp"),) + piece.shape[count + 1 :])
 
 
 def flip_dp(values, place):
@@ -382,13 +396,13 @@
     return jnp.stack(taps, axis=0).astype(bfloat)
 
 
-def fetch_weights(core, sources, held, sems):
-    own, others = sources
+def fetch_weights(core, begin, steps, sources, held, sems):
+    own, *others = sources
     rows = held.shape[-2]
     chunks = []
-    for chunk in range(4):
-        first, second = chunk // 2, chunk % 2
-        slot = chunk % 2
+    for step in range(steps):
+        first, second = (begin + step) // 2, (begin + step) % 2
+        slot = step % 2
         rank = rank_of(core, (first, second))
         place = pl.multiple_of(rank * rows, 16)
         copies = []
@@ -396,7 +410,7 @@
             target = held.at[slot, kind]
             copies.append((own.at[kind, pl.ds(place, rows)], target.at[0]))
             copies.append(
-                (others.at[first + 2 * second, :, kind * rows : (kind + 1) * rows], target.at[1:4])
+                (others[second].at[first, :, kind * rows : (kind + 1) * rows], target.at[1:4])
             )
         chunks.append(
             [
@@ -404,22 +418,25 @@
                 for number, (source, target) in enumerate(copies)
             ]
         )
-    for chunk in range(4):
-
-        @pl.when(pl.program_id(0) == chunk)
+    for step in range(steps):
+
+        @pl.when(pl.program_id(0) == step)
         def _():
-            if chunk == 0:
+            if step == 0:
                 for copy in chunks[0]:
                     copy.start()
-            if chunk < 3:
-                for copy in chunks[chunk + 1]:
+            if step + 1 < steps:
+                for copy in chunks[step + 1]:
                     copy.start()
-            for copy in chunks[chunk]:
+            for copy in chunks[step]:
                 copy.wait()
 
 
 def ffn_kernel(
     core,
+    begin,
+    steps,
+    adds,
     own_rows,
     own_pad,
     normed_ref,
@@ -430,15 +447,25 @@
     small_ref,
     *refs,
 ):
-    count = 2 if core is not None else 1
+    count = 3 if core is not None else 1
     sources = refs[:count]
+    added = None
+    if adds:
+        added = refs[count]
+        count += 1
     ffn_ref, dnormed_ref, dweight_ref, dsmall_ref = refs[count : count + 4]
     active, slope, dconv, glu, dexpand, *buffers = refs[count + 4 :]
+
+    def store_grad(kind, grad):
+        if added is not None:
+            grad = grad + added[0, kind].astype(single)
+        dweight_ref[0, kind] = grad.astype(bfloat)
+
     if core is None:
         weight = lambda kind: sources[0][0, kind]
     else:
         held, sems = buffers
-        fetch_weights(core, sources, held, sems)
+        fetch_weights(core, begin, steps, sources, held, sems)
         slot = lax.rem(pl.program_id(0), 2)
         weight = lambda kind: held[slot, kind].reshape(-1, held.shape[-1])
     @pl.when(pl.program_id(0) == 0)
@@ -483,7 +510,7 @@
         glu_own = jnp.where(here, glu_own.astype(single), 0.0).astype(bfloat)
     grad_own = grad_ref[REACH : REACH + own_pad, :]
     ffn_ref[...] += dot_nn(glu_own, weight(2))
-    dweight_ref[0, 2] = dot_tn(glu_own, grad_own).astype(bfloat)
+    store_grad(2, dot_tn(glu_own, grad_own))
     normed_own = normed_ref[2 * REACH : 2 * REACH + own_pad, :]
     for half in range(2):
         dconv_own = dconv[half, REACH : REACH + own_pad, :].astype(single)
@@ -515,19 +542,18 @@
     for half in range(2):
         grad = dexpand[half]
         dnormed_ref[...] += dot_nn(grad, weight(half))
-        dweight_ref[0, half] = dot_tn(grad, normed_own).astype(bfloat)
-
-
-def ffn_call(core, own_rows, own_pad, normed, grad, reach, back, last, weights, small):
+        store_grad(half, dot_tn(grad, normed_own))
+
+
+def ffn_call(core, begin, steps, added, own_rows, own_pad, normed, grad, reach, back, last, weights, small):
     wide, features = normed.shape
     tall = grad.shape[0]
-    count = small.shape[2]
-    steps = 4
-    channels = count // steps
+    channels = small.shape[2] // 4
+    count = channels * steps
     direct = len(weights) > 1
     whole = lambda array: pl.BlockSpec(array.shape, lambda i: (0,) * array.ndim)
-    rows = pl.BlockSpec((1, 3, channels, features), lambda i: (i, 0, 0, 0))
-    tiny = pl.BlockSpec((2, 16, channels), lambda i: (0, 0, i))
+    rows = lambda base: pl.BlockSpec((1, 3, channels, features), lambda i: (i + base, 0, 0, 0))
+    tiny = lambda base: pl.BlockSpec((2, 16, channels), lambda i: (0, 0, i + base))
     held = pl.BlockSpec((own_pad, features), lambda i: (0, 0))
     flops = 2 * count * features * (2 * wide + tall + 6 * own_pad) + 2 * count * 9 * 256 * 2 * (
         tall + own_pad
@@ -547,11 +573,14 @@
             pltpu.SemaphoreType.DMA((2, 6)),
         ]
     return pl.pallas_call(
-        functools.partial(ffn_kernel, core if direct else None, own_rows, own_pad),
+        functools.partial(
+            ffn_kernel, core if direct else None, begin, steps, len(added) > 0, own_rows, own_pad
+        ),
         grid=(steps,),
-        in_specs=[whole(normed), whole(grad), whole(reach), whole(back), whole(last), tiny]
-        + ([pl.BlockSpec(memory_space=pl.ANY)] * 2 if direct else [rows]),
-        out_specs=[held, held, rows, tiny],
+        in_specs=[whole(normed), whole(grad), whole(reach), whole(back), whole(last), tiny(begin)]
+        + ([pl.BlockSpec(memory_space=pl.ANY)] * 3 if direct else [rows(begin)])
+        + [rows(0)] * len(added),
+        out_specs=[held, held, rows(0), tiny(0)],
         out_shape=[
             jax.ShapeDtypeStruct((own_pad, features), single),
             jax.ShapeDtypeStruct((own_pad, features), single),
@@ -561,9 +590,135 @@
         scratch_shapes=scratch,
         compiler_params=pltpu.CompilerParams(vmem_limit_bytes=VMEM_BYTES),
         cost_estimate=pl.CostEstimate(
-            flops=flops, bytes_accessed=12 * count * features, transcendentals=2 * count * tall
+            flops=flops // 8, bytes_accessed=2 * count * features, transcendentals=count * tall // 4
         ),
-    )(normed, grad, reach, back, last, small, *weights)
+    )(normed, grad, reach, back, last, small, *weights, *added)
+
+
+def same_head():
+    row = lax.broadcasted_iota(jnp.int32, (LANES, LANES), 0) // HEAD
+    column = lax.broadcasted_iota(jnp.int32, (LANES, LANES), 1) // HEAD
+    return row == column
+
+
+def head_sums(left, right, extra):
+    full = jnp.where(same_head(), dot_tn(left, right), 0.0)
+    block = jnp.sum(full.reshape(LANES // HEAD, HEAD, LANES), axis=0)
+    rest = jnp.zeros((TABLE - HEAD - 1, LANES), single)
+    return jnp.concatenate([block, extra, rest], axis=0)
+
+
+def head_blocks(table):
+    tall = jnp.concatenate([table[:HEAD]] * (LANES // HEAD), axis=0)
+    return jnp.where(same_head(), tall, 0.0).astype(bfloat)
+
+
+def masked(values, column):
+    return (values.astype(single) * column).astype(bfloat)
+
+
+def softplus(values):
+    return jnp.maximum(values, 0.0) + jnp.log1p(jnp.exp(-jnp.abs(values)))
+
+
+def project_kernel(
+    normed, wq, wk, wv, first, second, pre_q, pre_k, query, keys, values, table_1, table_2
+):
+    rows = normed[...]
+    pre_q[...] = dot_nt(rows, wq[...])
+    query[...] = softplus(pre_q[...]).astype(bfloat)
+    pre_k[...] = dot_nt(rows, wk[...])
+    key = softplus(pre_k[...]).astype(bfloat)
+    keys[...] = key
+    value = dot_nt(rows, wv[...]).astype(bfloat)
+    values[...] = value
+    for column, table in ((first, table_1), (second, table_2)):
+        chosen = masked(key, column[...])
+        table[...] = head_sums(
+            chosen, value, jnp.sum(chosen.astype(single), axis=0, keepdims=True)
+        )
+
+
+def attend_kernel(query, state_1, state_2, first, second, wo, ratio, den, attn, out):
+    @pl.when(pl.program_id(0) == 0)
+    def _():
+        out[...] = jnp.zeros_like(out)
+
+    rows = query[...]
+    parts = ((first[...], state_1[...]), (second[...], state_2[...]))
+    numerator, weights = 0.0, 0.0
+    for column, state in parts:
+        numerator = numerator + dot_nn(masked(rows, column), head_blocks(state))
+        weights = weights + column * state[HEAD : HEAD + 1]
+    ones = same_head().astype(single).astype(bfloat)
+    den[...] = dot_nn((rows.astype(single) * weights).astype(bfloat), ones)
+    ratio[...] = numerator / den[...]
+    attn[...] = ratio[...].astype(bfloat)
+    out[...] += dot_nn(attn[...], wo[...])
+
+
+def attend_back_kernel(
+    grad, wo, ratio, den, query, pre_q, state_1, state_2, first, second, dquery, table_1, table_2
+):
+    dratio = dot_nt(grad[...], wo[...])
+    ones = same_head().astype(single).astype(bfloat)
+    dnumer = dratio / den[...]
+    dden = -dot_nn((dratio * ratio[...]).astype(bfloat), ones) / den[...]
+    rows = query[...]
+    total_grad, weights = 0.0, 0.0
+    for column, state, table in (
+        (first[...], state_1[...], table_1),
+        (second[...], state_2[...], table_2),
+    ):
+        chosen = (dnumer * column).astype(bfloat)
+        total_grad = total_grad + dot_nt(chosen, head_blocks(state))
+        weights = weights + column * state[HEAD : HEAD + 1]
+        extra = jnp.sum(rows.astype(single) * dden * column, axis=0, keepdims=True)
+        table[...] = head_sums(rows, chosen, extra)
+    total_grad = total_grad + weights * dden
+    dquery[...] = (total_grad * jax.nn.sigmoid(pre_q[...])).astype(bfloat)
+
+
+def project_back_kernel(
+    dquery, keys, values, pre_k, state_1, state_2, first, second, wq, wk, wv, dkeys, dvalues, dnormed
+):
+    @pl.when(pl.program_id(0) == 0)
+    def _():
+        dnormed[...] = jnp.zeros_like(dnormed)
+
+    key_grad, value_grad = 0.0, 0.0
+    for column, state in ((first[...], state_1[...]), (second[...], state_2[...])):
+        block = head_blocks(state)
+        key_grad = key_grad + dot_nt(masked(values[...], column), block)
+        key_grad = key_grad + column * state[HEAD : HEAD + 1]
+        value_grad = value_grad + dot_nn(masked(keys[...], column), block)
+    dkeys[...] = (key_grad * jax.nn.sigmoid(pre_k[...])).astype(bfloat)
+    dvalues[...] = value_grad.astype(bfloat)
+    dnormed[...] += (
+        dot_nn(dquery[...], wq[...]) + dot_nn(dkeys[...], wk[...]) + dot_nn(dvalues[...], wv[...])
+    )
+
+
+def lane_call(kernel, kinds, arrays, outs, rows, features):
+    specs = {
+        "l": pl.BlockSpec((rows, LANES), lambda g: (0, g)),
+        "w": pl.BlockSpec((LANES, features), lambda g: (g, 0)),
+        "t": pl.BlockSpec((TABLE, LANES), lambda g: (0, g)),
+        "c": pl.BlockSpec((rows, 1), lambda g: (0, 0)),
+        "a": pl.BlockSpec((rows, features), lambda g: (0, 0)),
+    }
+    shape = {"l": (rows, features), "t": (TABLE, features), "a": (rows, features)}
+    return pl.pallas_call(
+        kernel,
+        grid=(features // LANES,),
+        in_specs=[specs[kind] for kind in kinds],
+        out_specs=[specs[kind] for kind, _ in outs],
+        out_shape=[jax.ShapeDtypeStruct(shape[kind], dtype) for kind, dtype in outs],
+        compiler_params=pltpu.CompilerParams(vmem_limit_bytes=VMEM_BYTES),
+        cost_estimate=pl.CostEstimate(
+            flops=rows * features * features, bytes_accessed=rows * features, transcendentals=0
+        ),
+    )(*arrays)
 
 
 def head_probs(query, keys, lengths):
@@ -614,9 +769,9 @@
         out_shape=jax.ShapeDtypeStruct((rows, heads * XLANE), bfloat),
         compiler_params=pltpu.CompilerParams(vmem_limit_bytes=VMEM_BYTES),
         cost_estimate=pl.CostEstimate(
-            flops=4 * heads * rows * TXT_PAD * XLANE,
-            bytes_accessed=8 * rows * heads * XLANE,
-            transcendentals=heads * rows * TXT_PAD,
+            flops=heads * rows * TXT_PAD * XLANE,
+            bytes_accessed=2 * rows * heads * XLANE,
+            transcendentals=heads * rows * TXT_PAD // 8,
         ),
     )(query, keys, vals, lengths)
 
@@ -642,9 +797,9 @@
         ],
         compiler_params=pltpu.CompilerParams(vmem_limit_bytes=VMEM_BYTES),
         cost_estimate=pl.CostEstimate(
-            flops=12 * heads * rows * TXT_PAD * XLANE,
-            bytes_accessed=12 * rows * heads * XLANE,
-            transcendentals=heads * rows * TXT_PAD,
+            flops=heads * rows * TXT_PAD * XLANE,
+            bytes_accessed=2 * rows * heads * XLANE,
+            transcendentals=heads * rows * TXT_PAD // 8,
         ),
     )(query, keys, vals, lengths, dmix)
 
@@ -672,10 +827,6 @@
     features = rows.shape[1]
     shaped = rows.reshape(heads, XHEAD, features)
     return jnp.pad(shaped, ((0, 0), (0, XLANE - XHEAD), (0, 0))).reshape(heads * XLANE, features)
-
-
-def drop_lanes(values, heads):
-    return values.reshape(-1, heads, XLANE)[:, :, :XHEAD].reshape(-1, heads * XHEAD)
 
 
 def local(
@@ -736,8 +887,6 @@
     own_mix = rows_mix.reshape(ranks, att_piece, width)
     piece_1 = lax.dynamic_index_in_dim(own_qkv, me_d, 0, keepdims=False)
     piece_2 = lax.dynamic_index_in_dim(own_mix, me_d, 0, keepdims=False)
-    piece_3 = lax.dynamic_slice_in_dim(rows_ffn, me_d * ffn_piece, ffn_piece, 1)
-    piece_3 = piece_3.reshape(3 * ffn_piece, width)
 
     def near_z(piece, far):
         near = swap(jnp.stack([piece, far]), "tensor", 1)
@@ -746,95 +895,16 @@
     def turn(values, number):
         return jnp.stack([values, swap_path(values, number)])
 
-    def rest_turns(values):
-        for number in range(1, len(bits)):
+    def mid_turns(values):
+        for number in range(1, len(bits) - 1):
             values = turn(values, number)
         return values.reshape((-1,) + values.shape[-3:])
 
-    wave_1 = near_z(piece_1, swap(piece_1, "tensor", 2))
-    piece_2, wave_1 = tie(piece_2, wave_1)
-    far_2 = swap(piece_2, "tensor", 2)
-    wave_1 = turn(wave_1, 0)
-    far_2, wave_1 = tie(far_2, wave_1)
-    wave_1 = rest_turns(wave_1)
-    wave_2 = near_z(piece_2, far_2)
-    wave_1, wave_2, piece_3, text_tokens = tie(wave_1, wave_2, piece_3, text_tokens)
-    other_1 = swap(wave_1, "dp", 1)
-    wave_2 = turn(wave_2, 0)
-    far_3 = swap(piece_3, "tensor", 2)
-    text_all = gather_z(text_tokens, True).reshape(TXT, width)
-    wave_2, other_1 = tie(wave_2, other_1)
-    wave_2 = rest_turns(wave_2)
-    far_3, wave_2 = tie(far_3, wave_2)
-    wave_3 = near_z(piece_3, far_3)
-    other_2 = swap(wave_2, "dp", 1)
-    wave_3, other_2 = tie(wave_3, other_2)
-    wave_3 = turn(wave_3, 0)
-    wave_3 = rest_turns(wave_3)
-    other_3 = swap(wave_3, "dp", 1)
-
-    wq, wk, wv = [
-        part.reshape(width, width) for part in assemble(own_qkv, wave_1, other_1, cols)
-    ]
-    wo, wxq, wxo = [
-        part.reshape(width, width) for part in assemble(own_mix, wave_2, other_2, cols)
-    ]
-    wxq_pad = pad_heads(wxq, xheads)
-    wxo_pad = pad_heads(wxo, xheads)
-
-    def ffn_half(core):
-        count = len(bits)
-        own = flip_dp(rows_ffn.reshape(3, ranks, ffn_piece, width), 1)
-        own = own.reshape((3,) + (2,) * (count + 1) + (ffn_piece, width))
-        own = jnp.moveaxis(lax.index_in_dim(own, core, count + 1, keepdims=False), 0, count)
-        own = own_turns(own.transpose(tuple(range(count))[::-1] + (count, count + 1, count + 2)), 0, core == 1)
-        others = (wave_3, other_3)[core]
-        others = others.reshape((2,) * count + (group - 1, 3, ffn_piece, width))
-        others = others.transpose(tuple(range(count))[::-1] + tuple(range(count, count + 4)))
-        joined = jnp.concatenate([jnp.expand_dims(own, count), others], axis=count)
-        joined = jnp.moveaxis(joined, count + 1, 2)
-        return joined.reshape(4, 3, half_count // 4, width)
-
-    direct = ffn_piece % 16 == 0 and len(bits) == 2
-    weights_ffn = [
-        [rows_ffn, (wave_3, other_3)[core]] if direct else [ffn_half(core)] for core in (0, 1)
-    ]
-
-    text_kv = jnp.einsum("td,dke->tke", text_all, w_xkv, preferred_element_type=single)
-    xkv_own = jnp.stack([text_kv[:, 0], text_kv[:, 1] + xv_bias], axis=0).astype(bfloat)
-    xkv_all = gather_z(xkv_own, True).reshape(group, 2, TXT, cols // XHEAD, XHEAD)
-    xkv_all = xkv_all.transpose(1, 0, 3, 2, 4).reshape(2, xheads, TXT, XHEAD)
-    xkv_all = jnp.pad(xkv_all, ((0, 0), (0, 0), (0, TXT_PAD - TXT), (0, XLANE - XHEAD)))
-    xkeys, xvals = xkv_all[0], xkv_all[1]
-
-    small = jnp.concatenate([dw_weight, dw_bias[None], in_bias[None]], axis=0)
-    small = jnp.pad(small, ((0, 5), (0, 0), (0, padded_channels - channels)))
-    small = flip_dp(small.reshape(16, 2, ranks, ffn_piece), 2)
-    sizes = small.size
-    small = jnp.concatenate([small.reshape(-1), xq_bias])
-    small, other_1 = tie(small, other_1)
-    small = gather_z(small, False).reshape(group, -1)
-    xq_rel = small[:, sizes:]
-    small = small[:, :sizes].reshape((group, 16, 2) + (2,) * (len(bits) + 1) + (ffn_piece,))
-    small = jnp.moveaxis(small, 0, len(bits) + 3)
-    down = tuple(range(2, 2 + len(bits)))
-    small = small.transpose((len(bits) + 2, 1, 0) + down[::-1] + (len(bits) + 3, len(bits) + 4))
-    small = [
-        own_turns(small[core], 2, core == 1).reshape(2, 16, half_count) for core in (0, 1)
-    ]
-    xq_bias_all = jnp.stack(
-        [lax.dynamic_index_in_dim(xq_rel, me_z ^ peer, 0, keepdims=False) for peer in range(group)]
-    ).reshape(xheads, XHEAD)
-    xq_bias_all = jnp.pad(xq_bias_all, ((0, 0), (0, XLANE - XHEAD))).reshape(xheads * XLANE)
-
-    slots = own_start + jnp.arange(own_rows, dtype=jnp.int32)
-    item = slots // ITEM_SLOTS
-    inner = slots % ITEM_SLOTS
-    bucket = look_up(item_bucket, item)
-    grid_h, grid_w = grid_table(bucket)
-    valid = inner < grid_h * grid_w
-    live = valid.astype(single)[:, None]
-    lengths = look_up(text_len, item)[:, None]
+    def last_turn(values):
+        return swap_path(values, len(bits) - 1)
+
+    own_slots = own_start + jnp.arange(own_rows, dtype=jnp.int32)
+    item = own_slots // ITEM_SLOTS
     in_first = (item == first_item)[:, None]
     in_second = jnp.logical_not(in_first)
     mod_first = shift_table + lax.dynamic_index_in_dim(t_mod, first_item, 0, keepdims=False)
@@ -843,11 +913,34 @@
     shift_a, scale_a, gate_a, shift_f, scale_f, gate_f = [row_mod(number) for number in range(6)]
     tokens_f = tokens.astype(single)
     grad_out = cotangent.astype(single)
-
+    normal_a, inv_std_a = norm_parts(tokens_f)
+    normed = (normal_a * (1.0 + scale_a) + shift_a).astype(bfloat)
+
+    far_1 = swap(piece_1, "tensor", 2)
+    far_1, normed = tie(far_1, normed)
+    wave_1 = near_z(piece_1, far_1)
+    wave_1, rows_ffn, item_bucket, piece_2 = tie(wave_1, rows_ffn, item_bucket, piece_2)
+    far_2 = swap(piece_2, "tensor", 2)
+    wave_1 = turn(wave_1, 0)
+    inner = own_slots % ITEM_SLOTS
+    grid_h, grid_w = grid_table(look_up(item_bucket, item))
+    valid = inner < grid_h * grid_w
+    live = valid.astype(single)[:, None]
     tall_slots = own_start - REACH + jnp.arange(tall, dtype=jnp.int32)
     reach = shift_blocks(tall_slots, total_rows, item_bucket, 1, tall)
     reach = reach.reshape(9, tall // BLOCK, BLOCK, -1).transpose(1, 0, 2, 3)
     reach = reach.reshape(tall // BLOCK, 9 * BLOCK, -1)
+    far_2, wave_1, reach, text_tokens = tie(far_2, wave_1, reach, text_tokens)
+    wave_1 = mid_turns(wave_1)
+    last_1 = last_turn(wave_1)
+    core_1 = swap(wave_1, "dp", 1)
+    wave_2 = near_z(piece_2, far_2)
+    text_rows_here = text_tokens.shape[0]
+    text_half = pad_rows(text_tokens, -(-text_rows_here // 16) * 16)
+    text_half = lax.dynamic_index_in_dim(
+        text_half.reshape(2, -1, width), me_d % 2, 0, keepdims=False
+    )
+    text_far = swap(text_half, "tensor", 2)
     pad_slots = own_start + jnp.arange(own_pad, dtype=jnp.int32)
     back = shift_blocks(pad_slots, total_rows, item_bucket, -1, own_rows)
     full_blocks = own_pad // BLOCK
@@ -856,33 +949,34 @@
     back_full = back_full.reshape(full_blocks, 9 * BLOCK, -1)
     rest = max(rest, 32)
     back_last = back[:, own_pad - rest :, : rest + 2 * REACH].reshape(9 * rest, -1)
-
     d_ffn = (grad_out * live * gate_f).astype(bfloat)
-    above = shift_devices(d_ffn[own_rows - REACH :], 1)
-    below = shift_devices(d_ffn[:REACH], -1)
-    d_ffn_ext = pad_rows(jnp.concatenate([above, d_ffn, below], axis=0), tall)
-
-    normal_a, inv_std_a = norm_parts(tokens_f)
-    normed = (normal_a * (1.0 + scale_a) + shift_a).astype(bfloat)
-    pre_q = dot_nt(normed, wq)
-    pre_k = dot_nt(normed, wk)
-    query = jax.nn.softplus(pre_q).astype(bfloat)
-    keys = jax.nn.softplus(pre_k).astype(bfloat)
-    values = dot_nt(normed, wv).astype(bfloat)
-    lane = jnp.arange(width, dtype=jnp.int32) // HEAD
-    same_head = lane[:, None] == lane[None, :]
-    head_ones = same_head.astype(bfloat)
-    zero = jnp.zeros((), bfloat)
-    first_live = in_first & valid[:, None]
-    second_live = in_second & valid[:, None]
-
-    def packed(left, right, extra):
-        full = jnp.where(same_head, dot_tn(left, right), 0.0)
-        block = jnp.sum(full.reshape(heads, HEAD, width), axis=0)
-        return jnp.concatenate([block, extra[None]], axis=0)
-
-    def unpacked(block):
-        return jnp.where(same_head, jnp.tile(block[:HEAD].astype(bfloat), (heads, 1)), zero)
+    wave_1, last_1, core_1, wave_2, back_full, back_last, d_ffn, text_far = tie(
+        wave_1, last_1, core_1, wave_2, back_full, back_last, d_ffn, text_far
+    )
+    core_last_1 = swap(last_1, "dp", 1)
+    piece_3 = lax.dynamic_slice_in_dim(rows_ffn, me_d * ffn_piece, ffn_piece, 1)
+    piece_3 = piece_3.reshape(3 * ffn_piece, width)
+    core_last_1, wave_2, piece_3 = tie(core_last_1, wave_2, piece_3)
+    wave_2 = turn(wave_2, 0)
+    far_3 = swap(piece_3, "tensor", 2)
+    text_near = swap(jnp.stack([text_half, text_far]), "tensor", 1)
+    wq, wk, wv = [
+        part.reshape(width, width) for part in assemble(own_qkv, (wave_1, last_1, core_1, core_last_1), cols)
+    ]
+    wq, wk, wv, wave_2 = tie(wq, wk, wv, wave_2)
+    wave_2 = mid_turns(wave_2)
+    last_2 = last_turn(wave_2)
+    core_2 = swap(wave_2, "dp", 1)
+    first_live = (in_first & valid[:, None]).astype(single)
+    second_live = (in_second & valid[:, None]).astype(single)
+    first_all, second_all = in_first.astype(single), in_second.astype(single)
+    over_lanes = functools.partial(lane_call, rows=own_rows, features=width)
+    pre_q, pre_k, query, keys, values, table_1, table_2 = over_lanes(
+        project_kernel,
+        "awwwcc",
+        (normed, wq, wk, wv, first_live, second_live),
+        (("l", single), ("l", single), ("l", bfloat), ("l", bfloat), ("l", bfloat), ("t", single), ("t", single)),
+    )
 
     span_rows = own_rows * group
     span_start = me_d * span_rows
@@ -890,82 +984,179 @@
     span_last = (span_start + span_rows - 1) // ITEM_SLOTS
     span_items = (span_rows - 2) // ITEM_SLOTS + 2
 
-    def over_items(first_part, second_part):
+    def item_table(first_part, second_part):
         parts = []
         for number in range(span_items):
             chosen = jnp.where(first_item - span_first == number, first_part, 0.0)
             also = two_items & (last_item - span_first == number)
             parts.append(chosen + jnp.where(also, second_part, 0.0))
-        table = jnp.stack(parts)
-        for bit in (1, 2):
-            table = table + swap(table.astype(bfloat), "tensor", bit).astype(single)
+        return jnp.stack(parts).astype(bfloat)
+
+    def item_sums(table):
         count = ranks - 1
-        head_part = table[0].astype(bfloat)
         tail_part = lax.dynamic_index_in_dim(table, span_last - span_first, 0, keepdims=False)
-        below = lax.ppermute(tail_part.astype(bfloat), "dp", [(i, i + 1) for i in range(count)])
-        above = lax.ppermute(head_part, "dp", [(i + 1, i) for i in range(count)])
+        below = lax.ppermute(tail_part, "dp", [(i, i + 1) for i in range(count)])
+        above = lax.ppermute(table[0], "dp", [(i + 1, i) for i in range(count)])
         below_same = (span_start - 1) // ITEM_SLOTS == span_first
         above_same = (span_start + span_rows) // ITEM_SLOTS == span_last
         sums = []
         for number in (first_item, last_item):
             part = lax.dynamic_index_in_dim(table, number - span_first, 0, keepdims=False)
+            part = part.astype(single)
             part = part + jnp.where(below_same & (number == span_first), below.astype(single), 0.0)
             part = part + jnp.where(above_same & (number == span_last), above.astype(single), 0.0)
             sums.append(part)
         return sums
 
-    keys_1 = jnp.where(first_live, keys, zero)
-    keys_2 = jnp.where(second_live, keys, zero)
-    state_1, state_2 = over_items(
-        packed(keys_1, values, jnp.sum(keys_1, axis=0, dtype=single)),
-        packed(keys_2, values, jnp.sum(keys_2, axis=0, dtype=single)),
-    )
-    dense_1, dense_2 = unpacked(state_1), unpacked(state_2)
-    total_row = jnp.where(in_first, state_1[HEAD][None], state_2[HEAD][None])
-    query_1 = jnp.where(in_first, query, zero)
-    query_2 = jnp.where(in_second, query, zero)
-    numerator = dot_nn(query_1, dense_1) + dot_nn(query_2, dense_2)
-    denominator = dot_nn((query.astype(single) * total_row).astype(bfloat), head_ones)
-    attn_ratio = numerator / denominator
-    attn = attn_ratio.astype(bfloat)
-    attn_out = dot_nn(attn, wo) + out_bias
+    small_rel = jnp.concatenate([dw_weight, dw_bias[None], in_bias[None]], axis=0)
+    small_rel = jnp.pad(small_rel, ((0, 5), (0, 0), (0, padded_channels - channels)))
+    sizes = small_rel.size
+    small_rel = jnp.concatenate([small_rel.reshape(-1), xq_bias])
+    down = tuple(range(2, 2 + len(bits)))
+
+    table = item_table(table_1, table_2)
+    table, far_3, text_near = tie(table, far_3, text_near)
+    table = total([table, swap(table, "tensor", 1)])
+    wave_3 = near_z(piece_3, far_3)
+    in_order = lambda rel: [
+        lax.dynamic_index_in_dim(rel, me_z ^ peer, 0, keepdims=False) for peer in range(group)
+    ]
+    by_core = lambda one, two: jnp.stack(
+        [jnp.where(me_d % 2 == 0, one, two), jnp.where(me_d % 2 == 0, two, one)]
+    )
+    text_rel = jnp.stack([text_half, text_near[0], text_far, text_near[1]])
+    text_other = swap(text_rel, "dp", 1)
+    table, last_2, core_2, text_other = tie(table, last_2, core_2, text_other)
+    table = total([table, swap(table, "tensor", 2)])
+    core_last_2 = swap(last_2, "dp", 1)
+    text_rel = by_core(text_rel, text_other).swapaxes(0, 1).reshape(group, -1, width)
+    text_all = jnp.concatenate(in_order(text_rel[:, :text_rows_here]))
+    text_kv = jnp.einsum("td,dke->tke", text_all, w_xkv, preferred_element_type=single)
+    xkv_own = jnp.stack([text_kv[:, 0], text_kv[:, 1] + xv_bias], axis=0).astype(bfloat)
+    xkv_half = lax.dynamic_index_in_dim(xkv_own, me_d % 2, 0, keepdims=False)
+    table, core_last_2, xkv_half = tie(table, core_last_2, xkv_half)
+    wo, wxq, wxo = [
+        part.reshape(width, width) for part in assemble(own_mix, (wave_2, last_2, core_2, core_last_2), cols)
+    ]
+    wxq_pad = pad_heads(wxq, xheads)
+    wxo_pad = pad_heads(wxo, xheads)
+
+    state_1, state_2 = item_sums(table)
+    xkv_far = swap(xkv_half, "tensor", 2)
+    state_1, state_2, wo, wxq_pad, wxo_pad, wave_3, d_ffn = tie(
+        state_1, state_2, wo, wxq_pad, wxo_pad, wave_3, d_ffn
+    )
+    wave_3 = turn(wave_3, 0)
+    above = shift_devices(d_ffn[own_rows - REACH :], 1)
+    below = shift_devices(d_ffn[:REACH], -1)
+    attn_ratio, denominator, attn, attn_sum = over_lanes(
+        attend_kernel,
+        "lttccw",
+        (query, state_1, state_2, first_all, second_all, wo),
+        (("l", single), ("l", single), ("l", bfloat), ("a", single)),
+    )
+    attn_out = attn_sum + out_bias
     after_attn = tokens_f + live * gate_a * attn_out
 
     cross_in = after_attn.astype(bfloat)
-    xquery = (dot_nt(cross_in, wxq_pad) + xq_bias_all).astype(bfloat)
+    xq_product = dot_nt(cross_in, wxq_pad)
+    wave_3, xkv_far, xq_product, above, below, small_rel = tie(
+        wave_3, xkv_far, xq_product, above, below, small_rel
+    )
+    d_ffn_ext = pad_rows(jnp.concatenate([above, d_ffn, below], axis=0), tall)
+    wave_3 = mid_turns(wave_3)
+    last_3 = last_turn(wave_3)
+    core_3 = swap(wave_3, "dp", 1)
+    xkv_near = swap(jnp.stack([xkv_half, xkv_far]), "tensor", 1)
+    xkv_rel = jnp.stack([xkv_half, xkv_near[0], xkv_far, xkv_near[1]])
+    small_half = lax.dynamic_index_in_dim(small_rel.reshape(2, -1), me_d % 2, 0, keepdims=False)
+    small_far = swap(small_half, "tensor", 2)
+    xkv_rel, small_far = tie(xkv_rel, small_far)
+    xkv_other = swap(xkv_rel, "dp", 1)
+    small_near = swap(jnp.stack([small_half, small_far]), "tensor", 1)
+    small = jnp.stack([small_half, small_near[0], small_far, small_near[1]])
+    small_other = swap(small, "dp", 1)
+    xkv_all = by_core(xkv_rel, xkv_other).swapaxes(0, 1)
+    xkv_all = jnp.stack(in_order(xkv_all)).reshape(group, 2, TXT, cols // XHEAD, XHEAD)
+    xkv_all = xkv_all.transpose(1, 0, 3, 2, 4).reshape(2, xheads, TXT, XHEAD)
+    xkv_all = jnp.pad(xkv_all, ((0, 0), (0, 0), (0, TXT_PAD - TXT), (0, XLANE - XHEAD)))
+    xkeys, xvals = xkv_all[0], xkv_all[1]
+    small = by_core(small, small_other).swapaxes(0, 1).reshape(group, -1)
+    xq_rel = small[:, sizes:]
+    small = flip_dp(small[:, :sizes].reshape(group, 16, 2, ranks, ffn_piece), 3)
+    small = small.reshape((group, 16, 2) + (2,) * (len(bits) + 1) + (ffn_piece,))
+    small = jnp.moveaxis(small, 0, len(bits) + 3)
+    small = small.transpose((len(bits) + 2, 1, 0) + down[::-1] + (len(bits) + 3, len(bits) + 4))
+    small = [
+        own_turns(small[core], 2, core == 1).reshape(2, 16, half_count) for core in (0, 1)
+    ]
+    xq_bias_all = jnp.stack(in_order(xq_rel)).reshape(xheads, XHEAD)
+    xq_bias_all = jnp.pad(xq_bias_all, ((0, 0), (0, XLANE - XHEAD))).reshape(xheads * XLANE)
+    lengths = look_up(text_len, item)[:, None]
+    xquery = (xq_product + xq_bias_all).astype(bfloat)
     cross_mix = cross_call(xquery, xkeys, xvals, lengths)
     cross_out = dot_nn(cross_mix, wxo_pad) + xo_bias
     after_cross = after_attn + live * cross_out
 
     normal_f, inv_std_f = norm_parts(after_cross)
     normed_ffn = (normal_f * (1.0 + scale_f) + shift_f).astype(bfloat)
+    normed_ffn, wave_3, last_3, core_3, *small = tie(normed_ffn, wave_3, last_3, core_3, *small)
+    core_last_3 = swap(last_3, "dp", 1)
+    def ffn_half(core):
+        count = len(bits)
+        own = flip_dp(rows_ffn.reshape(3, ranks, ffn_piece, width), 1)
+        own = own.reshape((3,) + (2,) * (count + 1) + (ffn_piece, width))
+        own = jnp.moveaxis(lax.index_in_dim(own, core, count + 1, keepdims=False), 0, count)
+        own = own_turns(own.transpose(tuple(range(count))[::-1] + (count, count + 1, count + 2)), 0, core == 1)
+        others = jnp.concatenate(((wave_3, last_3), (core_3, core_last_3))[core])
+        others = others.reshape((2,) * count + (group - 1, 3, ffn_piece, width))
+        others = others.transpose(tuple(range(count))[::-1] + tuple(range(count, count + 4)))
+        joined = jnp.concatenate([jnp.expand_dims(own, count), others], axis=count)
+        joined = jnp.moveaxis(joined, count + 1, 2)
+        return joined.reshape(4, 3, half_count // 4, width)
+
+    direct = ffn_piece % 16 == 0 and len(bits) == 2
+    weights_ffn = [
+        [rows_ffn, *((wave_3, last_3), (core_3, core_last_3))[core]] if direct else [ffn_half(core)]
+        for core in (0, 1)
+    ]
+
     above = shift_devices(normed_ffn[own_rows - 2 * REACH :], 1)
     below = shift_devices(normed_ffn[: 2 * REACH], -1)
     normed_ext = pad_rows(jnp.concatenate([above, normed_ffn, below], axis=0), wide)
     tables = (reach, back_full, back_last)
-    part_1 = ffn_call(
-        1, own_rows, own_pad, normed_ext, d_ffn_ext, *tables, weights_ffn[1], small[1]
-    )
-    normed_ext, *part_1 = tie(normed_ext, *part_1)
-    part_0 = ffn_call(
-        0, own_rows, own_pad, normed_ext, d_ffn_ext, *tables, weights_ffn[0], small[0]
-    )
-    ffn_out = (part_0[0] + part_1[0])[:own_rows]
-    d_normed_ffn = (part_0[1] + part_1[1])[:own_rows]
-    ffn_other = swap(part_1[2], "dp", 1)
-    d_normed_ffn, ffn_other = tie(d_normed_ffn, ffn_other)
-    ffn_shape = (2, 2, 3) + (2,) * len(bits) + (ffn_piece, width)
-    ffn_terms = [part_0[2].reshape(ffn_shape), ffn_other.reshape(ffn_shape)]
-    ffn_terms = halve_path(ffn_terms, 0, 0)
+    def ffn_part(core, begin, *added):
+        return ffn_call(
+            core, begin, 2, added, own_rows, own_pad, normed_ext, d_ffn_ext, *tables, weights_ffn[core], small[core]
+        )
+
+    part_3 = ffn_part(1, 2)
+    normed_ext, *part_3 = tie(normed_ext, *part_3)
+    other_3 = swap(part_3[2], "dp", 1)
+    part_2 = ffn_part(1, 0)
+    normed_ext, other_3, *part_2 = tie(normed_ext, other_3, *part_2)
+    other_2 = swap(part_2[2], "dp", 1)
+    part_1 = ffn_part(0, 2, other_3)
+    normed_ext, other_2, *part_1 = tie(normed_ext, other_2, *part_1)
+    turn_shape = (2, 3) + (2,) * len(bits) + (ffn_piece, width)
+    ffn_got = swap_path(part_1[2].reshape(turn_shape), 0)
+    part_0 = ffn_part(0, 0, other_2)
+    parts = (part_0, part_1, part_2, part_3)
+    ffn_out = sum(part[0] for part in parts)[:own_rows]
+    d_normed_ffn = sum(part[1] for part in parts)[:own_rows]
+    ffn_terms = [part_0[2].reshape(turn_shape), ffn_got]
+    d_small_half = [
+        jnp.concatenate([low[3], high[3]], axis=2) for low, high in ((part_0, part_1), (part_2, part_3))
+    ]
 
     d_small = jnp.stack(
         [
             own_turns(
-                part[3].astype(bfloat).reshape((2, 16) + (2,) * (len(bits) + 2) + (ffn_piece,)),
+                part.astype(bfloat).reshape((2, 16) + (2,) * (len(bits) + 2) + (ffn_piece,)),
                 2,
                 core == 1,
             )
-            for core, part in ((0, part_0), (1, part_1))
+            for core, part in enumerate(d_small_half)
         ],
         axis=len(bits) + 2,
     )
@@ -984,18 +1175,19 @@
     d_cross = grad_cross * live
     d_xo_bias = jnp.sum(d_cross, axis=0)
     d_cross_low = d_cross.astype(bfloat)
+    d_cross_low, ffn_terms[-1] = tie(d_cross_low, ffn_terms[-1])
+    for stage in range(1, len(bits)):
+        ffn_terms = halve_path(ffn_terms, stage, 0 if stage == 1 else 1)
     d_mix = dot_nt(d_cross_low, wxo_pad).astype(bfloat)
     d_query_low, d_keys, d_vals, d_xq_part = cross_back_call(xquery, xkeys, xvals, lengths, d_mix)
+    d_query_low, ffn_terms[-1] = tie(d_query_low, ffn_terms[-1])
+    ffn_terms = halve_z_once(ffn_terms, 1, 1)
     grad_attn = grad_cross + dot_nn(d_query_low, wxq_pad)
-    grad_attn, ffn_terms[-1] = tie(grad_attn, ffn_terms[-1])
-    for stage in range(1, len(bits)):
-        ffn_terms = halve_path(ffn_terms, stage, 0 if stage == 1 else 1)
 
     d_attn_out = grad_attn * live * gate_a
     d_gate_a = grad_attn * live * attn_out
     d_out_bias = jnp.sum(d_attn_out, axis=0)
     d_attn_low = d_attn_out.astype(bfloat)
-    d_ratio = dot_nt(d_attn_low, wo)
 
     text_rows = 2 * cols * TXT_PAD // width
     mix_rows = -(-(att_rows + text_rows + small_rows) // (16 * ranks)) * 16
@@ -1006,41 +1198,22 @@
     d_kv = jnp.concatenate(
         [d_kv[:, number * text_rows : (number + 1) * text_rows] for number in range(lanes)], axis=2
     )
-    mix_grads = grads_call(
-        [attn, d_attn_low, drop_lanes(d_query_low, xheads), cross_in, drop_lanes(cross_mix, xheads), d_cross_low],
-        ((0, 1), (2, 3), (4, 5)),
-        jnp.concatenate([d_kv, d_small], axis=1),
-        mix_rows,
-        cols,
-    )
-    mix_terms = core_terms(*mix_grads)
-    d_numer = (d_ratio / denominator).astype(bfloat)
-    d_denom = -dot_nn((d_ratio * attn_ratio).astype(bfloat), head_ones) / denominator
-    d_numer_1 = jnp.where(in_first, d_numer, zero)
-    d_numer_2 = jnp.where(in_second, d_numer, zero)
-    query_f = query.astype(single)
-    weighted = query_f * d_denom
-    d_state_1, d_state_2 = over_items(
-        packed(query, d_numer_1, jnp.sum(jnp.where(in_first, weighted, 0.0), axis=0)),
-        packed(query, d_numer_2, jnp.sum(jnp.where(in_second, weighted, 0.0), axis=0)),
-    )
-    d_state_1, d_state_2, ffn_terms[-1], mix_terms[1] = tie(
-        d_state_1, d_state_2, ffn_terms[-1], mix_terms[1]
-    )
-    for stage in range(len(bits)):
-        mix_terms = halve_path(mix_terms, stage, 0)
-    d_query = dot_nt(d_numer_1, dense_1) + dot_nt(d_numer_2, dense_2) + total_row * d_denom
-    d_dense_1, d_dense_2 = unpacked(d_state_1), unpacked(d_state_2)
-    values_1 = jnp.where(first_live, values, zero)
-    values_2 = jnp.where(second_live, values, zero)
-    d_total_row = jnp.where(in_first, d_state_1[HEAD][None], d_state_2[HEAD][None])
-    d_keys_h = dot_nt(values_1, d_dense_1) + dot_nt(values_2, d_dense_2) + live * d_total_row
-    d_values_low = (dot_nn(keys_1, d_dense_1) + dot_nn(keys_2, d_dense_2)).astype(bfloat)
-    d_query_in = (d_query * jax.nn.sigmoid(pre_q)).astype(bfloat)
-    d_keys_in = (d_keys_h * jax.nn.sigmoid(pre_k)).astype(bfloat)
-    d_normed = dot_nn(d_query_in, wq) + dot_nn(d_keys_in, wk) + dot_nn(d_values_low, wv)
-    d_tokens = grad_attn + norm_back(d_normed, normal_a, inv_std_a, scale_a)
-
+    mix_arrays = [
+        attn,
+        d_attn_low,
+        d_query_low,
+        cross_in,
+        cross_mix,
+        d_cross_low,
+    ]
+    mix_extra = jnp.concatenate([d_kv, d_small], axis=1)
+    d_query_in, table_1, table_2 = over_lanes(
+        attend_back_kernel,
+        "awllllttcc",
+        (d_attn_low, wo, attn_ratio, denominator, query, pre_q, state_1, state_2, first_all, second_all),
+        (("l", bfloat), ("t", single), ("t", single)),
+    )
+    d_table = item_table(table_1, table_2)
     def mod_sum(rows):
         return jnp.stack(
             [
@@ -1049,20 +1222,29 @@
             ]
         )
 
-    sums = jnp.stack(
-        [
-            mod_sum(rows)
-            for rows in (
-                d_normed,
-                d_normed * normal_a,
-                d_gate_a,
-                d_normed_ffn,
-                d_normed_ffn * normal_f,
-                d_gate_f,
-            )
-        ],
-        axis=1,
-    )
+    d_table, mix_extra = tie(d_table, mix_extra)
+    d_table = total([d_table, swap(d_table, "tensor", 1)])
+    mod_sums = [
+        mod_sum(rows) for rows in (d_gate_a, d_normed_ffn, d_normed_ffn * normal_f, d_gate_f)
+    ]
+    d_table, d_out_bias, d_xo_bias, *mod_sums = tie(d_table, d_out_bias, d_xo_bias, *mod_sums)
+    d_table = total([d_table, swap(d_table, "tensor", 2)])
+    mix_grads = grads_call(mix_arrays, ((0, 1), (2, 3), (4, 5)), mix_extra, mix_rows, cols)
+    d_table, mix_grads[1], ffn_terms[-1] = tie(d_table, mix_grads[1], ffn_terms[-1])
+    mix_terms = core_terms(*mix_grads)
+    d_state_1, d_state_2 = item_sums(d_table)
+    d_state_1, d_state_2, mix_terms[1] = tie(d_state_1, d_state_2, mix_terms[1])
+    mix_terms = halve_path(mix_terms, 0, 0)
+    ffn_terms = halve_z_once(ffn_terms, 2, 1)
+    d_keys_in, d_values_low, d_normed = over_lanes(
+        project_back_kernel,
+        "llllttccwww",
+        (d_query_in, keys, values, pre_k, d_state_1, d_state_2, first_live, second_live, wq, wk, wv),
+        (("l", bfloat), ("l", bfloat), ("a", single)),
+    )
+    d_tokens = grad_attn + norm_back(d_normed, normal_a, inv_std_a, scale_a)
+
+    sums = jnp.stack([mod_sum(d_normed), mod_sum(d_normed * normal_a)] + mod_sums, axis=1)
     items = jnp.arange(item_count, dtype=jnp.int32)[:, None, None]
     mod_table = jnp.where(items == first_item, sums[0][None], 0.0) + jnp.where(
         (items == first_item + 1), sums[1][None], 0.0
@@ -1071,28 +1253,54 @@
     rows_all = jnp.concatenate(
         [mod_table.reshape(-1, width), jnp.stack([d_out_bias, d_xo_bias, xq_row], axis=0)], axis=0
     )
-    spare = att_pad - att_rows
     rows_count = rows_all.shape[0]
-    rows_all = pad_rows(rows_all.astype(bfloat), spare * group).reshape(group, spare, width)
+    last_rows = -(-(att_rows + rows_count) // (16 * ranks)) * 16
+    spare = -(-rows_count // 16) * 16
+    rows_all = pad_rows(rows_all.astype(bfloat), spare)
+    rows_all = jnp.broadcast_to(rows_all[None], (group, spare, width))
 
     qkv_grads = grads_call(
         [d_query_in, d_keys_in, d_values_low, normed],
         ((0, 3), (1, 3), (2, 3)),
         rows_all,
-        att_piece,
+        last_rows,
         cols,
     )
+    qkv_grads[1], mix_terms[-1] = tie(qkv_grads[1], mix_terms[-1])
     qkv_terms = core_terms(*qkv_grads)
-    qkv_terms[1], mix_terms[-1] = tie(qkv_terms[1], mix_terms[-1])
-    for stage in range(len(bits)):
+    for stage in range(1, len(bits)):
+        mix_terms = halve_path(mix_terms, stage, 0)
+    qkv_terms[1], mix_terms[-1], ffn_terms[-1] = tie(qkv_terms[1], mix_terms[-1], ffn_terms[-1])
+    qkv_terms = halve_path(qkv_terms, 0, 0)
+    mix_terms = halve_z_once(mix_terms, 1, 0)
+    qkv_terms[-1], mix_terms[-1] = tie(qkv_terms[-1], mix_terms[-1])
+    for stage in range(1, len(bits)):
         qkv_terms = halve_path(qkv_terms, stage, 0)
-
-    d_ffn_all = share_dp(halve_z(ffn_terms, 1)).transpose(1, 0, 2, 3)
+    mix_terms = halve_z_once(mix_terms, 2, 0)
+    qkv_terms[-1], mix_terms[-1] = tie(qkv_terms[-1], mix_terms[-1])
+    qkv_terms = halve_z_once(qkv_terms, 1, 0)
+    d_mix_all = share_turn(total(mix_terms), 0)
+    d_ffn_all = share_turn(total(ffn_terms), 0)
+    qkv_terms[-1], d_mix_all, d_ffn_all = tie(qkv_terms[-1], d_mix_all, d_ffn_all)
+    qkv_terms = halve_z_once(qkv_terms, 2, 0)
+    for stage in range(1, len(bits)):
+        d_mix_all = share_turn(d_mix_all, stage)
+    qkv_terms[-1], d_mix_all = tie(qkv_terms[-1], d_mix_all)
+    d_qkv_all = share_turn(total(qkv_terms), 0)
+    d_mix_all = share_core(d_mix_all)
+    for stage in range(1, len(bits)):
+        d_ffn_all = share_turn(d_ffn_all, stage)
+    d_qkv_all, d_mix_all, d_ffn_all = tie(d_qkv_all, d_mix_all, d_ffn_all)
+    for stage in range(1, len(bits)):
+        d_qkv_all = share_turn(d_qkv_all, stage)
+    d_ffn_all = share_core(d_ffn_all)
+    d_qkv_all = share_core(d_qkv_all)
+    d_ffn_all = d_ffn_all.transpose(1, 0, 2, 3)
     d_ffn_all = d_ffn_all.reshape(3, padded_channels, width)[:, :channels]
     d_w_in = jnp.stack([d_ffn_all[0].T, d_ffn_all[1].T], axis=1).astype(single)
     d_w_pt = d_ffn_all[2].astype(single)
 
-    d_mix_all = share_dp(halve_z(mix_terms, 0)).reshape(-1, width)
+    d_mix_all = d_mix_all.reshape(-1, width)
     d_w_out = d_mix_all[:cols].astype(single)
     d_w_xq = d_mix_all[cols : 2 * cols].T.astype(single)
     d_w_xo = d_mix_all[2 * cols : 3 * cols].astype(single)
@@ -1110,9 +1318,9 @@
     d_small = d_small.swapaxes(0, 1).astype(single)
     d_dw_weight, d_dw_bias, d_in_bias = d_small[:9], d_small[9], d_small[10]
 
-    d_qkv_all = share_dp(halve_z(qkv_terms, 0)).reshape(-1, width)
+    d_qkv_all = d_qkv_all.reshape(-1, width)
     d_w_qkv = d_qkv_all[:att_rows].reshape(3, cols, width).transpose(2, 0, 1).astype(single)
-    rows_all = gather_z(d_qkv_all[att_rows:], True).reshape(-1, width)[:rows_count].astype(single)
+    rows_all = d_qkv_all[att_rows : att_rows + rows_count].astype(single)
     d_t_mod = rows_all[:-3].reshape(mod_table.shape)
     d_out_bias, d_xo_bias = rows_all[-3], rows_all[-2]
     d_xq_bias = lax.dynamic_slice_in_dim(rows_all[-1], me_z * cols, cols, 0)

time: 951 us -> 820 us (0.86)
  waiting for transfers between devices: 320 us -> 248 us
  matrix products: 86.5 us -> 24.1 us
  Pallas kernels: 170 us -> 228 us
  other arithmetic: 158 us -> 128 us
  local copies, waits for them, and re-layouts: 138 us -> 111 us
    ppermute x18, waiting for transfers between devices: 136 us -> 65.4 us  [swap_path(): lax.ppermute(values, 'dp', [(i, i ^ turns(i % 2)[number]) for i in range(...]
    pallas_call x2 -> x8, Pallas kernels: 96.2 us -> 152 us  [the longest x4 112 us: ffn_call(): pl.pallas_call(functools.partial(ffn_kernel, core if direct else None, be...]
    dot_general x12 -> x2, matrix products: 32.7 us -> 8.67 us  [dot_nn(): lax.dot_general(a, b, (((1,), (0,)), ((), ())), preferred_element_type=si...]
    dot_general x10 -> x2, matrix products: 29.5 us -> 10.5 us  [dot_nt(): lax.dot_general(a, b, (((1,), (1,)), ((), ())), preferred_element_type=si...]
    dot_general x4 -> x0, matrix products: 18.2 us -> none  [dot_tn(): lax.dot_general(a, b, (((0,), (0,)), ((), ())), preferred_element_type=si...]
    another operation x6 -> x3, other arithmetic: 24 us -> 7.33 us  [turn(): return jnp.stack([values, swap_path(values, number)])]
    reduce_sum x4 -> x0, other arithmetic: 11.2 us -> none  [packed(): block = jnp.sum(full.reshape(heads, HEAD, width), axis=0)]
    reshape x10 -> x5, local copies, waits for them, and re-layouts: 17.3 us -> 6.75 us  [the longest x1 5.39 us: local(): ffn_got = swap_path(part_1[2].reshape(turn_shape), 0)]
  transfers between devices with their start and end apart: 61 -> 66, of which waited for: 39 -> 29; matrix products, arithmetic and copies ran while one was open for 32% -> 25% of each run, Pallas kernels for 12% -> 24%
where the time goes in v2:
time: 820 us; the launch traced here: 814 us
  waiting for transfers between devices  248 us (30%)
  Pallas kernels  228 us (28%)
  other arithmetic  128 us (16%)
  local copies, waits for them, and re-layouts  111 us (14%)
  starting transfers between devices  70.2 us (9%)
  matrix products  24.1 us (3%)
    ppermute x40, waiting for transfers between devices, swap(): return lax.ppermute(values, axis, [(i, i ^ bit) for i in range(count)])  172 us
    pallas_call x4, Pallas kernels, ffn_call(): pl.pallas_call(functools.partial(ffn_kernel, core if direct else None, be...  112 us
    ppermute x18, waiting for transfers between devices, swap_path(): lax.ppermute(values, 'dp', [(i, i ^ turns(i % 2)[number]) for i in range(...  65.4 us
    pallas_call x4, Pallas kernels, lane_call(): pl.pallas_call(kernel, grid=(features // LANES,), in_specs=[specs[kind] f...  39.8 us
    ppermute x40, starting transfers between devices, swap(): return lax.ppermute(values, axis, [(i, i ^ bit) for i in range(count)])  26.3 us
    pallas_call x2, Pallas kernels, grads_call(): pl.pallas_call(functools.partial(grads_kernel, ranks, group, rows, cols,...  26.3 us
    ppermute x18, starting transfers between devices, swap_path(): lax.ppermute(values, 'dp', [(i, i ^ turns(i % 2)[number]) for i in range(...  25.2 us
    unnamed x246, local copies, waits for them, and re-layouts  20.8 us
  transfers between devices with their start and end apart: 66, of which 29 were waited for; matrix products, arithmetic and copies ran while one was open for 25% of the time, Pallas kernels for 24%

profile of v2, /device:TPU:0, one launch (start us, length us, event | category | flops | bytes accessed | tf_op | source)
XLA Modules:
  0.0 813.6 jit_solution(14708719401295312264)
XLA Ops:
  3.9 4.1 collective-permute-start
  25.2 6.0 pad_maximum_fusion.refs_0_
  31.2 5.6 collective-permute-done.1
  50.7 7.3 collective-permute-done.2
  61.1 13.9 %collective-permute-done.6 = bf16[2,112,1152]{2,1,0:T(8,128)(2,1)S(1)} collective-permute-done((bf16[2,112,1152]{2,1,0:T(8,128)(2,1)S(1)}, bf16[2,112,1152]{2,1,0:T(8,128)(2,1)S(1)}, u32[]{:S(2)}, u32[]{:S(2)}) %collective-permute-start.6) | collective-permute-done | bytes 516128 | tf_op jit(solution)/shard_map/ppermute | solution.py:42
  87.2 7.8 shard_map.348
  97.7 11.3 %shard_map.349 = (f32[416,1152]{1,0:T(8,128)}, f32[416,1152]{1,0:T(8,128)}, bf16[416,1152]{1,0:T(8,128)(2,1)}, bf16[416,1152]{1,0:T(8,128)(2,1)}, bf16[416,1152]...) custom-call(bf16[416,1152]{1,0:T(8,128)(2,1)} %fusion.27.normed.refs_3_, bf16[1152,1152]{1,0:T(8,128)(2,1)} %bitcast.524, ...), custom_call_target="tpu_custom_call" | custom-call | flops 552075264 | bytes 479232 | tf_op jit(solution)/shard_map/pallas_call | solution.py:711
  110.9 5.7 collective-permute-done.10
  125.4 29.4 %collective-permute-done.12 = bf16[3,40,1152]{2,1,0:T(8,128)(2,1)S(1)} collective-permute-done((bf16[3,40,1152]{2,1,0:T(8,128)(2,1)}, bf16[3,40,1152]{2,1,0:T(8,128)(2,1)S(1)}, u32[]{:S(2)}, u32[]{:S(2)}) %collective-permute-start.12) | collective-permute-done | bytes 276512 | tf_op jit(solution)/shard_map/ppermute | solution.py:42
  160.3 11.0 %collective-permute-done.16 = bf16[3,40,1152]{2,1,0:T(8,128)(2,1)S(1)} collective-permute-done((bf16[3,40,1152]{2,1,0:T(8,128)(2,1)S(1)}, bf16[3,40,1152]{2,1,0:T(8,128)(2,1)S(1)}, u32[]{:S(2)}, u32[]{:S(2)}) %collective-permute-start.16) | collective-permute-done | bytes 276512 | tf_op jit(solution)/shard_map/ppermute | solution.py:42
  174.5 3.7 collective-permute-start.18
  180.8 7.9 shard_map.350
  188.7 4.8 pad.54
  202.8 4.6 collective-permute-start.23
  207.4 6.9 shard_map.351
  216.5 6.9 fusion.233
  224.4 4.5 pad_maximum_fusion.2.refs_1_
  234.0 9.3 %collective-permute-done.25 = bf16[2,300,288]{1,2,0:T(8,128)(2,1)S(1)} collective-permute-done((bf16[2,300,288]{1,2,0:T(8,128)(2,1)S(1)}, bf16[2,300,288]{1,2,0:T(8,128)(2,1)S(1)}, u32[]{:S(2)}, u32[]{:S(2)}) %collective-permute-start.25) | collective-permute-done | bytes 345632 | tf_op jit(solution)/shard_map/ppermute | solution.py:42
  244.7 5.3 collective-permute-done.27
  272.1 4.2 fusion.48
  276.3 16.4 %shard_map.352.refs_4_ = bf16[416,2048]{1,0:T(8,128)(2,1)} custom-call(bf16[416,2048]{1,0:T(8,128)(2,1)} %add_convert_fusion.query_ref, bf16[16,384,128]{2,1,0:T(8,128)(2,1)} %get-tuple-element.514.keys_ref, bf16[16,384,128]{2,1,0:T(8,128)(2,1)} %get-tuple-element.513.vals_ref, s32[416,1]{1,0:T(8,128)} %copy.211.length_ref), custom_call_target="tpu_custom_call" | custom-call | flops 327155712 | bytes 1703936 | tf_op jit(solution)/shard_map/pallas_call | solution.py:764
  292.8 6.3 fusion.232
  312.5 5.5 collective-permute-done.33
  318.7 27.4 %shard_map.353 = (f32[416,1152]{1,0:T(8,128)}, f32[416,1152]{1,0:T(8,128)}, bf16[2,3,384,1152]{3,2,1,0:T(8,128)(2,1)}, f32[2,16,768]{2,1,0:T(8,128)}) custom-call(bf16[608,1152]{1,0:T(8,128)(2,1)} %constant_dynamic-update-slice_fusion.normed_ref, bf16[512,1152]{1,0:T(8,128)(2,1)} %constant_dynamic-update-slice_fusion.3.grad_ref, ...), custom_call_target="tpu_custom_call" | custom-call | flops 1755316224 | bytes 1769472 | tf_op jit(solution)/shard_map/pallas_call | solution.py:575
  346.2 27.4 %shard_map.354 = (f32[416,1152]{1,0:T(8,128)}, f32[416,1152]{1,0:T(8,128)}, bf16[2,3,384,1152]{3,2,1,0:T(8,128)(2,1)}, f32[2,16,768]{2,1,0:T(8,128)}) custom-call(bf16[608,1152]{1,0:T(8,128)(2,1)} %constant_dynamic-update-slice_fusion.normed_ref, bf16[512,1152]{1,0:T(8,128)(2,1)} %constant_dynamic-update-slice_fusion.3.grad_ref, ...), custom_call_target="tpu_custom_call" | custom-call | flops 1755316224 | bytes 1769472 | tf_op jit(solution)/shard_map/pallas_call | solution.py:575
  375.3 28.5 %shard_map.355 = (f32[416,1152]{1,0:T(8,128)}, f32[416,1152]{1,0:T(8,128)}, bf16[2,3,384,1152]{3,2,1,0:T(8,128)(2,1)}, f32[2,16,768]{2,1,0:T(8,128)}) custom-call(bf16[608,1152]{1,0:T(8,128)(2,1)} %constant_dynamic-update-slice_fusion.normed_ref, bf16[512,1152]{1,0:T(8,128)(2,1)} %constant_dynamic-update-slice_fusion.3.grad_ref, ...), custom_call_target="tpu_custom_call" | custom-call | flops 1755316224 | bytes 1769472 | tf_op jit(solution)/shard_map/pallas_call | solution.py:575
  404.0 5.4 copy.216
  410.1 28.6 %shard_map.356 = (f32[416,1152]{1,0:T(8,128)}, f32[416,1152]{1,0:T(8,128)}, bf16[2,3,384,1152]{3,2,1,0:T(8,128)(2,1)}, f32[2,16,768]{2,1,0:T(8,128)}) custom-call(bf16[608,1152]{1,0:T(8,128)(2,1)} %constant_dynamic-update-slice_fusion.normed_ref, bf16[512,1152]{1,0:T(8,128)(2,1)} %constant_dynamic-update-slice_fusion.3.grad_ref, ...), custom_call_target="tpu_custom_call" | custom-call | flops 1755316224 | bytes 1769472 | tf_op jit(solution)/shard_map/pallas_call | solution.py:575
  438.8 6.7 select_reduce_fusion.7
  458.6 11.5 %collective-permute-done.37 = bf16[2,3,2,2,96,1152]{5,4,1,2,3,0:T(8,128)(2,1)} collective-permute-done((bf16[2,3,2,2,96,1152]{5,4,1,2,3,0:T(8,128)(2,1)}, bf16[2,3,2,2,96,1152]{5,4,1,2,3,0:T(8,128)(2,1)}, u32[]{:S(2)}, u32[]{:S(2)}) %collective-permute-start.37) | collective-permute-done | bytes 5308448 | tf_op jit(solution)/shard_map/ppermute | solution.py:79
  470.1 4.0 fusion.1
  481.6 18.2 %shard_map.357 = (bf16[416,2048]{1,0:T(8,128)(2,1)}, bf16[16,72,384]{2,1,0:T(8,128)(2,1)}, bf16[16,72,384]{2,1,0:T(8,128)(2,1)}, f32[1,2048]{1,0:T(1,128)}) custom-call(bf16[416,2048]{1,0:T(8,128)(2,1)} %add_convert_fusion.query_ref, bf16[16,384,128]{2,1,0:T(8,128)(2,1)} %get-tuple-element.514.keys_ref, bf16[16,384,128]{2,1,0:T(8,128)(2,1)} %get-tuple-element.513.vals_ref, ...), custom_call_target="tpu_custom_call" | custom-call | flops 327155712 | bytes 1703936 | tf_op jit(solution)/shard_map/pallas_call | solution.py:782
  502.1 3.7 slice_bitcast_fusion
  516.5 9.2 %shard_map.358 = (bf16[416,1152]{1,0:T(8,128)(2,1)}, f32[40,1152]{1,0:T(8,128)}, f32[40,1152]{1,0:T(8,128)}) custom-call(bf16[416,1152]{1,0:T(8,128)(2,1)} %get-tuple-element.517.grad.refs_1_, bf16[1152,1152]{1,0:T(8,128)(2,1)} %bitcast.531, f32[416,1152]{1,0:T(8,128)} %get-tuple-element.274.ratio, f32[416,1152]{1,0:T(8,128)} %get-tuple-element.275.den, ...), custom_call_target="tpu_custom_call" | custom-call | flops 552075264 | bytes 479232 | tf_op jit(solution)/shard_map/pallas_call | solution.py:711
  532.7 5.9 collective-permute-done.39
  538.7 15.2 %shard_map.359 = (bf16[4,4,144,1152]{3,2,1,0:T(8,128)(2,1)}, bf16[4,4,144,1152]{3,2,1,0:T(8,128)(2,1)}) custom-call(bf16[416,1152]{1,0:T(8,128)(2,1)} %get-tuple-element.291.refs_0_, bf16[416,1152]{1,0:T(8,128)(2,1)} %get-tuple-element.517.grad.refs_1_, bf16[416,2048]{1,0:T(8,128)(2,1)} %get-tuple-element.273.refs_2_, bf16[416,1152]{1,0:T(8,128)(2,1)} %copy-done.17, ...), custom_call_target="tpu_custom_call" | custom-call | flops 552075264 | bytes 2654208 | tf_op jit(solution)/shard_map/pallas_call | solution.py:294
  554.0 11.9 %collective-permute-done.40 = bf16[3,40,1152]{2,1,0:T(8,128)(2,1)S(1)} collective-permute-done((bf16[3,40,1152]{2,1,0:T(8,128)(2,1)S(1)}, bf16[3,40,1152]{2,1,0:T(8,128)(2,1)S(1)}, u32[]{:S(2)}, u32[]{:S(2)}) %collective-permute-start.40) | collective-permute-done | bytes 276512 | tf_op jit(solution)/shard_map/ppermute | solution.py:42
  582.6 12.3 %shard_map.360 = (bf16[416,1152]{1,0:T(8,128)(2,1)}, bf16[416,1152]{1,0:T(8,128)(2,1)}, f32[416,1152]{1,0:T(8,128)}) custom-call(bf16[416,1152]{1,0:T(8,128)(2,1)} %get-tuple-element.277.dquery.refs_0_, bf16[416,1152]{1,0:T(8,128)(2,1)} %get-tuple-element.278.keys, bf16[416,1152]{1,0:T(8,128)(2,1)} %get-tuple-element.279.values, ...), custom_call_target="tpu_custom_call" | custom-call | flops 552075264 | bytes 479232 | tf_op jit(solution)/shard_map/pallas_call | solution.py:711
  606.1 11.0 %shard_map.361 = (bf16[4,4,128,1152]{3,2,1,0:T(8,128)(2,1)}, bf16[4,4,128,1152]{3,2,1,0:T(8,128)(2,1)}) custom-call(bf16[416,1152]{1,0:T(8,128)(2,1)} %get-tuple-element.277.dquery.refs_0_, bf16[416,1152]{1,0:T(8,128)(2,1)} %get-tuple-element.300.refs_1_, bf16[416,1152]{1,0:T(8,128)(2,1)} %get-tuple-element.301.refs_2_, ...), custom_call_target="tpu_custom_call" | custom-call | flops 552075264 | bytes 2359296 | tf_op jit(solution)/shard_map/pallas_call | solution.py:294
  630.6 26.5 %collective-permute-done.48 = bf16[3,96,1152]{2,1,0:T(8,128)(2,1)S(1)} collective-permute-done((bf16[3,96,1152]{2,1,0:T(8,128)(2,1)S(1)}, bf16[3,96,1152]{2,1,0:T(8,128)(2,1)S(1)}, u32[]{:S(2)}, u32[]{:S(2)}) %collective-permute-start.48) | collective-permute-done | bytes 663584 | tf_op jit(solution)/shard_map/ppermute | solution.py:42
  666.3 29.2 %collective-permute-done.55 = bf16[3,96,1152]{2,1,0:T(8,128)(2,1)S(1)} collective-permute-done((bf16[3,96,1152]{2,1,0:T(8,128)(2,1)S(1)}, bf16[3,96,1152]{2,1,0:T(8,128)(2,1)S(1)}, u32[]{:S(2)}, u32[]{:S(2)}) %collective-permute-start.55) | collective-permute-done | bytes 663584 | tf_op jit(solution)/shard_map/ppermute | solution.py:79
  699.6 15.7 %collective-permute-done.52 = bf16[144,1152]{1,0:T(8,128)(2,1)S(1)} collective-permute-done((bf16[144,1152]{1,0:T(8,128)(2,1)S(1)}, bf16[144,1152]{1,0:T(8,128)(2,1)S(1)}, u32[]{:S(2)}, u32[]{:S(2)}) %collective-permute-start.52) | collective-permute-done | bytes 331808 | tf_op jit(solution)/shard_map/ppermute | solution.py:42
  717.2 5.9 collective-permute-done.54
  723.2 9.4 %collective-permute-done.53 = bf16[2,128,1152]{2,1,0:T(8,128)(2,1)S(1)} collective-permute-done((bf16[2,128,1152]{2,1,0:T(8,128)(2,1)S(1)}, bf16[2,128,1152]{2,1,0:T(8,128)(2,1)S(1)}, u32[]{:S(2)}, u32[]{:S(2)}) %collective-permute-start.53) | collective-permute-done | bytes 589856 | tf_op jit(solution)/shard_map/ppermute | solution.py:42
  735.2 8.0 collective-permute-done.57
  743.5 4.8 collective-permute-done.56
  753.1 5.5 collective-permute-done.58
  783.4 7.0 collective-permute-done.64
  (663 shorter events, 282.3 us)
Async XLA Ops:
  3.9 19.6 %collective-permute-start = (bf16[112,1152]{1,0:T(8,128)(2,1)S(1)}, bf16[112,1152]{1,0:T(8,128)(2,1)S(1)}, u32[]{:S(2)}, u32[]{:S(2)}) collective-permute-start(bf16[112,1152]{1,0:T(8,128)(2,1)S(1)} %fusion.245), channel_id=1, source_target_pairs={{0,2},{1,3},{2,0},{3,1},{4,6},{5,7},{6,4},{7,5},{8,10},{9,11},{10,... | collective-permute-start | bytes 774152 | tf_op jit(solution)/shard_map/ppermute | solution.py:42
  23.5 13.3 %collective-permute-start.1 = (bf16[2,112,1152]{2,1,0:T(8,128)(2,1)S(1)}, bf16[2,112,1152]{2,1,0:T(8,128)(2,1)S(1)}, u32[]{:S(2)}, u32[]{:S(2)}) collective-permute-start(bf16[2,112,1152]{2,1,0:T(8,128)(2,1)S(1)} %pad_maximum_fusion.18), channel_id=1, source_target_pairs={{0,1},{1,0},{2,3},{3,2},{4,5},{5,4},{6,7},{7,6},{8,9},{9,8},{10,11... | collective-permute-start | bytes 1548296 | tf_op jit(solution)/shard_map/ppermute | solution.py:42
  45.0 13.0 %collective-permute-start.2 = (bf16[112,1152]{1,0:T(8,128)(2,1)S(1)}, bf16[112,1152]{1,0:T(8,128)(2,1)S(1)}, u32[]{:S(2)}, u32[]{:S(2)}) collective-permute-start(bf16[112,1152]{1,0:T(8,128)(2,1)S(1)} %dynamic-slice_bitcast_fusion.1), channel_id=1, source_target_pairs={{0,2},{1,3},{2,0},{3,1},{4,6},{5,7},{6,4},{7,5},{8,10},{9,11},{10,... | collective-permute-start | bytes 774152 | tf_op jit(solution)/shard_map/ppermute | solution.py:42
  58.1 18.0 %collective-permute-start.5 = (bf16[2,3,112,1152]{3,2,1,0:T(8,128)(2,1)S(1)}, bf16[2,3,112,1152]{3,2,1,0:T(8,128)(2,1)S(1)}, u32[]{:S(2)}, u32[]{:S(2)}) collective-permute-start(bf16[2,3,112,1152]{3,2,1,0:T(8,128)(2,1)S(1)} %pad_maximum_fusion.7.refs_0_), channel_id=1, source_target_pairs={{0,4},{4,0},{8,12},{12,8},{16,20},{20,16},{24,28},{28,24},{1,5},{5... | collective-permute-start | bytes 4644872 | tf_op jit(solution)/shard_map/ppermute | solution.py:42
  58.1 20.3 %collective-permute-start.4 = (bf16[2,3,112,1152]{3,2,1,0:T(8,128)(2,1)S(1)}, bf16[2,3,112,1152]{3,2,1,0:T(8,128)(2,1)}, u32[]{:S(2)}, u32[]{:S(2)}) collective-permute-start(bf16[2,3,112,1152]{3,2,1,0:T(8,128)(2,1)S(1)} %pad_maximum_fusion.7.refs_0_), channel_id=1, source_target_pairs={{0,16},{4,12},{8,24},{12,4},{16,0},{20,28},{24,8},{28,20},{1,17},{... | collective-permute-start | bytes 4644872 | tf_op jit(solution)/shard_map/ppermute | solution.py:79
  58.6 16.4 %collective-permute-start.6 = (bf16[2,112,1152]{2,1,0:T(8,128)(2,1)S(1)}, bf16[2,112,1152]{2,1,0:T(8,128)(2,1)S(1)}, u32[]{:S(2)}, u32[]{:S(2)}) collective-permute-start(bf16[2,112,1152]{2,1,0:T(8,128)(2,1)S(1)} %pad_maximum_fusion.19), channel_id=1, source_target_pairs={{0,1},{1,0},{2,3},{3,2},{4,5},{5,4},{6,7},{7,6},{8,9},{9,8},{10,11... | collective-permute-start | bytes 1548296 | tf_op jit(solution)/shard_map/ppermute | solution.py:42
  59.2 16.9 %collective-permute-start.7 = (bf16[40,1152]{1,0:T(8,128)(2,1)S(1)}, bf16[40,1152]{1,0:T(8,128)(2,1)S(1)}, u32[]{:S(2)}, u32[]{:S(2)}) collective-permute-start(bf16[40,1152]{1,0:T(8,128)(2,1)S(1)} %fusion.244), channel_id=1, source_target_pairs={{0,2},{1,3},{2,0},{3,1},{4,6},{5,7},{6,4},{7,5},{8,10},{9,11},{10,... | collective-permute-start | bytes 276488 | tf_op jit(solution)/shard_map/ppermute | solution.py:42
  82.0 13.0 %collective-permute-start.9 = (bf16[3,112,1152]{2,1,0:T(8,128)(2,1)}, bf16[3,112,1152]{2,1,0:T(8,128)(2,1)}, u32[]{:S(2)}, u32[]{:S(2)}) collective-permute-start(bf16[3,112,1152]{2,1,0:T(8,128)(2,1)} %pad_maximum_fusion.15), channel_id=1, source_target_pairs={{0,8},{4,20},{8,0},{12,28},{16,24},{20,4},{24,16},{28,12},{1,9},{5... | collective-permute-start | bytes 2322440 | tf_op jit(solution)/shard_map/ppermute | solution.py:79
  85.4 25.6 %collective-permute-start.11 = (bf16[2,40,1152]{2,1,0:T(8,128)(2,1)S(1)}, bf16[2,40,1152]{2,1,0:T(8,128)(2,1)}, u32[]{:S(2)}, u32[]{:S(2)}) collective-permute-start(bf16[2,40,1152]{2,1,0:T(8,128)(2,1)S(1)} %pad_maximum_fusion.26), channel_id=1, source_target_pairs={{0,1},{1,0},{2,3},{3,2},{4,5},{5,4},{6,7},{7,6},{8,9},{9,8},{10,11... | collective-permute-start | bytes 552968 | tf_op jit(solution)/shard_map/ppermute | solution.py:42
  85.4 31.2 %collective-permute-start.10 = (bf16[288,1152]{1,0:T(8,128)(2,1)}, bf16[288,1152]{1,0:T(8,128)(2,1)}, u32[]{:S(2)}, u32[]{:S(2)}) collective-permute-start(bf16[288,1152]{1,0:T(8,128)(2,1)} %bitcast.31), channel_id=1, source_target_pairs={{0,2},{1,3},{2,0},{3,1},{4,6},{5,7},{6,4},{7,5},{8,10},{9,11},{10,... | collective-permute-start | bytes 1990664 | tf_op jit(solution)/shard_map/ppermute | solution.py:42
  119.2 36.7 %collective-permute-start.20 = (bf16[2,288,1152]{2,1,0:T(8,128)(2,1)}, bf16[2,288,1152]{2,1,0:T(8,128)(2,1)}, u32[]{:S(2)}, u32[]{:S(2)}) collective-permute-start(bf16[2,288,1152]{2,1,0:T(8,128)(2,1)} %pad_maximum_fusion.9), channel_id=1, source_target_pairs={{0,1},{1,0},{2,3},{3,2},{4,5},{5,4},{6,7},{7,6},{8,9},{9,8},{10,11... | collective-permute-start | bytes 3981320 | tf_op jit(solution)/shard_map/ppermute | solution.py:42
  120.7 36.5 %collective-permute-start.14 = (bf16[2,3,112,1152]{3,2,1,0:T(8,128)(2,1)}, bf16[2,3,112,1152]{3,2,1,0:T(8,128)(2,1)S(1)}, u32[]{:S(2)}, u32[]{:S(2)}) collective-permute-start(bf16[2,3,112,1152]{3,2,1,0:T(8,128)(2,1)} %pad_maximum_fusion.8.refs_0_), channel_id=1, source_target_pairs={{0,4},{4,0},{8,12},{12,8},{16,20},{20,16},{24,28},{28,24},{1,5},{5... | collective-permute-start | bytes 4644872 | tf_op jit(solution)/shard_map/ppermute | solution.py:42
  120.7 36.5 %collective-permute-start.13 = (bf16[2,3,112,1152]{3,2,1,0:T(8,128)(2,1)}, bf16[2,3,112,1152]{3,2,1,0:T(8,128)(2,1)S(1)}, u32[]{:S(2)}, u32[]{:S(2)}) collective-permute-start(bf16[2,3,112,1152]{3,2,1,0:T(8,128)(2,1)} %pad_maximum_fusion.8.refs_0_), channel_id=1, source_target_pairs={{0,16},{4,12},{8,24},{12,4},{16,0},{20,28},{24,8},{28,20},{1,17},{... | collective-permute-start | bytes 4644872 | tf_op jit(solution)/shard_map/ppermute | solution.py:79
  122.3 32.6 %collective-permute-start.12 = (bf16[3,40,1152]{2,1,0:T(8,128)(2,1)}, bf16[3,40,1152]{2,1,0:T(8,128)(2,1)S(1)}, u32[]{:S(2)}, u32[]{:S(2)}) collective-permute-start(bf16[3,40,1152]{2,1,0:T(8,128)(2,1)} %pad_maximum_fusion.23), channel_id=1, source_target_pairs={{0,1},{1,0},{2,3},{3,2},{4,5},{5,4},{6,7},{7,6},{8,9},{9,8},{10,11... | collective-permute-start | bytes 829448 | tf_op jit(solution)/shard_map/ppermute | solution.py:42
  125.3 32.0 %collective-permute-start.15 = (bf16[4,40,1152]{2,1,0:T(8,128)(2,1)S(1)}, bf16[4,40,1152]{2,1,0:T(8,128)(2,1)S(1)}, u32[]{:S(2)}, u32[]{:S(2)}) collective-permute-start(bf16[4,40,1152]{2,1,0:T(8,128)(2,1)S(1)} %pad_maximum_fusion.22), channel_id=1, source_target_pairs={{0,4},{4,0},{8,12},{12,8},{16,20},{20,16},{24,28},{28,24},{1,5},{5... | collective-permute-start | bytes 1105928 | tf_op jit(solution)/shard_map/ppermute | solution.py:42
  158.4 12.9 %collective-permute-start.16 = (bf16[3,40,1152]{2,1,0:T(8,128)(2,1)S(1)}, bf16[3,40,1152]{2,1,0:T(8,128)(2,1)S(1)}, u32[]{:S(2)}, u32[]{:S(2)}) collective-permute-start(bf16[3,40,1152]{2,1,0:T(8,128)(2,1)S(1)} %add_convert_fusion.9), channel_id=1, source_target_pairs={{0,2},{1,3},{2,0},{3,1},{4,6},{5,7},{6,4},{7,5},{8,10},{9,11},{10,... | collective-permute-start | bytes 829448 | tf_op jit(solution)/shard_map/ppermute | solution.py:42
  158.9 12.5 %collective-permute-start.17 = (bf16[2,3,112,1152]{3,2,1,0:T(8,128)(2,1)S(1)}, bf16[2,3,112,1152]{3,2,1,0:T(8,128)(2,1)S(1)}, u32[]{:S(2)}, u32[]{:S(2)}) collective-permute-start(bf16[2,3,112,1152]{3,2,1,0:T(8,128)(2,1)S(1)} %collective-permute-done.13.refs_1_), channel_id=1, source_target_pairs={{0,4},{4,0},{8,12},{12,8},{16,20},{20,16},{24,28},{28,24},{1,5},{5... | collective-permute-start | bytes 4644872 | tf_op jit(solution)/shard_map/ppermute | solution.py:42
  173.2 23.1 %collective-permute-start.19 = (bf16[40,1152]{1,0:T(8,128)(2,1)}, bf16[40,1152]{1,0:T(8,128)(2,1)S(1)}, u32[]{:S(2)}, u32[]{:S(2)}) collective-permute-start(bf16[40,1152]{1,0:T(8,128)(2,1)} %get-tuple-element.571), channel_id=1, source_target_pairs={{4,0},{8,4},{12,8},{16,12},{20,16},{24,20},{28,24},{5,1},{9,5},{13... | collective-permute-start | bytes 276488 | tf_op jit(solution)/shard_map/ppermute | solution.py:999
  174.5 21.8 %collective-permute-start.18 = (bf16[40,1152]{1,0:T(8,128)(2,1)S(1)}, bf16[40,1152]{1,0:T(8,128)(2,1)}, u32[]{:S(2)}, u32[]{:S(2)}) collective-permute-start(bf16[40,1152]{1,0:T(8,128)(2,1)S(1)} %get-tuple-element.572), channel_id=1, source_target_pairs={{0,4},{4,8},{8,12},{12,16},{16,20},{20,24},{24,28},{1,5},{5,9},{9,... | collective-permute-start | bytes 276488 | tf_op jit(solution)/shard_map/ppermute | solution.py:998
  198.0 26.4 %collective-permute-start.21 = (bf16[3,288,1152]{2,1,0:T(8,128)(2,1)}, bf16[3,288,1152]{2,1,0:T(8,128)(2,1)}, u32[]{:S(2)}, u32[]{:S(2)}) collective-permute-start(bf16[3,288,1152]{2,1,0:T(8,128)(2,1)} %pad_maximum_fusion.6), channel_id=1, source_target_pairs={{0,8},{4,20},{8,0},{12,28},{16,24},{20,4},{24,16},{28,12},{1,9},{5... | collective-permute-start | bytes 5971976 | tf_op jit(solution)/shard_map/ppermute | solution.py:79
  201.5 27.5 %collective-permute-start.22 = (bf16[300,288]{0,1:T(8,128)(2,1)S(1)}, bf16[300,288]{0,1:T(8,128)(2,1)S(1)}, u32[]{:S(2)}, u32[]{:S(2)}) collective-permute-start(bf16[300,288]{0,1:T(8,128)(2,1)S(1)} %fusion.120), channel_id=1, source_target_pairs={{0,2},{1,3},{2,0},{3,1},{4,6},{5,7},{6,4},{7,5},{8,10},{9,11},{10,... | collective-permute-start | bytes 518408 | tf_op jit(solution)/shard_map/ppermute | solution.py:42
  201.5 27.5 %collective-permute-start.24 = (bf16[48,1152]{1,0:T(8,128)(2,1)S(1)}, bf16[48,1152]{1,0:T(8,128)(2,1)S(1)}, u32[]{:S(2)}, u32[]{:S(2)}) collective-permute-start(bf16[48,1152]{1,0:T(8,128)(2,1)S(1)} %get-tuple-element.534), channel_id=1, source_target_pairs={{1,0},{2,1},{3,2},{4,3},{5,4},{6,5},{7,6},{8,7},{9,8},{10,9},{11,1... | collective-permute-start | bytes 331784 | tf_op jit(solution)/shard_map/ppermute | solution.py:48
  202.8 26.2 %collective-permute-start.23 = (bf16[48,1152]{1,0:T(8,128)(2,1)S(1)}, bf16[48,1152]{1,0:T(8,128)(2,1)S(1)}, u32[]{:S(2)}, u32[]{:S(2)}) collective-permute-start(bf16[48,1152]{1,0:T(8,128)(2,1)S(1)} %get-tuple-element.535), channel_id=1, source_target_pairs={{0,1},{1,2},{2,3},{3,4},{4,5},{5,6},{6,7},{7,8},{8,9},{9,10},{10,1... | collective-permute-start | bytes 331784 | tf_op jit(solution)/shard_map/ppermute | solution.py:48
  229.8 13.5 %collective-permute-start.25 = (bf16[2,300,288]{1,2,0:T(8,128)(2,1)S(1)}, bf16[2,300,288]{1,2,0:T(8,128)(2,1)S(1)}, u32[]{:S(2)}, u32[]{:S(2)}) collective-permute-start(bf16[2,300,288]{1,2,0:T(8,128)(2,1)S(1)} %pad_maximum_fusion.20), channel_id=1, source_target_pairs={{0,1},{1,0},{2,3},{3,2},{4,5},{5,4},{6,7},{7,6},{8,9},{9,8},{10,11... | collective-permute-start | bytes 1036808 | tf_op jit(solution)/shard_map/ppermute | solution.py:42
  231.0 13.5 %collective-permute-start.26 = (f32[12432]{0:T(1024)S(1)}, f32[12432]{0:T(1024)S(1)}, u32[]{:S(2)}, u32[]{:S(2)}) collective-permute-start(f32[12432]{0:T(1024)S(1)} %get-tuple-element.449), channel_id=1, source_target_pairs={{0,2},{1,3},{2,0},{3,1},{4,6},{5,7},{6,4},{7,5},{8,10},{9,11},{10,... | collective-permute-start | bytes 149192 | tf_op jit(solution)/shard_map/ppermute | solution.py:42
  251.3 49.1 %collective-permute-start.31 = (bf16[2,3,288,1152]{3,2,1,0:T(8,128)(2,1)}, bf16[2,3,288,1152]{3,2,1,0:T(8,128)(2,1)}, u32[]{:S(2)}, u32[]{:S(2)}) collective-permute-start(bf16[2,3,288,1152]{3,2,1,0:T(8,128)(2,1)} %pad_maximum_fusion.2.refs_1_), channel_id=1, source_target_pairs={{0,4},{4,0},{8,12},{12,8},{16,20},{20,16},{24,28},{28,24},{1,5},{5... | collective-permute-start | bytes 11943944 | tf_op jit(solution)/shard_map/ppermute | solution.py:42
  251.7 48.7 %collective-permute-start.30 = (bf16[2,3,288,1152]{3,2,1,0:T(8,128)(2,1)}, bf16[2,3,288,1152]{3,2,1,0:T(8,128)(2,1)}, u32[]{:S(2)}, u32[]{:S(2)}) collective-permute-start(bf16[2,3,288,1152]{3,2,1,0:T(8,128)(2,1)} %pad_maximum_fusion.2.refs_1_), channel_id=1, source_target_pairs={{0,16},{4,12},{8,24},{12,4},{16,0},{20,28},{24,8},{28,20},{1,17},{... | collective-permute-start | bytes 11943944 | tf_op jit(solution)/shard_map/ppermute | solution.py:79
  300.4 18.3 %collective-permute-start.34 = (bf16[2,3,288,1152]{3,2,1,0:T(8,128)(2,1)}, bf16[2,3,288,1152]{3,2,1,0:T(8,128)(2,1)}, u32[]{:S(2)}, u32[]{:S(2)}) collective-permute-start(bf16[2,3,288,1152]{3,2,1,0:T(8,128)(2,1)} %collective-permute-done.30.refs_2_), channel_id=1, source_target_pairs={{0,4},{4,0},{8,12},{12,8},{16,20},{20,16},{24,28},{28,24},{1,5},{5... | collective-permute-start | bytes 11943944 | tf_op jit(solution)/shard_map/ppermute | solution.py:42
  346.1 27.5 %collective-permute-start.35 = (bf16[2,3,384,1152]{3,2,1,0:T(8,128)(2,1)}, bf16[2,3,384,1152]{3,2,1,0:T(8,128)(2,1)}, u32[]{:S(2)}, u32[]{:S(2)}) collective-permute-start(bf16[2,3,384,1152]{3,2,1,0:T(8,128)(2,1)} %get-tuple-element.244), channel_id=1, source_target_pairs={{0,4},{4,0},{8,12},{12,8},{16,20},{20,16},{24,28},{28,24},{1,5},{5... | collective-permute-start | bytes 15925256 | tf_op jit(solution)/shard_map/ppermute | solution.py:42
  373.6 30.3 %collective-permute-start.36 = (bf16[2,3,384,1152]{3,2,1,0:T(8,128)(2,1)}, bf16[2,3,384,1152]{3,2,1,0:T(8,128)(2,1)}, u32[]{:S(2)}, u32[]{:S(2)}) collective-permute-start(bf16[2,3,384,1152]{3,2,1,0:T(8,128)(2,1)} %get-tuple-element.250), channel_id=1, source_target_pairs={{0,4},{4,0},{8,12},{12,8},{16,20},{20,16},{24,28},{28,24},{1,5},{5... | collective-permute-start | bytes 15925256 | tf_op jit(solution)/shard_map/ppermute | solution.py:42
  409.3 60.8 %collective-permute-start.37 = (bf16[2,3,2,2,96,1152]{5,4,1,2,3,0:T(8,128)(2,1)}, bf16[2,3,2,2,96,1152]{5,4,1,2,3,0:T(8,128)(2,1)}, u32[]{:S(2)}, u32[]{:S(2)}) collective-permute-start(bf16[2,3,2,2,96,1152]{5,4,1,2,3,0:T(8,128)(2,1)} %copy.216), channel_id=1, source_target_pairs={{0,8},{4,20},{8,0},{12,28},{16,24},{20,4},{24,16},{28,12},{1,9},{5... | collective-permute-start | bytes 15925256 | tf_op jit(solution)/shard_map/ppermute | solution.py:79
  474.1 33.2 %collective-permute-start.38 = (bf16[3,2,2,96,1152]{4,3,0,1,2:T(8,128)(2,1)}, bf16[3,2,2,96,1152]{4,3,0,1,2:T(8,128)(2,1)}, u32[]{:S(2)}, u32[]{:S(2)}) collective-permute-start(bf16[3,2,2,96,1152]{4,3,0,1,2:T(8,128)(2,1)} %fusion.1), channel_id=1, source_target_pairs={{0,16},{4,12},{8,24},{12,4},{16,0},{20,28},{24,8},{28,20},{1,17},{... | collective-permute-start | bytes 7962632 | tf_op jit(solution)/shard_map/ppermute | solution.py:79
  531.1 36.8 %collective-permute-start.41 = (bf16[3,2,96,1152]{3,2,0,1:T(8,128)(2,1)}, bf16[3,2,96,1152]{3,2,0,1:T(8,128)(2,1)}, u32[]{:S(2)}, u32[]{:S(2)}) collective-permute-start(bf16[3,2,96,1152]{3,2,0,1:T(8,128)(2,1)} %fusion.49), channel_id=1, source_target_pairs={{0,1},{1,0},{2,3},{3,2},{4,5},{5,4},{6,7},{7,6},{8,9},{9,8},{10,11... | collective-permute-start | bytes 3981320 | tf_op jit(solution)/shard_map/ppermute | solution.py:42
  538.7 27.2 %collective-permute-start.40 = (bf16[3,40,1152]{2,1,0:T(8,128)(2,1)S(1)}, bf16[3,40,1152]{2,1,0:T(8,128)(2,1)S(1)}, u32[]{:S(2)}, u32[]{:S(2)}) collective-permute-start(bf16[3,40,1152]{2,1,0:T(8,128)(2,1)S(1)} %add_convert_fusion.7), channel_id=1, source_target_pairs={{0,2},{1,3},{2,0},{3,1},{4,6},{5,7},{6,4},{7,5},{8,10},{9,11},{10,... | collective-permute-start | bytes 829448 | tf_op jit(solution)/shard_map/ppermute | solution.py:42
  580.8 36.3 %collective-permute-start.45 = (bf16[2,2,2,144,1152]{4,3,2,1,0:T(8,128)(2,1)}, bf16[2,2,2,144,1152]{4,3,2,1,0:T(8,128)(2,1)}, u32[]{:S(2)}, u32[]{:S(2)}) collective-permute-start(bf16[2,2,2,144,1152]{4,3,2,1,0:T(8,128)(2,1)} %fusion), channel_id=1, source_target_pairs={{0,8},{4,20},{8,0},{12,28},{16,24},{20,4},{24,16},{28,12},{1,9},{5... | collective-permute-start | bytes 7962632 | tf_op jit(solution)/shard_map/ppermute | solution.py:79
  617.1 40.0 %collective-permute-start.46 = (bf16[4,4,128,1152]{3,2,1,0:T(8,128)(2,1)}, bf16[4,4,128,1152]{3,2,1,0:T(8,128)(2,1)}, u32[]{:S(2)}, u32[]{:S(2)}) collective-permute-start(bf16[4,4,128,1152]{3,2,1,0:T(8,128)(2,1)} %get-tuple-element.313), channel_id=1, source_target_pairs={{0,4},{4,0},{8,12},{12,8},{16,20},{20,16},{24,28},{28,24},{1,5},{5... | collective-permute-start | bytes 14155784 | tf_op jit(solution)/shard_map/ppermute | solution.py:42
  624.7 32.5 %collective-permute-start.48 = (bf16[3,96,1152]{2,1,0:T(8,128)(2,1)S(1)}, bf16[3,96,1152]{2,1,0:T(8,128)(2,1)S(1)}, u32[]{:S(2)}, u32[]{:S(2)}) collective-permute-start(bf16[3,96,1152]{2,1,0:T(8,128)(2,1)S(1)} %fusion.59), channel_id=1, source_target_pairs={{0,2},{1,3},{2,0},{3,1},{4,6},{5,7},{6,4},{7,5},{8,10},{9,11},{10,... | collective-permute-start | bytes 1990664 | tf_op jit(solution)/shard_map/ppermute | solution.py:42
  628.2 29.0 %collective-permute-start.47 = (bf16[2,2,144,1152]{3,2,1,0:T(8,128)(2,1)S(1)}, bf16[2,2,144,1152]{3,2,1,0:T(8,128)(2,1)S(1)}, u32[]{:S(2)}, u32[]{:S(2)}) collective-permute-start(bf16[2,2,144,1152]{3,2,1,0:T(8,128)(2,1)S(1)} %fusion.13), channel_id=1, source_target_pairs={{0,16},{4,12},{8,24},{12,4},{16,0},{20,28},{24,8},{28,20},{1,17},{... | collective-permute-start | bytes 3981320 | tf_op jit(solution)/shard_map/ppermute | solution.py:79
  659.4 36.2 %collective-permute-start.49 = (bf16[2,2,2,128,1152]{4,3,2,1,0:T(8,128)(2,1)S(1)}, bf16[2,2,2,128,1152]{4,3,2,1,0:T(8,128)(2,1)S(1)}, u32[]{:S(2)}, u32[]{:S(2)}) collective-permute-start(bf16[2,2,2,128,1152]{4,3,2,1,0:T(8,128)(2,1)S(1)} %fusion.2), channel_id=1, source_target_pairs={{0,8},{4,20},{8,0},{12,28},{16,24},{20,4},{24,16},{28,12},{1,9},{5... | collective-permute-start | bytes 7077896 | tf_op jit(solution)/shard_map/ppermute | solution.py:79
  663.6 31.9 %collective-permute-start.55 = (bf16[3,96,1152]{2,1,0:T(8,128)(2,1)S(1)}, bf16[3,96,1152]{2,1,0:T(8,128)(2,1)S(1)}, u32[]{:S(2)}, u32[]{:S(2)}) collective-permute-start(bf16[3,96,1152]{2,1,0:T(8,128)(2,1)S(1)} %fusion.52), channel_id=1, source_target_pairs={{0,8},{4,20},{8,0},{12,28},{16,24},{20,4},{24,16},{28,12},{1,9},{5... | collective-permute-start | bytes 1990664 | tf_op jit(solution)/shard_map/ppermute | solution.py:79
  664.9 30.7 %collective-permute-start.50 = (bf16[2,144,1152]{2,1,0:T(8,128)(2,1)S(1)}, bf16[2,144,1152]{2,1,0:T(8,128)(2,1)S(1)}, u32[]{:S(2)}, u32[]{:S(2)}) collective-permute-start(bf16[2,144,1152]{2,1,0:T(8,128)(2,1)S(1)} %fusion.60), channel_id=1, source_target_pairs={{0,1},{1,0},{2,3},{3,2},{4,5},{5,4},{6,7},{7,6},{8,9},{9,8},{10,11... | collective-permute-start | bytes 1990664 | tf_op jit(solution)/shard_map/ppermute | solution.py:42
  697.3 18.0 %collective-permute-start.51 = (bf16[2,2,128,1152]{3,2,1,0:T(8,128)(2,1)S(1)}, bf16[2,2,128,1152]{3,2,1,0:T(8,128)(2,1)S(1)}, u32[]{:S(2)}, u32[]{:S(2)}) collective-permute-start(bf16[2,2,128,1152]{3,2,1,0:T(8,128)(2,1)S(1)} %fusion.16), channel_id=1, source_target_pairs={{0,16},{4,12},{8,24},{12,4},{16,0},{20,28},{24,8},{28,20},{1,17},{... | collective-permute-start | bytes 3538952 | tf_op jit(solution)/shard_map/ppermute | solution.py:79
  699.4 15.9 %collective-permute-start.52 = (bf16[144,1152]{1,0:T(8,128)(2,1)S(1)}, bf16[144,1152]{1,0:T(8,128)(2,1)S(1)}, u32[]{:S(2)}, u32[]{:S(2)}) collective-permute-start(bf16[144,1152]{1,0:T(8,128)(2,1)S(1)} %fusion.63), channel_id=1, source_target_pairs={{0,2},{1,3},{2,0},{3,1},{4,6},{5,7},{6,4},{7,5},{8,10},{9,11},{10,... | collective-permute-start | bytes 995336 | tf_op jit(solution)/shard_map/ppermute | solution.py:42
  717.1 15.5 %collective-permute-start.53 = (bf16[2,128,1152]{2,1,0:T(8,128)(2,1)S(1)}, bf16[2,128,1152]{2,1,0:T(8,128)(2,1)S(1)}, u32[]{:S(2)}, u32[]{:S(2)}) collective-permute-start(bf16[2,128,1152]{2,1,0:T(8,128)(2,1)S(1)} %fusion.64), channel_id=1, source_target_pairs={{0,1},{1,0},{2,3},{3,2},{4,5},{5,4},{6,7},{7,6},{8,9},{9,8},{10,11... | collective-permute-start | bytes 1769480 | tf_op jit(solution)/shard_map/ppermute | solution.py:42
  733.4 14.8 %collective-permute-start.56 = (bf16[128,1152]{1,0:T(8,128)(2,1)S(1)}, bf16[128,1152]{1,0:T(8,128)(2,1)S(1)}, u32[]{:S(2)}, u32[]{:S(2)}) collective-permute-start(bf16[128,1152]{1,0:T(8,128)(2,1)S(1)} %fusion.65), channel_id=1, source_target_pairs={{0,2},{1,3},{2,0},{3,1},{4,6},{5,7},{6,4},{7,5},{8,10},{9,11},{10,... | collective-permute-start | bytes 884744 | tf_op jit(solution)/shard_map/ppermute | solution.py:42
  734.1 26.5 %collective-permute-start.60 = (bf16[2,3,96,1152]{3,2,1,0:T(8,128)(2,1)S(1)}, bf16[2,3,96,1152]{3,2,1,0:T(8,128)(2,1)S(1)}, u32[]{:S(2)}, u32[]{:S(2)}) collective-permute-start(bf16[2,3,96,1152]{3,2,1,0:T(8,128)(2,1)S(1)} %pad_maximum_fusion.10), channel_id=1, source_target_pairs={{0,16},{4,12},{8,24},{12,4},{16,0},{20,28},{24,8},{28,20},{1,17},{... | collective-permute-start | bytes 3981320 | tf_op jit(solution)/shard_map/ppermute | solution.py:79
  778.2 12.9 %collective-permute-start.62 = (bf16[2,2,128,1152]{3,2,0,1:T(8,128)(2,1)S(1)}, bf16[2,2,128,1152]{3,2,0,1:T(8,128)(2,1)S(1)}, u32[]{:S(2)}, u32[]{:S(2)}) collective-permute-start(bf16[2,2,128,1152]{3,2,0,1:T(8,128)(2,1)S(1)} %pad_maximum_fusion.12), channel_id=1, source_target_pairs={{0,4},{4,0},{8,12},{12,8},{16,20},{20,16},{24,28},{28,24},{1,5},{5... | collective-permute-start | bytes 3538952 | tf_op jit(solution)/shard_map/ppermute | solution.py:42
  782.5 20.9 %collective-permute-start.65 = (bf16[2,2,3,96,1152]{4,3,2,0,1:T(8,128)(2,1)}, bf16[2,2,3,96,1152]{4,3,2,0,1:T(8,128)(2,1)}, u32[]{:S(2)}, u32[]{:S(2)}) collective-permute-start(bf16[2,2,3,96,1152]{4,3,2,0,1:T(8,128)(2,1)} %pad_maximum_fusion.4), channel_id=1, source_target_pairs={{0,4},{4,0},{8,12},{12,8},{16,20},{20,16},{24,28},{28,24},{1,5},{5... | collective-permute-start | bytes 7962632 | tf_op jit(solution)/shard_map/ppermute | solution.py:42
  (135 other events, 1794.3 us)

commit v3 on v2

--- a/solution.py
+++ b/solution.py
@@ -81,6 +81,29 @@
     )
 
 
+def swap_z(values, number):
+    ranks, group = lax.axis_size("dp"), lax.axis_size("tensor")
+    pairs = []
+    for rank in range(ranks):
+        bit = (2, 1)[(rank + number) % 2]
+        pairs += [(rank * group + peer, rank * group + (peer ^ bit)) for peer in range(group)]
+    return lax.ppermute(values, ("dp", "tensor"), pairs)
+
+
+def peer_of(place, sibling=False):
+    core = lax.axis_index("dp") % 2
+    if place in (1, 2):
+        place = jnp.where(core == (1 if sibling else 0), place, 3 - place)
+    return jnp.bitwise_xor(lax.axis_index("tensor"), place)
+
+
+def turn_z(values, place, sibling=False):
+    core = lax.axis_index("dp") % 2
+    return jnp.where(
+        core == (1 if sibling else 0), values, jnp.swapaxes(values, place, place + 1)
+    )
+
+
 def turn_axes(values, place):
     count = len(upper_bits())
     axes = list(range(values.ndim))
@@ -161,7 +184,7 @@
 
 def halve_z_once(terms, bit, place):
     place = place + 1 if bit == 1 else place
-    other = swap(total(pick_at(terms, place, 1)), "tensor", bit)
+    other = swap_z(total(pick_at(terms, place, 1)), 1 if bit == 1 else 0)
     return pick_at(terms, place, 0) + [other]
 
 
@@ -206,7 +229,7 @@
                 put(
                     source.at[upper, peer - 1, low:high],
                     rank,
-                    jnp.bitwise_xor(me_z, peer),
+                    peer_of(peer, step % 2 == 1),
                     low,
                     high,
                 )
@@ -250,7 +273,6 @@
 
 def grads_kernel(ranks, group, rows, cols, pairs, *refs):
     inputs, (extra, keep, send, whole, block, sems) = refs[:-6], refs[-6:]
-    me_z = lax.axis_index("tensor")
     count = len(upper_bits())
     for kind, (left, right) in enumerate(pairs):
         grad = dot_tn(inputs[left][...], inputs[right][...])
@@ -275,7 +297,7 @@
         parts = bits_of(step // 2, count)[::-1]
         place = pl.multiple_of(rank_of(step, parts) * rows, 16)
         for peer in range(group):
-            source = whole.at[jnp.bitwise_xor(me_z, peer), pl.ds(place, rows)]
+            source = whole.at[peer_of(peer, step % 2 == 1), pl.ds(place, rows)]
             target = (keep, send)[step % 2].at[step // 2, peer]
             copies.append(pltpu.make_async_copy(source, target, sems.at[len(copies)]))
     for copy in copies:
@@ -889,7 +911,7 @@
     piece_2 = lax.dynamic_index_in_dim(own_mix, me_d, 0, keepdims=False)
 
     def near_z(piece, far):
-        near = swap(jnp.stack([piece, far]), "tensor", 1)
+        near = swap_z(jnp.stack([piece, far]), 1)
         return jnp.stack([near[0], far, near[1]])
 
     def turn(values, number):
@@ -916,11 +938,11 @@
     normal_a, inv_std_a = norm_parts(tokens_f)
     normed = (normal_a * (1.0 + scale_a) + shift_a).astype(bfloat)
 
-    far_1 = swap(piece_1, "tensor", 2)
+    far_1 = swap_z(piece_1, 0)
     far_1, normed = tie(far_1, normed)
     wave_1 = near_z(piece_1, far_1)
     wave_1, rows_ffn, item_bucket, piece_2 = tie(wave_1, rows_ffn, item_bucket, piece_2)
-    far_2 = swap(piece_2, "tensor", 2)
+    far_2 = swap_z(piece_2, 0)
     wave_1 = turn(wave_1, 0)
     inner = own_slots % ITEM_SLOTS
     grid_h, grid_w = grid_table(look_up(item_bucket, item))
@@ -958,15 +980,24 @@
     piece_3 = piece_3.reshape(3 * ffn_piece, width)
     core_last_1, wave_2, piece_3 = tie(core_last_1, wave_2, piece_3)
     wave_2 = turn(wave_2, 0)
-    far_3 = swap(piece_3, "tensor", 2)
+    far_3 = swap_z(piece_3, 0)
     text_near = swap(jnp.stack([text_half, text_far]), "tensor", 1)
     wq, wk, wv = [
         part.reshape(width, width) for part in assemble(own_qkv, (wave_1, last_1, core_1, core_last_1), cols)
     ]
-    wq, wk, wv, wave_2 = tie(wq, wk, wv, wave_2)
+    wq, wk, wv, wave_2, text_near = tie(wq, wk, wv, wave_2, text_near)
     wave_2 = mid_turns(wave_2)
     last_2 = last_turn(wave_2)
     core_2 = swap(wave_2, "dp", 1)
+    in_order = lambda rel: [
+        lax.dynamic_index_in_dim(rel, me_z ^ peer, 0, keepdims=False) for peer in range(group)
+    ]
+    by_core = lambda one, two: jnp.stack(
+        [jnp.where(me_d % 2 == 0, one, two), jnp.where(me_d % 2 == 0, two, one)]
+    )
+    text_rel = jnp.stack([text_half, text_near[0], text_far, text_near[1]])
+    text_other = swap(text_rel, "dp", 1)
+
     first_live = (in_first & valid[:, None]).astype(single)
     second_live = (in_second & valid[:, None]).astype(single)
     first_all, second_all = in_first.astype(single), in_second.astype(single)
@@ -1011,44 +1042,42 @@
     small_rel = jnp.concatenate([dw_weight, dw_bias[None], in_bias[None]], axis=0)
     small_rel = jnp.pad(small_rel, ((0, 5), (0, 0), (0, padded_channels - channels)))
     sizes = small_rel.size
-    small_rel = jnp.concatenate([small_rel.reshape(-1), xq_bias])
+    small_rel = jnp.concatenate([small_rel.reshape(-1), xq_bias]).astype(bfloat)
+    small_tall = -(-small_rel.size // (32 * cols)) * 16
+    small_rel = jnp.pad(small_rel, (0, 2 * small_tall * cols - small_rel.size))
+    small_half = lax.dynamic_index_in_dim(
+        small_rel.reshape(2, small_tall, cols), me_d % 2, 0, keepdims=False
+    )
     down = tuple(range(2, 2 + len(bits)))
 
     table = item_table(table_1, table_2)
-    table, far_3, text_near = tie(table, far_3, text_near)
+    table, text_other, far_3 = tie(table, text_other, far_3)
     table = total([table, swap(table, "tensor", 1)])
-    wave_3 = near_z(piece_3, far_3)
-    in_order = lambda rel: [
-        lax.dynamic_index_in_dim(rel, me_z ^ peer, 0, keepdims=False) for peer in range(group)
-    ]
-    by_core = lambda one, two: jnp.stack(
-        [jnp.where(me_d % 2 == 0, one, two), jnp.where(me_d % 2 == 0, two, one)]
-    )
-    text_rel = jnp.stack([text_half, text_near[0], text_far, text_near[1]])
-    text_other = swap(text_rel, "dp", 1)
-    table, last_2, core_2, text_other = tie(table, last_2, core_2, text_other)
-    table = total([table, swap(table, "tensor", 2)])
-    core_last_2 = swap(last_2, "dp", 1)
     text_rel = by_core(text_rel, text_other).swapaxes(0, 1).reshape(group, -1, width)
     text_all = jnp.concatenate(in_order(text_rel[:, :text_rows_here]))
     text_kv = jnp.einsum("td,dke->tke", text_all, w_xkv, preferred_element_type=single)
     xkv_own = jnp.stack([text_kv[:, 0], text_kv[:, 1] + xv_bias], axis=0).astype(bfloat)
-    xkv_half = lax.dynamic_index_in_dim(xkv_own, me_d % 2, 0, keepdims=False)
-    table, core_last_2, xkv_half = tie(table, core_last_2, xkv_half)
+    both_half = jnp.concatenate(
+        [lax.dynamic_index_in_dim(xkv_own, me_d % 2, 0, keepdims=False), small_half], axis=0
+    )
+    table, both_half, last_2, core_2 = tie(table, both_half, last_2, core_2)
+    table = total([table, swap(table, "tensor", 2)])
+    both_far = swap(both_half, "tensor", 2)
+    core_last_2 = swap(last_2, "dp", 1)
+    table, both_far, core_last_2, far_3 = tie(table, both_far, core_last_2, far_3)
+    state_1, state_2 = item_sums(table)
+    wave_3 = near_z(piece_3, far_3)
+    both_near = swap(jnp.stack([both_half, both_far]), "tensor", 1)
     wo, wxq, wxo = [
         part.reshape(width, width) for part in assemble(own_mix, (wave_2, last_2, core_2, core_last_2), cols)
     ]
     wxq_pad = pad_heads(wxq, xheads)
     wxo_pad = pad_heads(wxo, xheads)
-
-    state_1, state_2 = item_sums(table)
-    xkv_far = swap(xkv_half, "tensor", 2)
-    state_1, state_2, wo, wxq_pad, wxo_pad, wave_3, d_ffn = tie(
-        state_1, state_2, wo, wxq_pad, wxo_pad, wave_3, d_ffn
-    )
-    wave_3 = turn(wave_3, 0)
-    above = shift_devices(d_ffn[own_rows - REACH :], 1)
-    below = shift_devices(d_ffn[:REACH], -1)
+    state_1, state_2, wo, wxq_pad, wxo_pad, both_near = tie(
+        state_1, state_2, wo, wxq_pad, wxo_pad, both_near
+    )
+    both_rel = jnp.stack([both_half, both_near[0], both_far, both_near[1]])
+    both_other = swap(both_rel, "dp", 1)
     attn_ratio, denominator, attn, attn_sum = over_lanes(
         attend_kernel,
         "lttccw",
@@ -1058,42 +1087,37 @@
     attn_out = attn_sum + out_bias
     after_attn = tokens_f + live * gate_a * attn_out
 
+    after_attn, wave_3, both_other = tie(after_attn, wave_3, both_other)
+    wave_3 = turn(wave_3, 0)
     cross_in = after_attn.astype(bfloat)
     xq_product = dot_nt(cross_in, wxq_pad)
-    wave_3, xkv_far, xq_product, above, below, small_rel = tie(
-        wave_3, xkv_far, xq_product, above, below, small_rel
-    )
-    d_ffn_ext = pad_rows(jnp.concatenate([above, d_ffn, below], axis=0), tall)
-    wave_3 = mid_turns(wave_3)
-    last_3 = last_turn(wave_3)
-    core_3 = swap(wave_3, "dp", 1)
-    xkv_near = swap(jnp.stack([xkv_half, xkv_far]), "tensor", 1)
-    xkv_rel = jnp.stack([xkv_half, xkv_near[0], xkv_far, xkv_near[1]])
-    small_half = lax.dynamic_index_in_dim(small_rel.reshape(2, -1), me_d % 2, 0, keepdims=False)
-    small_far = swap(small_half, "tensor", 2)
-    xkv_rel, small_far = tie(xkv_rel, small_far)
-    xkv_other = swap(xkv_rel, "dp", 1)
-    small_near = swap(jnp.stack([small_half, small_far]), "tensor", 1)
-    small = jnp.stack([small_half, small_near[0], small_far, small_near[1]])
-    small_other = swap(small, "dp", 1)
-    xkv_all = by_core(xkv_rel, xkv_other).swapaxes(0, 1)
+    both = by_core(both_rel, both_other)
+    xkv_all = both[:, :, :TXT].swapaxes(0, 1)
     xkv_all = jnp.stack(in_order(xkv_all)).reshape(group, 2, TXT, cols // XHEAD, XHEAD)
     xkv_all = xkv_all.transpose(1, 0, 3, 2, 4).reshape(2, xheads, TXT, XHEAD)
     xkv_all = jnp.pad(xkv_all, ((0, 0), (0, 0), (0, TXT_PAD - TXT), (0, XLANE - XHEAD)))
     xkeys, xvals = xkv_all[0], xkv_all[1]
-    small = by_core(small, small_other).swapaxes(0, 1).reshape(group, -1)
-    xq_rel = small[:, sizes:]
+    small = both[:, :, TXT:].swapaxes(0, 1).reshape(group, -1).astype(single)
+    xq_rel = small[:, sizes : sizes + cols]
     small = flip_dp(small[:, :sizes].reshape(group, 16, 2, ranks, ffn_piece), 3)
     small = small.reshape((group, 16, 2) + (2,) * (len(bits) + 1) + (ffn_piece,))
     small = jnp.moveaxis(small, 0, len(bits) + 3)
     small = small.transpose((len(bits) + 2, 1, 0) + down[::-1] + (len(bits) + 3, len(bits) + 4))
+    small = small.reshape(small.shape[:-2] + (2, 2, ffn_piece))
     small = [
-        own_turns(small[core], 2, core == 1).reshape(2, 16, half_count) for core in (0, 1)
+        turn_z(own_turns(small[core], 2, core == 1), 2 + len(bits), core == 1).reshape(
+            2, 16, half_count
+        )
+        for core in (0, 1)
     ]
     xq_bias_all = jnp.stack(in_order(xq_rel)).reshape(xheads, XHEAD)
     xq_bias_all = jnp.pad(xq_bias_all, ((0, 0), (0, XLANE - XHEAD))).reshape(xheads * XLANE)
     lengths = look_up(text_len, item)[:, None]
     xquery = (xq_product + xq_bias_all).astype(bfloat)
+    xquery, wave_3 = tie(xquery, wave_3)
+    wave_3 = mid_turns(wave_3)
+    last_3 = last_turn(wave_3)
+    core_3 = swap(wave_3, "dp", 1)
     cross_mix = cross_call(xquery, xkeys, xvals, lengths)
     cross_out = dot_nn(cross_mix, wxo_pad) + xo_bias
     after_cross = after_attn + live * cross_out
@@ -1121,9 +1145,16 @@
         for core in (0, 1)
     ]
 
-    above = shift_devices(normed_ffn[own_rows - 2 * REACH :], 1)
-    below = shift_devices(normed_ffn[: 2 * REACH], -1)
-    normed_ext = pad_rows(jnp.concatenate([above, normed_ffn, below], axis=0), wide)
+    above = shift_devices(
+        jnp.concatenate([normed_ffn[own_rows - 2 * REACH :], d_ffn[own_rows - REACH :]], axis=0), 1
+    )
+    below = shift_devices(jnp.concatenate([normed_ffn[: 2 * REACH], d_ffn[:REACH]], axis=0), -1)
+    normed_ext = pad_rows(
+        jnp.concatenate([above[: 2 * REACH], normed_ffn, below[: 2 * REACH]], axis=0), wide
+    )
+    d_ffn_ext = pad_rows(
+        jnp.concatenate([above[2 * REACH :], d_ffn, below[2 * REACH :]], axis=0), tall
+    )
     tables = (reach, back_full, back_last)
     def ffn_part(core, begin, *added):
         return ffn_call(
@@ -1139,7 +1170,7 @@
     part_1 = ffn_part(0, 2, other_3)
     normed_ext, other_2, *part_1 = tie(normed_ext, other_2, *part_1)
     turn_shape = (2, 3) + (2,) * len(bits) + (ffn_piece, width)
-    ffn_got = swap_path(part_1[2].reshape(turn_shape), 0)
+    ffn_got = swap_path(part_1[2], 0).reshape(turn_shape)
     part_0 = ffn_part(0, 0, other_2)
     parts = (part_0, part_1, part_2, part_3)
     ffn_out = sum(part[0] for part in parts)[:own_rows]
@@ -1151,9 +1182,13 @@
 
     d_small = jnp.stack(
         [
-            own_turns(
-                part.astype(bfloat).reshape((2, 16) + (2,) * (len(bits) + 2) + (ffn_piece,)),
-                2,
+            turn_z(
+                own_turns(
+                    part.astype(bfloat).reshape((2, 16) + (2,) * (len(bits) + 2) + (ffn_piece,)),
+                    2,
+                    core == 1,
+                ),
+                2 + len(bits),
                 core == 1,
             )
             for core, part in enumerate(d_small_half)
@@ -1222,7 +1257,7 @@
             ]
         )
 
-    d_table, mix_extra = tie(d_table, mix_extra)
+    d_table, mix_extra, ffn_terms[-1] = tie(d_table, mix_extra, ffn_terms[-1])
     d_table = total([d_table, swap(d_table, "tensor", 1)])
     mod_sums = [
         mod_sum(rows) for rows in (d_gate_a, d_normed_ffn, d_normed_ffn * normal_f, d_gate_f)
@@ -1230,7 +1265,7 @@
     d_table, d_out_bias, d_xo_bias, *mod_sums = tie(d_table, d_out_bias, d_xo_bias, *mod_sums)
     d_table = total([d_table, swap(d_table, "tensor", 2)])
     mix_grads = grads_call(mix_arrays, ((0, 1), (2, 3), (4, 5)), mix_extra, mix_rows, cols)
-    d_table, mix_grads[1], ffn_terms[-1] = tie(d_table, mix_grads[1], ffn_terms[-1])
+    d_table, mix_grads[1] = tie(d_table, mix_grads[1])
     mix_terms = core_terms(*mix_grads)
     d_state_1, d_state_2 = item_sums(d_table)
     d_state_1, d_state_2, mix_terms[1] = tie(d_state_1, d_state_2, mix_terms[1])
@@ -1266,18 +1301,18 @@
         last_rows,
         cols,
     )
-    qkv_grads[1], mix_terms[-1] = tie(qkv_grads[1], mix_terms[-1])
+    qkv_grads[1], mix_terms[-1], ffn_terms[-1] = tie(qkv_grads[1], mix_terms[-1], ffn_terms[-1])
     qkv_terms = core_terms(*qkv_grads)
     for stage in range(1, len(bits)):
         mix_terms = halve_path(mix_terms, stage, 0)
-    qkv_terms[1], mix_terms[-1], ffn_terms[-1] = tie(qkv_terms[1], mix_terms[-1], ffn_terms[-1])
+    qkv_terms[1], mix_terms[-1] = tie(qkv_terms[1], mix_terms[-1])
     qkv_terms = halve_path(qkv_terms, 0, 0)
     mix_terms = halve_z_once(mix_terms, 1, 0)
     qkv_terms[-1], mix_terms[-1] = tie(qkv_terms[-1], mix_terms[-1])
     for stage in range(1, len(bits)):
         qkv_terms = halve_path(qkv_terms, stage, 0)
     mix_terms = halve_z_once(mix_terms, 2, 0)
-    qkv_terms[-1], mix_terms[-1] = tie(qkv_terms[-1], mix_terms[-1])
+    qkv_terms[-1], mix_terms[-1], *ffn_terms = tie(qkv_terms[-1], mix_terms[-1], *ffn_terms)
     qkv_terms = halve_z_once(qkv_terms, 1, 0)
     d_mix_all = share_turn(total(mix_terms), 0)
     d_ffn_all = share_turn(total(ffn_terms), 0)
@@ -1294,6 +1329,7 @@
     for stage in range(1, len(bits)):
         d_qkv_all = share_turn(d_qkv_all, stage)
     d_ffn_all = share_core(d_ffn_all)
+    d_qkv_all, d_ffn_all = tie(d_qkv_all, d_ffn_all)
     d_qkv_all = share_core(d_qkv_all)
     d_ffn_all = d_ffn_all.transpose(1, 0, 2, 3)
     d_ffn_all = d_ffn_all.reshape(3, padded_channels, width)[:, :channels]

time: 820 us -> 777 us (0.948)
  waiting for transfers between devices: 248 us -> 198 us
  starting transfers between devices: 70.2 us -> 79.4 us
    ppermute x40 -> x25, waiting for transfers between devices: 172 us -> 44.5 us  [swap(): return lax.ppermute(values, axis, [(i, i ^ bit) for i in range(count)])]
    ppermute x0 -> x12, waiting for transfers between devices: none -> 65.3 us  [swap_z(): return lax.ppermute(values, ('dp', 'tensor'), pairs)]
    ppermute x0 -> x12, starting transfers between devices: none -> 17.8 us  [swap_z(): return lax.ppermute(values, ('dp', 'tensor'), pairs)]
    ppermute x18, waiting for transfers between devices: 65.4 us -> 80.2 us  [swap_path(): lax.ppermute(values, 'dp', [(i, i ^ turns(i % 2)[number]) for i in range(...]
    ppermute x40 -> x25, starting transfers between devices: 26.3 us -> 19.5 us  [swap(): return lax.ppermute(values, axis, [(i, i ^ bit) for i in range(count)])]
    unnamed x246 -> x248, local copies, waits for them, and re-layouts: 20.8 us -> 14.1 us
  transfers between devices with their start and end apart: 66 -> 61, of which waited for: 29 -> 31; matrix products, arithmetic and copies ran while one was open for 25% -> 28% of each run, Pallas kernels for 24% -> 26%
where the time goes in v3:
time: 777 us; the launch traced here: 771 us
  Pallas kernels  229 us (29%)
  waiting for transfers between devices  198 us (25%)
  other arithmetic  131 us (17%)
  local copies, waits for them, and re-layouts  107 us (14%)
  starting transfers between devices  79.4 us (10%)
  matrix products  22.9 us (3%)
    pallas_call x4, Pallas kernels, ffn_call(): pl.pallas_call(functools.partial(ffn_kernel, core if direct else None, be...  112 us
    ppermute x18, waiting for transfers between devices, swap_path(): lax.ppermute(values, 'dp', [(i, i ^ turns(i % 2)[number]) for i in range(...  80.2 us
    ppermute x12, waiting for transfers between devices, swap_z(): return lax.ppermute(values, ('dp', 'tensor'), pairs)  65.3 us
    ppermute x25, waiting for transfers between devices, swap(): return lax.ppermute(values, axis, [(i, i ^ bit) for i in range(count)])  44.5 us
    pallas_call x4, Pallas kernels, lane_call(): pl.pallas_call(kernel, grid=(features // LANES,), in_specs=[specs[kind] f...  40 us
    ppermute x18, starting transfers between devices, swap_path(): lax.ppermute(values, 'dp', [(i, i ^ turns(i % 2)[number]) for i in range(...  27.3 us
    pallas_call x2, Pallas kernels, grads_call(): pl.pallas_call(functools.partial(grads_kernel, ranks, group, rows, cols,...  26.2 us
    convert_element_type x16, other arithmetic, total(): return summed.astype(bfloat)  20.3 us
  transfers between devices with their start and end apart: 61, of which 31 were waited for; matrix products, arithmetic and copies ran while one was open for 28% of the time, Pallas kernels for 26%

profile of v3, /device:TPU:0, one launch (start us, length us, event | category | flops | bytes accessed | tf_op | source)
XLA Modules:
  0.0 770.7 jit_solution(11937300980975648882)
XLA Ops:
  3.9 4.1 collective-permute-start
  25.1 6.0 pad_maximum_fusion.refs_0_
  31.2 6.8 collective-permute-done.1
  51.9 4.3 collective-permute-done.2
  60.7 11.3 %collective-permute-done.6 = bf16[2,112,1152]{2,1,0:T(8,128)(2,1)S(1)} collective-permute-done((bf16[2,112,1152]{2,1,0:T(8,128)(2,1)S(1)}, bf16[2,112,1152]{2,1,0:T(8,128)(2,1)S(1)}, u32[]{:S(2)}, u32[]{:S(2)}) %collective-permute-start.6) | collective-permute-done | bytes 516128 | tf_op jit(solution)/shard_map/ppermute | solution.py:90
  72.2 4.2 collective-permute-done.4.refs_1_
  85.3 7.8 %shard_map.348 = (bf16[4,288,1152]{2,1,0:T(8,128)(2,1)}, bf16[4,288,1152]{2,1,0:T(8,128)(2,1)}, bf16[4,288,1152]{2,1,0:T(8,128)(2,1)}) custom-call(bf16[8,112,1152]{2,1,0:T(8,128)(2,1)} %bitcast.554, bf16[2,3,112,1152]{3,2,1,0:T(8,128)(2,1)} %copy-done.14, bf16[2,3,112,1152]{3,2,1,0:T(8,128)(2,1)} %collective-permute-done.4.refs_1_, ...), custom_call_target="tpu_custom_call" | custom-call | bytes 4128768 | tf_op jit(solution)/shard_map/pallas_call | solution.py:257
  98.0 11.5 %shard_map.349 = (f32[416,1152]{1,0:T(8,128)}, f32[416,1152]{1,0:T(8,128)}, bf16[416,1152]{1,0:T(8,128)(2,1)}, bf16[416,1152]{1,0:T(8,128)(2,1)}, bf16[416,1152]...) custom-call(bf16[416,1152]{1,0:T(8,128)(2,1)} %fusion.27.normed.refs_3_, bf16[1152,1152]{1,0:T(8,128)(2,1)} %bitcast.541, ...), custom_call_target="tpu_custom_call" | custom-call | flops 552075264 | bytes 479232 | tf_op jit(solution)/shard_map/pallas_call | solution.py:733
  112.5 7.5 collective-permute-done.13
  124.2 16.4 %collective-permute-done.16 = bf16[3,40,1152]{2,1,0:T(8,128)(2,1)S(1)} collective-permute-done((bf16[3,40,1152]{2,1,0:T(8,128)(2,1)S(1)}, bf16[3,40,1152]{2,1,0:T(8,128)(2,1)S(1)}, u32[]{:S(2)}, u32[]{:S(2)}) %collective-permute-start.16) | collective-permute-done | bytes 276512 | tf_op jit(solution)/shard_map/ppermute | solution.py:42
  140.6 4.6 collective-permute-done.17
  155.0 7.9 %shard_map.350 = (bf16[4,288,1152]{2,1,0:T(8,128)(2,1)}, bf16[4,288,1152]{2,1,0:T(8,128)(2,1)}, bf16[4,288,1152]{2,1,0:T(8,128)(2,1)}) custom-call(bf16[8,112,1152]{2,1,0:T(8,128)(2,1)} %bitcast.561, bf16[2,3,112,1152]{3,2,1,0:T(8,128)(2,1)} %pad_maximum_fusion.8.refs_0_, bf16[2,3,112,1152]{3,2,1,0:T(8,128)(2,1)} %collective-permute-done.14.refs_1_, ...), custom_call_target="tpu_custom_call" | custom-call | bytes 4128768 | tf_op jit(solution)/shard_map/pallas_call | solution.py:257
  162.9 4.8 pad.61
  179.6 7.0 shard_map.351
  211.8 6.0 add_convert_fusion.query_ref
  221.5 4.5 pad_maximum_fusion.2.refs_1_
  234.7 4.2 fusion.48
  239.0 16.6 %shard_map.352.refs_4_ = bf16[416,2048]{1,0:T(8,128)(2,1)} custom-call(bf16[416,2048]{1,0:T(8,128)(2,1)} %add_convert_fusion.query_ref, bf16[16,384,128]{2,1,0:T(8,128)(2,1)} %get-tuple-element.522.keys_ref, bf16[16,384,128]{2,1,0:T(8,128)(2,1)} %get-tuple-element.521.vals_ref, s32[416,1]{1,0:T(8,128)} %copy.254.length_ref), custom_call_target="tpu_custom_call" | custom-call | flops 327155712 | bytes 1703936 | tf_op jit(solution)/shard_map/pallas_call | solution.py:786
  255.6 6.0 fusion.240
  262.9 9.6 %collective-permute-done.25.refs_2_ = bf16[2,3,288,1152]{3,2,1,0:T(8,128)(2,1)} collective-permute-done((bf16[2,3,288,1152]{3,2,1,0:T(8,128)(2,1)}, bf16[2,3,288,1152]{3,2,1,0:T(8,128)(2,1)}, u32[]{:S(2)}, u32[]{:S(2)}) %collective-permute-start.25) | collective-permute-done | bytes 3981344 | tf_op jit(solution)/shard_map/ppermute | solution.py:79
  274.0 4.6 collective-permute-start.27
  278.6 6.2 collective-permute-done.28
  289.1 27.3 %shard_map.353 = (f32[416,1152]{1,0:T(8,128)}, f32[416,1152]{1,0:T(8,128)}, bf16[2,3,384,1152]{3,2,1,0:T(8,128)(2,1)}, f32[2,16,768]{2,1,0:T(8,128)}) custom-call(bf16[608,1152]{1,0:T(8,128)(2,1)} %pad_maximum_fusion.9.normed_ref, bf16[512,1152]{1,0:T(8,128)(2,1)} %pad_maximum_fusion.13.grad_ref, bf16[4,1152,224]{2,1,0:T(8,128)(2,1)} %bitcast.531, ...), custom_call_target="tpu_custom_call" | custom-call | flops 1755316224 | bytes 1769472 | tf_op jit(solution)/shard_map/pallas_call | solution.py:597
  316.4 5.3 collective-permute-start.30
  321.7 27.4 %shard_map.354 = (f32[416,1152]{1,0:T(8,128)}, f32[416,1152]{1,0:T(8,128)}, bf16[2,3,384,1152]{3,2,1,0:T(8,128)(2,1)}, f32[2,16,768]{2,1,0:T(8,128)}) custom-call(bf16[608,1152]{1,0:T(8,128)(2,1)} %pad_maximum_fusion.9.normed_ref, bf16[512,1152]{1,0:T(8,128)(2,1)} %pad_maximum_fusion.13.grad_ref, bf16[4,1152,224]{2,1,0:T(8,128)(2,1)} %bitcast.532, ...), custom_call_target="tpu_custom_call" | custom-call | flops 1755316224 | bytes 1769472 | tf_op jit(solution)/shard_map/pallas_call | solution.py:597
  350.4 28.6 %shard_map.355 = (f32[416,1152]{1,0:T(8,128)}, f32[416,1152]{1,0:T(8,128)}, bf16[2,3,384,1152]{3,2,1,0:T(8,128)(2,1)}, f32[2,16,768]{2,1,0:T(8,128)}) custom-call(bf16[608,1152]{1,0:T(8,128)(2,1)} %pad_maximum_fusion.9.normed_ref, bf16[512,1152]{1,0:T(8,128)(2,1)} %pad_maximum_fusion.13.grad_ref, bf16[4,1152,224]{2,1,0:T(8,128)(2,1)} %bitcast.533, ...), custom_call_target="tpu_custom_call" | custom-call | flops 1755316224 | bytes 1769472 | tf_op jit(solution)/shard_map/pallas_call | solution.py:597
  381.1 28.5 %shard_map.356 = (f32[416,1152]{1,0:T(8,128)}, f32[416,1152]{1,0:T(8,128)}, bf16[2,3,384,1152]{3,2,1,0:T(8,128)(2,1)}, f32[2,16,768]{2,1,0:T(8,128)}) custom-call(bf16[608,1152]{1,0:T(8,128)(2,1)} %pad_maximum_fusion.9.normed_ref, bf16[512,1152]{1,0:T(8,128)(2,1)} %pad_maximum_fusion.13.grad_ref, bf16[4,1152,224]{2,1,0:T(8,128)(2,1)} %bitcast.534, ...), custom_call_target="tpu_custom_call" | custom-call | flops 1755316224 | bytes 1769472 | tf_op jit(solution)/shard_map/pallas_call | solution.py:597
  409.6 6.7 select_reduce_fusion.7
  429.5 10.5 %collective-permute-done.32 = bf16[2,3,384,1152]{3,2,1,0:T(8,128)(2,1)} collective-permute-done((bf16[2,3,384,1152]{3,2,1,0:T(8,128)(2,1)}, bf16[2,3,384,1152]{3,2,1,0:T(8,128)(2,1)}, u32[]{:S(2)}, u32[]{:S(2)}) %collective-permute-start.32) | collective-permute-done | bytes 5308448 | tf_op jit(solution)/shard_map/ppermute | solution.py:79
  439.9 4.0 fusion.1
  452.0 18.3 %shard_map.357 = (bf16[416,2048]{1,0:T(8,128)(2,1)}, bf16[16,72,384]{2,1,0:T(8,128)(2,1)}, bf16[16,72,384]{2,1,0:T(8,128)(2,1)}, f32[1,2048]{1,0:T(1,128)}) custom-call(bf16[416,2048]{1,0:T(8,128)(2,1)} %add_convert_fusion.query_ref, bf16[16,384,128]{2,1,0:T(8,128)(2,1)} %get-tuple-element.522.keys_ref, bf16[16,384,128]{2,1,0:T(8,128)(2,1)} %get-tuple-element.521.vals_ref, ...), custom_call_target="tpu_custom_call" | custom-call | flops 327155712 | bytes 1703936 | tf_op jit(solution)/shard_map/pallas_call | solution.py:804
  490.0 9.2 %shard_map.358 = (bf16[416,1152]{1,0:T(8,128)(2,1)}, f32[40,1152]{1,0:T(8,128)}, f32[40,1152]{1,0:T(8,128)}) custom-call(bf16[416,1152]{1,0:T(8,128)(2,1)} %get-tuple-element.525.grad.refs_1_, bf16[1152,1152]{1,0:T(8,128)(2,1)} %bitcast.548, f32[416,1152]{1,0:T(8,128)} %get-tuple-element.277.ratio, f32[416,1152]{1,0:T(8,128)} %get-tuple-element.278.den, ...), custom_call_target="tpu_custom_call" | custom-call | flops 552075264 | bytes 479232 | tf_op jit(solution)/shard_map/pallas_call | solution.py:733
  500.3 11.5 %collective-permute-done.34 = bf16[3,2,96,1152]{3,2,0,1:T(8,128)(2,1)} collective-permute-done((bf16[3,2,96,1152]{3,2,0,1:T(8,128)(2,1)}, bf16[3,2,96,1152]{3,2,0,1:T(8,128)(2,1)}, u32[]{:S(2)}, u32[]{:S(2)}) %collective-permute-start.34) | collective-permute-done | bytes 1327136 | tf_op jit(solution)/shard_map/ppermute | solution.py:90
  513.8 5.6 collective-permute-done.35
  521.7 15.2 %shard_map.359 = (bf16[4,4,144,1152]{3,2,1,0:T(8,128)(2,1)}, bf16[4,4,144,1152]{3,2,1,0:T(8,128)(2,1)}) custom-call(bf16[416,1152]{1,0:T(8,128)(2,1)} %get-tuple-element.295.refs_0_, bf16[416,1152]{1,0:T(8,128)(2,1)} %get-tuple-element.525.grad.refs_1_, bf16[416,2048]{1,0:T(8,128)(2,1)} %get-tuple-element.276.refs_2_, ...), custom_call_target="tpu_custom_call" | custom-call | flops 552075264 | bytes 2654208 | tf_op jit(solution)/shard_map/pallas_call | solution.py:316
  555.1 4.0 fusion
  566.2 12.3 %shard_map.360 = (bf16[416,1152]{1,0:T(8,128)(2,1)}, bf16[416,1152]{1,0:T(8,128)(2,1)}, f32[416,1152]{1,0:T(8,128)}) custom-call(bf16[416,1152]{1,0:T(8,128)(2,1)} %get-tuple-element.280.dquery.refs_0_, bf16[416,1152]{1,0:T(8,128)(2,1)} %get-tuple-element.281.keys, bf16[416,1152]{1,0:T(8,128)(2,1)} %get-tuple-element.282.values, ...), custom_call_target="tpu_custom_call" | custom-call | flops 552075264 | bytes 479232 | tf_op jit(solution)/shard_map/pallas_call | solution.py:733
  589.7 11.0 %shard_map.361 = (bf16[4,4,128,1152]{3,2,1,0:T(8,128)(2,1)}, bf16[4,4,128,1152]{3,2,1,0:T(8,128)(2,1)}) custom-call(bf16[416,1152]{1,0:T(8,128)(2,1)} %get-tuple-element.280.dquery.refs_0_, bf16[416,1152]{1,0:T(8,128)(2,1)} %get-tuple-element.303.refs_1_, bf16[416,1152]{1,0:T(8,128)(2,1)} %get-tuple-element.304.refs_2_, ...), custom_call_target="tpu_custom_call" | custom-call | flops 552075264 | bytes 2359296 | tf_op jit(solution)/shard_map/pallas_call | solution.py:316
  609.5 14.6 %collective-permute-done.43 = bf16[2,2,144,1152]{3,2,1,0:T(8,128)(2,1)S(1)} collective-permute-done((bf16[2,2,144,1152]{3,2,1,0:T(8,128)(2,1)S(1)}, bf16[2,2,144,1152]{3,2,1,0:T(8,128)(2,1)S(1)}, u32[]{:S(2)}, u32[]{:S(2)}) %collective-permute-start.43) | collective-permute-done | bytes 1327136 | tf_op jit(solution)/shard_map/ppermute | solution.py:79
  632.1 15.5 %collective-permute-done.45 = bf16[2,144,1152]{2,1,0:T(8,128)(2,1)S(1)} collective-permute-done((bf16[2,144,1152]{2,1,0:T(8,128)(2,1)S(1)}, bf16[2,144,1152]{2,1,0:T(8,128)(2,1)S(1)}, u32[]{:S(2)}, u32[]{:S(2)}) %collective-permute-start.45) | collective-permute-done | bytes 663584 | tf_op jit(solution)/shard_map/ppermute | solution.py:90
  647.6 7.8 %collective-permute-done.44 = bf16[2,2,2,128,1152]{4,3,2,1,0:T(8,128)(2,1)S(1)} collective-permute-done((bf16[2,2,2,128,1152]{4,3,2,1,0:T(8,128)(2,1)S(1)}, bf16[2,2,2,128,1152]{4,3,2,1,0:T(8,128)(2,1)S(1)}, u32[]{:S(2)}, u32[]{:S(2)}) %collective-permute-start.44) | collective-permute-done | bytes 2359328 | tf_op jit(solution)/shard_map/ppermute | solution.py:79
  662.2 9.7 %collective-permute-done.47 = bf16[144,1152]{1,0:T(8,128)(2,1)S(1)} collective-permute-done((bf16[144,1152]{1,0:T(8,128)(2,1)S(1)}, bf16[144,1152]{1,0:T(8,128)(2,1)S(1)}, u32[]{:S(2)}, u32[]{:S(2)}) %collective-permute-start.47) | collective-permute-done | bytes 331808 | tf_op jit(solution)/shard_map/ppermute | solution.py:90
  680.9 7.5 collective-permute-done.50
  695.4 6.3 collective-permute-done.52
  707.4 6.7 collective-permute-done.53
  715.1 4.0 collective-permute-done.55
  737.2 4.3 collective-permute-start.60
  743.5 6.7 collective-permute-done.60
  (666 shorter events, 296.7 us)
Async XLA Ops:
  3.9 19.5 %collective-permute-start = (bf16[112,1152]{1,0:T(8,128)(2,1)S(1)}, bf16[112,1152]{1,0:T(8,128)(2,1)S(1)}, u32[]{:S(2)}, u32[]{:S(2)}) collective-permute-start(bf16[112,1152]{1,0:T(8,128)(2,1)S(1)} %fusion.252), channel_id=1, source_target_pairs={{0,2},{1,3},{2,0},{3,1},{4,5},{5,4},{6,7},{7,6},{8,10},{9,11},{10,... | collective-permute-start | bytes 774152 | tf_op jit(solution)/shard_map/ppermute | solution.py:90
  23.5 14.4 %collective-permute-start.1 = (bf16[2,112,1152]{2,1,0:T(8,128)(2,1)S(1)}, bf16[2,112,1152]{2,1,0:T(8,128)(2,1)S(1)}, u32[]{:S(2)}, u32[]{:S(2)}) collective-permute-start(bf16[2,112,1152]{2,1,0:T(8,128)(2,1)S(1)} %pad_maximum_fusion.20), channel_id=1, source_target_pairs={{0,1},{1,0},{2,3},{3,2},{4,6},{5,7},{6,4},{7,5},{8,9},{9,8},{10,11... | collective-permute-start | bytes 1548296 | tf_op jit(solution)/shard_map/ppermute | solution.py:90
  39.8 11.9 %collective-permute-start.3 = (bf16[3,112,1152]{2,1,0:T(8,128)(2,1)S(1)}, bf16[3,112,1152]{2,1,0:T(8,128)(2,1)S(1)}, u32[]{:S(2)}, u32[]{:S(2)}) collective-permute-start(bf16[3,112,1152]{2,1,0:T(8,128)(2,1)S(1)} %pad_maximum_fusion.16), channel_id=1, source_target_pairs={{0,8},{4,20},{8,0},{12,28},{16,24},{20,4},{24,16},{28,12},{1,9},{5... | collective-permute-start | bytes 2322440 | tf_op jit(solution)/shard_map/ppermute | solution.py:79
  56.2 16.1 %collective-permute-start.5 = (bf16[2,3,112,1152]{3,2,1,0:T(8,128)(2,1)S(1)}, bf16[2,3,112,1152]{3,2,1,0:T(8,128)(2,1)S(1)}, u32[]{:S(2)}, u32[]{:S(2)}) collective-permute-start(bf16[2,3,112,1152]{3,2,1,0:T(8,128)(2,1)S(1)} %pad_maximum_fusion.7.refs_0_), channel_id=1, source_target_pairs={{0,4},{4,0},{8,12},{12,8},{16,20},{20,16},{24,28},{28,24},{1,5},{5... | collective-permute-start | bytes 4644872 | tf_op jit(solution)/shard_map/ppermute | solution.py:42
  56.2 20.3 %collective-permute-start.4 = (bf16[2,3,112,1152]{3,2,1,0:T(8,128)(2,1)S(1)}, bf16[2,3,112,1152]{3,2,1,0:T(8,128)(2,1)}, u32[]{:S(2)}, u32[]{:S(2)}) collective-permute-start(bf16[2,3,112,1152]{3,2,1,0:T(8,128)(2,1)S(1)} %pad_maximum_fusion.7.refs_0_), channel_id=1, source_target_pairs={{0,16},{4,12},{8,24},{12,4},{16,0},{20,28},{24,8},{28,20},{1,17},{... | collective-permute-start | bytes 4644872 | tf_op jit(solution)/shard_map/ppermute | solution.py:79
  57.7 14.3 %collective-permute-start.6 = (bf16[2,112,1152]{2,1,0:T(8,128)(2,1)S(1)}, bf16[2,112,1152]{2,1,0:T(8,128)(2,1)S(1)}, u32[]{:S(2)}, u32[]{:S(2)}) collective-permute-start(bf16[2,112,1152]{2,1,0:T(8,128)(2,1)S(1)} %pad_maximum_fusion.21), channel_id=1, source_target_pairs={{0,1},{1,0},{2,3},{3,2},{4,6},{5,7},{6,4},{7,5},{8,9},{9,8},{10,11... | collective-permute-start | bytes 1548296 | tf_op jit(solution)/shard_map/ppermute | solution.py:90
  59.2 13.0 %collective-permute-start.7 = (bf16[40,1152]{1,0:T(8,128)(2,1)S(1)}, bf16[40,1152]{1,0:T(8,128)(2,1)S(1)}, u32[]{:S(2)}, u32[]{:S(2)}) collective-permute-start(bf16[40,1152]{1,0:T(8,128)(2,1)S(1)} %fusion.251), channel_id=1, source_target_pairs={{0,2},{1,3},{2,0},{3,1},{4,6},{5,7},{6,4},{7,5},{8,10},{9,11},{10,... | collective-permute-start | bytes 276488 | tf_op jit(solution)/shard_map/ppermute | solution.py:42
  80.3 12.8 %collective-permute-start.9 = (bf16[3,112,1152]{2,1,0:T(8,128)(2,1)S(1)}, bf16[3,112,1152]{2,1,0:T(8,128)(2,1)}, u32[]{:S(2)}, u32[]{:S(2)}) collective-permute-start(bf16[3,112,1152]{2,1,0:T(8,128)(2,1)S(1)} %pad_maximum_fusion.17), channel_id=1, source_target_pairs={{0,8},{4,20},{8,0},{12,28},{16,24},{20,4},{24,16},{28,12},{1,9},{5... | collective-permute-start | bytes 2322440 | tf_op jit(solution)/shard_map/ppermute | solution.py:79
  82.8 12.8 %collective-permute-start.10 = (bf16[2,40,1152]{2,1,0:T(8,128)(2,1)S(1)}, bf16[2,40,1152]{2,1,0:T(8,128)(2,1)S(1)}, u32[]{:S(2)}, u32[]{:S(2)}) collective-permute-start(bf16[2,40,1152]{2,1,0:T(8,128)(2,1)S(1)} %pad_maximum_fusion.30), channel_id=1, source_target_pairs={{0,1},{1,0},{2,3},{3,2},{4,5},{5,4},{6,7},{7,6},{8,9},{9,8},{10,11... | collective-permute-start | bytes 552968 | tf_op jit(solution)/shard_map/ppermute | solution.py:42
  82.9 27.8 %collective-permute-start.12 = (bf16[288,1152]{1,0:T(8,128)(2,1)}, bf16[288,1152]{1,0:T(8,128)(2,1)}, u32[]{:S(2)}, u32[]{:S(2)}) collective-permute-start(bf16[288,1152]{1,0:T(8,128)(2,1)} %bitcast.31), channel_id=1, source_target_pairs={{0,2},{1,3},{2,0},{3,1},{4,5},{5,4},{6,7},{7,6},{8,10},{9,11},{10,... | collective-permute-start | bytes 1990664 | tf_op jit(solution)/shard_map/ppermute | solution.py:90
  95.6 24.5 %collective-permute-start.15 = (bf16[2,3,112,1152]{3,2,1,0:T(8,128)(2,1)}, bf16[2,3,112,1152]{3,2,1,0:T(8,128)(2,1)}, u32[]{:S(2)}, u32[]{:S(2)}) collective-permute-start(bf16[2,3,112,1152]{3,2,1,0:T(8,128)(2,1)} %pad_maximum_fusion.8.refs_0_), channel_id=1, source_target_pairs={{0,4},{4,0},{8,12},{12,8},{16,20},{20,16},{24,28},{28,24},{1,5},{5... | collective-permute-start | bytes 4644872 | tf_op jit(solution)/shard_map/ppermute | solution.py:42
  95.8 24.3 %collective-permute-start.14 = (bf16[2,3,112,1152]{3,2,1,0:T(8,128)(2,1)}, bf16[2,3,112,1152]{3,2,1,0:T(8,128)(2,1)}, u32[]{:S(2)}, u32[]{:S(2)}) collective-permute-start(bf16[2,3,112,1152]{3,2,1,0:T(8,128)(2,1)} %pad_maximum_fusion.8.refs_0_), channel_id=1, source_target_pairs={{0,16},{4,12},{8,24},{12,4},{16,0},{20,28},{24,8},{28,20},{1,17},{... | collective-permute-start | bytes 4644872 | tf_op jit(solution)/shard_map/ppermute | solution.py:79
  98.0 12.7 %collective-permute-start.11 = (bf16[4,40,1152]{2,1,0:T(8,128)(2,1)}, bf16[4,40,1152]{2,1,0:T(8,128)(2,1)S(1)}, u32[]{:S(2)}, u32[]{:S(2)}) collective-permute-start(bf16[4,40,1152]{2,1,0:T(8,128)(2,1)} %pad_maximum_fusion.24), channel_id=1, source_target_pairs={{0,4},{4,0},{8,12},{12,8},{16,20},{20,16},{24,28},{28,24},{1,5},{5... | collective-permute-start | bytes 1105928 | tf_op jit(solution)/shard_map/ppermute | solution.py:42
  120.1 25.1 %collective-permute-start.18 = (bf16[2,3,112,1152]{3,2,1,0:T(8,128)(2,1)}, bf16[2,3,112,1152]{3,2,1,0:T(8,128)(2,1)}, u32[]{:S(2)}, u32[]{:S(2)}) collective-permute-start(bf16[2,3,112,1152]{3,2,1,0:T(8,128)(2,1)} %collective-permute-done.14.refs_1_), channel_id=1, source_target_pairs={{0,4},{4,0},{8,12},{12,8},{16,20},{20,16},{24,28},{28,24},{1,5},{5... | collective-permute-start | bytes 4644872 | tf_op jit(solution)/shard_map/ppermute | solution.py:42
  120.2 20.4 %collective-permute-start.16 = (bf16[3,40,1152]{2,1,0:T(8,128)(2,1)S(1)}, bf16[3,40,1152]{2,1,0:T(8,128)(2,1)S(1)}, u32[]{:S(2)}, u32[]{:S(2)}) collective-permute-start(bf16[3,40,1152]{2,1,0:T(8,128)(2,1)S(1)} %add_convert_fusion.10), channel_id=1, source_target_pairs={{0,2},{1,3},{2,0},{3,1},{4,6},{5,7},{6,4},{7,5},{8,10},{9,11},{10,... | collective-permute-start | bytes 829448 | tf_op jit(solution)/shard_map/ppermute | solution.py:42
  122.1 23.2 %collective-permute-start.17 = (bf16[348,288]{0,1:T(8,128)(2,1)S(1)}, bf16[348,288]{0,1:T(8,128)(2,1)S(1)}, u32[]{:S(2)}, u32[]{:S(2)}) collective-permute-start(bf16[348,288]{0,1:T(8,128)(2,1)S(1)} %pad_maximum_fusion.29), channel_id=1, source_target_pairs={{0,2},{1,3},{2,0},{3,1},{4,6},{5,7},{6,4},{7,5},{8,10},{9,11},{10,... | collective-permute-start | bytes 601352 | tf_op jit(solution)/shard_map/ppermute | solution.py:42
  145.3 25.3 %collective-permute-start.20 = (bf16[40,1152]{1,0:T(8,128)(2,1)S(1)}, bf16[40,1152]{1,0:T(8,128)(2,1)S(1)}, u32[]{:S(2)}, u32[]{:S(2)}) collective-permute-start(bf16[40,1152]{1,0:T(8,128)(2,1)S(1)} %get-tuple-element.577), channel_id=1, source_target_pairs={{4,0},{8,4},{12,8},{16,12},{20,16},{24,20},{28,24},{5,1},{9,5},{13... | collective-permute-start | bytes 276488 | tf_op jit(solution)/shard_map/ppermute | solution.py:1030
  146.6 24.0 %collective-permute-start.19 = (bf16[40,1152]{1,0:T(8,128)(2,1)S(1)}, bf16[40,1152]{1,0:T(8,128)(2,1)S(1)}, u32[]{:S(2)}, u32[]{:S(2)}) collective-permute-start(bf16[40,1152]{1,0:T(8,128)(2,1)S(1)} %get-tuple-element.578), channel_id=1, source_target_pairs={{0,4},{4,8},{8,12},{12,16},{16,20},{20,24},{24,28},{1,5},{5,9},{9,... | collective-permute-start | bytes 276488 | tf_op jit(solution)/shard_map/ppermute | solution.py:1029
  150.5 24.6 %collective-permute-start.21 = (bf16[2,348,288]{1,2,0:T(8,128)(2,1)}, bf16[2,348,288]{1,2,0:T(8,128)(2,1)S(1)}, u32[]{:S(2)}, u32[]{:S(2)}) collective-permute-start(bf16[2,348,288]{1,2,0:T(8,128)(2,1)} %pad_maximum_fusion.22), channel_id=1, source_target_pairs={{0,1},{1,0},{2,3},{3,2},{4,5},{5,4},{6,7},{7,6},{8,9},{9,8},{10,11... | collective-permute-start | bytes 1202696 | tf_op jit(solution)/shard_map/ppermute | solution.py:42
  153.0 39.3 %collective-permute-start.22 = (bf16[2,288,1152]{2,1,0:T(8,128)(2,1)}, bf16[2,288,1152]{2,1,0:T(8,128)(2,1)}, u32[]{:S(2)}, u32[]{:S(2)}) collective-permute-start(bf16[2,288,1152]{2,1,0:T(8,128)(2,1)} %pad_maximum_fusion.10), channel_id=1, source_target_pairs={{0,1},{1,0},{2,3},{3,2},{4,6},{5,7},{6,4},{7,5},{8,9},{9,8},{10,11... | collective-permute-start | bytes 3981320 | tf_op jit(solution)/shard_map/ppermute | solution.py:90
  178.0 18.3 %collective-permute-start.23 = (bf16[4,348,288]{1,2,0:T(8,128)(2,1)}, bf16[4,348,288]{1,2,0:T(8,128)(2,1)}, u32[]{:S(2)}, u32[]{:S(2)}) collective-permute-start(bf16[4,348,288]{1,2,0:T(8,128)(2,1)} %pad_maximum_fusion.15), channel_id=1, source_target_pairs={{0,4},{4,0},{8,12},{12,8},{16,20},{20,16},{24,28},{28,24},{1,5},{5... | collective-permute-start | bytes 2405384 | tf_op jit(solution)/shard_map/ppermute | solution.py:42
  196.3 25.2 %collective-permute-start.24 = (bf16[3,288,1152]{2,1,0:T(8,128)(2,1)}, bf16[3,288,1152]{2,1,0:T(8,128)(2,1)}, u32[]{:S(2)}, u32[]{:S(2)}) collective-permute-start(bf16[3,288,1152]{2,1,0:T(8,128)(2,1)} %pad_maximum_fusion.6), channel_id=1, source_target_pairs={{0,8},{4,20},{8,0},{12,28},{16,24},{20,4},{24,16},{28,12},{1,9},{5... | collective-permute-start | bytes 5971976 | tf_op jit(solution)/shard_map/ppermute | solution.py:79
  226.0 36.9 %collective-permute-start.26 = (bf16[2,3,288,1152]{3,2,1,0:T(8,128)(2,1)}, bf16[2,3,288,1152]{3,2,1,0:T(8,128)(2,1)}, u32[]{:S(2)}, u32[]{:S(2)}) collective-permute-start(bf16[2,3,288,1152]{3,2,1,0:T(8,128)(2,1)} %pad_maximum_fusion.2.refs_1_), channel_id=1, source_target_pairs={{0,4},{4,0},{8,12},{12,8},{16,20},{20,16},{24,28},{28,24},{1,5},{5... | collective-permute-start | bytes 11943944 | tf_op jit(solution)/shard_map/ppermute | solution.py:42
  226.0 46.5 %collective-permute-start.25 = (bf16[2,3,288,1152]{3,2,1,0:T(8,128)(2,1)}, bf16[2,3,288,1152]{3,2,1,0:T(8,128)(2,1)}, u32[]{:S(2)}, u32[]{:S(2)}) collective-permute-start(bf16[2,3,288,1152]{3,2,1,0:T(8,128)(2,1)} %pad_maximum_fusion.2.refs_1_), channel_id=1, source_target_pairs={{0,16},{4,12},{8,24},{12,4},{16,0},{20,28},{24,8},{28,20},{1,17},{... | collective-permute-start | bytes 11943944 | tf_op jit(solution)/shard_map/ppermute | solution.py:79
  272.5 16.6 %collective-permute-start.29 = (bf16[2,3,288,1152]{3,2,1,0:T(8,128)(2,1)}, bf16[2,3,288,1152]{3,2,1,0:T(8,128)(2,1)}, u32[]{:S(2)}, u32[]{:S(2)}) collective-permute-start(bf16[2,3,288,1152]{3,2,1,0:T(8,128)(2,1)} %collective-permute-done.25.refs_2_), channel_id=1, source_target_pairs={{0,4},{4,0},{8,12},{12,8},{16,20},{20,16},{24,28},{28,24},{1,5},{5... | collective-permute-start | bytes 11943944 | tf_op jit(solution)/shard_map/ppermute | solution.py:42
  272.7 12.1 %collective-permute-start.28 = (bf16[144,1152]{1,0:T(8,128)(2,1)S(1)}, bf16[144,1152]{1,0:T(8,128)(2,1)S(1)}, u32[]{:S(2)}, u32[]{:S(2)}) collective-permute-start(bf16[144,1152]{1,0:T(8,128)(2,1)S(1)} %pad_maximum_fusion.26), channel_id=1, source_target_pairs={{1,0},{2,1},{3,2},{4,3},{5,4},{6,5},{7,6},{8,7},{9,8},{10,9},{11,1... | collective-permute-start | bytes 995336 | tf_op jit(solution)/shard_map/ppermute | solution.py:48
  274.0 12.8 %collective-permute-start.27 = (bf16[144,1152]{1,0:T(8,128)(2,1)S(1)}, bf16[144,1152]{1,0:T(8,128)(2,1)S(1)}, u32[]{:S(2)}, u32[]{:S(2)}) collective-permute-start(bf16[144,1152]{1,0:T(8,128)(2,1)S(1)} %pad_maximum_fusion.25), channel_id=1, source_target_pairs={{0,1},{1,2},{2,3},{3,4},{4,5},{5,6},{6,7},{7,8},{8,9},{9,10},{10,1... | collective-permute-start | bytes 995336 | tf_op jit(solution)/shard_map/ppermute | solution.py:48
  316.4 32.7 %collective-permute-start.30 = (bf16[2,3,384,1152]{3,2,1,0:T(8,128)(2,1)}, bf16[2,3,384,1152]{3,2,1,0:T(8,128)(2,1)}, u32[]{:S(2)}, u32[]{:S(2)}) collective-permute-start(bf16[2,3,384,1152]{3,2,1,0:T(8,128)(2,1)} %get-tuple-element.247), channel_id=1, source_target_pairs={{0,4},{4,0},{8,12},{12,8},{16,20},{20,16},{24,28},{28,24},{1,5},{5... | collective-permute-start | bytes 15925256 | tf_op jit(solution)/shard_map/ppermute | solution.py:42
  349.1 30.0 %collective-permute-start.31 = (bf16[2,3,384,1152]{3,2,1,0:T(8,128)(2,1)}, bf16[2,3,384,1152]{3,2,1,0:T(8,128)(2,1)}, u32[]{:S(2)}, u32[]{:S(2)}) collective-permute-start(bf16[2,3,384,1152]{3,2,1,0:T(8,128)(2,1)} %get-tuple-element.253), channel_id=1, source_target_pairs={{0,4},{4,0},{8,12},{12,8},{16,20},{20,16},{24,28},{28,24},{1,5},{5... | collective-permute-start | bytes 15925256 | tf_op jit(solution)/shard_map/ppermute | solution.py:42
  379.1 60.8 %collective-permute-start.32 = (bf16[2,3,384,1152]{3,2,1,0:T(8,128)(2,1)}, bf16[2,3,384,1152]{3,2,1,0:T(8,128)(2,1)}, u32[]{:S(2)}, u32[]{:S(2)}) collective-permute-start(bf16[2,3,384,1152]{3,2,1,0:T(8,128)(2,1)} %get-tuple-element.271), channel_id=1, source_target_pairs={{0,8},{4,20},{8,0},{12,28},{16,24},{20,4},{24,16},{28,12},{1,9},{5... | collective-permute-start | bytes 15925256 | tf_op jit(solution)/shard_map/ppermute | solution.py:79
  443.9 33.0 %collective-permute-start.33 = (bf16[3,2,2,96,1152]{4,3,0,1,2:T(8,128)(2,1)}, bf16[3,2,2,96,1152]{4,3,0,1,2:T(8,128)(2,1)}, u32[]{:S(2)}, u32[]{:S(2)}) collective-permute-start(bf16[3,2,2,96,1152]{4,3,0,1,2:T(8,128)(2,1)} %fusion.1), channel_id=1, source_target_pairs={{0,16},{4,12},{8,24},{12,4},{16,0},{20,28},{24,8},{28,20},{1,17},{... | collective-permute-start | bytes 7962632 | tf_op jit(solution)/shard_map/ppermute | solution.py:79
  480.6 31.2 %collective-permute-start.34 = (bf16[3,2,96,1152]{3,2,0,1:T(8,128)(2,1)}, bf16[3,2,96,1152]{3,2,0,1:T(8,128)(2,1)}, u32[]{:S(2)}, u32[]{:S(2)}) collective-permute-start(bf16[3,2,96,1152]{3,2,0,1:T(8,128)(2,1)} %fusion.49), channel_id=1, source_target_pairs={{0,1},{1,0},{2,3},{3,2},{4,6},{5,7},{6,4},{7,5},{8,9},{9,8},{10,11... | collective-permute-start | bytes 3981320 | tf_op jit(solution)/shard_map/ppermute | solution.py:90
  519.5 17.5 %collective-permute-start.36 = (bf16[3,40,1152]{2,1,0:T(8,128)(2,1)S(1)}, bf16[3,40,1152]{2,1,0:T(8,128)(2,1)S(1)}, u32[]{:S(2)}, u32[]{:S(2)}) collective-permute-start(bf16[3,40,1152]{2,1,0:T(8,128)(2,1)S(1)} %add_convert_fusion.8), channel_id=1, source_target_pairs={{0,2},{1,3},{2,0},{3,1},{4,6},{5,7},{6,4},{7,5},{8,10},{9,11},{10,... | collective-permute-start | bytes 829448 | tf_op jit(solution)/shard_map/ppermute | solution.py:42
  537.0 18.1 %collective-permute-start.39 = (bf16[4,4,144,1152]{3,2,1,0:T(8,128)(2,1)}, bf16[4,4,144,1152]{3,2,1,0:T(8,128)(2,1)}, u32[]{:S(2)}, u32[]{:S(2)}) collective-permute-start(bf16[4,4,144,1152]{3,2,1,0:T(8,128)(2,1)} %get-tuple-element.299), channel_id=1, source_target_pairs={{0,4},{4,0},{8,12},{12,8},{16,20},{20,16},{24,28},{28,24},{1,5},{5... | collective-permute-start | bytes 15925256 | tf_op jit(solution)/shard_map/ppermute | solution.py:42
  559.2 41.5 %collective-permute-start.40 = (bf16[2,2,2,144,1152]{4,3,2,1,0:T(8,128)(2,1)}, bf16[2,2,2,144,1152]{4,3,2,1,0:T(8,128)(2,1)}, u32[]{:S(2)}, u32[]{:S(2)}) collective-permute-start(bf16[2,2,2,144,1152]{4,3,2,1,0:T(8,128)(2,1)} %fusion), channel_id=1, source_target_pairs={{0,8},{4,20},{8,0},{12,28},{16,24},{20,4},{24,16},{28,12},{1,9},{5... | collective-permute-start | bytes 7962632 | tf_op jit(solution)/shard_map/ppermute | solution.py:79
  565.3 35.4 %collective-permute-start.41 = (bf16[3,96,1152]{2,1,0:T(8,128)(2,1)}, bf16[3,96,1152]{2,1,0:T(8,128)(2,1)}, u32[]{:S(2)}, u32[]{:S(2)}) collective-permute-start(bf16[3,96,1152]{2,1,0:T(8,128)(2,1)} %fusion.58), channel_id=1, source_target_pairs={{0,2},{1,3},{2,0},{3,1},{4,5},{5,4},{6,7},{7,6},{8,10},{9,11},{10,... | collective-permute-start | bytes 1990664 | tf_op jit(solution)/shard_map/ppermute | solution.py:90
  600.7 23.5 %collective-permute-start.42 = (bf16[4,4,128,1152]{3,2,1,0:T(8,128)(2,1)}, bf16[4,4,128,1152]{3,2,1,0:T(8,128)(2,1)}, u32[]{:S(2)}, u32[]{:S(2)}) collective-permute-start(bf16[4,4,128,1152]{3,2,1,0:T(8,128)(2,1)} %get-tuple-element.317), channel_id=1, source_target_pairs={{0,4},{4,0},{8,12},{12,8},{16,20},{20,16},{24,28},{28,24},{1,5},{5... | collective-permute-start | bytes 14155784 | tf_op jit(solution)/shard_map/ppermute | solution.py:42
  606.3 17.8 %collective-permute-start.43 = (bf16[2,2,144,1152]{3,2,1,0:T(8,128)(2,1)S(1)}, bf16[2,2,144,1152]{3,2,1,0:T(8,128)(2,1)S(1)}, u32[]{:S(2)}, u32[]{:S(2)}) collective-permute-start(bf16[2,2,144,1152]{3,2,1,0:T(8,128)(2,1)S(1)} %fusion.13), channel_id=1, source_target_pairs={{0,16},{4,12},{8,24},{12,4},{16,0},{20,28},{24,8},{28,20},{1,17},{... | collective-permute-start | bytes 3981320 | tf_op jit(solution)/shard_map/ppermute | solution.py:79
  626.4 28.9 %collective-permute-start.44 = (bf16[2,2,2,128,1152]{4,3,2,1,0:T(8,128)(2,1)S(1)}, bf16[2,2,2,128,1152]{4,3,2,1,0:T(8,128)(2,1)S(1)}, u32[]{:S(2)}, u32[]{:S(2)}) collective-permute-start(bf16[2,2,2,128,1152]{4,3,2,1,0:T(8,128)(2,1)S(1)} %fusion.2), channel_id=1, source_target_pairs={{0,8},{4,20},{8,0},{12,28},{16,24},{20,4},{24,16},{28,12},{1,9},{5... | collective-permute-start | bytes 7077896 | tf_op jit(solution)/shard_map/ppermute | solution.py:79
  631.1 16.5 %collective-permute-start.45 = (bf16[2,144,1152]{2,1,0:T(8,128)(2,1)S(1)}, bf16[2,144,1152]{2,1,0:T(8,128)(2,1)S(1)}, u32[]{:S(2)}, u32[]{:S(2)}) collective-permute-start(bf16[2,144,1152]{2,1,0:T(8,128)(2,1)S(1)} %fusion.59), channel_id=1, source_target_pairs={{0,1},{1,0},{2,3},{3,2},{4,6},{5,7},{6,4},{7,5},{8,9},{9,8},{10,11... | collective-permute-start | bytes 1990664 | tf_op jit(solution)/shard_map/ppermute | solution.py:90
  657.1 16.3 %collective-permute-start.46 = (bf16[2,2,128,1152]{3,2,1,0:T(8,128)(2,1)S(1)}, bf16[2,2,128,1152]{3,2,1,0:T(8,128)(2,1)S(1)}, u32[]{:S(2)}, u32[]{:S(2)}) collective-permute-start(bf16[2,2,128,1152]{3,2,1,0:T(8,128)(2,1)S(1)} %fusion.16), channel_id=1, source_target_pairs={{0,16},{4,12},{8,24},{12,4},{16,0},{20,28},{24,8},{28,20},{1,17},{... | collective-permute-start | bytes 3538952 | tf_op jit(solution)/shard_map/ppermute | solution.py:79
  660.3 11.6 %collective-permute-start.47 = (bf16[144,1152]{1,0:T(8,128)(2,1)S(1)}, bf16[144,1152]{1,0:T(8,128)(2,1)S(1)}, u32[]{:S(2)}, u32[]{:S(2)}) collective-permute-start(bf16[144,1152]{1,0:T(8,128)(2,1)S(1)} %fusion.62), channel_id=1, source_target_pairs={{0,2},{1,3},{2,0},{3,1},{4,5},{5,4},{6,7},{7,6},{8,10},{9,11},{10,... | collective-permute-start | bytes 995336 | tf_op jit(solution)/shard_map/ppermute | solution.py:90
  675.3 15.7 %collective-permute-start.48 = (bf16[2,128,1152]{2,1,0:T(8,128)(2,1)S(1)}, bf16[2,128,1152]{2,1,0:T(8,128)(2,1)S(1)}, u32[]{:S(2)}, u32[]{:S(2)}) collective-permute-start(bf16[2,128,1152]{2,1,0:T(8,128)(2,1)S(1)} %fusion.63), channel_id=1, source_target_pairs={{0,1},{1,0},{2,3},{3,2},{4,6},{5,7},{6,4},{7,5},{8,9},{9,8},{10,11... | collective-permute-start | bytes 1769480 | tf_op jit(solution)/shard_map/ppermute | solution.py:90
  695.4 23.7 %collective-permute-start.55 = (bf16[2,3,96,1152]{3,2,1,0:T(8,128)(2,1)S(1)}, bf16[2,3,96,1152]{3,2,1,0:T(8,128)(2,1)S(1)}, u32[]{:S(2)}, u32[]{:S(2)}) collective-permute-start(bf16[2,3,96,1152]{3,2,1,0:T(8,128)(2,1)S(1)} %pad_maximum_fusion.11), channel_id=1, source_target_pairs={{0,16},{4,12},{8,24},{12,4},{16,0},{20,28},{24,8},{28,20},{1,17},{... | collective-permute-start | bytes 3981320 | tf_op jit(solution)/shard_map/ppermute | solution.py:79
  707.4 13.6 %collective-permute-start.54 = (bf16[2,2,144,1152]{3,2,0,1:T(8,128)(2,1)S(1)}, bf16[2,2,144,1152]{3,2,0,1:T(8,128)(2,1)S(1)}, u32[]{:S(2)}, u32[]{:S(2)}) collective-permute-start(bf16[2,2,144,1152]{3,2,0,1:T(8,128)(2,1)S(1)} %pad_maximum_fusion.12), channel_id=1, source_target_pairs={{0,4},{4,0},{8,12},{12,8},{16,20},{20,16},{24,28},{28,24},{1,5},{5... | collective-permute-start | bytes 3981320 | tf_op jit(solution)/shard_map/ppermute | solution.py:42
  723.7 27.1 %collective-permute-start.56 = (bf16[2,128,1152]{2,1,0:T(8,128)(2,1)}, bf16[2,128,1152]{2,1,0:T(8,128)(2,1)}, u32[]{:S(2)}, u32[]{:S(2)}) collective-permute-start(bf16[2,128,1152]{2,1,0:T(8,128)(2,1)} %pad_maximum_fusion.19), channel_id=1, source_target_pairs={{0,16},{4,12},{8,24},{12,4},{16,0},{20,28},{24,8},{28,20},{1,17},{... | collective-permute-start | bytes 1769480 | tf_op jit(solution)/shard_map/ppermute | solution.py:79
  734.1 18.2 %collective-permute-start.57 = (bf16[2,2,3,96,1152]{4,3,2,0,1:T(8,128)(2,1)S(1)}, bf16[2,2,3,96,1152]{4,3,2,0,1:T(8,128)(2,1)S(1)}, u32[]{:S(2)}, u32[]{:S(2)}) collective-permute-start(bf16[2,2,3,96,1152]{4,3,2,0,1:T(8,128)(2,1)S(1)} %copy-done.4), channel_id=1, source_target_pairs={{0,4},{4,0},{8,12},{12,8},{16,20},{20,16},{24,28},{28,24},{1,5},{5... | collective-permute-start | bytes 7962632 | tf_op jit(solution)/shard_map/ppermute | solution.py:42
  737.2 12.9 %collective-permute-start.60 = (bf16[75,1152]{1,0:T(8,128)(2,1)S(1)}, bf16[75,1152]{1,0:T(8,128)(2,1)S(1)}, u32[]{:S(2)}, u32[]{:S(2)}) collective-permute-start(bf16[75,1152]{1,0:T(8,128)(2,1)S(1)} %dynamic-slice_bitcast_fusion.2), channel_id=1, source_target_pairs={{0,2},{1,3},{2,0},{3,1},{4,6},{5,7},{6,4},{7,5},{8,10},{9,11},{10,... | collective-permute-start | bytes 518408 | tf_op jit(solution)/shard_map/ppermute | solution.py:42
  (133 other events, 1603.6 us)

commit v4 on v3

--- a/solution.py
+++ b/solution.py
@@ -168,13 +168,11 @@
     return values
 
 
-def reduce_z(values):
-    for bit, place in ((1, 1), (2, 0)):
-        own = bit_set("tensor", bit)
-        keep = lax.dynamic_index_in_dim(values, own, place, keepdims=False)
-        send = lax.dynamic_index_in_dim(values, 1 - own, place, keepdims=False)
-        values = total([keep, swap(send, "tensor", bit)])
-    return values
+def reduce_z(values, bit, place):
+    own = bit_set("tensor", bit)
+    keep = lax.dynamic_index_in_dim(values, own, place, keepdims=False)
+    send = lax.dynamic_index_in_dim(values, 1 - own, place, keepdims=False)
+    return total([keep, swap(send, "tensor", bit)])
 
 
 def halve_path(terms, number, place):
@@ -941,7 +939,7 @@
     far_1 = swap_z(piece_1, 0)
     far_1, normed = tie(far_1, normed)
     wave_1 = near_z(piece_1, far_1)
-    wave_1, rows_ffn, item_bucket, piece_2 = tie(wave_1, rows_ffn, item_bucket, piece_2)
+    wave_1, item_bucket, piece_2 = tie(wave_1, item_bucket, piece_2)
     far_2 = swap_z(piece_2, 0)
     wave_1 = turn(wave_1, 0)
     inner = own_slots % ITEM_SLOTS
@@ -952,7 +950,7 @@
     reach = shift_blocks(tall_slots, total_rows, item_bucket, 1, tall)
     reach = reach.reshape(9, tall // BLOCK, BLOCK, -1).transpose(1, 0, 2, 3)
     reach = reach.reshape(tall // BLOCK, 9 * BLOCK, -1)
-    far_2, wave_1, reach, text_tokens = tie(far_2, wave_1, reach, text_tokens)
+    wave_1, reach, text_tokens = tie(wave_1, reach, text_tokens)
     wave_1 = mid_turns(wave_1)
     last_1 = last_turn(wave_1)
     core_1 = swap(wave_1, "dp", 1)
@@ -972,8 +970,8 @@
     rest = max(rest, 32)
     back_last = back[:, own_pad - rest :, : rest + 2 * REACH].reshape(9 * rest, -1)
     d_ffn = (grad_out * live * gate_f).astype(bfloat)
-    wave_1, last_1, core_1, wave_2, back_full, back_last, d_ffn, text_far = tie(
-        wave_1, last_1, core_1, wave_2, back_full, back_last, d_ffn, text_far
+    wave_1, last_1, core_1, wave_2, back_full, back_last, d_ffn, text_far, rows_ffn = tie(
+        wave_1, last_1, core_1, wave_2, back_full, back_last, d_ffn, text_far, rows_ffn
     )
     core_last_1 = swap(last_1, "dp", 1)
     piece_3 = lax.dynamic_slice_in_dim(rows_ffn, me_d * ffn_piece, ffn_piece, 1)
@@ -1052,7 +1050,7 @@
 
     table = item_table(table_1, table_2)
     table, text_other, far_3 = tie(table, text_other, far_3)
-    table = total([table, swap(table, "tensor", 1)])
+    table = total([table, swap_z(table, 0)])
     text_rel = by_core(text_rel, text_other).swapaxes(0, 1).reshape(group, -1, width)
     text_all = jnp.concatenate(in_order(text_rel[:, :text_rows_here]))
     text_kv = jnp.einsum("td,dke->tke", text_all, w_xkv, preferred_element_type=single)
@@ -1061,7 +1059,7 @@
         [lax.dynamic_index_in_dim(xkv_own, me_d % 2, 0, keepdims=False), small_half], axis=0
     )
     table, both_half, last_2, core_2 = tie(table, both_half, last_2, core_2)
-    table = total([table, swap(table, "tensor", 2)])
+    table = total([table, swap_z(table, 1)])
     both_far = swap(both_half, "tensor", 2)
     core_last_2 = swap(last_2, "dp", 1)
     table, both_far, core_last_2, far_3 = tie(table, both_far, core_last_2, far_3)
@@ -1258,12 +1256,12 @@
         )
 
     d_table, mix_extra, ffn_terms[-1] = tie(d_table, mix_extra, ffn_terms[-1])
-    d_table = total([d_table, swap(d_table, "tensor", 1)])
+    d_table = total([d_table, swap_z(d_table, 0)])
     mod_sums = [
         mod_sum(rows) for rows in (d_gate_a, d_normed_ffn, d_normed_ffn * normal_f, d_gate_f)
     ]
     d_table, d_out_bias, d_xo_bias, *mod_sums = tie(d_table, d_out_bias, d_xo_bias, *mod_sums)
-    d_table = total([d_table, swap(d_table, "tensor", 2)])
+    d_table = total([d_table, swap_z(d_table, 1)])
     mix_grads = grads_call(mix_arrays, ((0, 1), (2, 3), (4, 5)), mix_extra, mix_rows, cols)
     d_table, mix_grads[1] = tie(d_table, mix_grads[1])
     mix_terms = core_terms(*mix_grads)
@@ -1294,6 +1292,9 @@
     rows_all = pad_rows(rows_all.astype(bfloat), spare)
     rows_all = jnp.broadcast_to(rows_all[None], (group, spare, width))
 
+    rows_all, mix_terms[-1] = tie(rows_all, mix_terms[-1])
+    for stage in range(1, len(bits)):
+        mix_terms = halve_path(mix_terms, stage, 0)
     qkv_grads = grads_call(
         [d_query_in, d_keys_in, d_values_low, normed],
         ((0, 3), (1, 3), (2, 3)),
@@ -1301,10 +1302,8 @@
         last_rows,
         cols,
     )
-    qkv_grads[1], mix_terms[-1], ffn_terms[-1] = tie(qkv_grads[1], mix_terms[-1], ffn_terms[-1])
+    qkv_grads[1], ffn_terms[-1], mix_terms[-1] = tie(qkv_grads[1], ffn_terms[-1], mix_terms[-1])
     qkv_terms = core_terms(*qkv_grads)
-    for stage in range(1, len(bits)):
-        mix_terms = halve_path(mix_terms, stage, 0)
     qkv_terms[1], mix_terms[-1] = tie(qkv_terms[1], mix_terms[-1])
     qkv_terms = halve_path(qkv_terms, 0, 0)
     mix_terms = halve_z_once(mix_terms, 1, 0)
@@ -1329,26 +1328,27 @@
     for stage in range(1, len(bits)):
         d_qkv_all = share_turn(d_qkv_all, stage)
     d_ffn_all = share_core(d_ffn_all)
-    d_qkv_all, d_ffn_all = tie(d_qkv_all, d_ffn_all)
+    d_mix_all = d_mix_all.reshape(-1, width)
+    d_kv = d_mix_all[att_rows : att_rows + text_rows]
+    d_kv = jnp.concatenate(
+        [d_kv[:, number * TXT_PAD : (number + 1) * TXT_PAD] for number in range(lanes)], axis=0
+    )
+    d_kv = d_kv.reshape(2, cols, TXT_PAD)[:, :, :TXT]
+    d_xv_bias = jnp.sum(d_kv[1].astype(single), axis=1)
+    d_w_xkv = jnp.einsum("td,ket->dke", text_all, d_kv, preferred_element_type=single)
+    d_text = jnp.einsum("ket,dke->td", d_kv, w_xkv, preferred_element_type=single)
+    d_text = reduce_z(d_text.astype(bfloat).reshape(2, 2, TXT // group, width), 1, 1)
+    d_qkv_all, d_ffn_all, d_text = tie(d_qkv_all, d_ffn_all, d_text)
     d_qkv_all = share_core(d_qkv_all)
+    d_text = reduce_z(d_text, 2, 0).astype(single)
     d_ffn_all = d_ffn_all.transpose(1, 0, 2, 3)
     d_ffn_all = d_ffn_all.reshape(3, padded_channels, width)[:, :channels]
     d_w_in = jnp.stack([d_ffn_all[0].T, d_ffn_all[1].T], axis=1).astype(single)
     d_w_pt = d_ffn_all[2].astype(single)
 
-    d_mix_all = d_mix_all.reshape(-1, width)
     d_w_out = d_mix_all[:cols].astype(single)
     d_w_xq = d_mix_all[cols : 2 * cols].T.astype(single)
     d_w_xo = d_mix_all[2 * cols : 3 * cols].astype(single)
-    d_kv = d_mix_all[att_rows : att_rows + text_rows]
-    d_kv = jnp.concatenate(
-        [d_kv[:, number * TXT_PAD : (number + 1) * TXT_PAD] for number in range(lanes)], axis=0
-    )
-    d_kv = d_kv.reshape(2, cols, TXT_PAD)[:, :, :TXT]
-    d_xv_bias = jnp.sum(d_kv[1].astype(single), axis=1)
-    d_w_xkv = jnp.einsum("td,ket->dke", text_all, d_kv, preferred_element_type=single)
-    d_text = jnp.einsum("ket,dke->td", d_kv, w_xkv, preferred_element_type=single)
-    d_text = reduce_z(d_text.astype(bfloat).reshape(2, 2, TXT // group, width)).astype(single)
     d_small = d_mix_all[att_rows + text_rows : att_rows + text_rows + small_rows].reshape(-1)
     d_small = d_small[: 22 * padded_channels].reshape(2, 11, padded_channels)[:, :, :channels]
     d_small = d_small.swapaxes(0, 1).astype(single)

time: 777 us -> 776 us (level)
  waiting for transfers between devices: 198 us -> 187 us
    ppermute x25 -> x21, waiting for transfers between devices: 44.5 us -> 16.8 us  [swap(): return lax.ppermute(values, axis, [(i, i ^ bit) for i in range(count)])]
    ppermute x12 -> x16, waiting for transfers between devices: 65.3 us -> 90.2 us  [swap_z(): return lax.ppermute(values, ('dp', 'tensor'), pairs)]
    ppermute x18, waiting for transfers between devices: 80.2 us -> 71.3 us  [swap_path(): lax.ppermute(values, 'dp', [(i, i ^ turns(i % 2)[number]) for i in range(...]
    ppermute x12 -> x16, starting transfers between devices: 17.8 us -> 21.5 us  [swap_z(): return lax.ppermute(values, ('dp', 'tensor'), pairs)]
    ppermute x25 -> x21, starting transfers between devices: 19.5 us -> 18.2 us  [swap(): return lax.ppermute(values, axis, [(i, i ^ bit) for i in range(count)])]
  transfers between devices with their start and end apart: 61 -> 61, of which waited for: 31 -> 33; matrix products, arithmetic and copies ran while one was open for 28% -> 28% of each run, Pallas kernels for 26% -> 26%
where the time goes in v4:
time: 776 us; the launch traced here: 769 us
  Pallas kernels  229 us (30%)
  waiting for transfers between devices  187 us (24%)
  other arithmetic  136 us (18%)
  local copies, waits for them, and re-layouts  110 us (14%)
  starting transfers between devices  81.7 us (11%)
  matrix products  22.9 us (3%)
    pallas_call x4, Pallas kernels, ffn_call(): pl.pallas_call(functools.partial(ffn_kernel, core if direct else None, be...  112 us
    ppermute x16, waiting for transfers between devices, swap_z(): return lax.ppermute(values, ('dp', 'tensor'), pairs)  90.2 us
    ppermute x18, waiting for transfers between devices, swap_path(): lax.ppermute(values, 'dp', [(i, i ^ turns(i % 2)[number]) for i in range(...  71.3 us
    pallas_call x4, Pallas kernels, lane_call(): pl.pallas_call(kernel, grid=(features // LANES,), in_specs=[specs[kind] f...  40.1 us
    pallas_call x2, Pallas kernels, grads_call(): pl.pallas_call(functools.partial(grads_kernel, ranks, group, rows, cols,...  26.3 us
    ppermute x18, starting transfers between devices, swap_path(): lax.ppermute(values, 'dp', [(i, i ^ turns(i % 2)[number]) for i in range(...  25.4 us
    convert_element_type x16, other arithmetic, total(): return summed.astype(bfloat)  23.4 us
    ppermute x16, starting transfers between devices, swap_z(): return lax.ppermute(values, ('dp', 'tensor'), pairs)  21.5 us
  transfers between devices with their start and end apart: 61, of which 33 were waited for; matrix products, arithmetic and copies ran while one was open for 28% of the time, Pallas kernels for 26%

profile of v4, /device:TPU:0, one launch (start us, length us, event | category | flops | bytes accessed | tf_op | source)
XLA Modules:
  0.0 769.5 jit_solution(7241406257999146687)
XLA Ops:
  3.9 4.1 collective-permute-start
  23.8 6.0 pad_maximum_fusion.refs_0_
  29.9 6.8 collective-permute-done.1
  57.2 8.5 %collective-permute-done.6 = bf16[2,112,1152]{2,1,0:T(8,128)(2,1)S(1)} collective-permute-done((bf16[2,112,1152]{2,1,0:T(8,128)(2,1)S(1)}, bf16[2,112,1152]{2,1,0:T(8,128)(2,1)S(1)}, u32[]{:S(2)}, u32[]{:S(2)}) %collective-permute-start.6) | collective-permute-done | bytes 516128 | tf_op jit(solution)/shard_map/ppermute | solution.py:90
  67.1 4.0 collective-permute-done.3.refs_1_
  81.7 7.8 %shard_map.348 = (bf16[4,288,1152]{2,1,0:T(8,128)(2,1)}, bf16[4,288,1152]{2,1,0:T(8,128)(2,1)}, bf16[4,288,1152]{2,1,0:T(8,128)(2,1)}) custom-call(bf16[8,112,1152]{2,1,0:T(8,128)(2,1)} %bitcast.554, bf16[2,3,112,1152]{3,2,1,0:T(8,128)(2,1)} %copy-done.15, bf16[2,3,112,1152]{3,2,1,0:T(8,128)(2,1)} %collective-permute-done.3.refs_1_, ...), custom_call_target="tpu_custom_call" | custom-call | bytes 4128768 | tf_op jit(solution)/shard_map/pallas_call | solution.py:255
  94.9 11.5 %shard_map.349 = (f32[416,1152]{1,0:T(8,128)}, f32[416,1152]{1,0:T(8,128)}, bf16[416,1152]{1,0:T(8,128)(2,1)}, bf16[416,1152]{1,0:T(8,128)(2,1)}, bf16[416,1152]...) custom-call(bf16[416,1152]{1,0:T(8,128)(2,1)} %fusion.27.normed.refs_3_, bf16[1152,1152]{1,0:T(8,128)(2,1)} %bitcast.541, ...), custom_call_target="tpu_custom_call" | custom-call | flops 552075264 | bytes 479232 | tf_op jit(solution)/shard_map/pallas_call | solution.py:731
  109.9 8.4 %collective-permute-done.13 = bf16[3,40,1152]{2,1,0:T(8,128)(2,1)S(1)} collective-permute-done((bf16[3,40,1152]{2,1,0:T(8,128)(2,1)S(1)}, bf16[3,40,1152]{2,1,0:T(8,128)(2,1)S(1)}, u32[]{:S(2)}, u32[]{:S(2)}) %collective-permute-start.13) | collective-permute-done | bytes 276512 | tf_op jit(solution)/shard_map/ppermute | solution.py:90
  120.9 6.7 collective-permute-done.16
  127.7 6.9 collective-permute-done.17
  135.9 4.5 collective-permute-start.19
  145.7 7.9 %shard_map.350 = (bf16[4,288,1152]{2,1,0:T(8,128)(2,1)}, bf16[4,288,1152]{2,1,0:T(8,128)(2,1)}, bf16[4,288,1152]{2,1,0:T(8,128)(2,1)}) custom-call(bf16[8,112,1152]{2,1,0:T(8,128)(2,1)} %bitcast.561, bf16[2,3,112,1152]{3,2,1,0:T(8,128)(2,1)} %pad_maximum_fusion.8.refs_0_, bf16[2,3,112,1152]{3,2,1,0:T(8,128)(2,1)} %collective-permute-done.14.refs_1_, ...), custom_call_target="tpu_custom_call" | custom-call | bytes 4128768 | tf_op jit(solution)/shard_map/pallas_call | solution.py:255
  153.7 4.8 pad.61
  170.8 7.0 shard_map.351
  202.9 5.9 add_convert_fusion.query_ref
  212.3 4.5 pad_maximum_fusion.2.refs_1_
  226.7 4.2 fusion.48
  230.9 16.6 %shard_map.352.refs_4_ = bf16[416,2048]{1,0:T(8,128)(2,1)} custom-call(bf16[416,2048]{1,0:T(8,128)(2,1)} %add_convert_fusion.query_ref, bf16[16,384,128]{2,1,0:T(8,128)(2,1)} %get-tuple-element.526.keys_ref, bf16[16,384,128]{2,1,0:T(8,128)(2,1)} %get-tuple-element.525.vals_ref, s32[416,1]{1,0:T(8,128)} %copy.254.length_ref), custom_call_target="tpu_custom_call" | custom-call | flops 327155712 | bytes 1703936 | tf_op jit(solution)/shard_map/pallas_call | solution.py:784
  247.5 6.0 fusion.240
  254.8 8.6 %collective-permute-done.25.refs_2_ = bf16[2,3,288,1152]{3,2,1,0:T(8,128)(2,1)} collective-permute-done((bf16[2,3,288,1152]{3,2,1,0:T(8,128)(2,1)}, bf16[2,3,288,1152]{3,2,1,0:T(8,128)(2,1)}, u32[]{:S(2)}, u32[]{:S(2)}) %collective-permute-start.25) | collective-permute-done | bytes 3981344 | tf_op jit(solution)/shard_map/ppermute | solution.py:79
  264.8 4.6 collective-permute-start.27
  269.4 6.2 collective-permute-done.28
  280.0 27.3 %shard_map.353 = (f32[416,1152]{1,0:T(8,128)}, f32[416,1152]{1,0:T(8,128)}, bf16[2,3,384,1152]{3,2,1,0:T(8,128)(2,1)}, f32[2,16,768]{2,1,0:T(8,128)}) custom-call(bf16[608,1152]{1,0:T(8,128)(2,1)} %pad_maximum_fusion.9.normed_ref, bf16[512,1152]{1,0:T(8,128)(2,1)} %pad_maximum_fusion.13.grad_ref, bf16[4,1152,224]{2,1,0:T(8,128)(2,1)} %bitcast.531, ...), custom_call_target="tpu_custom_call" | custom-call | flops 1755316224 | bytes 1769472 | tf_op jit(solution)/shard_map/pallas_call | solution.py:595
  307.3 5.3 collective-permute-start.30
  312.6 27.4 %shard_map.354 = (f32[416,1152]{1,0:T(8,128)}, f32[416,1152]{1,0:T(8,128)}, bf16[2,3,384,1152]{3,2,1,0:T(8,128)(2,1)}, f32[2,16,768]{2,1,0:T(8,128)}) custom-call(bf16[608,1152]{1,0:T(8,128)(2,1)} %pad_maximum_fusion.9.normed_ref, bf16[512,1152]{1,0:T(8,128)(2,1)} %pad_maximum_fusion.13.grad_ref, bf16[4,1152,224]{2,1,0:T(8,128)(2,1)} %bitcast.532, ...), custom_call_target="tpu_custom_call" | custom-call | flops 1755316224 | bytes 1769472 | tf_op jit(solution)/shard_map/pallas_call | solution.py:595
  341.3 28.6 %shard_map.355 = (f32[416,1152]{1,0:T(8,128)}, f32[416,1152]{1,0:T(8,128)}, bf16[2,3,384,1152]{3,2,1,0:T(8,128)(2,1)}, f32[2,16,768]{2,1,0:T(8,128)}) custom-call(bf16[608,1152]{1,0:T(8,128)(2,1)} %pad_maximum_fusion.9.normed_ref, bf16[512,1152]{1,0:T(8,128)(2,1)} %pad_maximum_fusion.13.grad_ref, bf16[4,1152,224]{2,1,0:T(8,128)(2,1)} %bitcast.533, ...), custom_call_target="tpu_custom_call" | custom-call | flops 1755316224 | bytes 1769472 | tf_op jit(solution)/shard_map/pallas_call | solution.py:595
  372.0 28.5 %shard_map.356 = (f32[416,1152]{1,0:T(8,128)}, f32[416,1152]{1,0:T(8,128)}, bf16[2,3,384,1152]{3,2,1,0:T(8,128)(2,1)}, f32[2,16,768]{2,1,0:T(8,128)}) custom-call(bf16[608,1152]{1,0:T(8,128)(2,1)} %pad_maximum_fusion.9.normed_ref, bf16[512,1152]{1,0:T(8,128)(2,1)} %pad_maximum_fusion.13.grad_ref, bf16[4,1152,224]{2,1,0:T(8,128)(2,1)} %bitcast.534, ...), custom_call_target="tpu_custom_call" | custom-call | flops 1755316224 | bytes 1769472 | tf_op jit(solution)/shard_map/pallas_call | solution.py:595
  400.5 6.7 select_reduce_fusion.7
  420.4 10.4 %collective-permute-done.32 = bf16[2,3,384,1152]{3,2,1,0:T(8,128)(2,1)} collective-permute-done((bf16[2,3,384,1152]{3,2,1,0:T(8,128)(2,1)}, bf16[2,3,384,1152]{3,2,1,0:T(8,128)(2,1)}, u32[]{:S(2)}, u32[]{:S(2)}) %collective-permute-start.32) | collective-permute-done | bytes 5308448 | tf_op jit(solution)/shard_map/ppermute | solution.py:79
  430.8 4.0 fusion.1
  443.2 18.2 %shard_map.357 = (bf16[416,2048]{1,0:T(8,128)(2,1)}, bf16[16,72,384]{2,1,0:T(8,128)(2,1)}, bf16[16,72,384]{2,1,0:T(8,128)(2,1)}, f32[1,2048]{1,0:T(1,128)}) custom-call(bf16[416,2048]{1,0:T(8,128)(2,1)} %add_convert_fusion.query_ref, bf16[16,384,128]{2,1,0:T(8,128)(2,1)} %get-tuple-element.526.keys_ref, bf16[16,384,128]{2,1,0:T(8,128)(2,1)} %get-tuple-element.525.vals_ref, ...), custom_call_target="tpu_custom_call" | custom-call | flops 327155712 | bytes 1703936 | tf_op jit(solution)/shard_map/pallas_call | solution.py:802
  481.6 9.2 %shard_map.358 = (bf16[416,1152]{1,0:T(8,128)(2,1)}, f32[40,1152]{1,0:T(8,128)}, f32[40,1152]{1,0:T(8,128)}) custom-call(bf16[416,1152]{1,0:T(8,128)(2,1)} %get-tuple-element.529.grad.refs_1_, bf16[1152,1152]{1,0:T(8,128)(2,1)} %bitcast.548, f32[416,1152]{1,0:T(8,128)} %get-tuple-element.278.ratio, f32[416,1152]{1,0:T(8,128)} %get-tuple-element.279.den, ...), custom_call_target="tpu_custom_call" | custom-call | flops 552075264 | bytes 479232 | tf_op jit(solution)/shard_map/pallas_call | solution.py:731
  492.0 11.0 %collective-permute-done.34 = bf16[3,2,96,1152]{3,2,0,1:T(8,128)(2,1)} collective-permute-done((bf16[3,2,96,1152]{3,2,0,1:T(8,128)(2,1)}, bf16[3,2,96,1152]{3,2,0,1:T(8,128)(2,1)}, u32[]{:S(2)}, u32[]{:S(2)}) %collective-permute-start.34) | collective-permute-done | bytes 1327136 | tf_op jit(solution)/shard_map/ppermute | solution.py:90
  506.4 10.9 %collective-permute-done.35 = bf16[3,40,1152]{2,1,0:T(8,128)(2,1)S(1)} collective-permute-done((bf16[3,40,1152]{2,1,0:T(8,128)(2,1)S(1)}, bf16[3,40,1152]{2,1,0:T(8,128)(2,1)S(1)}, u32[]{:S(2)}, u32[]{:S(2)}) %collective-permute-start.35) | collective-permute-done | bytes 276512 | tf_op jit(solution)/shard_map/ppermute | solution.py:90
  518.6 15.2 %shard_map.359 = (bf16[4,4,144,1152]{3,2,1,0:T(8,128)(2,1)}, bf16[4,4,144,1152]{3,2,1,0:T(8,128)(2,1)}) custom-call(bf16[416,1152]{1,0:T(8,128)(2,1)} %get-tuple-element.296.refs_0_, bf16[416,1152]{1,0:T(8,128)(2,1)} %get-tuple-element.529.grad.refs_1_, bf16[416,2048]{1,0:T(8,128)(2,1)} %get-tuple-element.277.refs_2_, ...), custom_call_target="tpu_custom_call" | custom-call | flops 552075264 | bytes 2654208 | tf_op jit(solution)/shard_map/pallas_call | solution.py:314
  543.7 3.7 collective-permute-start.37
  553.3 4.0 fusion
  560.4 12.3 %shard_map.360 = (bf16[416,1152]{1,0:T(8,128)(2,1)}, bf16[416,1152]{1,0:T(8,128)(2,1)}, f32[416,1152]{1,0:T(8,128)}) custom-call(bf16[416,1152]{1,0:T(8,128)(2,1)} %get-tuple-element.281.dquery.refs_0_, bf16[416,1152]{1,0:T(8,128)(2,1)} %get-tuple-element.282.keys, bf16[416,1152]{1,0:T(8,128)(2,1)} %get-tuple-element.283.values, ...), custom_call_target="tpu_custom_call" | custom-call | flops 552075264 | bytes 479232 | tf_op jit(solution)/shard_map/pallas_call | solution.py:731
  583.0 6.7 collective-permute-done.40
  604.0 11.0 %shard_map.361 = (bf16[4,4,128,1152]{3,2,1,0:T(8,128)(2,1)}, bf16[4,4,128,1152]{3,2,1,0:T(8,128)(2,1)}) custom-call(bf16[416,1152]{1,0:T(8,128)(2,1)} %get-tuple-element.281.dquery.refs_0_, bf16[416,1152]{1,0:T(8,128)(2,1)} %get-tuple-element.304.refs_1_, bf16[416,1152]{1,0:T(8,128)(2,1)} %get-tuple-element.305.refs_2_, ...), custom_call_target="tpu_custom_call" | custom-call | flops 552075264 | bytes 2359296 | tf_op jit(solution)/shard_map/pallas_call | solution.py:314
  615.0 5.0 collective-permute-done.41
  636.2 17.1 %collective-permute-done.45 = bf16[2,144,1152]{2,1,0:T(8,128)(2,1)S(1)} collective-permute-done((bf16[2,144,1152]{2,1,0:T(8,128)(2,1)S(1)}, bf16[2,144,1152]{2,1,0:T(8,128)(2,1)S(1)}, u32[]{:S(2)}, u32[]{:S(2)}) %collective-permute-start.45) | collective-permute-done | bytes 663584 | tf_op jit(solution)/shard_map/ppermute | solution.py:90
  653.3 6.2 collective-permute-done.44
  664.3 11.4 %collective-permute-done.47 = bf16[144,1152]{1,0:T(8,128)(2,1)S(1)} collective-permute-done((bf16[144,1152]{1,0:T(8,128)(2,1)S(1)}, bf16[144,1152]{1,0:T(8,128)(2,1)S(1)}, u32[]{:S(2)}, u32[]{:S(2)}) %collective-permute-start.47) | collective-permute-done | bytes 331808 | tf_op jit(solution)/shard_map/ppermute | solution.py:90
  686.1 7.0 collective-permute-done.50
  698.3 7.9 %collective-permute-done.52 = bf16[2,144,1152]{2,1,0:T(8,128)(2,1)S(1)} collective-permute-done((bf16[2,144,1152]{2,1,0:T(8,128)(2,1)S(1)}, bf16[2,144,1152]{2,1,0:T(8,128)(2,1)S(1)}, u32[]{:S(2)}, u32[]{:S(2)}) %collective-permute-start.52) | collective-permute-done | bytes 663584 | tf_op jit(solution)/shard_map/ppermute | solution.py:79
  712.1 5.2 collective-permute-done.53
  718.2 5.3 collective-permute-done.55
  (677 shorter events, 308.6 us)
Async XLA Ops:
  3.9 18.2 %collective-permute-start = (bf16[112,1152]{1,0:T(8,128)(2,1)S(1)}, bf16[112,1152]{1,0:T(8,128)(2,1)S(1)}, u32[]{:S(2)}, u32[]{:S(2)}) collective-permute-start(bf16[112,1152]{1,0:T(8,128)(2,1)S(1)} %fusion.252), channel_id=1, source_target_pairs={{0,2},{1,3},{2,0},{3,1},{4,5},{5,4},{6,7},{7,6},{8,10},{9,11},{10,... | collective-permute-start | bytes 774152 | tf_op jit(solution)/shard_map/ppermute | solution.py:90
  22.2 14.4 %collective-permute-start.1 = (bf16[2,112,1152]{2,1,0:T(8,128)(2,1)S(1)}, bf16[2,112,1152]{2,1,0:T(8,128)(2,1)S(1)}, u32[]{:S(2)}, u32[]{:S(2)}) collective-permute-start(bf16[2,112,1152]{2,1,0:T(8,128)(2,1)S(1)} %pad_maximum_fusion.20), channel_id=1, source_target_pairs={{0,1},{1,0},{2,3},{3,2},{4,6},{5,7},{6,4},{7,5},{8,9},{9,8},{10,11... | collective-permute-start | bytes 1548296 | tf_op jit(solution)/shard_map/ppermute | solution.py:90
  38.5 14.0 %collective-permute-start.5 = (bf16[112,1152]{1,0:T(8,128)(2,1)S(1)}, bf16[112,1152]{1,0:T(8,128)(2,1)S(1)}, u32[]{:S(2)}, u32[]{:S(2)}) collective-permute-start(bf16[112,1152]{1,0:T(8,128)(2,1)S(1)} %dynamic-slice_bitcast_fusion.1), channel_id=1, source_target_pairs={{0,2},{1,3},{2,0},{3,1},{4,5},{5,4},{6,7},{7,6},{8,10},{9,11},{10,... | collective-permute-start | bytes 774152 | tf_op jit(solution)/shard_map/ppermute | solution.py:90
  38.5 11.9 %collective-permute-start.2 = (bf16[3,112,1152]{2,1,0:T(8,128)(2,1)S(1)}, bf16[3,112,1152]{2,1,0:T(8,128)(2,1)S(1)}, u32[]{:S(2)}, u32[]{:S(2)}) collective-permute-start(bf16[3,112,1152]{2,1,0:T(8,128)(2,1)S(1)} %pad_maximum_fusion.16), channel_id=1, source_target_pairs={{0,8},{4,20},{8,0},{12,28},{16,24},{20,4},{24,16},{28,12},{1,9},{5... | collective-permute-start | bytes 2322440 | tf_op jit(solution)/shard_map/ppermute | solution.py:79
  50.7 16.4 %collective-permute-start.4 = (bf16[2,3,112,1152]{3,2,1,0:T(8,128)(2,1)S(1)}, bf16[2,3,112,1152]{3,2,1,0:T(8,128)(2,1)S(1)}, u32[]{:S(2)}, u32[]{:S(2)}) collective-permute-start(bf16[2,3,112,1152]{3,2,1,0:T(8,128)(2,1)S(1)} %pad_maximum_fusion.7.refs_0_), channel_id=1, source_target_pairs={{0,4},{4,0},{8,12},{12,8},{16,20},{20,16},{24,28},{28,24},{1,5},{5... | collective-permute-start | bytes 4644872 | tf_op jit(solution)/shard_map/ppermute | solution.py:42
  50.7 20.3 %collective-permute-start.3 = (bf16[2,3,112,1152]{3,2,1,0:T(8,128)(2,1)S(1)}, bf16[2,3,112,1152]{3,2,1,0:T(8,128)(2,1)}, u32[]{:S(2)}, u32[]{:S(2)}) collective-permute-start(bf16[2,3,112,1152]{3,2,1,0:T(8,128)(2,1)S(1)} %pad_maximum_fusion.7.refs_0_), channel_id=1, source_target_pairs={{0,16},{4,12},{8,24},{12,4},{16,0},{20,28},{24,8},{28,20},{1,17},{... | collective-permute-start | bytes 4644872 | tf_op jit(solution)/shard_map/ppermute | solution.py:79
  52.5 13.2 %collective-permute-start.6 = (bf16[2,112,1152]{2,1,0:T(8,128)(2,1)S(1)}, bf16[2,112,1152]{2,1,0:T(8,128)(2,1)S(1)}, u32[]{:S(2)}, u32[]{:S(2)}) collective-permute-start(bf16[2,112,1152]{2,1,0:T(8,128)(2,1)S(1)} %pad_maximum_fusion.21), channel_id=1, source_target_pairs={{0,1},{1,0},{2,3},{3,2},{4,6},{5,7},{6,4},{7,5},{8,9},{9,8},{10,11... | collective-permute-start | bytes 1548296 | tf_op jit(solution)/shard_map/ppermute | solution.py:90
  55.1 11.9 %collective-permute-start.7 = (bf16[40,1152]{1,0:T(8,128)(2,1)S(1)}, bf16[40,1152]{1,0:T(8,128)(2,1)S(1)}, u32[]{:S(2)}, u32[]{:S(2)}) collective-permute-start(bf16[40,1152]{1,0:T(8,128)(2,1)S(1)} %fusion.251), channel_id=1, source_target_pairs={{0,2},{1,3},{2,0},{3,1},{4,6},{5,7},{6,4},{7,5},{8,10},{9,11},{10,... | collective-permute-start | bytes 276488 | tf_op jit(solution)/shard_map/ppermute | solution.py:42
  76.3 13.2 %collective-permute-start.9 = (bf16[3,112,1152]{2,1,0:T(8,128)(2,1)S(1)}, bf16[3,112,1152]{2,1,0:T(8,128)(2,1)}, u32[]{:S(2)}, u32[]{:S(2)}) collective-permute-start(bf16[3,112,1152]{2,1,0:T(8,128)(2,1)S(1)} %pad_maximum_fusion.17), channel_id=1, source_target_pairs={{0,8},{4,20},{8,0},{12,28},{16,24},{20,4},{24,16},{28,12},{1,9},{5... | collective-permute-start | bytes 2322440 | tf_op jit(solution)/shard_map/ppermute | solution.py:79
  78.5 13.4 %collective-permute-start.10 = (bf16[2,40,1152]{2,1,0:T(8,128)(2,1)S(1)}, bf16[2,40,1152]{2,1,0:T(8,128)(2,1)S(1)}, u32[]{:S(2)}, u32[]{:S(2)}) collective-permute-start(bf16[2,40,1152]{2,1,0:T(8,128)(2,1)S(1)} %pad_maximum_fusion.30), channel_id=1, source_target_pairs={{0,1},{1,0},{2,3},{3,2},{4,5},{5,4},{6,7},{7,6},{8,9},{9,8},{10,11... | collective-permute-start | bytes 552968 | tf_op jit(solution)/shard_map/ppermute | solution.py:42
  79.7 27.9 %collective-permute-start.12 = (bf16[288,1152]{1,0:T(8,128)(2,1)}, bf16[288,1152]{1,0:T(8,128)(2,1)}, u32[]{:S(2)}, u32[]{:S(2)}) collective-permute-start(bf16[288,1152]{1,0:T(8,128)(2,1)} %bitcast.31), channel_id=1, source_target_pairs={{0,2},{1,3},{2,0},{3,1},{4,5},{5,4},{6,7},{7,6},{8,10},{9,11},{10,... | collective-permute-start | bytes 1990664 | tf_op jit(solution)/shard_map/ppermute | solution.py:90
  91.9 26.4 %collective-permute-start.15 = (bf16[2,3,112,1152]{3,2,1,0:T(8,128)(2,1)}, bf16[2,3,112,1152]{3,2,1,0:T(8,128)(2,1)}, u32[]{:S(2)}, u32[]{:S(2)}) collective-permute-start(bf16[2,3,112,1152]{3,2,1,0:T(8,128)(2,1)} %pad_maximum_fusion.8.refs_0_), channel_id=1, source_target_pairs={{0,4},{4,0},{8,12},{12,8},{16,20},{20,16},{24,28},{28,24},{1,5},{5... | collective-permute-start | bytes 4644872 | tf_op jit(solution)/shard_map/ppermute | solution.py:42
  91.9 26.4 %collective-permute-start.14 = (bf16[2,3,112,1152]{3,2,1,0:T(8,128)(2,1)}, bf16[2,3,112,1152]{3,2,1,0:T(8,128)(2,1)}, u32[]{:S(2)}, u32[]{:S(2)}) collective-permute-start(bf16[2,3,112,1152]{3,2,1,0:T(8,128)(2,1)} %pad_maximum_fusion.8.refs_0_), channel_id=1, source_target_pairs={{0,16},{4,12},{8,24},{12,4},{16,0},{20,28},{24,8},{28,20},{1,17},{... | collective-permute-start | bytes 4644872 | tf_op jit(solution)/shard_map/ppermute | solution.py:79
  94.5 13.1 %collective-permute-start.11 = (bf16[4,40,1152]{2,1,0:T(8,128)(2,1)}, bf16[4,40,1152]{2,1,0:T(8,128)(2,1)S(1)}, u32[]{:S(2)}, u32[]{:S(2)}) collective-permute-start(bf16[4,40,1152]{2,1,0:T(8,128)(2,1)} %pad_maximum_fusion.24), channel_id=1, source_target_pairs={{0,4},{4,0},{8,12},{12,8},{16,20},{20,16},{24,28},{28,24},{1,5},{5... | collective-permute-start | bytes 1105928 | tf_op jit(solution)/shard_map/ppermute | solution.py:42
  118.4 16.2 %collective-permute-start.18 = (bf16[2,3,112,1152]{3,2,1,0:T(8,128)(2,1)}, bf16[2,3,112,1152]{3,2,1,0:T(8,128)(2,1)}, u32[]{:S(2)}, u32[]{:S(2)}) collective-permute-start(bf16[2,3,112,1152]{3,2,1,0:T(8,128)(2,1)} %collective-permute-done.14.refs_1_), channel_id=1, source_target_pairs={{0,4},{4,0},{8,12},{12,8},{16,20},{20,16},{24,28},{28,24},{1,5},{5... | collective-permute-start | bytes 4644872 | tf_op jit(solution)/shard_map/ppermute | solution.py:42
  119.5 15.0 %collective-permute-start.17 = (bf16[348,288]{0,1:T(8,128)(2,1)S(1)}, bf16[348,288]{0,1:T(8,128)(2,1)S(1)}, u32[]{:S(2)}, u32[]{:S(2)}) collective-permute-start(bf16[348,288]{0,1:T(8,128)(2,1)S(1)} %pad_maximum_fusion.29), channel_id=1, source_target_pairs={{0,2},{1,3},{2,0},{3,1},{4,6},{5,7},{6,4},{7,5},{8,10},{9,11},{10,... | collective-permute-start | bytes 601352 | tf_op jit(solution)/shard_map/ppermute | solution.py:42
  134.6 26.7 %collective-permute-start.20 = (bf16[40,1152]{1,0:T(8,128)(2,1)S(1)}, bf16[40,1152]{1,0:T(8,128)(2,1)S(1)}, u32[]{:S(2)}, u32[]{:S(2)}) collective-permute-start(bf16[40,1152]{1,0:T(8,128)(2,1)S(1)} %get-tuple-element.581), channel_id=1, source_target_pairs={{4,0},{8,4},{12,8},{16,12},{20,16},{24,20},{28,24},{5,1},{9,5},{13... | collective-permute-start | bytes 276488 | tf_op jit(solution)/shard_map/ppermute | solution.py:1028
  135.9 25.4 %collective-permute-start.19 = (bf16[40,1152]{1,0:T(8,128)(2,1)S(1)}, bf16[40,1152]{1,0:T(8,128)(2,1)S(1)}, u32[]{:S(2)}, u32[]{:S(2)}) collective-permute-start(bf16[40,1152]{1,0:T(8,128)(2,1)S(1)} %get-tuple-element.582), channel_id=1, source_target_pairs={{0,4},{4,8},{8,12},{12,16},{16,20},{20,24},{24,28},{1,5},{5,9},{9,... | collective-permute-start | bytes 276488 | tf_op jit(solution)/shard_map/ppermute | solution.py:1027
  141.2 23.4 %collective-permute-start.21 = (bf16[2,348,288]{1,2,0:T(8,128)(2,1)}, bf16[2,348,288]{1,2,0:T(8,128)(2,1)S(1)}, u32[]{:S(2)}, u32[]{:S(2)}) collective-permute-start(bf16[2,348,288]{1,2,0:T(8,128)(2,1)} %pad_maximum_fusion.22), channel_id=1, source_target_pairs={{0,1},{1,0},{2,3},{3,2},{4,5},{5,4},{6,7},{7,6},{8,9},{9,8},{10,11... | collective-permute-start | bytes 1202696 | tf_op jit(solution)/shard_map/ppermute | solution.py:42
  143.7 39.3 %collective-permute-start.22 = (bf16[2,288,1152]{2,1,0:T(8,128)(2,1)}, bf16[2,288,1152]{2,1,0:T(8,128)(2,1)}, u32[]{:S(2)}, u32[]{:S(2)}) collective-permute-start(bf16[2,288,1152]{2,1,0:T(8,128)(2,1)} %pad_maximum_fusion.10), channel_id=1, source_target_pairs={{0,1},{1,0},{2,3},{3,2},{4,6},{5,7},{6,4},{7,5},{8,9},{9,8},{10,11... | collective-permute-start | bytes 3981320 | tf_op jit(solution)/shard_map/ppermute | solution.py:90
  167.6 19.4 %collective-permute-start.23 = (bf16[4,348,288]{1,2,0:T(8,128)(2,1)}, bf16[4,348,288]{1,2,0:T(8,128)(2,1)}, u32[]{:S(2)}, u32[]{:S(2)}) collective-permute-start(bf16[4,348,288]{1,2,0:T(8,128)(2,1)} %pad_maximum_fusion.15), channel_id=1, source_target_pairs={{0,4},{4,0},{8,12},{12,8},{16,20},{20,16},{24,28},{28,24},{1,5},{5... | collective-permute-start | bytes 2405384 | tf_op jit(solution)/shard_map/ppermute | solution.py:42
  187.1 25.2 %collective-permute-start.24 = (bf16[3,288,1152]{2,1,0:T(8,128)(2,1)}, bf16[3,288,1152]{2,1,0:T(8,128)(2,1)}, u32[]{:S(2)}, u32[]{:S(2)}) collective-permute-start(bf16[3,288,1152]{2,1,0:T(8,128)(2,1)} %pad_maximum_fusion.6), channel_id=1, source_target_pairs={{0,8},{4,20},{8,0},{12,28},{16,24},{20,4},{24,16},{28,12},{1,9},{5... | collective-permute-start | bytes 5971976 | tf_op jit(solution)/shard_map/ppermute | solution.py:79
  216.8 38.1 %collective-permute-start.26 = (bf16[2,3,288,1152]{3,2,1,0:T(8,128)(2,1)}, bf16[2,3,288,1152]{3,2,1,0:T(8,128)(2,1)}, u32[]{:S(2)}, u32[]{:S(2)}) collective-permute-start(bf16[2,3,288,1152]{3,2,1,0:T(8,128)(2,1)} %pad_maximum_fusion.2.refs_1_), channel_id=1, source_target_pairs={{0,4},{4,0},{8,12},{12,8},{16,20},{20,16},{24,28},{28,24},{1,5},{5... | collective-permute-start | bytes 11943944 | tf_op jit(solution)/shard_map/ppermute | solution.py:42
  216.8 46.6 %collective-permute-start.25 = (bf16[2,3,288,1152]{3,2,1,0:T(8,128)(2,1)}, bf16[2,3,288,1152]{3,2,1,0:T(8,128)(2,1)}, u32[]{:S(2)}, u32[]{:S(2)}) collective-permute-start(bf16[2,3,288,1152]{3,2,1,0:T(8,128)(2,1)} %pad_maximum_fusion.2.refs_1_), channel_id=1, source_target_pairs={{0,16},{4,12},{8,24},{12,4},{16,0},{20,28},{24,8},{28,20},{1,17},{... | collective-permute-start | bytes 11943944 | tf_op jit(solution)/shard_map/ppermute | solution.py:79
  263.4 16.6 %collective-permute-start.29 = (bf16[2,3,288,1152]{3,2,1,0:T(8,128)(2,1)}, bf16[2,3,288,1152]{3,2,1,0:T(8,128)(2,1)}, u32[]{:S(2)}, u32[]{:S(2)}) collective-permute-start(bf16[2,3,288,1152]{3,2,1,0:T(8,128)(2,1)} %collective-permute-done.25.refs_2_), channel_id=1, source_target_pairs={{0,4},{4,0},{8,12},{12,8},{16,20},{20,16},{24,28},{28,24},{1,5},{5... | collective-permute-start | bytes 11943944 | tf_op jit(solution)/shard_map/ppermute | solution.py:42
  263.5 12.1 %collective-permute-start.28 = (bf16[144,1152]{1,0:T(8,128)(2,1)S(1)}, bf16[144,1152]{1,0:T(8,128)(2,1)S(1)}, u32[]{:S(2)}, u32[]{:S(2)}) collective-permute-start(bf16[144,1152]{1,0:T(8,128)(2,1)S(1)} %pad_maximum_fusion.26), channel_id=1, source_target_pairs={{1,0},{2,1},{3,2},{4,3},{5,4},{6,5},{7,6},{8,7},{9,8},{10,9},{11,1... | collective-permute-start | bytes 995336 | tf_op jit(solution)/shard_map/ppermute | solution.py:48
  264.8 12.8 %collective-permute-start.27 = (bf16[144,1152]{1,0:T(8,128)(2,1)S(1)}, bf16[144,1152]{1,0:T(8,128)(2,1)S(1)}, u32[]{:S(2)}, u32[]{:S(2)}) collective-permute-start(bf16[144,1152]{1,0:T(8,128)(2,1)S(1)} %pad_maximum_fusion.25), channel_id=1, source_target_pairs={{0,1},{1,2},{2,3},{3,4},{4,5},{5,6},{6,7},{7,8},{8,9},{9,10},{10,1... | collective-permute-start | bytes 995336 | tf_op jit(solution)/shard_map/ppermute | solution.py:48
  307.3 32.7 %collective-permute-start.30 = (bf16[2,3,384,1152]{3,2,1,0:T(8,128)(2,1)}, bf16[2,3,384,1152]{3,2,1,0:T(8,128)(2,1)}, u32[]{:S(2)}, u32[]{:S(2)}) collective-permute-start(bf16[2,3,384,1152]{3,2,1,0:T(8,128)(2,1)} %get-tuple-element.248), channel_id=1, source_target_pairs={{0,4},{4,0},{8,12},{12,8},{16,20},{20,16},{24,28},{28,24},{1,5},{5... | collective-permute-start | bytes 15925256 | tf_op jit(solution)/shard_map/ppermute | solution.py:42
  340.0 30.0 %collective-permute-start.31 = (bf16[2,3,384,1152]{3,2,1,0:T(8,128)(2,1)}, bf16[2,3,384,1152]{3,2,1,0:T(8,128)(2,1)}, u32[]{:S(2)}, u32[]{:S(2)}) collective-permute-start(bf16[2,3,384,1152]{3,2,1,0:T(8,128)(2,1)} %get-tuple-element.254), channel_id=1, source_target_pairs={{0,4},{4,0},{8,12},{12,8},{16,20},{20,16},{24,28},{28,24},{1,5},{5... | collective-permute-start | bytes 15925256 | tf_op jit(solution)/shard_map/ppermute | solution.py:42
  370.0 60.8 %collective-permute-start.32 = (bf16[2,3,384,1152]{3,2,1,0:T(8,128)(2,1)}, bf16[2,3,384,1152]{3,2,1,0:T(8,128)(2,1)}, u32[]{:S(2)}, u32[]{:S(2)}) collective-permute-start(bf16[2,3,384,1152]{3,2,1,0:T(8,128)(2,1)} %get-tuple-element.272), channel_id=1, source_target_pairs={{0,8},{4,20},{8,0},{12,28},{16,24},{20,4},{24,16},{28,12},{1,9},{5... | collective-permute-start | bytes 15925256 | tf_op jit(solution)/shard_map/ppermute | solution.py:79
  434.8 33.3 %collective-permute-start.33 = (bf16[3,2,2,96,1152]{4,3,0,1,2:T(8,128)(2,1)}, bf16[3,2,2,96,1152]{4,3,0,1,2:T(8,128)(2,1)}, u32[]{:S(2)}, u32[]{:S(2)}) collective-permute-start(bf16[3,2,2,96,1152]{4,3,0,1,2:T(8,128)(2,1)} %fusion.1), channel_id=1, source_target_pairs={{0,16},{4,12},{8,24},{12,4},{16,0},{20,28},{24,8},{28,20},{1,17},{... | collective-permute-start | bytes 7962632 | tf_op jit(solution)/shard_map/ppermute | solution.py:79
  471.8 31.1 %collective-permute-start.34 = (bf16[3,2,96,1152]{3,2,0,1:T(8,128)(2,1)}, bf16[3,2,96,1152]{3,2,0,1:T(8,128)(2,1)}, u32[]{:S(2)}, u32[]{:S(2)}) collective-permute-start(bf16[3,2,96,1152]{3,2,0,1:T(8,128)(2,1)} %fusion.49), channel_id=1, source_target_pairs={{0,1},{1,0},{2,3},{3,2},{4,6},{5,7},{6,4},{7,5},{8,9},{9,8},{10,11... | collective-permute-start | bytes 3981320 | tf_op jit(solution)/shard_map/ppermute | solution.py:90
  502.9 14.3 %collective-permute-start.35 = (bf16[3,40,1152]{2,1,0:T(8,128)(2,1)S(1)}, bf16[3,40,1152]{2,1,0:T(8,128)(2,1)S(1)}, u32[]{:S(2)}, u32[]{:S(2)}) collective-permute-start(bf16[3,40,1152]{2,1,0:T(8,128)(2,1)S(1)} %pad_maximum_fusion.28), channel_id=1, source_target_pairs={{0,2},{1,3},{2,0},{3,1},{4,5},{5,4},{6,7},{7,6},{8,10},{9,11},{10,... | collective-permute-start | bytes 829448 | tf_op jit(solution)/shard_map/ppermute | solution.py:90
  517.3 16.5 %collective-permute-start.36 = (bf16[3,40,1152]{2,1,0:T(8,128)(2,1)S(1)}, bf16[3,40,1152]{2,1,0:T(8,128)(2,1)S(1)}, u32[]{:S(2)}, u32[]{:S(2)}) collective-permute-start(bf16[3,40,1152]{2,1,0:T(8,128)(2,1)S(1)} %add_convert_fusion.8), channel_id=1, source_target_pairs={{0,1},{1,0},{2,3},{3,2},{4,6},{5,7},{6,4},{7,5},{8,9},{9,8},{10,11... | collective-permute-start | bytes 829448 | tf_op jit(solution)/shard_map/ppermute | solution.py:90
  533.9 19.3 %collective-permute-start.39 = (bf16[4,4,144,1152]{3,2,1,0:T(8,128)(2,1)}, bf16[4,4,144,1152]{3,2,1,0:T(8,128)(2,1)}, u32[]{:S(2)}, u32[]{:S(2)}) collective-permute-start(bf16[4,4,144,1152]{3,2,1,0:T(8,128)(2,1)} %get-tuple-element.300), channel_id=1, source_target_pairs={{0,4},{4,0},{8,12},{12,8},{16,20},{20,16},{24,28},{28,24},{1,5},{5... | collective-permute-start | bytes 15925256 | tf_op jit(solution)/shard_map/ppermute | solution.py:42
  557.3 32.4 %collective-permute-start.40 = (bf16[2,2,2,144,1152]{4,3,2,1,0:T(8,128)(2,1)}, bf16[2,2,2,144,1152]{4,3,2,1,0:T(8,128)(2,1)}, u32[]{:S(2)}, u32[]{:S(2)}) collective-permute-start(bf16[2,2,2,144,1152]{4,3,2,1,0:T(8,128)(2,1)} %fusion), channel_id=1, source_target_pairs={{0,8},{4,20},{8,0},{12,28},{16,24},{20,4},{24,16},{28,12},{1,9},{5... | collective-permute-start | bytes 7962632 | tf_op jit(solution)/shard_map/ppermute | solution.py:79
  594.0 26.1 %collective-permute-start.42 = (bf16[2,2,144,1152]{3,2,1,0:T(8,128)(2,1)}, bf16[2,2,144,1152]{3,2,1,0:T(8,128)(2,1)}, u32[]{:S(2)}, u32[]{:S(2)}) collective-permute-start(bf16[2,2,144,1152]{3,2,1,0:T(8,128)(2,1)} %fusion.13), channel_id=1, source_target_pairs={{0,16},{4,12},{8,24},{12,4},{16,0},{20,28},{24,8},{28,20},{1,17},{... | collective-permute-start | bytes 3981320 | tf_op jit(solution)/shard_map/ppermute | solution.py:79
  600.6 19.5 %collective-permute-start.41 = (bf16[3,96,1152]{2,1,0:T(8,128)(2,1)}, bf16[3,96,1152]{2,1,0:T(8,128)(2,1)}, u32[]{:S(2)}, u32[]{:S(2)}) collective-permute-start(bf16[3,96,1152]{2,1,0:T(8,128)(2,1)} %fusion.58), channel_id=1, source_target_pairs={{0,2},{1,3},{2,0},{3,1},{4,5},{5,4},{6,7},{7,6},{8,10},{9,11},{10,... | collective-permute-start | bytes 1990664 | tf_op jit(solution)/shard_map/ppermute | solution.py:90
  630.6 28.9 %collective-permute-start.44 = (bf16[2,2,2,128,1152]{4,3,2,1,0:T(8,128)(2,1)S(1)}, bf16[2,2,2,128,1152]{4,3,2,1,0:T(8,128)(2,1)S(1)}, u32[]{:S(2)}, u32[]{:S(2)}) collective-permute-start(bf16[2,2,2,128,1152]{4,3,2,1,0:T(8,128)(2,1)S(1)} %fusion.2), channel_id=1, source_target_pairs={{0,8},{4,20},{8,0},{12,28},{16,24},{20,4},{24,16},{28,12},{1,9},{5... | collective-permute-start | bytes 7077896 | tf_op jit(solution)/shard_map/ppermute | solution.py:79
  635.5 17.8 %collective-permute-start.45 = (bf16[2,144,1152]{2,1,0:T(8,128)(2,1)S(1)}, bf16[2,144,1152]{2,1,0:T(8,128)(2,1)S(1)}, u32[]{:S(2)}, u32[]{:S(2)}) collective-permute-start(bf16[2,144,1152]{2,1,0:T(8,128)(2,1)S(1)} %fusion.59), channel_id=1, source_target_pairs={{0,1},{1,0},{2,3},{3,2},{4,6},{5,7},{6,4},{7,5},{8,9},{9,8},{10,11... | collective-permute-start | bytes 1990664 | tf_op jit(solution)/shard_map/ppermute | solution.py:90
  661.3 16.3 %collective-permute-start.46 = (bf16[2,2,128,1152]{3,2,1,0:T(8,128)(2,1)S(1)}, bf16[2,2,128,1152]{3,2,1,0:T(8,128)(2,1)S(1)}, u32[]{:S(2)}, u32[]{:S(2)}) collective-permute-start(bf16[2,2,128,1152]{3,2,1,0:T(8,128)(2,1)S(1)} %fusion.16), channel_id=1, source_target_pairs={{0,16},{4,12},{8,24},{12,4},{16,0},{20,28},{24,8},{28,20},{1,17},{... | collective-permute-start | bytes 3538952 | tf_op jit(solution)/shard_map/ppermute | solution.py:79
  664.1 11.6 %collective-permute-start.47 = (bf16[144,1152]{1,0:T(8,128)(2,1)S(1)}, bf16[144,1152]{1,0:T(8,128)(2,1)S(1)}, u32[]{:S(2)}, u32[]{:S(2)}) collective-permute-start(bf16[144,1152]{1,0:T(8,128)(2,1)S(1)} %fusion.62), channel_id=1, source_target_pairs={{0,2},{1,3},{2,0},{3,1},{4,5},{5,4},{6,7},{7,6},{8,10},{9,11},{10,... | collective-permute-start | bytes 995336 | tf_op jit(solution)/shard_map/ppermute | solution.py:90
  679.4 16.2 %collective-permute-start.48 = (bf16[2,128,1152]{2,1,0:T(8,128)(2,1)S(1)}, bf16[2,128,1152]{2,1,0:T(8,128)(2,1)S(1)}, u32[]{:S(2)}, u32[]{:S(2)}) collective-permute-start(bf16[2,128,1152]{2,1,0:T(8,128)(2,1)S(1)} %fusion.63), channel_id=1, source_target_pairs={{0,1},{1,0},{2,3},{3,2},{4,6},{5,7},{6,4},{7,5},{8,9},{9,8},{10,11... | collective-permute-start | bytes 1769480 | tf_op jit(solution)/shard_map/ppermute | solution.py:90
  681.6 11.5 %collective-permute-start.50 = (bf16[3,96,1152]{2,1,0:T(8,128)(2,1)S(1)}, bf16[3,96,1152]{2,1,0:T(8,128)(2,1)S(1)}, u32[]{:S(2)}, u32[]{:S(2)}) collective-permute-start(bf16[3,96,1152]{2,1,0:T(8,128)(2,1)S(1)} %add_convert_fusion.3), channel_id=1, source_target_pairs={{0,8},{4,20},{8,0},{12,28},{16,24},{20,4},{24,16},{28,12},{1,9},{5... | collective-permute-start | bytes 1990664 | tf_op jit(solution)/shard_map/ppermute | solution.py:79
  697.0 26.5 %collective-permute-start.55 = (bf16[2,3,96,1152]{3,2,1,0:T(8,128)(2,1)S(1)}, bf16[2,3,96,1152]{3,2,1,0:T(8,128)(2,1)S(1)}, u32[]{:S(2)}, u32[]{:S(2)}) collective-permute-start(bf16[2,3,96,1152]{3,2,1,0:T(8,128)(2,1)S(1)} %pad_maximum_fusion.11), channel_id=1, source_target_pairs={{0,16},{4,12},{8,24},{12,4},{16,0},{20,28},{24,8},{28,20},{1,17},{... | collective-permute-start | bytes 3981320 | tf_op jit(solution)/shard_map/ppermute | solution.py:79
  712.1 13.5 %collective-permute-start.54 = (bf16[2,2,144,1152]{3,2,0,1:T(8,128)(2,1)S(1)}, bf16[2,2,144,1152]{3,2,0,1:T(8,128)(2,1)S(1)}, u32[]{:S(2)}, u32[]{:S(2)}) collective-permute-start(bf16[2,2,144,1152]{3,2,0,1:T(8,128)(2,1)S(1)} %pad_maximum_fusion.12), channel_id=1, source_target_pairs={{0,4},{4,0},{8,12},{12,8},{16,20},{20,16},{24,28},{28,24},{1,5},{5... | collective-permute-start | bytes 3981320 | tf_op jit(solution)/shard_map/ppermute | solution.py:42
  729.5 12.8 %collective-permute-start.56 = (bf16[2,128,1152]{2,1,0:T(8,128)(2,1)}, bf16[2,128,1152]{2,1,0:T(8,128)(2,1)}, u32[]{:S(2)}, u32[]{:S(2)}) collective-permute-start(bf16[2,128,1152]{2,1,0:T(8,128)(2,1)} %pad_maximum_fusion.19), channel_id=1, source_target_pairs={{0,16},{4,12},{8,24},{12,4},{16,0},{20,28},{24,8},{28,20},{1,17},{... | collective-permute-start | bytes 1769480 | tf_op jit(solution)/shard_map/ppermute | solution.py:79
  745.9 12.1 %collective-permute-start.60 = (bf16[75,1152]{1,0:T(8,128)(2,1)S(1)}, bf16[75,1152]{1,0:T(8,128)(2,1)S(1)}, u32[]{:S(2)}, u32[]{:S(2)}) collective-permute-start(bf16[75,1152]{1,0:T(8,128)(2,1)S(1)} %dynamic-slice_bitcast_fusion.2), channel_id=1, source_target_pairs={{0,2},{1,3},{2,0},{3,1},{4,6},{5,7},{6,4},{7,5},{8,10},{9,11},{10,... | collective-permute-start | bytes 518408 | tf_op jit(solution)/shard_map/ppermute | solution.py:42
  (138 other events, 1577.7 us)

commit v5 on v4

--- a/solution.py
+++ b/solution.py
@@ -1278,9 +1278,9 @@
     d_tokens = grad_attn + norm_back(d_normed, normal_a, inv_std_a, scale_a)
 
     sums = jnp.stack([mod_sum(d_normed), mod_sum(d_normed * normal_a)] + mod_sums, axis=1)
-    items = jnp.arange(item_count, dtype=jnp.int32)[:, None, None]
-    mod_table = jnp.where(items == first_item, sums[0][None], 0.0) + jnp.where(
-        (items == first_item + 1), sums[1][None], 0.0
+    items = jnp.arange(item_count, dtype=jnp.int32)[None, :, None]
+    mod_table = jnp.where(items == first_item, sums[0][:, None], 0.0) + jnp.where(
+        (items == first_item + 1), sums[1][:, None], 0.0
     )
     xq_row = d_xq_part.reshape(xheads, XLANE)[:, :XHEAD].reshape(width)
     rows_all = jnp.concatenate(
@@ -1311,7 +1311,9 @@
     for stage in range(1, len(bits)):
         qkv_terms = halve_path(qkv_terms, stage, 0)
     mix_terms = halve_z_once(mix_terms, 2, 0)
-    qkv_terms[-1], mix_terms[-1], *ffn_terms = tie(qkv_terms[-1], mix_terms[-1], *ffn_terms)
+    qkv_terms[-1], mix_terms[-1], ffn_terms[-1] = tie(
+        qkv_terms[-1], mix_terms[-1], ffn_terms[-1]
+    )
     qkv_terms = halve_z_once(qkv_terms, 1, 0)
     d_mix_all = share_turn(total(mix_terms), 0)
     d_ffn_all = share_turn(total(ffn_terms), 0)
@@ -1357,7 +1359,7 @@
     d_qkv_all = d_qkv_all.reshape(-1, width)
     d_w_qkv = d_qkv_all[:att_rows].reshape(3, cols, width).transpose(2, 0, 1).astype(single)
     rows_all = d_qkv_all[att_rows : att_rows + rows_count].astype(single)
-    d_t_mod = rows_all[:-3].reshape(mod_table.shape)
+    d_t_mod = rows_all[:-3].reshape(mod_table.shape).swapaxes(0, 1)
     d_out_bias, d_xo_bias = rows_all[-3], rows_all[-2]
     d_xq_bias = lax.dynamic_slice_in_dim(rows_all[-1], me_z * cols, cols, 0)
     d_shift_table = jnp.sum(d_t_mod, axis=0)

time: 776 us -> 774 us (level)
  no operation moved by 1% of the time
where the time goes in v5:
time: 774 us; the launch traced here: 768 us
  Pallas kernels  229 us (30%)
  waiting for transfers between devices  190 us (25%)
  other arithmetic  136 us (18%)
  local copies, waits for them, and re-layouts  105 us (14%)
  starting transfers between devices  81.4 us (11%)
  matrix products  22.9 us (3%)
    pallas_call x4, Pallas kernels, ffn_call(): pl.pallas_call(functools.partial(ffn_kernel, core if direct else None, be...  112 us
    ppermute x16, waiting for transfers between devices, swap_z(): return lax.ppermute(values, ('dp', 'tensor'), pairs)  90.1 us
    ppermute x18, waiting for transfers between devices, swap_path(): lax.ppermute(values, 'dp', [(i, i ^ turns(i % 2)[number]) for i in range(...  71.3 us
    pallas_call x4, Pallas kernels, lane_call(): pl.pallas_call(kernel, grid=(features // LANES,), in_specs=[specs[kind] f...  40 us
    pallas_call x2, Pallas kernels, grads_call(): pl.pallas_call(functools.partial(grads_kernel, ranks, group, rows, cols,...  26.2 us
    ppermute x18, starting transfers between devices, swap_path(): lax.ppermute(values, 'dp', [(i, i ^ turns(i % 2)[number]) for i in range(...  24.8 us
    convert_element_type x16, other arithmetic, total(): return summed.astype(bfloat)  23.5 us
    ppermute x16, starting transfers between devices, swap_z(): return lax.ppermute(values, ('dp', 'tensor'), pairs)  21.8 us
  transfers between devices with their start and end apart: 61, of which 33 were waited for; matrix products, arithmetic and copies ran while one was open for 28% of the time, Pallas kernels for 26%

profile of v5, /device:TPU:0, one launch (start us, length us, event | category | flops | bytes accessed | tf_op | source)
XLA Modules:
  0.0 767.6 jit_solution(8503095272555621399)
XLA Ops:
  3.9 4.1 collective-permute-start
  23.9 6.0 pad_maximum_fusion.refs_0_
  29.9 6.8 collective-permute-done.1
  57.3 8.5 %collective-permute-done.6 = bf16[2,112,1152]{2,1,0:T(8,128)(2,1)S(1)} collective-permute-done((bf16[2,112,1152]{2,1,0:T(8,128)(2,1)S(1)}, bf16[2,112,1152]{2,1,0:T(8,128)(2,1)S(1)}, u32[]{:S(2)}, u32[]{:S(2)}) %collective-permute-start.6) | collective-permute-done | bytes 516128 | tf_op jit(solution)/shard_map/ppermute | solution.py:90
  67.1 4.0 collective-permute-done.3.refs_1_
  81.7 7.8 %shard_map.348 = (bf16[4,288,1152]{2,1,0:T(8,128)(2,1)}, bf16[4,288,1152]{2,1,0:T(8,128)(2,1)}, bf16[4,288,1152]{2,1,0:T(8,128)(2,1)}) custom-call(bf16[8,112,1152]{2,1,0:T(8,128)(2,1)} %bitcast.552, bf16[2,3,112,1152]{3,2,1,0:T(8,128)(2,1)} %copy-done.15, bf16[2,3,112,1152]{3,2,1,0:T(8,128)(2,1)} %collective-permute-done.3.refs_1_, ...), custom_call_target="tpu_custom_call" | custom-call | bytes 4128768 | tf_op jit(solution)/shard_map/pallas_call | solution.py:255
  94.9 11.5 %shard_map.349 = (f32[416,1152]{1,0:T(8,128)}, f32[416,1152]{1,0:T(8,128)}, bf16[416,1152]{1,0:T(8,128)(2,1)}, bf16[416,1152]{1,0:T(8,128)(2,1)}, bf16[416,1152]...) custom-call(bf16[416,1152]{1,0:T(8,128)(2,1)} %fusion.27.normed.refs_3_, bf16[1152,1152]{1,0:T(8,128)(2,1)} %bitcast.539, ...), custom_call_target="tpu_custom_call" | custom-call | flops 552075264 | bytes 479232 | tf_op jit(solution)/shard_map/pallas_call | solution.py:731
  109.9 8.4 %collective-permute-done.13 = bf16[3,40,1152]{2,1,0:T(8,128)(2,1)S(1)} collective-permute-done((bf16[3,40,1152]{2,1,0:T(8,128)(2,1)S(1)}, bf16[3,40,1152]{2,1,0:T(8,128)(2,1)S(1)}, u32[]{:S(2)}, u32[]{:S(2)}) %collective-permute-start.13) | collective-permute-done | bytes 276512 | tf_op jit(solution)/shard_map/ppermute | solution.py:90
  120.9 6.7 collective-permute-done.16
  127.7 6.9 collective-permute-done.17
  135.9 4.5 collective-permute-start.19
  145.7 7.9 %shard_map.350 = (bf16[4,288,1152]{2,1,0:T(8,128)(2,1)}, bf16[4,288,1152]{2,1,0:T(8,128)(2,1)}, bf16[4,288,1152]{2,1,0:T(8,128)(2,1)}) custom-call(bf16[8,112,1152]{2,1,0:T(8,128)(2,1)} %bitcast.559, bf16[2,3,112,1152]{3,2,1,0:T(8,128)(2,1)} %pad_maximum_fusion.8.refs_0_, bf16[2,3,112,1152]{3,2,1,0:T(8,128)(2,1)} %collective-permute-done.14.refs_1_, ...), custom_call_target="tpu_custom_call" | custom-call | bytes 4128768 | tf_op jit(solution)/shard_map/pallas_call | solution.py:255
  153.7 4.8 pad.61
  170.8 7.0 shard_map.351
  202.9 6.0 add_convert_fusion.query_ref
  212.2 4.5 pad_maximum_fusion.2.refs_1_
  226.6 4.2 fusion.48
  230.8 16.6 %shard_map.352.refs_4_ = bf16[416,2048]{1,0:T(8,128)(2,1)} custom-call(bf16[416,2048]{1,0:T(8,128)(2,1)} %add_convert_fusion.query_ref, bf16[16,384,128]{2,1,0:T(8,128)(2,1)} %get-tuple-element.518.keys_ref, bf16[16,384,128]{2,1,0:T(8,128)(2,1)} %get-tuple-element.517.vals_ref, s32[416,1]{1,0:T(8,128)} %copy.254.length_ref), custom_call_target="tpu_custom_call" | custom-call | flops 327155712 | bytes 1703936 | tf_op jit(solution)/shard_map/pallas_call | solution.py:784
  247.4 6.0 fusion.241
  254.8 8.6 %collective-permute-done.25.refs_2_ = bf16[2,3,288,1152]{3,2,1,0:T(8,128)(2,1)} collective-permute-done((bf16[2,3,288,1152]{3,2,1,0:T(8,128)(2,1)}, bf16[2,3,288,1152]{3,2,1,0:T(8,128)(2,1)}, u32[]{:S(2)}, u32[]{:S(2)}) %collective-permute-start.25) | collective-permute-done | bytes 3981344 | tf_op jit(solution)/shard_map/ppermute | solution.py:79
  264.8 4.6 collective-permute-start.27
  269.4 6.2 collective-permute-done.28
  280.0 27.3 %shard_map.353 = (f32[416,1152]{1,0:T(8,128)}, f32[416,1152]{1,0:T(8,128)}, bf16[2,3,384,1152]{3,2,1,0:T(8,128)(2,1)}, f32[2,16,768]{2,1,0:T(8,128)}) custom-call(bf16[608,1152]{1,0:T(8,128)(2,1)} %pad_maximum_fusion.9.normed_ref, bf16[512,1152]{1,0:T(8,128)(2,1)} %pad_maximum_fusion.13.grad_ref, bf16[4,1152,224]{2,1,0:T(8,128)(2,1)} %bitcast.529, ...), custom_call_target="tpu_custom_call" | custom-call | flops 1755316224 | bytes 1769472 | tf_op jit(solution)/shard_map/pallas_call | solution.py:595
  307.3 5.3 collective-permute-start.30
  312.6 27.4 %shard_map.354 = (f32[416,1152]{1,0:T(8,128)}, f32[416,1152]{1,0:T(8,128)}, bf16[2,3,384,1152]{3,2,1,0:T(8,128)(2,1)}, f32[2,16,768]{2,1,0:T(8,128)}) custom-call(bf16[608,1152]{1,0:T(8,128)(2,1)} %pad_maximum_fusion.9.normed_ref, bf16[512,1152]{1,0:T(8,128)(2,1)} %pad_maximum_fusion.13.grad_ref, bf16[4,1152,224]{2,1,0:T(8,128)(2,1)} %bitcast.530, ...), custom_call_target="tpu_custom_call" | custom-call | flops 1755316224 | bytes 1769472 | tf_op jit(solution)/shard_map/pallas_call | solution.py:595
  341.3 28.6 %shard_map.355 = (f32[416,1152]{1,0:T(8,128)}, f32[416,1152]{1,0:T(8,128)}, bf16[2,3,384,1152]{3,2,1,0:T(8,128)(2,1)}, f32[2,16,768]{2,1,0:T(8,128)}) custom-call(bf16[608,1152]{1,0:T(8,128)(2,1)} %pad_maximum_fusion.9.normed_ref, bf16[512,1152]{1,0:T(8,128)(2,1)} %pad_maximum_fusion.13.grad_ref, bf16[4,1152,224]{2,1,0:T(8,128)(2,1)} %bitcast.531, ...), custom_call_target="tpu_custom_call" | custom-call | flops 1755316224 | bytes 1769472 | tf_op jit(solution)/shard_map/pallas_call | solution.py:595
  372.0 28.5 %shard_map.356 = (f32[416,1152]{1,0:T(8,128)}, f32[416,1152]{1,0:T(8,128)}, bf16[2,3,384,1152]{3,2,1,0:T(8,128)(2,1)}, f32[2,16,768]{2,1,0:T(8,128)}) custom-call(bf16[608,1152]{1,0:T(8,128)(2,1)} %pad_maximum_fusion.9.normed_ref, bf16[512,1152]{1,0:T(8,128)(2,1)} %pad_maximum_fusion.13.grad_ref, bf16[4,1152,224]{2,1,0:T(8,128)(2,1)} %bitcast.532, ...), custom_call_target="tpu_custom_call" | custom-call | flops 1755316224 | bytes 1769472 | tf_op jit(solution)/shard_map/pallas_call | solution.py:595
  400.5 6.7 select_reduce_fusion.7
  420.4 10.4 %collective-permute-done.32 = bf16[2,3,384,1152]{3,2,1,0:T(8,128)(2,1)} collective-permute-done((bf16[2,3,384,1152]{3,2,1,0:T(8,128)(2,1)}, bf16[2,3,384,1152]{3,2,1,0:T(8,128)(2,1)}, u32[]{:S(2)}, u32[]{:S(2)}) %collective-permute-start.32) | collective-permute-done | bytes 5308448 | tf_op jit(solution)/shard_map/ppermute | solution.py:79
  430.9 4.0 fusion.1
  443.2 18.2 %shard_map.357 = (bf16[416,2048]{1,0:T(8,128)(2,1)}, bf16[16,72,384]{2,1,0:T(8,128)(2,1)}, bf16[16,72,384]{2,1,0:T(8,128)(2,1)}, f32[1,2048]{1,0:T(1,128)}) custom-call(bf16[416,2048]{1,0:T(8,128)(2,1)} %add_convert_fusion.query_ref, bf16[16,384,128]{2,1,0:T(8,128)(2,1)} %get-tuple-element.518.keys_ref, bf16[16,384,128]{2,1,0:T(8,128)(2,1)} %get-tuple-element.517.vals_ref, ...), custom_call_target="tpu_custom_call" | custom-call | flops 327155712 | bytes 1703936 | tf_op jit(solution)/shard_map/pallas_call | solution.py:802
  481.7 9.2 %shard_map.358 = (bf16[416,1152]{1,0:T(8,128)(2,1)}, f32[40,1152]{1,0:T(8,128)}, f32[40,1152]{1,0:T(8,128)}) custom-call(bf16[416,1152]{1,0:T(8,128)(2,1)} %get-tuple-element.521.grad.refs_1_, bf16[1152,1152]{1,0:T(8,128)(2,1)} %bitcast.546, f32[416,1152]{1,0:T(8,128)} %get-tuple-element.274.ratio, f32[416,1152]{1,0:T(8,128)} %get-tuple-element.275.den, ...), custom_call_target="tpu_custom_call" | custom-call | flops 552075264 | bytes 479232 | tf_op jit(solution)/shard_map/pallas_call | solution.py:731
  492.0 10.9 %collective-permute-done.34 = bf16[3,2,96,1152]{3,2,0,1:T(8,128)(2,1)} collective-permute-done((bf16[3,2,96,1152]{3,2,0,1:T(8,128)(2,1)}, bf16[3,2,96,1152]{3,2,0,1:T(8,128)(2,1)}, u32[]{:S(2)}, u32[]{:S(2)}) %collective-permute-start.34) | collective-permute-done | bytes 1327136 | tf_op jit(solution)/shard_map/ppermute | solution.py:90
  506.5 10.9 %collective-permute-done.35 = bf16[3,40,1152]{2,1,0:T(8,128)(2,1)S(1)} collective-permute-done((bf16[3,40,1152]{2,1,0:T(8,128)(2,1)S(1)}, bf16[3,40,1152]{2,1,0:T(8,128)(2,1)S(1)}, u32[]{:S(2)}, u32[]{:S(2)}) %collective-permute-start.35) | collective-permute-done | bytes 276512 | tf_op jit(solution)/shard_map/ppermute | solution.py:90
  518.7 15.2 %shard_map.359 = (bf16[4,4,144,1152]{3,2,1,0:T(8,128)(2,1)}, bf16[4,4,144,1152]{3,2,1,0:T(8,128)(2,1)}) custom-call(bf16[416,1152]{1,0:T(8,128)(2,1)} %get-tuple-element.292.refs_0_, bf16[416,1152]{1,0:T(8,128)(2,1)} %get-tuple-element.521.grad.refs_1_, bf16[416,2048]{1,0:T(8,128)(2,1)} %get-tuple-element.273.refs_2_, ...), custom_call_target="tpu_custom_call" | custom-call | flops 552075264 | bytes 2654208 | tf_op jit(solution)/shard_map/pallas_call | solution.py:314
  553.2 4.0 fusion
  560.3 12.3 %shard_map.360 = (bf16[416,1152]{1,0:T(8,128)(2,1)}, bf16[416,1152]{1,0:T(8,128)(2,1)}, f32[416,1152]{1,0:T(8,128)}) custom-call(bf16[416,1152]{1,0:T(8,128)(2,1)} %get-tuple-element.277.dquery.refs_0_, bf16[416,1152]{1,0:T(8,128)(2,1)} %get-tuple-element.278.keys, bf16[416,1152]{1,0:T(8,128)(2,1)} %get-tuple-element.279.values, ...), custom_call_target="tpu_custom_call" | custom-call | flops 552075264 | bytes 479232 | tf_op jit(solution)/shard_map/pallas_call | solution.py:731
  582.8 6.8 collective-permute-done.40
  603.7 11.0 %shard_map.361 = (bf16[4,4,128,1152]{3,2,1,0:T(8,128)(2,1)}, bf16[4,4,128,1152]{3,2,1,0:T(8,128)(2,1)}) custom-call(bf16[416,1152]{1,0:T(8,128)(2,1)} %get-tuple-element.277.dquery.refs_0_, bf16[416,1152]{1,0:T(8,128)(2,1)} %get-tuple-element.300.refs_1_, bf16[416,1152]{1,0:T(8,128)(2,1)} %get-tuple-element.301.refs_2_, ...), custom_call_target="tpu_custom_call" | custom-call | flops 552075264 | bytes 2359296 | tf_op jit(solution)/shard_map/pallas_call | solution.py:314
  614.7 5.0 collective-permute-done.41
  621.8 6.2 collective-permute-done.43
  636.1 17.1 %collective-permute-done.45 = bf16[2,144,1152]{2,1,0:T(8,128)(2,1)S(1)} collective-permute-done((bf16[2,144,1152]{2,1,0:T(8,128)(2,1)S(1)}, bf16[2,144,1152]{2,1,0:T(8,128)(2,1)S(1)}, u32[]{:S(2)}, u32[]{:S(2)}) %collective-permute-start.45) | collective-permute-done | bytes 663584 | tf_op jit(solution)/shard_map/ppermute | solution.py:90
  653.1 6.2 collective-permute-done.44
  664.1 11.4 %collective-permute-done.47 = bf16[144,1152]{1,0:T(8,128)(2,1)S(1)} collective-permute-done((bf16[144,1152]{1,0:T(8,128)(2,1)S(1)}, bf16[144,1152]{1,0:T(8,128)(2,1)S(1)}, u32[]{:S(2)}, u32[]{:S(2)}) %collective-permute-start.47) | collective-permute-done | bytes 331808 | tf_op jit(solution)/shard_map/ppermute | solution.py:90
  686.0 7.0 collective-permute-done.50
  698.2 7.9 %collective-permute-done.52 = bf16[2,144,1152]{2,1,0:T(8,128)(2,1)S(1)} collective-permute-done((bf16[2,144,1152]{2,1,0:T(8,128)(2,1)S(1)}, bf16[2,144,1152]{2,1,0:T(8,128)(2,1)S(1)}, u32[]{:S(2)}, u32[]{:S(2)}) %collective-permute-start.52) | collective-permute-done | bytes 663584 | tf_op jit(solution)/shard_map/ppermute | solution.py:79
  711.9 5.2 collective-permute-done.53
  718.0 5.5 collective-permute-done.55
  (676 shorter events, 304.0 us)
Async XLA Ops:
  3.9 18.3 %collective-permute-start = (bf16[112,1152]{1,0:T(8,128)(2,1)S(1)}, bf16[112,1152]{1,0:T(8,128)(2,1)S(1)}, u32[]{:S(2)}, u32[]{:S(2)}) collective-permute-start(bf16[112,1152]{1,0:T(8,128)(2,1)S(1)} %fusion.253), channel_id=1, source_target_pairs={{0,2},{1,3},{2,0},{3,1},{4,5},{5,4},{6,7},{7,6},{8,10},{9,11},{10,... | collective-permute-start | bytes 774152 | tf_op jit(solution)/shard_map/ppermute | solution.py:90
  22.3 14.4 %collective-permute-start.1 = (bf16[2,112,1152]{2,1,0:T(8,128)(2,1)S(1)}, bf16[2,112,1152]{2,1,0:T(8,128)(2,1)S(1)}, u32[]{:S(2)}, u32[]{:S(2)}) collective-permute-start(bf16[2,112,1152]{2,1,0:T(8,128)(2,1)S(1)} %pad_maximum_fusion.20), channel_id=1, source_target_pairs={{0,1},{1,0},{2,3},{3,2},{4,6},{5,7},{6,4},{7,5},{8,9},{9,8},{10,11... | collective-permute-start | bytes 1548296 | tf_op jit(solution)/shard_map/ppermute | solution.py:90
  38.5 14.0 %collective-permute-start.5 = (bf16[112,1152]{1,0:T(8,128)(2,1)S(1)}, bf16[112,1152]{1,0:T(8,128)(2,1)S(1)}, u32[]{:S(2)}, u32[]{:S(2)}) collective-permute-start(bf16[112,1152]{1,0:T(8,128)(2,1)S(1)} %dynamic-slice_bitcast_fusion.1), channel_id=1, source_target_pairs={{0,2},{1,3},{2,0},{3,1},{4,5},{5,4},{6,7},{7,6},{8,10},{9,11},{10,... | collective-permute-start | bytes 774152 | tf_op jit(solution)/shard_map/ppermute | solution.py:90
  38.6 11.9 %collective-permute-start.2 = (bf16[3,112,1152]{2,1,0:T(8,128)(2,1)S(1)}, bf16[3,112,1152]{2,1,0:T(8,128)(2,1)S(1)}, u32[]{:S(2)}, u32[]{:S(2)}) collective-permute-start(bf16[3,112,1152]{2,1,0:T(8,128)(2,1)S(1)} %pad_maximum_fusion.16), channel_id=1, source_target_pairs={{0,8},{4,20},{8,0},{12,28},{16,24},{20,4},{24,16},{28,12},{1,9},{5... | collective-permute-start | bytes 2322440 | tf_op jit(solution)/shard_map/ppermute | solution.py:79
  50.7 16.4 %collective-permute-start.4 = (bf16[2,3,112,1152]{3,2,1,0:T(8,128)(2,1)S(1)}, bf16[2,3,112,1152]{3,2,1,0:T(8,128)(2,1)S(1)}, u32[]{:S(2)}, u32[]{:S(2)}) collective-permute-start(bf16[2,3,112,1152]{3,2,1,0:T(8,128)(2,1)S(1)} %pad_maximum_fusion.7.refs_0_), channel_id=1, source_target_pairs={{0,4},{4,0},{8,12},{12,8},{16,20},{20,16},{24,28},{28,24},{1,5},{5... | collective-permute-start | bytes 4644872 | tf_op jit(solution)/shard_map/ppermute | solution.py:42
  50.8 20.3 %collective-permute-start.3 = (bf16[2,3,112,1152]{3,2,1,0:T(8,128)(2,1)S(1)}, bf16[2,3,112,1152]{3,2,1,0:T(8,128)(2,1)}, u32[]{:S(2)}, u32[]{:S(2)}) collective-permute-start(bf16[2,3,112,1152]{3,2,1,0:T(8,128)(2,1)S(1)} %pad_maximum_fusion.7.refs_0_), channel_id=1, source_target_pairs={{0,16},{4,12},{8,24},{12,4},{16,0},{20,28},{24,8},{28,20},{1,17},{... | collective-permute-start | bytes 4644872 | tf_op jit(solution)/shard_map/ppermute | solution.py:79
  52.6 13.2 %collective-permute-start.6 = (bf16[2,112,1152]{2,1,0:T(8,128)(2,1)S(1)}, bf16[2,112,1152]{2,1,0:T(8,128)(2,1)S(1)}, u32[]{:S(2)}, u32[]{:S(2)}) collective-permute-start(bf16[2,112,1152]{2,1,0:T(8,128)(2,1)S(1)} %pad_maximum_fusion.21), channel_id=1, source_target_pairs={{0,1},{1,0},{2,3},{3,2},{4,6},{5,7},{6,4},{7,5},{8,9},{9,8},{10,11... | collective-permute-start | bytes 1548296 | tf_op jit(solution)/shard_map/ppermute | solution.py:90
  55.2 11.9 %collective-permute-start.7 = (bf16[40,1152]{1,0:T(8,128)(2,1)S(1)}, bf16[40,1152]{1,0:T(8,128)(2,1)S(1)}, u32[]{:S(2)}, u32[]{:S(2)}) collective-permute-start(bf16[40,1152]{1,0:T(8,128)(2,1)S(1)} %fusion.252), channel_id=1, source_target_pairs={{0,2},{1,3},{2,0},{3,1},{4,6},{5,7},{6,4},{7,5},{8,10},{9,11},{10,... | collective-permute-start | bytes 276488 | tf_op jit(solution)/shard_map/ppermute | solution.py:42
  76.3 13.2 %collective-permute-start.9 = (bf16[3,112,1152]{2,1,0:T(8,128)(2,1)S(1)}, bf16[3,112,1152]{2,1,0:T(8,128)(2,1)}, u32[]{:S(2)}, u32[]{:S(2)}) collective-permute-start(bf16[3,112,1152]{2,1,0:T(8,128)(2,1)S(1)} %pad_maximum_fusion.17), channel_id=1, source_target_pairs={{0,8},{4,20},{8,0},{12,28},{16,24},{20,4},{24,16},{28,12},{1,9},{5... | collective-permute-start | bytes 2322440 | tf_op jit(solution)/shard_map/ppermute | solution.py:79
  78.6 13.4 %collective-permute-start.10 = (bf16[2,40,1152]{2,1,0:T(8,128)(2,1)S(1)}, bf16[2,40,1152]{2,1,0:T(8,128)(2,1)S(1)}, u32[]{:S(2)}, u32[]{:S(2)}) collective-permute-start(bf16[2,40,1152]{2,1,0:T(8,128)(2,1)S(1)} %pad_maximum_fusion.30), channel_id=1, source_target_pairs={{0,1},{1,0},{2,3},{3,2},{4,5},{5,4},{6,7},{7,6},{8,9},{9,8},{10,11... | collective-permute-start | bytes 552968 | tf_op jit(solution)/shard_map/ppermute | solution.py:42
  79.7 27.8 %collective-permute-start.12 = (bf16[288,1152]{1,0:T(8,128)(2,1)}, bf16[288,1152]{1,0:T(8,128)(2,1)}, u32[]{:S(2)}, u32[]{:S(2)}) collective-permute-start(bf16[288,1152]{1,0:T(8,128)(2,1)} %bitcast.31), channel_id=1, source_target_pairs={{0,2},{1,3},{2,0},{3,1},{4,5},{5,4},{6,7},{7,6},{8,10},{9,11},{10,... | collective-permute-start | bytes 1990664 | tf_op jit(solution)/shard_map/ppermute | solution.py:90
  92.0 26.3 %collective-permute-start.15 = (bf16[2,3,112,1152]{3,2,1,0:T(8,128)(2,1)}, bf16[2,3,112,1152]{3,2,1,0:T(8,128)(2,1)}, u32[]{:S(2)}, u32[]{:S(2)}) collective-permute-start(bf16[2,3,112,1152]{3,2,1,0:T(8,128)(2,1)} %pad_maximum_fusion.8.refs_0_), channel_id=1, source_target_pairs={{0,4},{4,0},{8,12},{12,8},{16,20},{20,16},{24,28},{28,24},{1,5},{5... | collective-permute-start | bytes 4644872 | tf_op jit(solution)/shard_map/ppermute | solution.py:42
  92.0 26.3 %collective-permute-start.14 = (bf16[2,3,112,1152]{3,2,1,0:T(8,128)(2,1)}, bf16[2,3,112,1152]{3,2,1,0:T(8,128)(2,1)}, u32[]{:S(2)}, u32[]{:S(2)}) collective-permute-start(bf16[2,3,112,1152]{3,2,1,0:T(8,128)(2,1)} %pad_maximum_fusion.8.refs_0_), channel_id=1, source_target_pairs={{0,16},{4,12},{8,24},{12,4},{16,0},{20,28},{24,8},{28,20},{1,17},{... | collective-permute-start | bytes 4644872 | tf_op jit(solution)/shard_map/ppermute | solution.py:79
  94.5 13.0 %collective-permute-start.11 = (bf16[4,40,1152]{2,1,0:T(8,128)(2,1)}, bf16[4,40,1152]{2,1,0:T(8,128)(2,1)S(1)}, u32[]{:S(2)}, u32[]{:S(2)}) collective-permute-start(bf16[4,40,1152]{2,1,0:T(8,128)(2,1)} %pad_maximum_fusion.24), channel_id=1, source_target_pairs={{0,4},{4,0},{8,12},{12,8},{16,20},{20,16},{24,28},{28,24},{1,5},{5... | collective-permute-start | bytes 1105928 | tf_op jit(solution)/shard_map/ppermute | solution.py:42
  118.4 16.2 %collective-permute-start.18 = (bf16[2,3,112,1152]{3,2,1,0:T(8,128)(2,1)}, bf16[2,3,112,1152]{3,2,1,0:T(8,128)(2,1)}, u32[]{:S(2)}, u32[]{:S(2)}) collective-permute-start(bf16[2,3,112,1152]{3,2,1,0:T(8,128)(2,1)} %collective-permute-done.14.refs_1_), channel_id=1, source_target_pairs={{0,4},{4,0},{8,12},{12,8},{16,20},{20,16},{24,28},{28,24},{1,5},{5... | collective-permute-start | bytes 4644872 | tf_op jit(solution)/shard_map/ppermute | solution.py:42
  119.5 15.0 %collective-permute-start.17 = (bf16[348,288]{0,1:T(8,128)(2,1)S(1)}, bf16[348,288]{0,1:T(8,128)(2,1)S(1)}, u32[]{:S(2)}, u32[]{:S(2)}) collective-permute-start(bf16[348,288]{0,1:T(8,128)(2,1)S(1)} %pad_maximum_fusion.29), channel_id=1, source_target_pairs={{0,2},{1,3},{2,0},{3,1},{4,6},{5,7},{6,4},{7,5},{8,10},{9,11},{10,... | collective-permute-start | bytes 601352 | tf_op jit(solution)/shard_map/ppermute | solution.py:42
  134.6 26.7 %collective-permute-start.20 = (bf16[40,1152]{1,0:T(8,128)(2,1)S(1)}, bf16[40,1152]{1,0:T(8,128)(2,1)S(1)}, u32[]{:S(2)}, u32[]{:S(2)}) collective-permute-start(bf16[40,1152]{1,0:T(8,128)(2,1)S(1)} %get-tuple-element.573), channel_id=1, source_target_pairs={{4,0},{8,4},{12,8},{16,12},{20,16},{24,20},{28,24},{5,1},{9,5},{13... | collective-permute-start | bytes 276488 | tf_op jit(solution)/shard_map/ppermute | solution.py:1028
  135.9 25.4 %collective-permute-start.19 = (bf16[40,1152]{1,0:T(8,128)(2,1)S(1)}, bf16[40,1152]{1,0:T(8,128)(2,1)S(1)}, u32[]{:S(2)}, u32[]{:S(2)}) collective-permute-start(bf16[40,1152]{1,0:T(8,128)(2,1)S(1)} %get-tuple-element.574), channel_id=1, source_target_pairs={{0,4},{4,8},{8,12},{12,16},{16,20},{20,24},{24,28},{1,5},{5,9},{9,... | collective-permute-start | bytes 276488 | tf_op jit(solution)/shard_map/ppermute | solution.py:1027
  141.2 23.4 %collective-permute-start.21 = (bf16[2,348,288]{1,2,0:T(8,128)(2,1)}, bf16[2,348,288]{1,2,0:T(8,128)(2,1)S(1)}, u32[]{:S(2)}, u32[]{:S(2)}) collective-permute-start(bf16[2,348,288]{1,2,0:T(8,128)(2,1)} %pad_maximum_fusion.22), channel_id=1, source_target_pairs={{0,1},{1,0},{2,3},{3,2},{4,5},{5,4},{6,7},{7,6},{8,9},{9,8},{10,11... | collective-permute-start | bytes 1202696 | tf_op jit(solution)/shard_map/ppermute | solution.py:42
  143.7 39.3 %collective-permute-start.22 = (bf16[2,288,1152]{2,1,0:T(8,128)(2,1)}, bf16[2,288,1152]{2,1,0:T(8,128)(2,1)}, u32[]{:S(2)}, u32[]{:S(2)}) collective-permute-start(bf16[2,288,1152]{2,1,0:T(8,128)(2,1)} %pad_maximum_fusion.10), channel_id=1, source_target_pairs={{0,1},{1,0},{2,3},{3,2},{4,6},{5,7},{6,4},{7,5},{8,9},{9,8},{10,11... | collective-permute-start | bytes 3981320 | tf_op jit(solution)/shard_map/ppermute | solution.py:90
  167.6 19.4 %collective-permute-start.23 = (bf16[4,348,288]{1,2,0:T(8,128)(2,1)}, bf16[4,348,288]{1,2,0:T(8,128)(2,1)}, u32[]{:S(2)}, u32[]{:S(2)}) collective-permute-start(bf16[4,348,288]{1,2,0:T(8,128)(2,1)} %pad_maximum_fusion.15), channel_id=1, source_target_pairs={{0,4},{4,0},{8,12},{12,8},{16,20},{20,16},{24,28},{28,24},{1,5},{5... | collective-permute-start | bytes 2405384 | tf_op jit(solution)/shard_map/ppermute | solution.py:42
  187.0 25.2 %collective-permute-start.24 = (bf16[3,288,1152]{2,1,0:T(8,128)(2,1)}, bf16[3,288,1152]{2,1,0:T(8,128)(2,1)}, u32[]{:S(2)}, u32[]{:S(2)}) collective-permute-start(bf16[3,288,1152]{2,1,0:T(8,128)(2,1)} %pad_maximum_fusion.6), channel_id=1, source_target_pairs={{0,8},{4,20},{8,0},{12,28},{16,24},{20,4},{24,16},{28,12},{1,9},{5... | collective-permute-start | bytes 5971976 | tf_op jit(solution)/shard_map/ppermute | solution.py:79
  216.7 38.0 %collective-permute-start.26 = (bf16[2,3,288,1152]{3,2,1,0:T(8,128)(2,1)}, bf16[2,3,288,1152]{3,2,1,0:T(8,128)(2,1)}, u32[]{:S(2)}, u32[]{:S(2)}) collective-permute-start(bf16[2,3,288,1152]{3,2,1,0:T(8,128)(2,1)} %pad_maximum_fusion.2.refs_1_), channel_id=1, source_target_pairs={{0,4},{4,0},{8,12},{12,8},{16,20},{20,16},{24,28},{28,24},{1,5},{5... | collective-permute-start | bytes 11943944 | tf_op jit(solution)/shard_map/ppermute | solution.py:42
  216.7 46.7 %collective-permute-start.25 = (bf16[2,3,288,1152]{3,2,1,0:T(8,128)(2,1)}, bf16[2,3,288,1152]{3,2,1,0:T(8,128)(2,1)}, u32[]{:S(2)}, u32[]{:S(2)}) collective-permute-start(bf16[2,3,288,1152]{3,2,1,0:T(8,128)(2,1)} %pad_maximum_fusion.2.refs_1_), channel_id=1, source_target_pairs={{0,16},{4,12},{8,24},{12,4},{16,0},{20,28},{24,8},{28,20},{1,17},{... | collective-permute-start | bytes 11943944 | tf_op jit(solution)/shard_map/ppermute | solution.py:79
  263.4 16.6 %collective-permute-start.29 = (bf16[2,3,288,1152]{3,2,1,0:T(8,128)(2,1)}, bf16[2,3,288,1152]{3,2,1,0:T(8,128)(2,1)}, u32[]{:S(2)}, u32[]{:S(2)}) collective-permute-start(bf16[2,3,288,1152]{3,2,1,0:T(8,128)(2,1)} %collective-permute-done.25.refs_2_), channel_id=1, source_target_pairs={{0,4},{4,0},{8,12},{12,8},{16,20},{20,16},{24,28},{28,24},{1,5},{5... | collective-permute-start | bytes 11943944 | tf_op jit(solution)/shard_map/ppermute | solution.py:42
  263.5 12.1 %collective-permute-start.28 = (bf16[144,1152]{1,0:T(8,128)(2,1)S(1)}, bf16[144,1152]{1,0:T(8,128)(2,1)S(1)}, u32[]{:S(2)}, u32[]{:S(2)}) collective-permute-start(bf16[144,1152]{1,0:T(8,128)(2,1)S(1)} %pad_maximum_fusion.26), channel_id=1, source_target_pairs={{1,0},{2,1},{3,2},{4,3},{5,4},{6,5},{7,6},{8,7},{9,8},{10,9},{11,1... | collective-permute-start | bytes 995336 | tf_op jit(solution)/shard_map/ppermute | solution.py:48
  264.8 12.8 %collective-permute-start.27 = (bf16[144,1152]{1,0:T(8,128)(2,1)S(1)}, bf16[144,1152]{1,0:T(8,128)(2,1)S(1)}, u32[]{:S(2)}, u32[]{:S(2)}) collective-permute-start(bf16[144,1152]{1,0:T(8,128)(2,1)S(1)} %pad_maximum_fusion.25), channel_id=1, source_target_pairs={{0,1},{1,2},{2,3},{3,4},{4,5},{5,6},{6,7},{7,8},{8,9},{9,10},{10,1... | collective-permute-start | bytes 995336 | tf_op jit(solution)/shard_map/ppermute | solution.py:48
  307.3 32.7 %collective-permute-start.30 = (bf16[2,3,384,1152]{3,2,1,0:T(8,128)(2,1)}, bf16[2,3,384,1152]{3,2,1,0:T(8,128)(2,1)}, u32[]{:S(2)}, u32[]{:S(2)}) collective-permute-start(bf16[2,3,384,1152]{3,2,1,0:T(8,128)(2,1)} %get-tuple-element.244), channel_id=1, source_target_pairs={{0,4},{4,0},{8,12},{12,8},{16,20},{20,16},{24,28},{28,24},{1,5},{5... | collective-permute-start | bytes 15925256 | tf_op jit(solution)/shard_map/ppermute | solution.py:42
  340.0 30.0 %collective-permute-start.31 = (bf16[2,3,384,1152]{3,2,1,0:T(8,128)(2,1)}, bf16[2,3,384,1152]{3,2,1,0:T(8,128)(2,1)}, u32[]{:S(2)}, u32[]{:S(2)}) collective-permute-start(bf16[2,3,384,1152]{3,2,1,0:T(8,128)(2,1)} %get-tuple-element.250), channel_id=1, source_target_pairs={{0,4},{4,0},{8,12},{12,8},{16,20},{20,16},{24,28},{28,24},{1,5},{5... | collective-permute-start | bytes 15925256 | tf_op jit(solution)/shard_map/ppermute | solution.py:42
  370.0 60.8 %collective-permute-start.32 = (bf16[2,3,384,1152]{3,2,1,0:T(8,128)(2,1)}, bf16[2,3,384,1152]{3,2,1,0:T(8,128)(2,1)}, u32[]{:S(2)}, u32[]{:S(2)}) collective-permute-start(bf16[2,3,384,1152]{3,2,1,0:T(8,128)(2,1)} %get-tuple-element.268), channel_id=1, source_target_pairs={{0,8},{4,20},{8,0},{12,28},{16,24},{20,4},{24,16},{28,12},{1,9},{5... | collective-permute-start | bytes 15925256 | tf_op jit(solution)/shard_map/ppermute | solution.py:79
  434.9 33.3 %collective-permute-start.33 = (bf16[3,2,2,96,1152]{4,3,0,1,2:T(8,128)(2,1)}, bf16[3,2,2,96,1152]{4,3,0,1,2:T(8,128)(2,1)}, u32[]{:S(2)}, u32[]{:S(2)}) collective-permute-start(bf16[3,2,2,96,1152]{4,3,0,1,2:T(8,128)(2,1)} %fusion.1), channel_id=1, source_target_pairs={{0,16},{4,12},{8,24},{12,4},{16,0},{20,28},{24,8},{28,20},{1,17},{... | collective-permute-start | bytes 7962632 | tf_op jit(solution)/shard_map/ppermute | solution.py:79
  471.9 31.1 %collective-permute-start.34 = (bf16[3,2,96,1152]{3,2,0,1:T(8,128)(2,1)}, bf16[3,2,96,1152]{3,2,0,1:T(8,128)(2,1)}, u32[]{:S(2)}, u32[]{:S(2)}) collective-permute-start(bf16[3,2,96,1152]{3,2,0,1:T(8,128)(2,1)} %fusion.49), channel_id=1, source_target_pairs={{0,1},{1,0},{2,3},{3,2},{4,6},{5,7},{6,4},{7,5},{8,9},{9,8},{10,11... | collective-permute-start | bytes 3981320 | tf_op jit(solution)/shard_map/ppermute | solution.py:90
  503.0 14.4 %collective-permute-start.35 = (bf16[3,40,1152]{2,1,0:T(8,128)(2,1)S(1)}, bf16[3,40,1152]{2,1,0:T(8,128)(2,1)S(1)}, u32[]{:S(2)}, u32[]{:S(2)}) collective-permute-start(bf16[3,40,1152]{2,1,0:T(8,128)(2,1)S(1)} %pad_maximum_fusion.28), channel_id=1, source_target_pairs={{0,2},{1,3},{2,0},{3,1},{4,5},{5,4},{6,7},{7,6},{8,10},{9,11},{10,... | collective-permute-start | bytes 829448 | tf_op jit(solution)/shard_map/ppermute | solution.py:90
  517.4 16.5 %collective-permute-start.36 = (bf16[3,40,1152]{2,1,0:T(8,128)(2,1)S(1)}, bf16[3,40,1152]{2,1,0:T(8,128)(2,1)S(1)}, u32[]{:S(2)}, u32[]{:S(2)}) collective-permute-start(bf16[3,40,1152]{2,1,0:T(8,128)(2,1)S(1)} %add_convert_fusion.7), channel_id=1, source_target_pairs={{0,1},{1,0},{2,3},{3,2},{4,6},{5,7},{6,4},{7,5},{8,9},{9,8},{10,11... | collective-permute-start | bytes 829448 | tf_op jit(solution)/shard_map/ppermute | solution.py:90
  534.0 19.1 %collective-permute-start.39 = (bf16[4,4,144,1152]{3,2,1,0:T(8,128)(2,1)}, bf16[4,4,144,1152]{3,2,1,0:T(8,128)(2,1)}, u32[]{:S(2)}, u32[]{:S(2)}) collective-permute-start(bf16[4,4,144,1152]{3,2,1,0:T(8,128)(2,1)} %get-tuple-element.296), channel_id=1, source_target_pairs={{0,4},{4,0},{8,12},{12,8},{16,20},{20,16},{24,28},{28,24},{1,5},{5... | collective-permute-start | bytes 15925256 | tf_op jit(solution)/shard_map/ppermute | solution.py:42
  557.2 32.4 %collective-permute-start.40 = (bf16[2,2,2,144,1152]{4,3,2,1,0:T(8,128)(2,1)}, bf16[2,2,2,144,1152]{4,3,2,1,0:T(8,128)(2,1)}, u32[]{:S(2)}, u32[]{:S(2)}) collective-permute-start(bf16[2,2,2,144,1152]{4,3,2,1,0:T(8,128)(2,1)} %fusion), channel_id=1, source_target_pairs={{0,8},{4,20},{8,0},{12,28},{16,24},{20,4},{24,16},{28,12},{1,9},{5... | collective-permute-start | bytes 7962632 | tf_op jit(solution)/shard_map/ppermute | solution.py:79
  593.9 25.9 %collective-permute-start.42 = (bf16[2,2,144,1152]{3,2,1,0:T(8,128)(2,1)}, bf16[2,2,144,1152]{3,2,1,0:T(8,128)(2,1)}, u32[]{:S(2)}, u32[]{:S(2)}) collective-permute-start(bf16[2,2,144,1152]{3,2,1,0:T(8,128)(2,1)} %fusion.13), channel_id=1, source_target_pairs={{0,16},{4,12},{8,24},{12,4},{16,0},{20,28},{24,8},{28,20},{1,17},{... | collective-permute-start | bytes 3981320 | tf_op jit(solution)/shard_map/ppermute | solution.py:79
  600.3 19.5 %collective-permute-start.41 = (bf16[3,96,1152]{2,1,0:T(8,128)(2,1)}, bf16[3,96,1152]{2,1,0:T(8,128)(2,1)}, u32[]{:S(2)}, u32[]{:S(2)}) collective-permute-start(bf16[3,96,1152]{2,1,0:T(8,128)(2,1)} %fusion.59), channel_id=1, source_target_pairs={{0,2},{1,3},{2,0},{3,1},{4,5},{5,4},{6,7},{7,6},{8,10},{9,11},{10,... | collective-permute-start | bytes 1990664 | tf_op jit(solution)/shard_map/ppermute | solution.py:90
  630.4 28.9 %collective-permute-start.44 = (bf16[2,2,2,128,1152]{4,3,2,1,0:T(8,128)(2,1)S(1)}, bf16[2,2,2,128,1152]{4,3,2,1,0:T(8,128)(2,1)S(1)}, u32[]{:S(2)}, u32[]{:S(2)}) collective-permute-start(bf16[2,2,2,128,1152]{4,3,2,1,0:T(8,128)(2,1)S(1)} %fusion.2), channel_id=1, source_target_pairs={{0,8},{4,20},{8,0},{12,28},{16,24},{20,4},{24,16},{28,12},{1,9},{5... | collective-permute-start | bytes 7077896 | tf_op jit(solution)/shard_map/ppermute | solution.py:79
  635.3 17.8 %collective-permute-start.45 = (bf16[2,144,1152]{2,1,0:T(8,128)(2,1)S(1)}, bf16[2,144,1152]{2,1,0:T(8,128)(2,1)S(1)}, u32[]{:S(2)}, u32[]{:S(2)}) collective-permute-start(bf16[2,144,1152]{2,1,0:T(8,128)(2,1)S(1)} %fusion.60), channel_id=1, source_target_pairs={{0,1},{1,0},{2,3},{3,2},{4,6},{5,7},{6,4},{7,5},{8,9},{9,8},{10,11... | collective-permute-start | bytes 1990664 | tf_op jit(solution)/shard_map/ppermute | solution.py:90
  661.0 16.3 %collective-permute-start.46 = (bf16[2,2,128,1152]{3,2,1,0:T(8,128)(2,1)S(1)}, bf16[2,2,128,1152]{3,2,1,0:T(8,128)(2,1)S(1)}, u32[]{:S(2)}, u32[]{:S(2)}) collective-permute-start(bf16[2,2,128,1152]{3,2,1,0:T(8,128)(2,1)S(1)} %fusion.16), channel_id=1, source_target_pairs={{0,16},{4,12},{8,24},{12,4},{16,0},{20,28},{24,8},{28,20},{1,17},{... | collective-permute-start | bytes 3538952 | tf_op jit(solution)/shard_map/ppermute | solution.py:79
  663.9 11.6 %collective-permute-start.47 = (bf16[144,1152]{1,0:T(8,128)(2,1)S(1)}, bf16[144,1152]{1,0:T(8,128)(2,1)S(1)}, u32[]{:S(2)}, u32[]{:S(2)}) collective-permute-start(bf16[144,1152]{1,0:T(8,128)(2,1)S(1)} %fusion.63), channel_id=1, source_target_pairs={{0,2},{1,3},{2,0},{3,1},{4,5},{5,4},{6,7},{7,6},{8,10},{9,11},{10,... | collective-permute-start | bytes 995336 | tf_op jit(solution)/shard_map/ppermute | solution.py:90
  679.3 16.2 %collective-permute-start.48 = (bf16[2,128,1152]{2,1,0:T(8,128)(2,1)S(1)}, bf16[2,128,1152]{2,1,0:T(8,128)(2,1)S(1)}, u32[]{:S(2)}, u32[]{:S(2)}) collective-permute-start(bf16[2,128,1152]{2,1,0:T(8,128)(2,1)S(1)} %fusion.64), channel_id=1, source_target_pairs={{0,1},{1,0},{2,3},{3,2},{4,6},{5,7},{6,4},{7,5},{8,9},{9,8},{10,11... | collective-permute-start | bytes 1769480 | tf_op jit(solution)/shard_map/ppermute | solution.py:90
  682.1 10.9 %collective-permute-start.50 = (bf16[3,96,1152]{2,1,0:T(8,128)(2,1)S(1)}, bf16[3,96,1152]{2,1,0:T(8,128)(2,1)S(1)}, u32[]{:S(2)}, u32[]{:S(2)}) collective-permute-start(bf16[3,96,1152]{2,1,0:T(8,128)(2,1)S(1)} %fusion.52), channel_id=1, source_target_pairs={{0,8},{4,20},{8,0},{12,28},{16,24},{20,4},{24,16},{28,12},{1,9},{5... | collective-permute-start | bytes 1990664 | tf_op jit(solution)/shard_map/ppermute | solution.py:79
  697.0 26.5 %collective-permute-start.55 = (bf16[2,3,96,1152]{3,2,1,0:T(8,128)(2,1)S(1)}, bf16[2,3,96,1152]{3,2,1,0:T(8,128)(2,1)S(1)}, u32[]{:S(2)}, u32[]{:S(2)}) collective-permute-start(bf16[2,3,96,1152]{3,2,1,0:T(8,128)(2,1)S(1)} %pad_maximum_fusion.11), channel_id=1, source_target_pairs={{0,16},{4,12},{8,24},{12,4},{16,0},{20,28},{24,8},{28,20},{1,17},{... | collective-permute-start | bytes 3981320 | tf_op jit(solution)/shard_map/ppermute | solution.py:79
  711.9 13.6 %collective-permute-start.54 = (bf16[2,2,144,1152]{3,2,0,1:T(8,128)(2,1)S(1)}, bf16[2,2,144,1152]{3,2,0,1:T(8,128)(2,1)S(1)}, u32[]{:S(2)}, u32[]{:S(2)}) collective-permute-start(bf16[2,2,144,1152]{3,2,0,1:T(8,128)(2,1)S(1)} %pad_maximum_fusion.12), channel_id=1, source_target_pairs={{0,4},{4,0},{8,12},{12,8},{16,20},{20,16},{24,28},{28,24},{1,5},{5... | collective-permute-start | bytes 3981320 | tf_op jit(solution)/shard_map/ppermute | solution.py:42
  729.4 12.8 %collective-permute-start.56 = (bf16[2,128,1152]{2,1,0:T(8,128)(2,1)}, bf16[2,128,1152]{2,1,0:T(8,128)(2,1)}, u32[]{:S(2)}, u32[]{:S(2)}) collective-permute-start(bf16[2,128,1152]{2,1,0:T(8,128)(2,1)} %pad_maximum_fusion.19), channel_id=1, source_target_pairs={{0,16},{4,12},{8,24},{12,4},{16,0},{20,28},{24,8},{28,20},{1,17},{... | collective-permute-start | bytes 1769480 | tf_op jit(solution)/shard_map/ppermute | solution.py:79
  745.8 12.1 %collective-permute-start.60 = (bf16[75,1152]{1,0:T(8,128)(2,1)S(1)}, bf16[75,1152]{1,0:T(8,128)(2,1)S(1)}, u32[]{:S(2)}, u32[]{:S(2)}) collective-permute-start(bf16[75,1152]{1,0:T(8,128)(2,1)S(1)} %dynamic-slice_bitcast_fusion.2), channel_id=1, source_target_pairs={{0,2},{1,3},{2,0},{3,1},{4,6},{5,7},{6,4},{7,5},{8,10},{9,11},{10,... | collective-permute-start | bytes 518408 | tf_op jit(solution)/shard_map/ppermute | solution.py:42
  (140 other events, 1583.7 us)

commit v6 on v5

--- a/solution.py
+++ b/solution.py
@@ -1326,7 +1326,7 @@
     d_mix_all = share_core(d_mix_all)
     for stage in range(1, len(bits)):
         d_ffn_all = share_turn(d_ffn_all, stage)
-    d_qkv_all, d_mix_all, d_ffn_all = tie(d_qkv_all, d_mix_all, d_ffn_all)
+    d_qkv_all, d_mix_all = tie(d_qkv_all, d_mix_all)
     for stage in range(1, len(bits)):
         d_qkv_all = share_turn(d_qkv_all, stage)
     d_ffn_all = share_core(d_ffn_all)

time: 774 us -> 779 us (level)
  transfers between devices with their start and end apart: 61 -> 61, of which waited for: 33 -> 34; matrix products, arithmetic and copies ran while one was open for 28% -> 28% of each run, Pallas kernels for 26% -> 26%
where the time goes in v6:
time: 779 us; the launch traced here: 773 us
  Pallas kernels  229 us (29%)
  waiting for transfers between devices  195 us (25%)
  other arithmetic  139 us (18%)
  local copies, waits for them, and re-layouts  106 us (14%)
  starting transfers between devices  78.8 us (10%)
  matrix products  22.9 us (3%)
    pallas_call x4, Pallas kernels, ffn_call(): pl.pallas_call(functools.partial(ffn_kernel, core if direct else None, be...  112 us
    ppermute x16, waiting for transfers between devices, swap_z(): return lax.ppermute(values, ('dp', 'tensor'), pairs)  90.2 us
    ppermute x18, waiting for transfers between devices, swap_path(): lax.ppermute(values, 'dp', [(i, i ^ turns(i % 2)[number]) for i in range(...  71.3 us
    pallas_call x4, Pallas kernels, lane_call(): pl.pallas_call(kernel, grid=(features // LANES,), in_specs=[specs[kind] f...  40 us
    pallas_call x2, Pallas kernels, grads_call(): pl.pallas_call(functools.partial(grads_kernel, ranks, group, rows, cols,...  26.3 us
    ppermute x18, starting transfers between devices, swap_path(): lax.ppermute(values, 'dp', [(i, i ^ turns(i % 2)[number]) for i in range(...  25.2 us
    ppermute x21, waiting for transfers between devices, swap(): return lax.ppermute(values, axis, [(i, i ^ bit) for i in range(count)])  25 us
    convert_element_type x16, other arithmetic, total(): return summed.astype(bfloat)  23.5 us
  transfers between devices with their start and end apart: 61, of which 34 were waited for; matrix products, arithmetic and copies ran while one was open for 28% of the time, Pallas kernels for 26%

profile of v6, /device:TPU:0, one launch (start us, length us, event | category | flops | bytes accessed | tf_op | source)
XLA Modules:
  0.0 773.1 jit_solution(16929305573769553484)
XLA Ops:
  3.9 4.1 collective-permute-start
  23.8 6.0 pad_maximum_fusion.refs_0_
  29.9 6.8 collective-permute-done.1
  57.2 8.5 %collective-permute-done.6 = bf16[2,112,1152]{2,1,0:T(8,128)(2,1)S(1)} collective-permute-done((bf16[2,112,1152]{2,1,0:T(8,128)(2,1)S(1)}, bf16[2,112,1152]{2,1,0:T(8,128)(2,1)S(1)}, u32[]{:S(2)}, u32[]{:S(2)}) %collective-permute-start.6) | collective-permute-done | bytes 516128 | tf_op jit(solution)/shard_map/ppermute | solution.py:90
  81.7 7.8 %shard_map.348 = (bf16[4,288,1152]{2,1,0:T(8,128)(2,1)}, bf16[4,288,1152]{2,1,0:T(8,128)(2,1)}, bf16[4,288,1152]{2,1,0:T(8,128)(2,1)}) custom-call(bf16[8,112,1152]{2,1,0:T(8,128)(2,1)} %bitcast.552, bf16[2,3,112,1152]{3,2,1,0:T(8,128)(2,1)} %copy-done.16, bf16[2,3,112,1152]{3,2,1,0:T(8,128)(2,1)} %collective-permute-done.3.refs_1_, ...), custom_call_target="tpu_custom_call" | custom-call | bytes 4128768 | tf_op jit(solution)/shard_map/pallas_call | solution.py:255
  94.9 11.5 %shard_map.349 = (f32[416,1152]{1,0:T(8,128)}, f32[416,1152]{1,0:T(8,128)}, bf16[416,1152]{1,0:T(8,128)(2,1)}, bf16[416,1152]{1,0:T(8,128)(2,1)}, bf16[416,1152]...) custom-call(bf16[416,1152]{1,0:T(8,128)(2,1)} %fusion.27.normed.refs_3_, bf16[1152,1152]{1,0:T(8,128)(2,1)} %bitcast.539, ...), custom_call_target="tpu_custom_call" | custom-call | flops 552075264 | bytes 479232 | tf_op jit(solution)/shard_map/pallas_call | solution.py:731
  109.8 8.4 %collective-permute-done.13 = bf16[3,40,1152]{2,1,0:T(8,128)(2,1)S(1)} collective-permute-done((bf16[3,40,1152]{2,1,0:T(8,128)(2,1)S(1)}, bf16[3,40,1152]{2,1,0:T(8,128)(2,1)S(1)}, u32[]{:S(2)}, u32[]{:S(2)}) %collective-permute-start.13) | collective-permute-done | bytes 276512 | tf_op jit(solution)/shard_map/ppermute | solution.py:90
  120.9 6.8 collective-permute-done.16
  127.7 6.9 collective-permute-done.17
  135.9 4.5 collective-permute-start.19
  145.7 7.9 %shard_map.350 = (bf16[4,288,1152]{2,1,0:T(8,128)(2,1)}, bf16[4,288,1152]{2,1,0:T(8,128)(2,1)}, bf16[4,288,1152]{2,1,0:T(8,128)(2,1)}) custom-call(bf16[8,112,1152]{2,1,0:T(8,128)(2,1)} %bitcast.559, bf16[2,3,112,1152]{3,2,1,0:T(8,128)(2,1)} %pad_maximum_fusion.8.refs_0_, bf16[2,3,112,1152]{3,2,1,0:T(8,128)(2,1)} %collective-permute-done.14.refs_1_, ...), custom_call_target="tpu_custom_call" | custom-call | bytes 4128768 | tf_op jit(solution)/shard_map/pallas_call | solution.py:255
  153.6 4.8 pad.61
  170.7 7.0 shard_map.351
  202.9 6.0 add_convert_fusion.query_ref
  212.2 4.5 pad_maximum_fusion.2.refs_1_
  226.6 4.2 fusion.48
  230.8 16.6 %shard_map.352.refs_4_ = bf16[416,2048]{1,0:T(8,128)(2,1)} custom-call(bf16[416,2048]{1,0:T(8,128)(2,1)} %add_convert_fusion.query_ref, bf16[16,384,128]{2,1,0:T(8,128)(2,1)} %get-tuple-element.516.keys_ref, bf16[16,384,128]{2,1,0:T(8,128)(2,1)} %get-tuple-element.515.vals_ref, s32[416,1]{1,0:T(8,128)} %copy.254.length_ref), custom_call_target="tpu_custom_call" | custom-call | flops 327155712 | bytes 1703936 | tf_op jit(solution)/shard_map/pallas_call | solution.py:784
  247.4 6.0 fusion.241
  254.7 8.7 %collective-permute-done.25.refs_2_ = bf16[2,3,288,1152]{3,2,1,0:T(8,128)(2,1)} collective-permute-done((bf16[2,3,288,1152]{3,2,1,0:T(8,128)(2,1)}, bf16[2,3,288,1152]{3,2,1,0:T(8,128)(2,1)}, u32[]{:S(2)}, u32[]{:S(2)}) %collective-permute-start.25) | collective-permute-done | bytes 3981344 | tf_op jit(solution)/shard_map/ppermute | solution.py:79
  264.8 4.6 collective-permute-start.27
  269.4 6.2 collective-permute-done.28
  279.9 27.3 %shard_map.353 = (f32[416,1152]{1,0:T(8,128)}, f32[416,1152]{1,0:T(8,128)}, bf16[2,3,384,1152]{3,2,1,0:T(8,128)(2,1)}, f32[2,16,768]{2,1,0:T(8,128)}) custom-call(bf16[608,1152]{1,0:T(8,128)(2,1)} %pad_maximum_fusion.9.normed_ref, bf16[512,1152]{1,0:T(8,128)(2,1)} %pad_maximum_fusion.13.grad_ref, bf16[4,1152,224]{2,1,0:T(8,128)(2,1)} %bitcast.529, ...), custom_call_target="tpu_custom_call" | custom-call | flops 1755316224 | bytes 1769472 | tf_op jit(solution)/shard_map/pallas_call | solution.py:595
  307.2 5.3 collective-permute-start.30
  312.5 27.4 %shard_map.354 = (f32[416,1152]{1,0:T(8,128)}, f32[416,1152]{1,0:T(8,128)}, bf16[2,3,384,1152]{3,2,1,0:T(8,128)(2,1)}, f32[2,16,768]{2,1,0:T(8,128)}) custom-call(bf16[608,1152]{1,0:T(8,128)(2,1)} %pad_maximum_fusion.9.normed_ref, bf16[512,1152]{1,0:T(8,128)(2,1)} %pad_maximum_fusion.13.grad_ref, bf16[4,1152,224]{2,1,0:T(8,128)(2,1)} %bitcast.530, ...), custom_call_target="tpu_custom_call" | custom-call | flops 1755316224 | bytes 1769472 | tf_op jit(solution)/shard_map/pallas_call | solution.py:595
  341.2 28.6 %shard_map.355 = (f32[416,1152]{1,0:T(8,128)}, f32[416,1152]{1,0:T(8,128)}, bf16[2,3,384,1152]{3,2,1,0:T(8,128)(2,1)}, f32[2,16,768]{2,1,0:T(8,128)}) custom-call(bf16[608,1152]{1,0:T(8,128)(2,1)} %pad_maximum_fusion.9.normed_ref, bf16[512,1152]{1,0:T(8,128)(2,1)} %pad_maximum_fusion.13.grad_ref, bf16[4,1152,224]{2,1,0:T(8,128)(2,1)} %bitcast.531, ...), custom_call_target="tpu_custom_call" | custom-call | flops 1755316224 | bytes 1769472 | tf_op jit(solution)/shard_map/pallas_call | solution.py:595
  371.9 28.5 %shard_map.356 = (f32[416,1152]{1,0:T(8,128)}, f32[416,1152]{1,0:T(8,128)}, bf16[2,3,384,1152]{3,2,1,0:T(8,128)(2,1)}, f32[2,16,768]{2,1,0:T(8,128)}) custom-call(bf16[608,1152]{1,0:T(8,128)(2,1)} %pad_maximum_fusion.9.normed_ref, bf16[512,1152]{1,0:T(8,128)(2,1)} %pad_maximum_fusion.13.grad_ref, bf16[4,1152,224]{2,1,0:T(8,128)(2,1)} %bitcast.532, ...), custom_call_target="tpu_custom_call" | custom-call | flops 1755316224 | bytes 1769472 | tf_op jit(solution)/shard_map/pallas_call | solution.py:595
  400.5 6.7 select_reduce_fusion.7
  420.3 10.4 %collective-permute-done.32 = bf16[2,3,384,1152]{3,2,1,0:T(8,128)(2,1)} collective-permute-done((bf16[2,3,384,1152]{3,2,1,0:T(8,128)(2,1)}, bf16[2,3,384,1152]{3,2,1,0:T(8,128)(2,1)}, u32[]{:S(2)}, u32[]{:S(2)}) %collective-permute-start.32) | collective-permute-done | bytes 5308448 | tf_op jit(solution)/shard_map/ppermute | solution.py:79
  430.8 4.0 fusion.1
  443.2 18.2 %shard_map.357 = (bf16[416,2048]{1,0:T(8,128)(2,1)}, bf16[16,72,384]{2,1,0:T(8,128)(2,1)}, bf16[16,72,384]{2,1,0:T(8,128)(2,1)}, f32[1,2048]{1,0:T(1,128)}) custom-call(bf16[416,2048]{1,0:T(8,128)(2,1)} %add_convert_fusion.query_ref, bf16[16,384,128]{2,1,0:T(8,128)(2,1)} %get-tuple-element.516.keys_ref, bf16[16,384,128]{2,1,0:T(8,128)(2,1)} %get-tuple-element.515.vals_ref, ...), custom_call_target="tpu_custom_call" | custom-call | flops 327155712 | bytes 1703936 | tf_op jit(solution)/shard_map/pallas_call | solution.py:802
  481.6 9.2 %shard_map.358 = (bf16[416,1152]{1,0:T(8,128)(2,1)}, f32[40,1152]{1,0:T(8,128)}, f32[40,1152]{1,0:T(8,128)}) custom-call(bf16[416,1152]{1,0:T(8,128)(2,1)} %get-tuple-element.519.grad.refs_1_, bf16[1152,1152]{1,0:T(8,128)(2,1)} %bitcast.546, f32[416,1152]{1,0:T(8,128)} %get-tuple-element.273.ratio, f32[416,1152]{1,0:T(8,128)} %get-tuple-element.274.den, ...), custom_call_target="tpu_custom_call" | custom-call | flops 552075264 | bytes 479232 | tf_op jit(solution)/shard_map/pallas_call | solution.py:731
  492.0 11.0 %collective-permute-done.34 = bf16[3,2,96,1152]{3,2,0,1:T(8,128)(2,1)} collective-permute-done((bf16[3,2,96,1152]{3,2,0,1:T(8,128)(2,1)}, bf16[3,2,96,1152]{3,2,0,1:T(8,128)(2,1)}, u32[]{:S(2)}, u32[]{:S(2)}) %collective-permute-start.34) | collective-permute-done | bytes 1327136 | tf_op jit(solution)/shard_map/ppermute | solution.py:90
  506.4 11.1 %collective-permute-done.35 = bf16[3,40,1152]{2,1,0:T(8,128)(2,1)S(1)} collective-permute-done((bf16[3,40,1152]{2,1,0:T(8,128)(2,1)S(1)}, bf16[3,40,1152]{2,1,0:T(8,128)(2,1)S(1)}, u32[]{:S(2)}, u32[]{:S(2)}) %collective-permute-start.35) | collective-permute-done | bytes 276512 | tf_op jit(solution)/shard_map/ppermute | solution.py:90
  518.6 15.3 %shard_map.359 = (bf16[4,4,144,1152]{3,2,1,0:T(8,128)(2,1)}, bf16[4,4,144,1152]{3,2,1,0:T(8,128)(2,1)}) custom-call(bf16[416,1152]{1,0:T(8,128)(2,1)} %get-tuple-element.291.refs_0_, bf16[416,1152]{1,0:T(8,128)(2,1)} %get-tuple-element.519.grad.refs_1_, bf16[416,2048]{1,0:T(8,128)(2,1)} %get-tuple-element.272.refs_2_, ...), custom_call_target="tpu_custom_call" | custom-call | flops 552075264 | bytes 2654208 | tf_op jit(solution)/shard_map/pallas_call | solution.py:314
  553.1 4.0 fusion
  560.2 12.3 %shard_map.360 = (bf16[416,1152]{1,0:T(8,128)(2,1)}, bf16[416,1152]{1,0:T(8,128)(2,1)}, f32[416,1152]{1,0:T(8,128)}) custom-call(bf16[416,1152]{1,0:T(8,128)(2,1)} %get-tuple-element.276.dquery.refs_0_, bf16[416,1152]{1,0:T(8,128)(2,1)} %get-tuple-element.277.keys, bf16[416,1152]{1,0:T(8,128)(2,1)} %get-tuple-element.278.values, ...), custom_call_target="tpu_custom_call" | custom-call | flops 552075264 | bytes 479232 | tf_op jit(solution)/shard_map/pallas_call | solution.py:731
  582.8 6.8 collective-permute-done.40
  603.8 11.1 %shard_map.361 = (bf16[4,4,128,1152]{3,2,1,0:T(8,128)(2,1)}, bf16[4,4,128,1152]{3,2,1,0:T(8,128)(2,1)}) custom-call(bf16[416,1152]{1,0:T(8,128)(2,1)} %get-tuple-element.276.dquery.refs_0_, bf16[416,1152]{1,0:T(8,128)(2,1)} %get-tuple-element.299.refs_1_, bf16[416,1152]{1,0:T(8,128)(2,1)} %get-tuple-element.300.refs_2_, ...), custom_call_target="tpu_custom_call" | custom-call | flops 552075264 | bytes 2359296 | tf_op jit(solution)/shard_map/pallas_call | solution.py:314
  614.9 5.0 collective-permute-done.41
  621.9 6.2 collective-permute-done.43
  636.1 17.1 %collective-permute-done.45 = bf16[2,144,1152]{2,1,0:T(8,128)(2,1)S(1)} collective-permute-done((bf16[2,144,1152]{2,1,0:T(8,128)(2,1)S(1)}, bf16[2,144,1152]{2,1,0:T(8,128)(2,1)S(1)}, u32[]{:S(2)}, u32[]{:S(2)}) %collective-permute-start.45) | collective-permute-done | bytes 663584 | tf_op jit(solution)/shard_map/ppermute | solution.py:90
  653.1 6.3 collective-permute-done.44
  664.1 11.4 %collective-permute-done.47 = bf16[144,1152]{1,0:T(8,128)(2,1)S(1)} collective-permute-done((bf16[144,1152]{1,0:T(8,128)(2,1)S(1)}, bf16[144,1152]{1,0:T(8,128)(2,1)S(1)}, u32[]{:S(2)}, u32[]{:S(2)}) %collective-permute-start.47) | collective-permute-done | bytes 331808 | tf_op jit(solution)/shard_map/ppermute | solution.py:90
  686.1 7.0 collective-permute-done.50
  698.2 7.9 %collective-permute-done.52 = bf16[2,144,1152]{2,1,0:T(8,128)(2,1)S(1)} collective-permute-done((bf16[2,144,1152]{2,1,0:T(8,128)(2,1)S(1)}, bf16[2,144,1152]{2,1,0:T(8,128)(2,1)S(1)}, u32[]{:S(2)}, u32[]{:S(2)}) %collective-permute-start.52) | collective-permute-done | bytes 663584 | tf_op jit(solution)/shard_map/ppermute | solution.py:79
  712.1 5.2 collective-permute-done.53
  718.2 5.3 collective-permute-done.56
  758.5 4.9 collective-permute-done.60
  (684 shorter events, 308.3 us)
Async XLA Ops:
  3.9 18.2 %collective-permute-start = (bf16[112,1152]{1,0:T(8,128)(2,1)S(1)}, bf16[112,1152]{1,0:T(8,128)(2,1)S(1)}, u32[]{:S(2)}, u32[]{:S(2)}) collective-permute-start(bf16[112,1152]{1,0:T(8,128)(2,1)S(1)} %fusion.253), channel_id=1, source_target_pairs={{0,2},{1,3},{2,0},{3,1},{4,5},{5,4},{6,7},{7,6},{8,10},{9,11},{10,... | collective-permute-start | bytes 774152 | tf_op jit(solution)/shard_map/ppermute | solution.py:90
  22.2 14.4 %collective-permute-start.1 = (bf16[2,112,1152]{2,1,0:T(8,128)(2,1)S(1)}, bf16[2,112,1152]{2,1,0:T(8,128)(2,1)S(1)}, u32[]{:S(2)}, u32[]{:S(2)}) collective-permute-start(bf16[2,112,1152]{2,1,0:T(8,128)(2,1)S(1)} %pad_maximum_fusion.20), channel_id=1, source_target_pairs={{0,1},{1,0},{2,3},{3,2},{4,6},{5,7},{6,4},{7,5},{8,9},{9,8},{10,11... | collective-permute-start | bytes 1548296 | tf_op jit(solution)/shard_map/ppermute | solution.py:90
  38.5 14.0 %collective-permute-start.5 = (bf16[112,1152]{1,0:T(8,128)(2,1)S(1)}, bf16[112,1152]{1,0:T(8,128)(2,1)S(1)}, u32[]{:S(2)}, u32[]{:S(2)}) collective-permute-start(bf16[112,1152]{1,0:T(8,128)(2,1)S(1)} %dynamic-slice_bitcast_fusion.1), channel_id=1, source_target_pairs={{0,2},{1,3},{2,0},{3,1},{4,5},{5,4},{6,7},{7,6},{8,10},{9,11},{10,... | collective-permute-start | bytes 774152 | tf_op jit(solution)/shard_map/ppermute | solution.py:90
  38.5 11.9 %collective-permute-start.2 = (bf16[3,112,1152]{2,1,0:T(8,128)(2,1)S(1)}, bf16[3,112,1152]{2,1,0:T(8,128)(2,1)S(1)}, u32[]{:S(2)}, u32[]{:S(2)}) collective-permute-start(bf16[3,112,1152]{2,1,0:T(8,128)(2,1)S(1)} %pad_maximum_fusion.16), channel_id=1, source_target_pairs={{0,8},{4,20},{8,0},{12,28},{16,24},{20,4},{24,16},{28,12},{1,9},{5... | collective-permute-start | bytes 2322440 | tf_op jit(solution)/shard_map/ppermute | solution.py:79
  50.7 16.4 %collective-permute-start.4 = (bf16[2,3,112,1152]{3,2,1,0:T(8,128)(2,1)S(1)}, bf16[2,3,112,1152]{3,2,1,0:T(8,128)(2,1)S(1)}, u32[]{:S(2)}, u32[]{:S(2)}) collective-permute-start(bf16[2,3,112,1152]{3,2,1,0:T(8,128)(2,1)S(1)} %pad_maximum_fusion.7.refs_0_), channel_id=1, source_target_pairs={{0,4},{4,0},{8,12},{12,8},{16,20},{20,16},{24,28},{28,24},{1,5},{5... | collective-permute-start | bytes 4644872 | tf_op jit(solution)/shard_map/ppermute | solution.py:42
  50.7 20.3 %collective-permute-start.3 = (bf16[2,3,112,1152]{3,2,1,0:T(8,128)(2,1)S(1)}, bf16[2,3,112,1152]{3,2,1,0:T(8,128)(2,1)}, u32[]{:S(2)}, u32[]{:S(2)}) collective-permute-start(bf16[2,3,112,1152]{3,2,1,0:T(8,128)(2,1)S(1)} %pad_maximum_fusion.7.refs_0_), channel_id=1, source_target_pairs={{0,16},{4,12},{8,24},{12,4},{16,0},{20,28},{24,8},{28,20},{1,17},{... | collective-permute-start | bytes 4644872 | tf_op jit(solution)/shard_map/ppermute | solution.py:79
  52.5 13.2 %collective-permute-start.6 = (bf16[2,112,1152]{2,1,0:T(8,128)(2,1)S(1)}, bf16[2,112,1152]{2,1,0:T(8,128)(2,1)S(1)}, u32[]{:S(2)}, u32[]{:S(2)}) collective-permute-start(bf16[2,112,1152]{2,1,0:T(8,128)(2,1)S(1)} %pad_maximum_fusion.21), channel_id=1, source_target_pairs={{0,1},{1,0},{2,3},{3,2},{4,6},{5,7},{6,4},{7,5},{8,9},{9,8},{10,11... | collective-permute-start | bytes 1548296 | tf_op jit(solution)/shard_map/ppermute | solution.py:90
  55.1 11.9 %collective-permute-start.7 = (bf16[40,1152]{1,0:T(8,128)(2,1)S(1)}, bf16[40,1152]{1,0:T(8,128)(2,1)S(1)}, u32[]{:S(2)}, u32[]{:S(2)}) collective-permute-start(bf16[40,1152]{1,0:T(8,128)(2,1)S(1)} %fusion.252), channel_id=1, source_target_pairs={{0,2},{1,3},{2,0},{3,1},{4,6},{5,7},{6,4},{7,5},{8,10},{9,11},{10,... | collective-permute-start | bytes 276488 | tf_op jit(solution)/shard_map/ppermute | solution.py:42
  76.3 13.3 %collective-permute-start.9 = (bf16[3,112,1152]{2,1,0:T(8,128)(2,1)S(1)}, bf16[3,112,1152]{2,1,0:T(8,128)(2,1)}, u32[]{:S(2)}, u32[]{:S(2)}) collective-permute-start(bf16[3,112,1152]{2,1,0:T(8,128)(2,1)S(1)} %pad_maximum_fusion.17), channel_id=1, source_target_pairs={{0,8},{4,20},{8,0},{12,28},{16,24},{20,4},{24,16},{28,12},{1,9},{5... | collective-permute-start | bytes 2322440 | tf_op jit(solution)/shard_map/ppermute | solution.py:79
  78.5 13.4 %collective-permute-start.10 = (bf16[2,40,1152]{2,1,0:T(8,128)(2,1)S(1)}, bf16[2,40,1152]{2,1,0:T(8,128)(2,1)S(1)}, u32[]{:S(2)}, u32[]{:S(2)}) collective-permute-start(bf16[2,40,1152]{2,1,0:T(8,128)(2,1)S(1)} %pad_maximum_fusion.30), channel_id=1, source_target_pairs={{0,1},{1,0},{2,3},{3,2},{4,5},{5,4},{6,7},{7,6},{8,9},{9,8},{10,11... | collective-permute-start | bytes 552968 | tf_op jit(solution)/shard_map/ppermute | solution.py:42
  79.7 27.8 %collective-permute-start.12 = (bf16[288,1152]{1,0:T(8,128)(2,1)}, bf16[288,1152]{1,0:T(8,128)(2,1)}, u32[]{:S(2)}, u32[]{:S(2)}) collective-permute-start(bf16[288,1152]{1,0:T(8,128)(2,1)} %bitcast.31), channel_id=1, source_target_pairs={{0,2},{1,3},{2,0},{3,1},{4,5},{5,4},{6,7},{7,6},{8,10},{9,11},{10,... | collective-permute-start | bytes 1990664 | tf_op jit(solution)/shard_map/ppermute | solution.py:90
  92.0 26.4 %collective-permute-start.15 = (bf16[2,3,112,1152]{3,2,1,0:T(8,128)(2,1)}, bf16[2,3,112,1152]{3,2,1,0:T(8,128)(2,1)}, u32[]{:S(2)}, u32[]{:S(2)}) collective-permute-start(bf16[2,3,112,1152]{3,2,1,0:T(8,128)(2,1)} %pad_maximum_fusion.8.refs_0_), channel_id=1, source_target_pairs={{0,4},{4,0},{8,12},{12,8},{16,20},{20,16},{24,28},{28,24},{1,5},{5... | collective-permute-start | bytes 4644872 | tf_op jit(solution)/shard_map/ppermute | solution.py:42
  92.0 26.4 %collective-permute-start.14 = (bf16[2,3,112,1152]{3,2,1,0:T(8,128)(2,1)}, bf16[2,3,112,1152]{3,2,1,0:T(8,128)(2,1)}, u32[]{:S(2)}, u32[]{:S(2)}) collective-permute-start(bf16[2,3,112,1152]{3,2,1,0:T(8,128)(2,1)} %pad_maximum_fusion.8.refs_0_), channel_id=1, source_target_pairs={{0,16},{4,12},{8,24},{12,4},{16,0},{20,28},{24,8},{28,20},{1,17},{... | collective-permute-start | bytes 4644872 | tf_op jit(solution)/shard_map/ppermute | solution.py:79
  94.5 13.0 %collective-permute-start.11 = (bf16[4,40,1152]{2,1,0:T(8,128)(2,1)}, bf16[4,40,1152]{2,1,0:T(8,128)(2,1)S(1)}, u32[]{:S(2)}, u32[]{:S(2)}) collective-permute-start(bf16[4,40,1152]{2,1,0:T(8,128)(2,1)} %pad_maximum_fusion.24), channel_id=1, source_target_pairs={{0,4},{4,0},{8,12},{12,8},{16,20},{20,16},{24,28},{28,24},{1,5},{5... | collective-permute-start | bytes 1105928 | tf_op jit(solution)/shard_map/ppermute | solution.py:42
  118.3 16.2 %collective-permute-start.18 = (bf16[2,3,112,1152]{3,2,1,0:T(8,128)(2,1)}, bf16[2,3,112,1152]{3,2,1,0:T(8,128)(2,1)}, u32[]{:S(2)}, u32[]{:S(2)}) collective-permute-start(bf16[2,3,112,1152]{3,2,1,0:T(8,128)(2,1)} %collective-permute-done.14.refs_1_), channel_id=1, source_target_pairs={{0,4},{4,0},{8,12},{12,8},{16,20},{20,16},{24,28},{28,24},{1,5},{5... | collective-permute-start | bytes 4644872 | tf_op jit(solution)/shard_map/ppermute | solution.py:42
  119.5 15.0 %collective-permute-start.17 = (bf16[348,288]{0,1:T(8,128)(2,1)S(1)}, bf16[348,288]{0,1:T(8,128)(2,1)S(1)}, u32[]{:S(2)}, u32[]{:S(2)}) collective-permute-start(bf16[348,288]{0,1:T(8,128)(2,1)S(1)} %pad_maximum_fusion.29), channel_id=1, source_target_pairs={{0,2},{1,3},{2,0},{3,1},{4,6},{5,7},{6,4},{7,5},{8,10},{9,11},{10,... | collective-permute-start | bytes 601352 | tf_op jit(solution)/shard_map/ppermute | solution.py:42
  134.6 26.6 %collective-permute-start.20 = (bf16[40,1152]{1,0:T(8,128)(2,1)S(1)}, bf16[40,1152]{1,0:T(8,128)(2,1)S(1)}, u32[]{:S(2)}, u32[]{:S(2)}) collective-permute-start(bf16[40,1152]{1,0:T(8,128)(2,1)S(1)} %get-tuple-element.571), channel_id=1, source_target_pairs={{4,0},{8,4},{12,8},{16,12},{20,16},{24,20},{28,24},{5,1},{9,5},{13... | collective-permute-start | bytes 276488 | tf_op jit(solution)/shard_map/ppermute | solution.py:1028
  135.9 25.3 %collective-permute-start.19 = (bf16[40,1152]{1,0:T(8,128)(2,1)S(1)}, bf16[40,1152]{1,0:T(8,128)(2,1)S(1)}, u32[]{:S(2)}, u32[]{:S(2)}) collective-permute-start(bf16[40,1152]{1,0:T(8,128)(2,1)S(1)} %get-tuple-element.572), channel_id=1, source_target_pairs={{0,4},{4,8},{8,12},{12,16},{16,20},{20,24},{24,28},{1,5},{5,9},{9,... | collective-permute-start | bytes 276488 | tf_op jit(solution)/shard_map/ppermute | solution.py:1027
  141.2 23.4 %collective-permute-start.21 = (bf16[2,348,288]{1,2,0:T(8,128)(2,1)}, bf16[2,348,288]{1,2,0:T(8,128)(2,1)S(1)}, u32[]{:S(2)}, u32[]{:S(2)}) collective-permute-start(bf16[2,348,288]{1,2,0:T(8,128)(2,1)} %pad_maximum_fusion.22), channel_id=1, source_target_pairs={{0,1},{1,0},{2,3},{3,2},{4,5},{5,4},{6,7},{7,6},{8,9},{9,8},{10,11... | collective-permute-start | bytes 1202696 | tf_op jit(solution)/shard_map/ppermute | solution.py:42
  143.7 39.3 %collective-permute-start.22 = (bf16[2,288,1152]{2,1,0:T(8,128)(2,1)}, bf16[2,288,1152]{2,1,0:T(8,128)(2,1)}, u32[]{:S(2)}, u32[]{:S(2)}) collective-permute-start(bf16[2,288,1152]{2,1,0:T(8,128)(2,1)} %pad_maximum_fusion.10), channel_id=1, source_target_pairs={{0,1},{1,0},{2,3},{3,2},{4,6},{5,7},{6,4},{7,5},{8,9},{9,8},{10,11... | collective-permute-start | bytes 3981320 | tf_op jit(solution)/shard_map/ppermute | solution.py:90
  167.6 19.4 %collective-permute-start.23 = (bf16[4,348,288]{1,2,0:T(8,128)(2,1)}, bf16[4,348,288]{1,2,0:T(8,128)(2,1)}, u32[]{:S(2)}, u32[]{:S(2)}) collective-permute-start(bf16[4,348,288]{1,2,0:T(8,128)(2,1)} %pad_maximum_fusion.15), channel_id=1, source_target_pairs={{0,4},{4,0},{8,12},{12,8},{16,20},{20,16},{24,28},{28,24},{1,5},{5... | collective-permute-start | bytes 2405384 | tf_op jit(solution)/shard_map/ppermute | solution.py:42
  187.0 25.2 %collective-permute-start.24 = (bf16[3,288,1152]{2,1,0:T(8,128)(2,1)}, bf16[3,288,1152]{2,1,0:T(8,128)(2,1)}, u32[]{:S(2)}, u32[]{:S(2)}) collective-permute-start(bf16[3,288,1152]{2,1,0:T(8,128)(2,1)} %pad_maximum_fusion.6), channel_id=1, source_target_pairs={{0,8},{4,20},{8,0},{12,28},{16,24},{20,4},{24,16},{28,12},{1,9},{5... | collective-permute-start | bytes 5971976 | tf_op jit(solution)/shard_map/ppermute | solution.py:79
  216.7 38.0 %collective-permute-start.26 = (bf16[2,3,288,1152]{3,2,1,0:T(8,128)(2,1)}, bf16[2,3,288,1152]{3,2,1,0:T(8,128)(2,1)}, u32[]{:S(2)}, u32[]{:S(2)}) collective-permute-start(bf16[2,3,288,1152]{3,2,1,0:T(8,128)(2,1)} %pad_maximum_fusion.2.refs_1_), channel_id=1, source_target_pairs={{0,4},{4,0},{8,12},{12,8},{16,20},{20,16},{24,28},{28,24},{1,5},{5... | collective-permute-start | bytes 11943944 | tf_op jit(solution)/shard_map/ppermute | solution.py:42
  216.7 46.6 %collective-permute-start.25 = (bf16[2,3,288,1152]{3,2,1,0:T(8,128)(2,1)}, bf16[2,3,288,1152]{3,2,1,0:T(8,128)(2,1)}, u32[]{:S(2)}, u32[]{:S(2)}) collective-permute-start(bf16[2,3,288,1152]{3,2,1,0:T(8,128)(2,1)} %pad_maximum_fusion.2.refs_1_), channel_id=1, source_target_pairs={{0,16},{4,12},{8,24},{12,4},{16,0},{20,28},{24,8},{28,20},{1,17},{... | collective-permute-start | bytes 11943944 | tf_op jit(solution)/shard_map/ppermute | solution.py:79
  263.4 16.6 %collective-permute-start.29 = (bf16[2,3,288,1152]{3,2,1,0:T(8,128)(2,1)}, bf16[2,3,288,1152]{3,2,1,0:T(8,128)(2,1)}, u32[]{:S(2)}, u32[]{:S(2)}) collective-permute-start(bf16[2,3,288,1152]{3,2,1,0:T(8,128)(2,1)} %collective-permute-done.25.refs_2_), channel_id=1, source_target_pairs={{0,4},{4,0},{8,12},{12,8},{16,20},{20,16},{24,28},{28,24},{1,5},{5... | collective-permute-start | bytes 11943944 | tf_op jit(solution)/shard_map/ppermute | solution.py:42
  263.5 12.1 %collective-permute-start.28 = (bf16[144,1152]{1,0:T(8,128)(2,1)S(1)}, bf16[144,1152]{1,0:T(8,128)(2,1)S(1)}, u32[]{:S(2)}, u32[]{:S(2)}) collective-permute-start(bf16[144,1152]{1,0:T(8,128)(2,1)S(1)} %pad_maximum_fusion.26), channel_id=1, source_target_pairs={{1,0},{2,1},{3,2},{4,3},{5,4},{6,5},{7,6},{8,7},{9,8},{10,9},{11,1... | collective-permute-start | bytes 995336 | tf_op jit(solution)/shard_map/ppermute | solution.py:48
  264.8 12.8 %collective-permute-start.27 = (bf16[144,1152]{1,0:T(8,128)(2,1)S(1)}, bf16[144,1152]{1,0:T(8,128)(2,1)S(1)}, u32[]{:S(2)}, u32[]{:S(2)}) collective-permute-start(bf16[144,1152]{1,0:T(8,128)(2,1)S(1)} %pad_maximum_fusion.25), channel_id=1, source_target_pairs={{0,1},{1,2},{2,3},{3,4},{4,5},{5,6},{6,7},{7,8},{8,9},{9,10},{10,1... | collective-permute-start | bytes 995336 | tf_op jit(solution)/shard_map/ppermute | solution.py:48
  307.2 32.7 %collective-permute-start.30 = (bf16[2,3,384,1152]{3,2,1,0:T(8,128)(2,1)}, bf16[2,3,384,1152]{3,2,1,0:T(8,128)(2,1)}, u32[]{:S(2)}, u32[]{:S(2)}) collective-permute-start(bf16[2,3,384,1152]{3,2,1,0:T(8,128)(2,1)} %get-tuple-element.243), channel_id=1, source_target_pairs={{0,4},{4,0},{8,12},{12,8},{16,20},{20,16},{24,28},{28,24},{1,5},{5... | collective-permute-start | bytes 15925256 | tf_op jit(solution)/shard_map/ppermute | solution.py:42
  339.9 30.0 %collective-permute-start.31 = (bf16[2,3,384,1152]{3,2,1,0:T(8,128)(2,1)}, bf16[2,3,384,1152]{3,2,1,0:T(8,128)(2,1)}, u32[]{:S(2)}, u32[]{:S(2)}) collective-permute-start(bf16[2,3,384,1152]{3,2,1,0:T(8,128)(2,1)} %get-tuple-element.249), channel_id=1, source_target_pairs={{0,4},{4,0},{8,12},{12,8},{16,20},{20,16},{24,28},{28,24},{1,5},{5... | collective-permute-start | bytes 15925256 | tf_op jit(solution)/shard_map/ppermute | solution.py:42
  370.0 60.8 %collective-permute-start.32 = (bf16[2,3,384,1152]{3,2,1,0:T(8,128)(2,1)}, bf16[2,3,384,1152]{3,2,1,0:T(8,128)(2,1)}, u32[]{:S(2)}, u32[]{:S(2)}) collective-permute-start(bf16[2,3,384,1152]{3,2,1,0:T(8,128)(2,1)} %get-tuple-element.267), channel_id=1, source_target_pairs={{0,8},{4,20},{8,0},{12,28},{16,24},{20,4},{24,16},{28,12},{1,9},{5... | collective-permute-start | bytes 15925256 | tf_op jit(solution)/shard_map/ppermute | solution.py:79
  434.8 33.3 %collective-permute-start.33 = (bf16[3,2,2,96,1152]{4,3,0,1,2:T(8,128)(2,1)}, bf16[3,2,2,96,1152]{4,3,0,1,2:T(8,128)(2,1)}, u32[]{:S(2)}, u32[]{:S(2)}) collective-permute-start(bf16[3,2,2,96,1152]{4,3,0,1,2:T(8,128)(2,1)} %fusion.1), channel_id=1, source_target_pairs={{0,16},{4,12},{8,24},{12,4},{16,0},{20,28},{24,8},{28,20},{1,17},{... | collective-permute-start | bytes 7962632 | tf_op jit(solution)/shard_map/ppermute | solution.py:79
  471.8 31.2 %collective-permute-start.34 = (bf16[3,2,96,1152]{3,2,0,1:T(8,128)(2,1)}, bf16[3,2,96,1152]{3,2,0,1:T(8,128)(2,1)}, u32[]{:S(2)}, u32[]{:S(2)}) collective-permute-start(bf16[3,2,96,1152]{3,2,0,1:T(8,128)(2,1)} %fusion.49), channel_id=1, source_target_pairs={{0,1},{1,0},{2,3},{3,2},{4,6},{5,7},{6,4},{7,5},{8,9},{9,8},{10,11... | collective-permute-start | bytes 3981320 | tf_op jit(solution)/shard_map/ppermute | solution.py:90
  503.0 14.4 %collective-permute-start.35 = (bf16[3,40,1152]{2,1,0:T(8,128)(2,1)S(1)}, bf16[3,40,1152]{2,1,0:T(8,128)(2,1)S(1)}, u32[]{:S(2)}, u32[]{:S(2)}) collective-permute-start(bf16[3,40,1152]{2,1,0:T(8,128)(2,1)S(1)} %pad_maximum_fusion.28), channel_id=1, source_target_pairs={{0,2},{1,3},{2,0},{3,1},{4,5},{5,4},{6,7},{7,6},{8,10},{9,11},{10,... | collective-permute-start | bytes 829448 | tf_op jit(solution)/shard_map/ppermute | solution.py:90
  517.5 16.4 %collective-permute-start.36 = (bf16[3,40,1152]{2,1,0:T(8,128)(2,1)S(1)}, bf16[3,40,1152]{2,1,0:T(8,128)(2,1)S(1)}, u32[]{:S(2)}, u32[]{:S(2)}) collective-permute-start(bf16[3,40,1152]{2,1,0:T(8,128)(2,1)S(1)} %add_convert_fusion.7), channel_id=1, source_target_pairs={{0,1},{1,0},{2,3},{3,2},{4,6},{5,7},{6,4},{7,5},{8,9},{9,8},{10,11... | collective-permute-start | bytes 829448 | tf_op jit(solution)/shard_map/ppermute | solution.py:90
  534.0 19.2 %collective-permute-start.39 = (bf16[4,4,144,1152]{3,2,1,0:T(8,128)(2,1)}, bf16[4,4,144,1152]{3,2,1,0:T(8,128)(2,1)}, u32[]{:S(2)}, u32[]{:S(2)}) collective-permute-start(bf16[4,4,144,1152]{3,2,1,0:T(8,128)(2,1)} %get-tuple-element.295), channel_id=1, source_target_pairs={{0,4},{4,0},{8,12},{12,8},{16,20},{20,16},{24,28},{28,24},{1,5},{5... | collective-permute-start | bytes 15925256 | tf_op jit(solution)/shard_map/ppermute | solution.py:42
  557.2 32.4 %collective-permute-start.40 = (bf16[2,2,2,144,1152]{4,3,2,1,0:T(8,128)(2,1)}, bf16[2,2,2,144,1152]{4,3,2,1,0:T(8,128)(2,1)}, u32[]{:S(2)}, u32[]{:S(2)}) collective-permute-start(bf16[2,2,2,144,1152]{4,3,2,1,0:T(8,128)(2,1)} %fusion), channel_id=1, source_target_pairs={{0,8},{4,20},{8,0},{12,28},{16,24},{20,4},{24,16},{28,12},{1,9},{5... | collective-permute-start | bytes 7962632 | tf_op jit(solution)/shard_map/ppermute | solution.py:79
  593.8 26.1 %collective-permute-start.42 = (bf16[2,2,144,1152]{3,2,1,0:T(8,128)(2,1)}, bf16[2,2,144,1152]{3,2,1,0:T(8,128)(2,1)}, u32[]{:S(2)}, u32[]{:S(2)}) collective-permute-start(bf16[2,2,144,1152]{3,2,1,0:T(8,128)(2,1)} %fusion.13), channel_id=1, source_target_pairs={{0,16},{4,12},{8,24},{12,4},{16,0},{20,28},{24,8},{28,20},{1,17},{... | collective-permute-start | bytes 3981320 | tf_op jit(solution)/shard_map/ppermute | solution.py:79
  600.4 19.4 %collective-permute-start.41 = (bf16[3,96,1152]{2,1,0:T(8,128)(2,1)}, bf16[3,96,1152]{2,1,0:T(8,128)(2,1)}, u32[]{:S(2)}, u32[]{:S(2)}) collective-permute-start(bf16[3,96,1152]{2,1,0:T(8,128)(2,1)} %fusion.59), channel_id=1, source_target_pairs={{0,2},{1,3},{2,0},{3,1},{4,5},{5,4},{6,7},{7,6},{8,10},{9,11},{10,... | collective-permute-start | bytes 1990664 | tf_op jit(solution)/shard_map/ppermute | solution.py:90
  630.5 28.9 %collective-permute-start.44 = (bf16[2,2,2,128,1152]{4,3,2,1,0:T(8,128)(2,1)S(1)}, bf16[2,2,2,128,1152]{4,3,2,1,0:T(8,128)(2,1)S(1)}, u32[]{:S(2)}, u32[]{:S(2)}) collective-permute-start(bf16[2,2,2,128,1152]{4,3,2,1,0:T(8,128)(2,1)S(1)} %fusion.2), channel_id=1, source_target_pairs={{0,8},{4,20},{8,0},{12,28},{16,24},{20,4},{24,16},{28,12},{1,9},{5... | collective-permute-start | bytes 7077896 | tf_op jit(solution)/shard_map/ppermute | solution.py:79
  635.3 17.8 %collective-permute-start.45 = (bf16[2,144,1152]{2,1,0:T(8,128)(2,1)S(1)}, bf16[2,144,1152]{2,1,0:T(8,128)(2,1)S(1)}, u32[]{:S(2)}, u32[]{:S(2)}) collective-permute-start(bf16[2,144,1152]{2,1,0:T(8,128)(2,1)S(1)} %fusion.60), channel_id=1, source_target_pairs={{0,1},{1,0},{2,3},{3,2},{4,6},{5,7},{6,4},{7,5},{8,9},{9,8},{10,11... | collective-permute-start | bytes 1990664 | tf_op jit(solution)/shard_map/ppermute | solution.py:90
  661.1 16.3 %collective-permute-start.46 = (bf16[2,2,128,1152]{3,2,1,0:T(8,128)(2,1)S(1)}, bf16[2,2,128,1152]{3,2,1,0:T(8,128)(2,1)S(1)}, u32[]{:S(2)}, u32[]{:S(2)}) collective-permute-start(bf16[2,2,128,1152]{3,2,1,0:T(8,128)(2,1)S(1)} %fusion.16), channel_id=1, source_target_pairs={{0,16},{4,12},{8,24},{12,4},{16,0},{20,28},{24,8},{28,20},{1,17},{... | collective-permute-start | bytes 3538952 | tf_op jit(solution)/shard_map/ppermute | solution.py:79
  663.9 11.5 %collective-permute-start.47 = (bf16[144,1152]{1,0:T(8,128)(2,1)S(1)}, bf16[144,1152]{1,0:T(8,128)(2,1)S(1)}, u32[]{:S(2)}, u32[]{:S(2)}) collective-permute-start(bf16[144,1152]{1,0:T(8,128)(2,1)S(1)} %fusion.63), channel_id=1, source_target_pairs={{0,2},{1,3},{2,0},{3,1},{4,5},{5,4},{6,7},{7,6},{8,10},{9,11},{10,... | collective-permute-start | bytes 995336 | tf_op jit(solution)/shard_map/ppermute | solution.py:90
  679.3 16.2 %collective-permute-start.48 = (bf16[2,128,1152]{2,1,0:T(8,128)(2,1)S(1)}, bf16[2,128,1152]{2,1,0:T(8,128)(2,1)S(1)}, u32[]{:S(2)}, u32[]{:S(2)}) collective-permute-start(bf16[2,128,1152]{2,1,0:T(8,128)(2,1)S(1)} %fusion.64), channel_id=1, source_target_pairs={{0,1},{1,0},{2,3},{3,2},{4,6},{5,7},{6,4},{7,5},{8,9},{9,8},{10,11... | collective-permute-start | bytes 1769480 | tf_op jit(solution)/shard_map/ppermute | solution.py:90
  696.9 26.6 %collective-permute-start.56 = (bf16[2,3,96,1152]{3,2,1,0:T(8,128)(2,1)S(1)}, bf16[2,3,96,1152]{3,2,1,0:T(8,128)(2,1)S(1)}, u32[]{:S(2)}, u32[]{:S(2)}) collective-permute-start(bf16[2,3,96,1152]{3,2,1,0:T(8,128)(2,1)S(1)} %pad_maximum_fusion.11), channel_id=1, source_target_pairs={{0,16},{4,12},{8,24},{12,4},{16,0},{20,28},{24,8},{28,20},{1,17},{... | collective-permute-start | bytes 3981320 | tf_op jit(solution)/shard_map/ppermute | solution.py:79
  712.1 13.6 %collective-permute-start.54 = (bf16[2,2,144,1152]{3,2,0,1:T(8,128)(2,1)S(1)}, bf16[2,2,144,1152]{3,2,0,1:T(8,128)(2,1)S(1)}, u32[]{:S(2)}, u32[]{:S(2)}) collective-permute-start(bf16[2,2,144,1152]{3,2,0,1:T(8,128)(2,1)S(1)} %pad_maximum_fusion.12), channel_id=1, source_target_pairs={{0,4},{4,0},{8,12},{12,8},{16,20},{20,16},{24,28},{28,24},{1,5},{5... | collective-permute-start | bytes 3981320 | tf_op jit(solution)/shard_map/ppermute | solution.py:42
  725.7 22.8 %collective-permute-start.57 = (bf16[2,2,3,96,1152]{4,3,2,0,1:T(8,128)(2,1)}, bf16[2,2,3,96,1152]{4,3,2,0,1:T(8,128)(2,1)}, u32[]{:S(2)}, u32[]{:S(2)}) collective-permute-start(bf16[2,2,3,96,1152]{4,3,2,0,1:T(8,128)(2,1)} %pad_maximum_fusion.4), channel_id=1, source_target_pairs={{0,4},{4,0},{8,12},{12,8},{16,20},{20,16},{24,28},{28,24},{1,5},{5... | collective-permute-start | bytes 7962632 | tf_op jit(solution)/shard_map/ppermute | solution.py:42
  729.9 16.0 %collective-permute-start.55 = (bf16[2,128,1152]{2,1,0:T(8,128)(2,1)}, bf16[2,128,1152]{2,1,0:T(8,128)(2,1)}, u32[]{:S(2)}, u32[]{:S(2)}) collective-permute-start(bf16[2,128,1152]{2,1,0:T(8,128)(2,1)} %pad_maximum_fusion.19), channel_id=1, source_target_pairs={{0,16},{4,12},{8,24},{12,4},{16,0},{20,28},{24,8},{28,20},{1,17},{... | collective-permute-start | bytes 1769480 | tf_op jit(solution)/shard_map/ppermute | solution.py:79
  752.9 11.3 %collective-permute-start.59 = (bf16[2,2,128,1152]{3,2,0,1:T(8,128)(2,1)S(1)}, bf16[2,2,128,1152]{3,2,0,1:T(8,128)(2,1)S(1)}, u32[]{:S(2)}, u32[]{:S(2)}) collective-permute-start(bf16[2,2,128,1152]{3,2,0,1:T(8,128)(2,1)S(1)} %copy-done.27), channel_id=1, source_target_pairs={{0,4},{4,0},{8,12},{12,8},{16,20},{20,16},{24,28},{28,24},{1,5},{5... | collective-permute-start | bytes 3538952 | tf_op jit(solution)/shard_map/ppermute | solution.py:42
  (144 other events, 1602.2 us)
